TPU v7x, 256 devices: a whole 4x4x8 slice. The times are simulated.
256 devices in a mesh: row: 32 (over y_lo, z, core), col: 8 (over x, y_hi).
Axes of the slice: x: 4, y: 4 (y_hi: 2, y_lo: 2; y = y_hi * 2 + y_lo), z: 8, core: 2. Of those that a mesh axis runs over, the one named last changes fastest.
Arguments:
- features: bfloat16 [1024, 1024, 64], P('row', 'col'), may hold values from -6 to 6
- conv_weight: bfloat16 [3, 3, 64, 64], replicated, may hold values from -0.25 to 0.25
- head_weight: bfloat16 [64, 37], replicated, may hold values from -8 to 8
- head_bias: float32 [37], replicated, may hold values from -4 to 4
- labels: int32 [1024, 1024], P('row', 'col'), may hold values from 0 to 36
- valid: int32 [1024, 1024], P('row', 'col'), may hold values 0 or 1
Outputs:
- loss: float32 [], replicated
- grad_features: bfloat16 [1024, 1024, 64], P('row', 'col')
- conv_grad: float32 [3, 3, 64, 64], replicated
- head_grad: float32 [64, 37], replicated
- bias_grad: float32 [37], replicated
All inputs are finite; a program needn't handle non-finite values. No bound on the sum of `valid` on one device may be relied on, other than what follows from the above.
Results may differ from a plain program's by a relative error of at most 0.0035.
The roundings to bfloat16 on the way count: a program that leaves them out, or rounds other values in their place, can miss the bound.
Values may be sent and summed in bfloat16 or wider, within the bound.
No kernel may reach another device: no remote copies, remote signals or barrier semaphores. Data moves between devices by JAX's collectives and lax.ppermute only.
A program may use at most 64 MiB of HBM per device.

v0:
```python
import jax
import jax.numpy as jnp
from jax import lax
from jax.sharding import PartitionSpec as P

DILATION_STEP = 8


def padded(block, sides, width):
    for axis, dim in sides:
        count = lax.axis_size(axis)
        forward = [(i, i + 1) for i in range(count - 1)]
        backward = [(target, source) for source, target in forward]
        low = lax.ppermute(
            lax.slice_in_dim(block, block.shape[dim] - width, None, axis=dim), axis, forward
        )
        high = lax.ppermute(lax.slice_in_dim(block, 0, width, axis=dim), axis, backward)
        block = jnp.concatenate([low, block, high], axis=dim)
    return block


def taps_product(padded_input, weight, row_span, column_span, flip):
    width = padded_input.shape[-1]
    total = jnp.zeros((row_span * column_span, weight.shape[-1]), jnp.float32)
    for kernel_row in range(3):
        for kernel_column in range(3):
            row_offset = 2 - kernel_row if flip else kernel_row
            column_offset = 2 - kernel_column if flip else kernel_column
            input_window = padded_input[
                row_offset * DILATION_STEP : row_offset * DILATION_STEP + row_span,
                column_offset * DILATION_STEP : column_offset * DILATION_STEP + column_span,
            ]
            kernel = (
                weight[kernel_row, kernel_column].T if flip else weight[kernel_row, kernel_column]
            )
            total = total + jnp.dot(
                input_window.reshape(-1, width), kernel, preferred_element_type=jnp.float32
            )
    return total.reshape(row_span, column_span, -1)


def widen(output_patch):
    return padded(output_patch, (("row", 0), ("col", 1)), DILATION_STEP)


def reorder(settled, row_span, column_span):
    nrow = lax.axis_size("row")
    ncol = lax.axis_size("col")
    group = nrow // ncol
    part = row_span // ncol
    feat = settled.shape[-1]
    order = (
        settled.reshape(ncol, group, part, row_span, feat)
        .transpose(1, 0, 2, 3, 4)
        .reshape(column_span, row_span, feat)
    )
    return jnp.swapaxes(order, 0, 1)


def mirror_logits(output_patch):
    row_span, column_span = (output_patch.shape[0], output_patch.shape[1])
    spread = lax.all_to_all(
        lax.all_to_all(output_patch, "col", split_axis=0, concat_axis=1, tiled=True),
        "row",
        split_axis=1,
        concat_axis=0,
        tiled=True,
    )
    settled = lax.all_to_all(spread, "col", split_axis=0, concat_axis=0, tiled=True)
    return reorder(settled, row_span, column_span)


def mirror_grads(output_patch):
    row_span, column_span = (output_patch.shape[0], output_patch.shape[1])
    spread = lax.all_to_all(
        lax.all_to_all(output_patch, "col", split_axis=0, concat_axis=1, tiled=True),
        "row",
        split_axis=1,
        concat_axis=0,
        tiled=True,
    )
    settled = lax.all_to_all(spread, "col", split_axis=0, concat_axis=0, tiled=True)
    return reorder(settled, row_span, column_span)


def per_device(features, conv_weight, head_weight, head_bias, labels, valid):
    row_span, column_span, chans = features.shape
    bins = head_weight.shape[1]
    feat32 = features.astype(jnp.float32)
    activation = jax.nn.elu(feat32).astype(jnp.bfloat16)
    padded_input = widen(activation)
    conv_out = taps_product(padded_input, conv_weight, row_span, column_span, False)
    mixed = (feat32 + conv_out).astype(jnp.bfloat16)
    flat = mixed.reshape(-1, chans)
    logits = (jnp.dot(flat, head_weight, preferred_element_type=jnp.float32) + head_bias).reshape(
        row_span, column_span, bins
    )
    mirrored = mirror_logits(logits)
    sym = 0.5 * (logits + mirrored)
    lse = jax.nn.logsumexp(sym, axis=-1)
    bin_ids = jnp.arange(bins, dtype=jnp.int32)
    onehot = (labels[..., None] == bin_ids).astype(jnp.float32)
    picked = jnp.sum(sym * onehot, axis=-1)
    maskf = valid.astype(jnp.float32)
    loss_sum, valid_sum = lax.psum(
        (jnp.sum(maskf * (lse - picked)), jnp.sum(maskf)), ("row", "col")
    )
    count = jnp.maximum(valid_sum, 1.0)
    loss = loss_sum / count
    prob = jnp.exp(sym - lse[..., None])
    grad_cells = maskf[..., None] * (prob - onehot) / count
    grad_logits = 0.5 * (grad_cells + mirror_grads(grad_cells))
    glflat = grad_logits.reshape(-1, bins)
    head_part = jnp.dot(flat.astype(jnp.float32).T, glflat, precision=lax.Precision.HIGHEST)
    bias_part = jnp.sum(glflat, axis=0)
    grad_mixed = jnp.dot(
        glflat, head_weight.astype(jnp.float32).T, precision=lax.Precision.HIGHEST
    ).reshape(row_span, column_span, chans)
    lower_gradient = grad_mixed.astype(jnp.bfloat16)
    grad_padded = widen(lower_gradient)
    back = taps_product(grad_padded, conv_weight, row_span, column_span, True)
    slope = jnp.where(feat32 > 0, 1.0, jnp.exp(feat32))
    grad_features = (grad_mixed + slope * back).astype(jnp.bfloat16)
    lower = lower_gradient.reshape(-1, chans)
    parts = []
    for kernel_row in range(3):
        for kernel_column in range(3):
            input_window = padded_input[
                kernel_row * DILATION_STEP : kernel_row * DILATION_STEP + row_span,
                kernel_column * DILATION_STEP : kernel_column * DILATION_STEP + column_span,
            ].reshape(-1, chans)
            parts.append(jnp.dot(input_window.T, lower, preferred_element_type=jnp.float32))
    kernel_part = jnp.stack(parts).reshape(3, 3, chans, chans)
    conv_grad, head_grad, bias_grad = lax.psum((kernel_part, head_part, bias_part), ("row", "col"))
    return (loss, grad_features, conv_grad, head_grad, bias_grad)


def solution(mesh):
    placed = (P("row", "col", None), P(), P(), P(), P("row", "col"), P("row", "col"))
    return jax.shard_map(
        per_device,
        mesh=mesh,
        in_specs=placed,
        out_specs=(P(), P("row", "col", None), P(), P(), P()),
        check_vma=False,
    )
```

profile of v0, /device:TPU:24, one launch (start us, length us, event | category | flops | bytes accessed | tf_op | source)
XLA Modules:
  0.0 660.5 jit_solution(2215787454808522010)
XLA Ops:
  8.7 1.9 collective-permute-start
  10.6 7.4 %collective-permute-start.1 = (bf16[8,128,64]{1,2,0:T(8,128)(2,1)S(1)}, bf16[8,128,64]{1,2,0:T(8,128)(2,1)S(1)}, u32[]{:S(2)}, u32[]{:S(2)}) collective-permute-start(bf16[8,128,64]{1,2,0:T(8,128)(2,1)S(1)} %get-tuple-element.44), channel_id=1, source_target_pairs={{8,0},{16,8},{24,16},{32,24},{40,32},{48,40},{56,48},{64,56},{72,6... | collective-permute-start | bytes 393224 | tf_op jit(solution)/shard_map/ppermute | solution.py:17
  18.7 1.8 collective-permute-done.1
  22.2 3.8 collective-permute-start.2
  26.0 3.6 collective-permute-start.3
  30.5 4.7 collective-permute-done.3
  35.9 1.7 pad_maximum_fusion
  44.4 15.0 %all_to_all.82 = f32[32,128,37]{1,2,0:T(8,128)S(1)} all-to-all(f32[32,128,37]{1,2,0:T(8,128)S(1)} %copy.140), channel_id=1, replica_groups=mesh['row'=32,'col'=8] {'col'}, dimensions={0} | all-to-all | bytes 1212416 | tf_op jit(solution)/shard_map/all_to_all | solution.py:63
  60.4 1.8 copy.142
  62.2 3.9 reshape.157
  66.0 28.6 %all_to_all.83 = f32[32,1,4736]{2,1,0:T(1,128)S(1)} all-to-all(f32[32,1,4736]{2,1,0:T(1,128)} %reshape.157), channel_id=1, replica_groups=mesh['row'=32,'col'=8] {'row'}, dimensions={0} | all-to-all | bytes 1212416 | tf_op jit(solution)/shard_map/all_to_all | solution.py:62
  95.2 3.0 reduce.1
  98.2 4.2 reshape.158
  104.1 4.4 reshape.159
  108.4 5.9 all-to-all-start.2
  115.3 2.9 copy.146
  118.2 4.7 all-to-all-done.2
  122.9 3.1 reduce.2
  126.0 3.6 reshape.160
  132.4 2.6 select_reduce_fusion
  135.7 73.2 %psum.36 = f32[]{:T(128)} all-reduce(f32[]{:T(128)} %get-tuple-element.7), channel_id=1, replica_groups=mesh['row'=32,'col'=8] {'row','col'}, use_global_device_ids=true, to_apply=%region_6.7 | all-reduce | flops 1 | bytes 8 | tf_op jit(solution)/shard_map/psum | solution.py:105
  209.6 4.0 multiply_divide_fusion
  213.6 3.5 copy.148
  217.1 16.3 %all_to_all.84 = f32[32,128,37]{1,2,0:T(8,128)} all-to-all(f32[32,128,37]{1,2,0:T(8,128)} %copy.148), channel_id=1, replica_groups=mesh['row'=32,'col'=8] {'col'}, dimensions={0} | all-to-all | bytes 1212416 | tf_op jit(solution)/shard_map/all_to_all | solution.py:76
  233.4 2.7 copy.172
  236.1 4.7 reshape.161
  240.8 25.3 %all_to_all.85 = f32[32,1,4736]{2,1,0:T(1,128)} all-to-all(f32[32,1,4736]{2,1,0:T(1,128)} %reshape.161), channel_id=1, replica_groups=mesh['row'=32,'col'=8] {'row'}, dimensions={0} | all-to-all | bytes 1212416 | tf_op jit(solution)/shard_map/all_to_all | solution.py:75
  266.0 4.0 reduce.3
  270.0 5.6 reshape.162
  275.6 3.2 copy.174
  278.7 4.3 reshape.163
  283.0 15.4 %all_to_all.86 = f32[8,1,18944]{2,1,0:T(1,128)} all-to-all(f32[8,1,18944]{2,1,0:T(1,128)} %reshape.163), channel_id=1, replica_groups=mesh['row'=32,'col'=8] {'col'}, dimensions={0} | all-to-all | bytes 1212416 | tf_op jit(solution)/shard_map/all_to_all | solution.py:82
  298.5 4.0 reduce.4
  302.5 5.0 reshape.164
  307.5 1.8 copy.153
  309.3 3.2 fusion.117
  312.5 2.8 copy.154
  315.9 1.6 fusion.123
  318.2 2.0 fusion.12
  320.1 74.3 %all-reduce = (f32[]{:T(128)}, f32[64,37]{0,1:T(8,128)}, f32[37]{0:T(128)}) all-reduce(f32[]{:T(128)} %get-tuple-element.8, f32[64,37]{0,1:T(8,128)S(1)} %convolution_bitcast_fusion.9, f32[37]{0:T(128)S(1)} %get-tuple-element.12), channel_id=1, replica_groups=mesh['row'=32,'col'=8] {'row','col'}, use_global_device_ids=true, to_apply=%region_4.5 | all-reduce | flops 2406 | bytes 19248 | tf_op jit(solution)/shard_map/psum | solution.py:105
  395.2 2.1 collective-permute-start.4
  397.2 5.8 collective-permute-start.5
  414.7 3.3 collective-permute-start.6
  418.0 5.1 collective-permute-start.7
  423.2 1.8 fusion.65
  428.5 2.8 maximum_maximum_fusion.1
  436.9 213.7 %all-reduce.3.cloned.1.call-done = f32[3,3,64,64]{3,2,1,0:T(8,128)} async-done(((f32[3,3,64,64]{3,2,1,0:T(8,128)}), f32[3,3,64,64]{3,2,1,0:T(8,128)}) %all-reduce.3.cloned.1.call-update) | async-done | bytes 147472 | tf_op jit(solution)/shard_map/psum | solution.py:134
  650.6 1.7 copy.290
  (114 shorter events, 41.6 us)
Async XLA Ops:
  7.2 35.6 %copy-start = (bf16[64,37]{0,1:T(8,128)(2,1)S(1)}, bf16[64,37]{0,1:T(8,128)(2,1)}, u32[]{:S(2)}) copy-start(bf16[64,37]{0,1:T(8,128)(2,1)} %param.8) | copy-start | bytes 14212
  8.7 10.0 %collective-permute-start = (bf16[8,128,64]{1,2,0:T(8,128)(2,1)S(1)}, bf16[8,128,64]{1,2,0:T(8,128)(2,1)S(1)}, u32[]{:S(2)}, u32[]{:S(2)}) collective-permute-start(bf16[8,128,64]{1,2,0:T(8,128)(2,1)S(1)} %get-tuple-element.43), channel_id=1, source_target_pairs={{0,8},{8,16},{16,24},{24,32},{32,40},{40,48},{48,56},{56,64},{64,7... | collective-permute-start | bytes 393224 | tf_op jit(solution)/shard_map/ppermute | solution.py:14
  10.6 9.9 %collective-permute-start.1 = (bf16[8,128,64]{1,2,0:T(8,128)(2,1)S(1)}, bf16[8,128,64]{1,2,0:T(8,128)(2,1)S(1)}, u32[]{:S(2)}, u32[]{:S(2)}) collective-permute-start(bf16[8,128,64]{1,2,0:T(8,128)(2,1)S(1)} %get-tuple-element.44), channel_id=1, source_target_pairs={{8,0},{16,8},{24,16},{32,24},{40,32},{48,40},{56,48},{64,56},{72,6... | collective-permute-start | bytes 393224 | tf_op jit(solution)/shard_map/ppermute | solution.py:17
  22.2 13.3 %collective-permute-start.2 = (bf16[48,8,64]{2,1,0:T(8,128)(2,1)S(1)}, bf16[48,8,64]{2,1,0:T(8,128)(2,1)S(1)}, u32[]{:S(2)}, u32[]{:S(2)}) collective-permute-start(bf16[48,8,64]{2,1,0:T(8,128)(2,1)S(1)} %copy.125), channel_id=1, source_target_pairs={{0,1},{1,2},{2,3},{3,4},{4,5},{5,6},{6,7},{8,9},{9,10},{10,11},{11... | collective-permute-start | bytes 147464 | tf_op jit(solution)/shard_map/ppermute | solution.py:14
  26.0 9.1 %collective-permute-start.3 = (bf16[48,8,64]{2,1,0:T(8,128)(2,1)}, bf16[48,8,64]{2,1,0:T(8,128)(2,1)S(1)}, u32[]{:S(2)}, u32[]{:S(2)}) collective-permute-start(bf16[48,8,64]{2,1,0:T(8,128)(2,1)} %copy.129), channel_id=1, source_target_pairs={{1,0},{2,1},{3,2},{4,3},{5,4},{6,5},{7,6},{9,8},{10,9},{11,10},{12... | collective-permute-start | bytes 147464 | tf_op jit(solution)/shard_map/ppermute | solution.py:17
  37.6 1.2 copy-start.5
  37.6 1.6 copy-start.7
  37.6 1.6 copy-start.14
  41.0 1.0 copy-start.12
  42.0 1.0 copy-start.4
  42.0 1.0 copy-start.21
  43.1 1.0 copy-start.1
  44.1 16.3 %copy-start.9 = (f32[32,128,37]{1,0,2:T(8,128)}, f32[32,128,37]{1,0,2:T(8,128)S(1)}, u32[]{:S(2)}) copy-start(f32[32,128,37]{1,0,2:T(8,128)S(1)} %slice_bitcast_fusion) | copy-start | bytes 1818628
  104.1 10.3 %copy-start.19 = (s32[32,128]{1,0:T(8,128)S(1)}, s32[32,128]{1,0:T(8,128)}, u32[]{:S(2)}) copy-start(s32[32,128]{1,0:T(8,128)} %param.10) | copy-start | bytes 49156
  104.1 10.4 %copy-start.20 = (s32[32,128]{1,0:T(8,128)S(1)}, s32[32,128]{1,0:T(8,128)}, u32[]{:S(2)}) copy-start(s32[32,128]{1,0:T(8,128)} %param.11) | copy-start | bytes 49156
  104.1 11.2 %copy-start.10 = (f32[32,128,37]{1,0,2:T(8,128)S(1)}, f32[32,128,37]{1,0,2:T(8,128)}, u32[]{:S(2)}) copy-start(f32[32,128,37]{1,0,2:T(8,128)} %copy-done.9) | copy-start | bytes 1818628
  108.4 14.5 %all-to-all-start.2 = ((f32[8,1,18944]{2,1,0:T(1,128)}), f32[8,1,18944]{2,1,0:T(1,128)S(1)}, u32[]{:S(2)}, u32[]{:S(2)}) async-start(f32[8,1,18944]{2,1,0:T(1,128)} %reshape.159), calls=%async_computation.2 | async-start | bytes 1212416 | tf_op jit(solution)/shard_map/all_to_all | solution.py:69
  114.4 536.2 %all-reduce.3.cloned.1.call-start = ((), (), s32[]{:S(2)}) async-start(), calls=%async_computation.6 | async-start | bytes 589824 | tf_op jit(solution)/shard_map/psum | solution.py:134
  114.6 8.3 %copy-start.17 = (s32[32,128]{0,1:T(8,128)}, s32[32,128]{0,1:T(8,128)S(1)}, u32[]{:S(2)}) copy-start(s32[32,128]{0,1:T(8,128)S(1)} %copy.124) | copy-start | bytes 49156
  129.6 1.6 copy-start.3
  131.7 3.3 copy-start.18
  307.5 1.8 copy-start.16
  312.5 2.8 copy-start.2
  317.5 86.4 %copy-start.6 = (bf16[48,136,64]{1,2,0:T(8,128)(2,1)S(1)}, bf16[48,136,64]{1,2,0:T(8,128)(2,1)}, u32[]{:S(2)}) copy-start(bf16[48,136,64]{1,2,0:T(8,128)(2,1)} %copy-done.5) | copy-start | bytes 2506756
  395.2 9.7 %copy-start.8 = (bf16[48,136,64]{1,2,0:T(8,128)(2,1)S(1)}, bf16[48,136,64]{1,2,0:T(8,128)(2,1)}, u32[]{:S(2)}) copy-start(bf16[48,136,64]{1,2,0:T(8,128)(2,1)} %copy-done.7) | copy-start | bytes 2506756
  395.2 15.5 %collective-permute-start.4 = (bf16[8,128,64]{1,2,0:T(8,128)(2,1)}, bf16[8,128,64]{1,2,0:T(8,128)(2,1)S(1)}, u32[]{:S(2)}, u32[]{:S(2)}) collective-permute-start(bf16[8,128,64]{1,2,0:T(8,128)(2,1)} %get-tuple-element.37), channel_id=1, source_target_pairs={{0,8},{8,16},{16,24},{24,32},{32,40},{40,48},{48,56},{56,64},{64,7... | collective-permute-start | bytes 393224 | tf_op jit(solution)/shard_map/ppermute | solution.py:14
  397.2 13.5 %collective-permute-start.5 = (bf16[8,128,64]{1,2,0:T(8,128)(2,1)}, bf16[8,128,64]{1,2,0:T(8,128)(2,1)}, u32[]{:S(2)}, u32[]{:S(2)}) collective-permute-start(bf16[8,128,64]{1,2,0:T(8,128)(2,1)} %get-tuple-element.38), channel_id=1, source_target_pairs={{8,0},{16,8},{24,16},{32,24},{40,32},{48,40},{56,48},{64,56},{72,6... | collective-permute-start | bytes 393224 | tf_op jit(solution)/shard_map/ppermute | solution.py:17
  414.7 12.5 %collective-permute-start.6 = (bf16[48,8,64]{2,1,0:T(8,128)(2,1)S(1)}, bf16[48,8,64]{2,1,0:T(8,128)(2,1)S(1)}, u32[]{:S(2)}, u32[]{:S(2)}) collective-permute-start(bf16[48,8,64]{2,1,0:T(8,128)(2,1)S(1)} %copy.155), channel_id=1, source_target_pairs={{1,0},{2,1},{3,2},{4,3},{5,4},{6,5},{7,6},{9,8},{10,9},{11,10},{12... | collective-permute-start | bytes 147464 | tf_op jit(solution)/shard_map/ppermute | solution.py:17
  418.0 8.0 %collective-permute-start.7 = (bf16[48,8,64]{2,1,0:T(8,128)(2,1)S(1)}, bf16[48,8,64]{2,1,0:T(8,128)(2,1)S(1)}, u32[]{:S(2)}, u32[]{:S(2)}) collective-permute-start(bf16[48,8,64]{2,1,0:T(8,128)(2,1)S(1)} %copy.159), channel_id=1, source_target_pairs={{0,1},{1,2},{2,3},{3,4},{4,5},{5,6},{6,7},{8,9},{9,10},{10,11},{11... | collective-permute-start | bytes 147464 | tf_op jit(solution)/shard_map/ppermute | solution.py:14
  431.7 0.9 copy-start.15
  431.7 1.2 copy-start.13
  434.6 1.2 copy-start.11
Sparse Core Ops, SparseCore 0:
  410.8 239.7 all-reduce.2
where the time goes:
time: 671 us; the launch traced here: 660 us
  blocking collectives  248 us (37%)
  waiting for transfers between devices  227 us (34%)
  local copies, waits for them, and re-layouts  74.7 us (11%)
  starting transfers between devices  38.8 us (6%)
  other arithmetic  37.3 us (6%)
  matrix products  17.7 us (3%)
  between operations  17.2 us (3%)
    psum x1, waiting for transfers between devices, per_device(): lax.psum((kernel_part, head_part, bias_part), ('row', 'col'))  214 us
    psum x2, blocking collectives, per_device(): lax.psum((jnp.sum(maskf * (lse - picked)), jnp.sum(maskf)), ('row', 'col'))  148 us
    unnamed x59, local copies, waits for them, and re-layouts  43.9 us
    all_to_all x1, blocking collectives, mirror_logits(): lax.all_to_all(lax.all_to_all(output_patch, 'col', split_axis=0, concat_a...  28.6 us
    all_to_all x1, blocking collectives, mirror_grads(): lax.all_to_all(lax.all_to_all(output_patch, 'col', split_axis=0, concat_a...  25.3 us
    ppermute x4, starting transfers between devices, padded(): lax.ppermute(lax.slice_in_dim(block, 0, width, axis=dim), axis, backward)  20 us
    all_to_all x1, blocking collectives, mirror_grads(): lax.all_to_all(output_patch, 'col', split_axis=0, concat_axis=1, tiled=True)  16.3 us
    all_to_all x1, blocking collectives, mirror_grads(): lax.all_to_all(spread, 'col', split_axis=0, concat_axis=0, tiled=True)  15.4 us
  transfers between devices with their start and end apart: 10, of which 6 were waited for; matrix products, arithmetic and copies ran while one was open for 4% of the time, Pallas kernels for 0%

commit v1 on v0

v1 whole, which is shorter than its diff:
```python
import jax
import jax.numpy as jnp
from jax import lax
from jax.sharding import PartitionSpec as P

DILATION_STEP = 8
GRID = ("row", "col")


def send(block, target):
    nrow, ncol = lax.axis_size("row"), lax.axis_size("col")
    pairs = []
    for r in range(nrow):
        for c in range(ncol):
            r2, c2 = target(r, c)
            pairs.append((r * ncol + c, r2 * ncol + c2))
    return lax.ppermute(block, GRID, pairs)


def padded(block, sides, width):
    for axis, dim in sides:
        count = lax.axis_size(axis)
        forward = [(i, i + 1) for i in range(count - 1)]
        backward = [(target, source) for source, target in forward]
        low = lax.ppermute(
            lax.slice_in_dim(block, block.shape[dim] - width, None, axis=dim), axis, forward
        )
        high = lax.ppermute(lax.slice_in_dim(block, 0, width, axis=dim), axis, backward)
        block = jnp.concatenate([low, block, high], axis=dim)
    return block


def widen(block):
    return padded(block, (("row", 0), ("col", 1)), DILATION_STEP)


def taps_product(padded_input, weight, row_span, column_span, flip):
    width = padded_input.shape[-1]
    total = jnp.zeros((row_span * column_span, weight.shape[-1]), jnp.float32)
    for kernel_row in range(3):
        for kernel_column in range(3):
            row_offset = 2 - kernel_row if flip else kernel_row
            column_offset = 2 - kernel_column if flip else kernel_column
            window = padded_input[
                row_offset * DILATION_STEP : row_offset * DILATION_STEP + row_span,
                column_offset * DILATION_STEP : column_offset * DILATION_STEP + column_span,
            ]
            kernel = (
                weight[kernel_row, kernel_column].T if flip else weight[kernel_row, kernel_column]
            )
            total = total + jnp.dot(
                window.reshape(-1, width), kernel, preferred_element_type=jnp.float32
            )
    return total.reshape(row_span, column_span, -1)


def mirror(mixed, labels, valid):
    rows, cols, chans = mixed.shape
    parts = cols // rows
    place = lax.axis_index("row") % parts
    lab = labels.astype(jnp.bfloat16).reshape(rows, parts, rows).swapaxes(0, 1)
    val = valid.astype(jnp.bfloat16).reshape(rows, parts, rows).swapaxes(0, 1)
    mix = mixed.reshape(rows, parts, rows, chans).swapaxes(0, 1)
    cells = rows * rows
    split = cells * chans // 128
    load = jnp.concatenate(
        [
            mix.reshape(parts, split, 128),
            lab.reshape(parts, cells // 128, 128),
            val.reshape(parts, cells // 128, 128),
        ],
        axis=1,
    )
    got = []
    for step in range(parts):
        block = lax.dynamic_index_in_dim(load, place ^ step, 0, keepdims=False)
        got.append(send(block, lambda r, c: (parts * c + (r % parts ^ step), r // parts)))
    got = jnp.stack(got)
    got = jnp.stack(
        [lax.dynamic_index_in_dim(got, place ^ q, 0, keepdims=False) for q in range(parts)]
    )
    mix_t = got[:, :split].reshape(cols, rows, chans).swapaxes(0, 1)
    lab_t = got[:, split : split + cells // 128].reshape(cols, rows).T.astype(jnp.int32)
    val_t = got[:, split + cells // 128 :].reshape(cols, rows).T.astype(jnp.float32)
    return mix_t, lab_t, val_t


def partners(stage):
    if stage < 2:
        return lambda m: lambda r, c: (r ^ (m << (2 * stage)), c)
    if stage == 2:
        return lambda m: lambda r, c: (r ^ ((m & 1) << 4), c ^ (m >> 1))
    return lambda m: lambda r, c: (r, c ^ (m << 1))


def total_small(value):
    for bit in range(5):
        value = value + send(value, lambda r, c: (r ^ (1 << bit), c))
    for bit in range(3):
        value = value + send(value, lambda r, c: (r, c ^ (1 << bit)))
    return value


def total_rows(block):
    quarter = block.shape[0] // 4
    place = lax.axis_index("row") % 4
    near = partners(0)
    cut = block.reshape(4, quarter, block.shape[1])
    pick = lambda m: lax.dynamic_index_in_dim(cut, place ^ m, 0, keepdims=False)
    part = (pick(0) + send(pick(1), near(1))) + (send(pick(2), near(2)) + send(pick(3), near(3)))
    for stage in (1, 2, 3):
        to = partners(stage)
        part = (part + send(part, to(1))) + (send(part, to(2)) + send(part, to(3)))
    got = jnp.stack([part] + [send(part, near(m)) for m in (1, 2, 3)])
    return jnp.concatenate(
        [lax.dynamic_index_in_dim(got, place ^ q, 0, keepdims=False) for q in range(4)]
    )


def per_device(features, conv_weight, head_weight, head_bias, labels, valid):
    rows, cols, chans = features.shape
    bins = head_weight.shape[1]
    maskf = valid.astype(jnp.float32)
    count = jnp.maximum(total_small(jnp.full((8, 128), jnp.sum(maskf)))[0, 0], 1.0)
    feat32 = features.astype(jnp.float32)
    activation = jax.nn.elu(feat32).astype(jnp.bfloat16)
    padded_input = widen(activation)
    conv_out = taps_product(padded_input, conv_weight, rows, cols, False)
    mixed = (feat32 + conv_out).astype(jnp.bfloat16)
    flat = mixed.reshape(-1, chans)
    mixed_t, labels_t, mask_t = mirror(mixed, labels, valid)
    logits = jnp.dot(flat, head_weight, preferred_element_type=jnp.float32) + head_bias
    logits_t = (
        jnp.dot(mixed_t.reshape(-1, chans), head_weight, preferred_element_type=jnp.float32)
        + head_bias
    )
    sym = (0.5 * (logits + logits_t)).reshape(rows, cols, bins)
    lse = jax.nn.logsumexp(sym, axis=-1)
    bin_ids = jnp.arange(bins, dtype=jnp.int32)
    onehot = (labels[..., None] == bin_ids).astype(jnp.float32)
    onehot_t = (labels_t[..., None] == bin_ids).astype(jnp.float32)
    picked = jnp.sum(sym * onehot, axis=-1)
    loss_part = jnp.sum(maskf * (lse - picked))
    prob = jnp.exp(sym - lse[..., None])
    own = maskf[..., None] * (prob - onehot) / count
    other = mask_t[..., None] * (prob - onehot_t) / count
    glflat = (0.5 * (own + other)).reshape(-1, bins)
    head_part = jnp.dot(flat.astype(jnp.float32).T, glflat, precision=lax.Precision.HIGHEST)
    bias_part = jnp.sum(glflat, axis=0)
    grad_mixed = jnp.dot(
        glflat, head_weight.astype(jnp.float32).T, precision=lax.Precision.HIGHEST
    ).reshape(rows, cols, chans)
    lower_gradient = grad_mixed.astype(jnp.bfloat16)
    lower = lower_gradient.reshape(-1, chans)
    parts = []
    for kernel_row in range(3):
        for kernel_column in range(3):
            window = padded_input[
                kernel_row * DILATION_STEP : kernel_row * DILATION_STEP + rows,
                kernel_column * DILATION_STEP : kernel_column * DILATION_STEP + cols,
            ].reshape(-1, chans)
            parts.append(jnp.dot(window.T, lower, preferred_element_type=jnp.float32))
    flat_sums = jnp.concatenate(
        [
            jnp.stack(parts).reshape(-1),
            head_part.reshape(-1),
            bias_part,
            loss_part.reshape(1),
        ]
    )
    length = flat_sums.shape[0]
    lines = -(-length // 4096) * 32
    sums = total_rows(jnp.pad(flat_sums, (0, lines * 128 - length)).reshape(lines, 128)).reshape(-1)
    n_conv, n_head = 9 * chans * chans, chans * bins
    conv_grad = sums[:n_conv].reshape(3, 3, chans, chans)
    head_grad = sums[n_conv : n_conv + n_head].reshape(chans, bins)
    bias_grad = sums[n_conv + n_head : n_conv + n_head + bins]
    loss = sums[n_conv + n_head + bins] / count
    grad_padded = widen(lower_gradient)
    back = taps_product(grad_padded, conv_weight, rows, cols, True)
    slope = jnp.where(feat32 > 0, 1.0, jnp.exp(feat32))
    grad_features = (grad_mixed + slope * back).astype(jnp.bfloat16)
    return (loss, grad_features, conv_grad, head_grad, bias_grad)


def solution(mesh):
    placed = (P("row", "col", None), P(), P(), P(), P("row", "col"), P("row", "col"))
    return jax.shard_map(
        per_device,
        mesh=mesh,
        in_specs=placed,
        out_specs=(P(), P("row", "col", None), P(), P(), P()),
        check_vma=False,
    )
```

time: 671 us -> 202 us (0.30); the launches traced: 660 us -> 200 us
  blocking collectives: 248 us -> 0 us
  waiting for transfers between devices: 227 us -> 61.5 us
  local copies, waits for them, and re-layouts: 74.7 us -> 31.8 us
  starting transfers between devices: 38.8 us -> 74.2 us
  other arithmetic: 37.3 us -> 13.5 us
  between operations: 17.2 us -> 4.1 us
    psum x1 -> x0, waiting for transfers between devices: 214 us -> none  [per_device(): lax.psum((kernel_part, head_part, bias_part), ('row', 'col'))]
    psum x2 -> x0, blocking collectives: 148 us -> none  [per_device(): lax.psum((jnp.sum(maskf * (lse - picked)), jnp.sum(maskf)), ('row', 'col'))]
    all_to_all x5 -> x0, blocking collectives: 101 us -> none  [the longest x1 28.6 us: mirror_logits(): lax.all_to_all(lax.all_to_all(output_patch, 'col', split_axis=0, concat_a...]
    ppermute x0 -> x27, waiting for transfers between devices: none -> 50.8 us  [send(): return lax.ppermute(block, GRID, pairs)]
    ppermute x0 -> x27, starting transfers between devices: none -> 44 us  [send(): return lax.ppermute(block, GRID, pairs)]
    unnamed x59 -> x70, local copies, waits for them, and re-layouts: 43.9 us -> 8.54 us
    all_to_all x4 -> x0, other arithmetic: 14.1 us -> none  [the longest x1 3.99 us: mirror_grads(): lax.all_to_all(lax.all_to_all(output_patch, 'col', split_axis=0, concat_a...]
    all_to_all x6 -> x0, local copies, waits for them, and re-layouts: 10.7 us -> none  [the longest x1 3.16 us: mirror_grads(): lax.all_to_all(lax.all_to_all(output_patch, 'col', split_axis=0, concat_a...]
  transfers between devices with their start and end apart: 10 -> 35, of which waited for: 6 -> 20; matrix products, arithmetic and copies ran while one was open for 4% -> 8% of each run, Pallas kernels for 0% -> 0%
where the time goes in v1:
time: 202 us; the launch traced here: 200 us
  starting transfers between devices  74.2 us (37%)
  waiting for transfers between devices  61.5 us (30%)
  local copies, waits for them, and re-layouts  31.8 us (16%)
  matrix products  15.3 us (8%)
  other arithmetic  13.5 us (7%)
  between operations  4.1 us (2%)
    ppermute x27, waiting for transfers between devices, send(): return lax.ppermute(block, GRID, pairs)  50.8 us
    ppermute x27, starting transfers between devices, send(): return lax.ppermute(block, GRID, pairs)  44 us
    ppermute x4, starting transfers between devices, padded(): lax.ppermute(lax.slice_in_dim(block, 0, width, axis=dim), axis, backward)  16.2 us
    ppermute x4, starting transfers between devices, padded(): lax.ppermute(lax.slice_in_dim(block, block.shape[dim] - width, None, axis...  14 us
    unnamed x70, local copies, waits for them, and re-layouts  8.54 us
    ppermute x4, waiting for transfers between devices, padded(): lax.ppermute(lax.slice_in_dim(block, block.shape[dim] - width, None, axis...  8.14 us
    dot_general x18, matrix products, taps_product(): jnp.dot(window.reshape(-1, width), kernel, preferred_element_type=jnp.flo...  5.58 us
    concatenate x4, other arithmetic, padded(): block = jnp.concatenate([low, block, high], axis=dim)  4.57 us
  transfers between devices with their start and end apart: 35, of which 20 were waited for; matrix products, arithmetic and copies ran while one was open for 8% of the time, Pallas kernels for 0%

profile of v1, /device:TPU:24, one launch (start us, length us, event | category | flops | bytes accessed | tf_op | source)
XLA Modules:
  0.0 200.5 jit_solution(1610447553075326543)
XLA Ops:
  0.7 1.5 fusion.144
  2.2 7.4 %collective-permute-start.1 = (bf16[8,128,64]{1,2,0:T(8,128)(2,1)S(1)}, bf16[8,128,64]{1,2,0:T(8,128)(2,1)S(1)}, u32[]{:S(2)}, u32[]{:S(2)}) collective-permute-start(bf16[8,128,64]{1,2,0:T(8,128)(2,1)S(1)} %get-tuple-element.66), channel_id=1, source_target_pairs={{8,0},{16,8},{24,16},{32,24},{40,32},{48,40},{56,48},{64,56},{72,6... | collective-permute-start | bytes 393224 | tf_op jit(solution)/shard_map/ppermute | solution.py:28
  9.6 1.9 collective-permute-start
  13.8 4.3 %collective-permute-done = bf16[8,128,64]{1,2,0:T(8,128)(2,1)S(1)} collective-permute-done((bf16[8,128,64]{1,2,0:T(8,128)(2,1)S(1)}, bf16[8,128,64]{1,2,0:T(8,128)(2,1)S(1)}, u32[]{:S(2)}, u32[]{:S(2)}) %collective-permute-start) | collective-permute-done | bytes 131104 | tf_op jit(solution)/shard_map/ppermute | solution.py:25
  18.9 2.9 %collective-permute-start.3 = (bf16[48,8,64]{2,1,0:T(8,128)(2,1)S(1)}, bf16[48,8,64]{2,1,0:T(8,128)(2,1)S(1)}, u32[]{:S(2)}, u32[]{:S(2)}) collective-permute-start(bf16[48,8,64]{2,1,0:T(8,128)(2,1)S(1)} %copy.84), channel_id=1, source_target_pairs={{1,0},{2,1},{3,2},{4,3},{5,4},{6,5},{7,6},{9,8},{10,9},{11,10},{12... | collective-permute-start | bytes 147464 | tf_op jit(solution)/shard_map/ppermute | solution.py:28
  22.0 5.4 %collective-permute-start.2 = (bf16[48,8,64]{2,1,0:T(8,128)(2,1)S(1)}, bf16[48,8,64]{2,1,0:T(8,128)(2,1)S(1)}, u32[]{:S(2)}, u32[]{:S(2)}) collective-permute-start(bf16[48,8,64]{2,1,0:T(8,128)(2,1)S(1)} %copy.80), channel_id=1, source_target_pairs={{0,1},{1,2},{2,3},{3,4},{4,5},{5,6},{6,7},{8,9},{9,10},{10,11},{11... | collective-permute-start | bytes 147464 | tf_op jit(solution)/shard_map/ppermute | solution.py:25
  31.3 2.7 %pad_maximum_fusion = (bf16[48,136,64]{1,2,0:T(8,128)(2,1)S(1)}, bf16[48,136,64]{1,2,0:T(8,128)(2,1)S(1)}) fusion(bf16[48,8,64]{1,2,0:T(8,128)(2,1)S(1)} %copy.85, bf16[8,128,64]{1,2,0:T(8,128)(2,1)S(1)} %collective-permute-done.1, bf16[32,128,64]{1,2,0:T(8,128)(2,1)S(1)} %get-tuple-element.64, bf16[8,128,64]{1,2,0:T(8,128)(2,1)} %copy-done.17, ...), kind=kLoop, calls=%fused_computation.27 | loop fusion | flops 6684672 | bytes 2555904 | tf_op jit(solution)/shard_map/concatenate | solution.py:29
  40.6 1.3 copy.95
  41.9 2.3 %copy.96 = bf16[4,32,32,64]{3,2,1,0:T(8,128)(2,1)} copy(bf16[4,32,32,64]{3,2,0,1:T(8,128)(2,1)} %bitcast.309) | data formatting | bytes 1048576 | tf_op jit(solution)/shard_map/transpose | solution.py:63
  44.3 1.8 reshape.198
  46.2 2.8 %collective-permute-start.7 = (bf16[528,128]{1,0:T(8,128)(2,1)S(1)}, bf16[528,128]{1,0:T(8,128)(2,1)S(1)}, u32[]{:S(2)}, u32[]{:S(2)}) collective-permute-start(bf16[528,128]{1,0:T(8,128)(2,1)S(1)} %get-tuple-element.54), channel_id=1, source_target_pairs={{0,24},{1,56},{2,88},{3,120},{4,152},{5,184},{6,216},{7,248},{8,16... | collective-permute-start | bytes 405512 | tf_op jit(solution)/shard_map/ppermute | solution.py:17
  49.5 3.6 %collective-permute-start.5 = (bf16[528,128]{1,0:T(8,128)(2,1)S(1)}, bf16[528,128]{1,0:T(8,128)(2,1)S(1)}, u32[]{:S(2)}, u32[]{:S(2)}) collective-permute-start(bf16[528,128]{1,0:T(8,128)(2,1)S(1)} %get-tuple-element.56), channel_id=1, source_target_pairs={{0,8},{1,40},{2,72},{3,104},{4,136},{5,168},{6,200},{7,232},{8,0},... | collective-permute-start | bytes 405512 | tf_op jit(solution)/shard_map/ppermute | solution.py:17
  53.1 10.5 %collective-permute-start.4 = (bf16[528,128]{1,0:T(8,128)(2,1)S(1)}, bf16[528,128]{1,0:T(8,128)(2,1)S(1)}, u32[]{:S(2)}, u32[]{:S(2)}) collective-permute-start(bf16[528,128]{1,0:T(8,128)(2,1)S(1)} %get-tuple-element.53), channel_id=1, source_target_pairs={{0,0},{1,32},{2,64},{3,96},{4,128},{5,160},{6,192},{7,224},{8,8},{... | collective-permute-start | bytes 405512 | tf_op jit(solution)/shard_map/ppermute | solution.py:17
  64.7 2.2 %collective-permute-done.6 = bf16[528,128]{1,0:T(8,128)(2,1)S(1)} collective-permute-done((bf16[528,128]{1,0:T(8,128)(2,1)S(1)}, bf16[528,128]{1,0:T(8,128)(2,1)S(1)}, u32[]{:S(2)}, u32[]{:S(2)}) %collective-permute-start.6) | collective-permute-done | bytes 135200 | tf_op jit(solution)/shard_map/ppermute | solution.py:17
  66.9 13.5 %collective-permute-done.5 = bf16[528,128]{1,0:T(8,128)(2,1)S(1)} collective-permute-done((bf16[528,128]{1,0:T(8,128)(2,1)S(1)}, bf16[528,128]{1,0:T(8,128)(2,1)S(1)}, u32[]{:S(2)}, u32[]{:S(2)}) %collective-permute-start.5) | collective-permute-done | bytes 135200 | tf_op jit(solution)/shard_map/ppermute | solution.py:17
  80.4 2.9 %collective-permute-done.4 = bf16[528,128]{1,0:T(8,128)(2,1)S(1)} collective-permute-done((bf16[528,128]{1,0:T(8,128)(2,1)S(1)}, bf16[528,128]{1,0:T(8,128)(2,1)S(1)}, u32[]{:S(2)}, u32[]{:S(2)}) %collective-permute-start.4) | collective-permute-done | bytes 135200 | tf_op jit(solution)/shard_map/ppermute | solution.py:17
  85.0 1.6 reshape.203
  86.7 2.3 %copy.99 = bf16[32,128,64]{1,0,2:T(8,128)(2,1)} copy(bf16[32,128,64]{2,0,1:T(8,128)(2,1)S(1)} %bitcast.308) | data formatting | bytes 1048576 | tf_op jit(solution)/shard_map/transpose | solution.py:82
  89.0 1.6 fusion.152
  94.1 3.6 %collective-permute-done.9 = f32[8,128]{1,0:T(8,128)S(1)} collective-permute-done((f32[8,128]{1,0:T(8,128)S(1)}, f32[8,128]{1,0:T(8,128)S(1)}, u32[]{:S(2)}, u32[]{:S(2)}) %collective-permute-start.9) | collective-permute-done | bytes 4128 | tf_op jit(solution)/shard_map/ppermute | solution.py:17
  98.5 4.5 %collective-permute-done.10 = f32[8,128]{1,0:T(8,128)S(1)} collective-permute-done((f32[8,128]{1,0:T(8,128)S(1)}, f32[8,128]{1,0:T(8,128)S(1)}, u32[]{:S(2)}, u32[]{:S(2)}) %collective-permute-start.10) | collective-permute-done | bytes 4128 | tf_op jit(solution)/shard_map/ppermute | solution.py:17
  103.0 3.7 %collective-permute-start.11 = (f32[8,128]{1,0:T(8,128)S(1)}, f32[8,128]{1,0:T(8,128)S(1)}, u32[]{:S(2)}, u32[]{:S(2)}) collective-permute-start(f32[8,128]{1,0:T(8,128)S(1)} %add.201), channel_id=1, source_target_pairs={{0,64},{1,65},{2,66},{3,67},{4,68},{5,69},{6,70},{7,71},{8,72},{9,... | collective-permute-start | bytes 12296 | tf_op jit(solution)/shard_map/ppermute | solution.py:17
  106.7 3.8 %collective-permute-done.11 = f32[8,128]{1,0:T(8,128)S(1)} collective-permute-done((f32[8,128]{1,0:T(8,128)S(1)}, f32[8,128]{1,0:T(8,128)S(1)}, u32[]{:S(2)}, u32[]{:S(2)}) %collective-permute-start.11) | collective-permute-done | bytes 4128 | tf_op jit(solution)/shard_map/ppermute | solution.py:17
  110.6 3.5 %collective-permute-done.12 = f32[8,128]{1,0:T(8,128)S(1)} collective-permute-done((f32[8,128]{1,0:T(8,128)S(1)}, f32[8,128]{1,0:T(8,128)S(1)}, u32[]{:S(2)}, u32[]{:S(2)}) %collective-permute-start.12) | collective-permute-done | bytes 4128 | tf_op jit(solution)/shard_map/ppermute | solution.py:17
  115.0 4.3 %collective-permute-done.13 = f32[8,128]{1,0:T(8,128)S(1)} collective-permute-done((f32[8,128]{1,0:T(8,128)S(1)}, f32[8,128]{1,0:T(8,128)S(1)}, u32[]{:S(2)}, u32[]{:S(2)}) %collective-permute-start.13) | collective-permute-done | bytes 4128 | tf_op jit(solution)/shard_map/ppermute | solution.py:17
  119.2 2.9 %collective-permute-start.14 = (f32[8,128]{1,0:T(8,128)S(1)}, f32[8,128]{1,0:T(8,128)S(1)}, u32[]{:S(2)}, u32[]{:S(2)}) collective-permute-start(f32[8,128]{1,0:T(8,128)S(1)} %add.204), channel_id=1, source_target_pairs={{0,2},{1,3},{2,0},{3,1},{4,6},{5,7},{6,4},{7,5},{8,10},{9,11},{10,... | collective-permute-start | bytes 12296 | tf_op jit(solution)/shard_map/ppermute | solution.py:17
  122.2 1.6 collective-permute-done.14
  123.7 1.5 collective-permute-start.15
  125.6 3.3 %collective-permute-done.15 = f32[8,128]{1,0:T(8,128)S(1)} collective-permute-done((f32[8,128]{1,0:T(8,128)S(1)}, f32[8,128]{1,0:T(8,128)S(1)}, u32[]{:S(2)}, u32[]{:S(2)}) %collective-permute-start.15) | collective-permute-done | bytes 4128 | tf_op jit(solution)/shard_map/ppermute | solution.py:17
  130.7 1.9 fusion.153
  136.5 2.2 %convolution_bitcast_fusion.2 = f32[64,37]{1,0:T(8,128)S(1)} fusion(bf16[32,128,64]{1,2,0:T(8,128)(2,1)S(1)} %copy-done.4, f32[32,128,37]{1,0,2:T(8,128)} %slice_bitcast_fusion, s32[32,128]{1,0:T(8,128)S(1)} %copy.101, f32[32,128]{1,0:T(8,128)S(1)} %copy.100, f32[]{:T(128)} %bitcast.24, s32[32,128]{1,0:T(8,128)S(1)} %copy-done.22, ...), kind=kOutput, calls=%fused_computation.36 | convolution fusion | flops 118362112 | bytes 1221892 | tf_op jit(solution)/shard_map/dot_general | solution.py:148
  139.7 2.1 %collective-permute-start.17 = (f32[80,128]{1,0:T(8,128)S(1)}, f32[80,128]{1,0:T(8,128)S(1)}, u32[]{:S(2)}, u32[]{:S(2)}) collective-permute-start(f32[80,128]{1,0:T(8,128)S(1)} %get-tuple-element.74), channel_id=1, source_target_pairs={{0,16},{1,17},{2,18},{3,19},{4,20},{5,21},{6,22},{7,23},{8,24},{9,... | collective-permute-start | bytes 122888 | tf_op jit(solution)/shard_map/ppermute | solution.py:17
  141.8 2.1 %collective-permute-done.17 = f32[80,128]{1,0:T(8,128)S(1)} collective-permute-done((f32[80,128]{1,0:T(8,128)S(1)}, f32[80,128]{1,0:T(8,128)S(1)}, u32[]{:S(2)}, u32[]{:S(2)}) %collective-permute-start.17) | collective-permute-done | bytes 40992 | tf_op jit(solution)/shard_map/ppermute | solution.py:17
  143.9 1.4 collective-permute-done.18
  145.3 2.9 %collective-permute-start.20 = (f32[80,128]{1,0:T(8,128)S(1)}, f32[80,128]{1,0:T(8,128)S(1)}, u32[]{:S(2)}, u32[]{:S(2)}) collective-permute-start(f32[80,128]{1,0:T(8,128)S(1)} %fusion.97), channel_id=1, source_target_pairs={{0,64},{1,65},{2,66},{3,67},{4,68},{5,69},{6,70},{7,71},{8,72},{9,... | collective-permute-start | bytes 122888 | tf_op jit(solution)/shard_map/ppermute | solution.py:17
  149.0 2.9 %collective-permute-start.19 = (f32[80,128]{1,0:T(8,128)S(1)}, f32[80,128]{1,0:T(8,128)S(1)}, u32[]{:S(2)}, u32[]{:S(2)}) collective-permute-start(f32[80,128]{1,0:T(8,128)S(1)} %fusion.97), channel_id=1, source_target_pairs={{0,32},{1,33},{2,34},{3,35},{4,36},{5,37},{6,38},{7,39},{8,40},{9,... | collective-permute-start | bytes 122888 | tf_op jit(solution)/shard_map/ppermute | solution.py:17
  151.9 1.9 collective-permute-done.20
  155.0 1.8 collective-permute-start.23
  158.6 3.4 %collective-permute-start.32 = (bf16[8,128,64]{1,2,0:T(8,128)(2,1)S(1)}, bf16[8,128,64]{1,2,0:T(8,128)(2,1)S(1)}, u32[]{:S(2)}, u32[]{:S(2)}) collective-permute-start(bf16[8,128,64]{1,2,0:T(8,128)(2,1)S(1)} %get-tuple-element.60), channel_id=1, source_target_pairs={{8,0},{16,8},{24,16},{32,24},{40,32},{48,40},{56,48},{64,56},{72,6... | collective-permute-start | bytes 393224 | tf_op jit(solution)/shard_map/ppermute | solution.py:28
  162.0 1.9 collective-permute-start.31
  164.0 3.2 %collective-permute-start.26 = (f32[80,128]{1,0:T(8,128)S(1)}, f32[80,128]{1,0:T(8,128)S(1)}, u32[]{:S(2)}, u32[]{:S(2)}) collective-permute-start(f32[80,128]{1,0:T(8,128)S(1)} %add_add_fusion.1), channel_id=1, source_target_pairs={{0,4},{1,5},{2,6},{3,7},{4,0},{5,1},{6,2},{7,3},{8,12},{9,13},{10,... | collective-permute-start | bytes 122888 | tf_op jit(solution)/shard_map/ppermute | solution.py:17
  167.8 2.6 %collective-permute-done.31 = bf16[8,128,64]{1,2,0:T(8,128)(2,1)S(1)} collective-permute-done((bf16[8,128,64]{1,2,0:T(8,128)(2,1)S(1)}, bf16[8,128,64]{1,2,0:T(8,128)(2,1)S(1)}, u32[]{:S(2)}, u32[]{:S(2)}) %collective-permute-start.31) | collective-permute-done | bytes 131104 | tf_op jit(solution)/shard_map/ppermute | solution.py:25
  171.8 4.8 %collective-permute-start.34 = (bf16[48,8,64]{2,1,0:T(8,128)(2,1)}, bf16[48,8,64]{2,1,0:T(8,128)(2,1)S(1)}, u32[]{:S(2)}, u32[]{:S(2)}) collective-permute-start(bf16[48,8,64]{2,1,0:T(8,128)(2,1)} %copy.111), channel_id=1, source_target_pairs={{0,1},{1,2},{2,3},{3,4},{4,5},{5,6},{6,7},{8,9},{9,10},{10,11},{11... | collective-permute-start | bytes 147464 | tf_op jit(solution)/shard_map/ppermute | solution.py:25
  176.9 2.5 %collective-permute-start.33 = (bf16[48,8,64]{2,1,0:T(8,128)(2,1)S(1)}, bf16[48,8,64]{2,1,0:T(8,128)(2,1)}, u32[]{:S(2)}, u32[]{:S(2)}) collective-permute-start(bf16[48,8,64]{2,1,0:T(8,128)(2,1)S(1)} %copy.107), channel_id=1, source_target_pairs={{1,0},{2,1},{3,2},{4,3},{5,4},{6,5},{7,6},{9,8},{10,9},{11,10},{12... | collective-permute-start | bytes 147464 | tf_op jit(solution)/shard_map/ppermute | solution.py:28
  181.2 1.7 collective-permute-start.28
  183.4 2.6 %collective-permute-done.33 = bf16[48,8,64]{2,1,0:T(8,128)(2,1)} collective-permute-done((bf16[48,8,64]{2,1,0:T(8,128)(2,1)S(1)}, bf16[48,8,64]{2,1,0:T(8,128)(2,1)}, u32[]{:S(2)}, u32[]{:S(2)}) %collective-permute-start.33) | collective-permute-done | bytes 49184 | tf_op jit(solution)/shard_map/ppermute | solution.py:28
  186.0 1.3 copy.108
  187.2 1.7 maximum_maximum_fusion.1
  (203 shorter events, 46.1 us)
Async XLA Ops:
  0.6 63.0 %copy-start = (bf16[64,37]{0,1:T(8,128)(2,1)S(1)}, bf16[64,37]{0,1:T(8,128)(2,1)}, u32[]{:S(2)}) copy-start(bf16[64,37]{0,1:T(8,128)(2,1)} %param.8) | copy-start | bytes 14212
  0.6 10.9 %copy-start.21 = (s32[32,128]{1,0:T(8,128)S(1)}, s32[32,128]{1,0:T(8,128)}, u32[]{:S(2)}) copy-start(s32[32,128]{1,0:T(8,128)} %param.10) | copy-start | bytes 49156
  0.7 11.7 %copy-start.24 = (s32[32,128]{1,0:T(8,128)S(1)}, s32[32,128]{1,0:T(8,128)}, u32[]{:S(2)}) copy-start(s32[32,128]{1,0:T(8,128)} %param.11) | copy-start | bytes 49156
  2.2 11.6 %collective-permute-start.1 = (bf16[8,128,64]{1,2,0:T(8,128)(2,1)S(1)}, bf16[8,128,64]{1,2,0:T(8,128)(2,1)S(1)}, u32[]{:S(2)}, u32[]{:S(2)}) collective-permute-start(bf16[8,128,64]{1,2,0:T(8,128)(2,1)S(1)} %get-tuple-element.66), channel_id=1, source_target_pairs={{8,0},{16,8},{24,16},{32,24},{40,32},{48,40},{56,48},{64,56},{72,6... | collective-permute-start | bytes 393224 | tf_op jit(solution)/shard_map/ppermute | solution.py:28
  9.6 8.5 %collective-permute-start = (bf16[8,128,64]{1,2,0:T(8,128)(2,1)S(1)}, bf16[8,128,64]{1,2,0:T(8,128)(2,1)S(1)}, u32[]{:S(2)}, u32[]{:S(2)}) collective-permute-start(bf16[8,128,64]{1,2,0:T(8,128)(2,1)S(1)} %get-tuple-element.65), channel_id=1, source_target_pairs={{0,8},{8,16},{16,24},{24,32},{32,40},{40,48},{48,56},{56,64},{64,7... | collective-permute-start | bytes 393224 | tf_op jit(solution)/shard_map/ppermute | solution.py:25
  13.8 17.5 %copy-start.15 = (bf16[8,128,64]{1,2,0:T(8,128)(2,1)}, bf16[8,128,64]{1,2,0:T(8,128)(2,1)S(1)}, u32[]{:S(2)}) copy-start(bf16[8,128,64]{1,2,0:T(8,128)(2,1)S(1)} %collective-permute-done.1) | copy-start | bytes 393220
  18.1 9.3 %copy-start.17 = (bf16[8,128,64]{1,2,0:T(8,128)(2,1)}, bf16[8,128,64]{1,2,0:T(8,128)(2,1)S(1)}, u32[]{:S(2)}) copy-start(bf16[8,128,64]{1,2,0:T(8,128)(2,1)S(1)} %collective-permute-done) | copy-start | bytes 393220
  18.9 9.6 %collective-permute-start.3 = (bf16[48,8,64]{2,1,0:T(8,128)(2,1)S(1)}, bf16[48,8,64]{2,1,0:T(8,128)(2,1)S(1)}, u32[]{:S(2)}, u32[]{:S(2)}) collective-permute-start(bf16[48,8,64]{2,1,0:T(8,128)(2,1)S(1)} %copy.84), channel_id=1, source_target_pairs={{1,0},{2,1},{3,2},{4,3},{5,4},{6,5},{7,6},{9,8},{10,9},{11,10},{12... | collective-permute-start | bytes 147464 | tf_op jit(solution)/shard_map/ppermute | solution.py:28
  22.0 8.0 %collective-permute-start.2 = (bf16[48,8,64]{2,1,0:T(8,128)(2,1)S(1)}, bf16[48,8,64]{2,1,0:T(8,128)(2,1)S(1)}, u32[]{:S(2)}, u32[]{:S(2)}) collective-permute-start(bf16[48,8,64]{2,1,0:T(8,128)(2,1)S(1)} %copy.80), channel_id=1, source_target_pairs={{0,1},{1,2},{2,3},{3,4},{4,5},{5,6},{6,7},{8,9},{9,10},{10,11},{11... | collective-permute-start | bytes 147464 | tf_op jit(solution)/shard_map/ppermute | solution.py:25
  40.6 23.0 %copy-start.3 = (bf16[32,128,64]{1,2,0:T(8,128)(2,1)}, bf16[32,128,64]{1,2,0:T(8,128)(2,1)S(1)}, u32[]{:S(2)}) copy-start(bf16[32,128,64]{1,2,0:T(8,128)(2,1)S(1)} %fusion.19) | copy-start | bytes 1572868
  44.3 19.4 %copy-start.30 = (f32[37]{0:T(128)S(1)}, f32[37]{0:T(128)}, u32[]{:S(2)}) copy-start(f32[37]{0:T(128)} %param.9) | copy-start | bytes 448
  46.2 18.5 %collective-permute-start.7 = (bf16[528,128]{1,0:T(8,128)(2,1)S(1)}, bf16[528,128]{1,0:T(8,128)(2,1)S(1)}, u32[]{:S(2)}, u32[]{:S(2)}) collective-permute-start(bf16[528,128]{1,0:T(8,128)(2,1)S(1)} %get-tuple-element.54), channel_id=1, source_target_pairs={{0,24},{1,56},{2,88},{3,120},{4,152},{5,184},{6,216},{7,248},{8,16... | collective-permute-start | bytes 405512 | tf_op jit(solution)/shard_map/ppermute | solution.py:17
  49.0 17.9 %collective-permute-start.6 = (bf16[528,128]{1,0:T(8,128)(2,1)S(1)}, bf16[528,128]{1,0:T(8,128)(2,1)S(1)}, u32[]{:S(2)}, u32[]{:S(2)}) collective-permute-start(bf16[528,128]{1,0:T(8,128)(2,1)S(1)} %get-tuple-element.55), channel_id=1, source_target_pairs={{0,16},{1,48},{2,80},{3,112},{4,144},{5,176},{6,208},{7,240},{8,24... | collective-permute-start | bytes 405512 | tf_op jit(solution)/shard_map/ppermute | solution.py:17
  49.5 30.9 %collective-permute-start.5 = (bf16[528,128]{1,0:T(8,128)(2,1)S(1)}, bf16[528,128]{1,0:T(8,128)(2,1)S(1)}, u32[]{:S(2)}, u32[]{:S(2)}) collective-permute-start(bf16[528,128]{1,0:T(8,128)(2,1)S(1)} %get-tuple-element.56), channel_id=1, source_target_pairs={{0,8},{1,40},{2,72},{3,104},{4,136},{5,168},{6,200},{7,232},{8,0},... | collective-permute-start | bytes 405512 | tf_op jit(solution)/shard_map/ppermute | solution.py:17
  53.1 30.3 %collective-permute-start.4 = (bf16[528,128]{1,0:T(8,128)(2,1)S(1)}, bf16[528,128]{1,0:T(8,128)(2,1)S(1)}, u32[]{:S(2)}, u32[]{:S(2)}) collective-permute-start(bf16[528,128]{1,0:T(8,128)(2,1)S(1)} %get-tuple-element.53), channel_id=1, source_target_pairs={{0,0},{1,32},{2,64},{3,96},{4,128},{5,160},{6,192},{7,224},{8,8},{... | collective-permute-start | bytes 405512 | tf_op jit(solution)/shard_map/ppermute | solution.py:17
  86.7 3.9 %copy-start.22 = (s32[32,128]{1,0:T(8,128)S(1)}, s32[32,128]{1,0:T(8,128)}, u32[]{:S(2)}) copy-start(s32[32,128]{1,0:T(8,128)} %param.10) | copy-start | bytes 49156
  90.6 34.7 %copy-start.12 = (bf16[1,528,128]{2,1,0:T(8,128)(2,1)S(1)}, bf16[1,528,128]{2,1,0:T(8,128)(2,1)}, u32[]{:S(2)}) copy-start(bf16[1,528,128]{2,1,0:T(8,128)(2,1)} %copy-done.11) | copy-start | bytes 405508
  90.6 34.7 %copy-start.14 = (bf16[1,528,128]{2,1,0:T(8,128)(2,1)S(1)}, bf16[1,528,128]{2,1,0:T(8,128)(2,1)}, u32[]{:S(2)}) copy-start(bf16[1,528,128]{2,1,0:T(8,128)(2,1)} %copy-done.13) | copy-start | bytes 405508
  92.1 1.3 collective-permute-start.8
  94.0 3.7 %collective-permute-start.9 = (f32[8,128]{1,0:T(8,128)S(1)}, f32[8,128]{1,0:T(8,128)S(1)}, u32[]{:S(2)}, u32[]{:S(2)}) collective-permute-start(f32[8,128]{1,0:T(8,128)S(1)} %broadcast_add_fusion), channel_id=1, source_target_pairs={{0,16},{1,17},{2,18},{3,19},{4,20},{5,21},{6,22},{7,23},{8,24},{9,... | collective-permute-start | bytes 12296 | tf_op jit(solution)/shard_map/ppermute | solution.py:17
  98.4 4.6 %collective-permute-start.10 = (f32[8,128]{1,0:T(8,128)S(1)}, f32[8,128]{1,0:T(8,128)S(1)}, u32[]{:S(2)}, u32[]{:S(2)}) collective-permute-start(f32[8,128]{1,0:T(8,128)S(1)} %fusion.166), channel_id=1, source_target_pairs={{0,32},{1,33},{2,34},{3,35},{4,36},{5,37},{6,38},{7,39},{8,40},{9,... | collective-permute-start | bytes 12296 | tf_op jit(solution)/shard_map/ppermute | solution.py:17
  103.0 7.5 %collective-permute-start.11 = (f32[8,128]{1,0:T(8,128)S(1)}, f32[8,128]{1,0:T(8,128)S(1)}, u32[]{:S(2)}, u32[]{:S(2)}) collective-permute-start(f32[8,128]{1,0:T(8,128)S(1)} %add.201), channel_id=1, source_target_pairs={{0,64},{1,65},{2,66},{3,67},{4,68},{5,69},{6,70},{7,71},{8,72},{9,... | collective-permute-start | bytes 12296 | tf_op jit(solution)/shard_map/ppermute | solution.py:17
  110.5 3.6 %collective-permute-start.12 = (f32[8,128]{1,0:T(8,128)S(1)}, f32[8,128]{1,0:T(8,128)S(1)}, u32[]{:S(2)}, u32[]{:S(2)}) collective-permute-start(f32[8,128]{1,0:T(8,128)S(1)} %add.202), channel_id=1, source_target_pairs={{0,128},{1,129},{2,130},{3,131},{4,132},{5,133},{6,134},{7,135},{8... | collective-permute-start | bytes 12296 | tf_op jit(solution)/shard_map/ppermute | solution.py:17
  110.5 19.5 %copy-start.23 = (f32[4096]{0:T(1024)S(1)}, f32[4096]{0:T(1024)}, u32[]{:S(2)}) copy-start(f32[4096]{0:T(1024)} %get-tuple-element.77) | copy-start | bytes 49156
  114.1 5.1 %collective-permute-start.13 = (f32[8,128]{1,0:T(8,128)S(1)}, f32[8,128]{1,0:T(8,128)S(1)}, u32[]{:S(2)}, u32[]{:S(2)}) collective-permute-start(f32[8,128]{1,0:T(8,128)S(1)} %add.203), channel_id=1, source_target_pairs={{0,1},{1,0},{2,3},{3,2},{4,5},{5,4},{6,7},{7,6},{8,9},{9,8},{10,11... | collective-permute-start | bytes 12296 | tf_op jit(solution)/shard_map/ppermute | solution.py:17
  119.2 4.5 %collective-permute-start.14 = (f32[8,128]{1,0:T(8,128)S(1)}, f32[8,128]{1,0:T(8,128)S(1)}, u32[]{:S(2)}, u32[]{:S(2)}) collective-permute-start(f32[8,128]{1,0:T(8,128)S(1)} %add.204), channel_id=1, source_target_pairs={{0,2},{1,3},{2,0},{3,1},{4,6},{5,7},{6,4},{7,5},{8,10},{9,11},{10,... | collective-permute-start | bytes 12296 | tf_op jit(solution)/shard_map/ppermute | solution.py:17
  123.7 5.1 %collective-permute-start.15 = (f32[8,128]{1,0:T(8,128)S(1)}, f32[8,128]{1,0:T(8,128)S(1)}, u32[]{:S(2)}, u32[]{:S(2)}) collective-permute-start(f32[8,128]{1,0:T(8,128)S(1)} %add.205), channel_id=1, source_target_pairs={{0,4},{1,5},{2,6},{3,7},{4,0},{5,1},{6,2},{7,3},{8,12},{9,13},{10,... | collective-permute-start | bytes 12296 | tf_op jit(solution)/shard_map/ppermute | solution.py:17
  130.6 2.0 %copy-start.2 = (bf16[48,136,64]{1,2,0:T(8,128)(2,1)S(1)}, bf16[48,136,64]{1,2,0:T(8,128)(2,1)}, u32[]{:S(2)}) copy-start(bf16[48,136,64]{1,2,0:T(8,128)(2,1)} %copy-done.1) | copy-start | bytes 2506756
  130.7 2.2 %copy-start.18 = (bf16[8,128,64]{1,2,0:T(8,128)(2,1)S(1)}, bf16[8,128,64]{1,2,0:T(8,128)(2,1)}, u32[]{:S(2)}) copy-start(bf16[8,128,64]{1,2,0:T(8,128)(2,1)} %copy-done.17) | copy-start | bytes 393220
  139.6 2.3 %collective-permute-start.16 = (f32[80,128]{1,0:T(8,128)S(1)}, f32[80,128]{1,0:T(8,128)S(1)}, u32[]{:S(2)}, u32[]{:S(2)}) collective-permute-start(f32[80,128]{1,0:T(8,128)S(1)} %get-tuple-element.75), channel_id=1, source_target_pairs={{0,8},{1,9},{2,10},{3,11},{4,12},{5,13},{6,14},{7,15},{8,0},{9,1},... | collective-permute-start | bytes 122888 | tf_op jit(solution)/shard_map/ppermute | solution.py:17
  139.7 4.2 %collective-permute-start.17 = (f32[80,128]{1,0:T(8,128)S(1)}, f32[80,128]{1,0:T(8,128)S(1)}, u32[]{:S(2)}, u32[]{:S(2)}) collective-permute-start(f32[80,128]{1,0:T(8,128)S(1)} %get-tuple-element.74), channel_id=1, source_target_pairs={{0,16},{1,17},{2,18},{3,19},{4,20},{5,21},{6,22},{7,23},{8,24},{9,... | collective-permute-start | bytes 122888 | tf_op jit(solution)/shard_map/ppermute | solution.py:17
  141.8 3.5 %collective-permute-start.18 = (f32[80,128]{1,0:T(8,128)S(1)}, f32[80,128]{1,0:T(8,128)S(1)}, u32[]{:S(2)}, u32[]{:S(2)}) collective-permute-start(f32[80,128]{1,0:T(8,128)S(1)} %get-tuple-element.73), channel_id=1, source_target_pairs={{0,24},{1,25},{2,26},{3,27},{4,28},{5,29},{6,30},{7,31},{8,16},{9,... | collective-permute-start | bytes 122888 | tf_op jit(solution)/shard_map/ppermute | solution.py:17
  145.3 8.5 %collective-permute-start.20 = (f32[80,128]{1,0:T(8,128)S(1)}, f32[80,128]{1,0:T(8,128)S(1)}, u32[]{:S(2)}, u32[]{:S(2)}) collective-permute-start(f32[80,128]{1,0:T(8,128)S(1)} %fusion.97), channel_id=1, source_target_pairs={{0,64},{1,65},{2,66},{3,67},{4,68},{5,69},{6,70},{7,71},{8,72},{9,... | collective-permute-start | bytes 122888 | tf_op jit(solution)/shard_map/ppermute | solution.py:17
  148.2 6.1 %collective-permute-start.21 = (f32[80,128]{1,0:T(8,128)S(1)}, f32[80,128]{1,0:T(8,128)S(1)}, u32[]{:S(2)}, u32[]{:S(2)}) collective-permute-start(f32[80,128]{1,0:T(8,128)S(1)} %fusion.97), channel_id=1, source_target_pairs={{0,96},{1,97},{2,98},{3,99},{4,100},{5,101},{6,102},{7,103},{8,104... | collective-permute-start | bytes 122888 | tf_op jit(solution)/shard_map/ppermute | solution.py:17
  149.0 6.0 %collective-permute-start.19 = (f32[80,128]{1,0:T(8,128)S(1)}, f32[80,128]{1,0:T(8,128)S(1)}, u32[]{:S(2)}, u32[]{:S(2)}) collective-permute-start(f32[80,128]{1,0:T(8,128)S(1)} %fusion.97), channel_id=1, source_target_pairs={{0,32},{1,33},{2,34},{3,35},{4,36},{5,37},{6,38},{7,39},{8,40},{9,... | collective-permute-start | bytes 122888 | tf_op jit(solution)/shard_map/ppermute | solution.py:17
  155.0 9.0 %collective-permute-start.23 = (f32[80,128]{1,0:T(8,128)S(1)}, f32[80,128]{1,0:T(8,128)S(1)}, u32[]{:S(2)}, u32[]{:S(2)}) collective-permute-start(f32[80,128]{1,0:T(8,128)S(1)} %add_add_fusion.2), channel_id=1, source_target_pairs={{0,1},{1,0},{2,3},{3,2},{4,5},{5,4},{6,7},{7,6},{8,9},{9,8},{10,11... | collective-permute-start | bytes 122888 | tf_op jit(solution)/shard_map/ppermute | solution.py:17
  156.8 7.1 %collective-permute-start.24 = (f32[80,128]{1,0:T(8,128)S(1)}, f32[80,128]{1,0:T(8,128)S(1)}, u32[]{:S(2)}, u32[]{:S(2)}) collective-permute-start(f32[80,128]{1,0:T(8,128)S(1)} %add_add_fusion.2), channel_id=1, source_target_pairs={{0,129},{1,128},{2,131},{3,130},{4,133},{5,132},{6,135},{7,134},{8... | collective-permute-start | bytes 122888 | tf_op jit(solution)/shard_map/ppermute | solution.py:17
  157.9 6.0 %collective-permute-start.22 = (f32[80,128]{1,0:T(8,128)S(1)}, f32[80,128]{1,0:T(8,128)S(1)}, u32[]{:S(2)}, u32[]{:S(2)}) collective-permute-start(f32[80,128]{1,0:T(8,128)S(1)} %add_add_fusion.2), channel_id=1, source_target_pairs={{0,128},{1,129},{2,130},{3,131},{4,132},{5,133},{6,134},{7,135},{8... | collective-permute-start | bytes 122888 | tf_op jit(solution)/shard_map/ppermute | solution.py:17
  158.6 9.2 %collective-permute-start.32 = (bf16[8,128,64]{1,2,0:T(8,128)(2,1)S(1)}, bf16[8,128,64]{1,2,0:T(8,128)(2,1)S(1)}, u32[]{:S(2)}, u32[]{:S(2)}) collective-permute-start(bf16[8,128,64]{1,2,0:T(8,128)(2,1)S(1)} %get-tuple-element.60), channel_id=1, source_target_pairs={{8,0},{16,8},{24,16},{32,24},{40,32},{48,40},{56,48},{64,56},{72,6... | collective-permute-start | bytes 393224 | tf_op jit(solution)/shard_map/ppermute | solution.py:28
  162.0 8.4 %collective-permute-start.31 = (bf16[8,128,64]{1,2,0:T(8,128)(2,1)S(1)}, bf16[8,128,64]{1,2,0:T(8,128)(2,1)S(1)}, u32[]{:S(2)}, u32[]{:S(2)}) collective-permute-start(bf16[8,128,64]{1,2,0:T(8,128)(2,1)S(1)} %get-tuple-element.59), channel_id=1, source_target_pairs={{0,8},{8,16},{16,24},{24,32},{32,40},{40,48},{48,56},{56,64},{64,7... | collective-permute-start | bytes 393224 | tf_op jit(solution)/shard_map/ppermute | solution.py:25
  164.0 15.6 %collective-permute-start.26 = (f32[80,128]{1,0:T(8,128)S(1)}, f32[80,128]{1,0:T(8,128)S(1)}, u32[]{:S(2)}, u32[]{:S(2)}) collective-permute-start(f32[80,128]{1,0:T(8,128)S(1)} %add_add_fusion.1), channel_id=1, source_target_pairs={{0,4},{1,5},{2,6},{3,7},{4,0},{5,1},{6,2},{7,3},{8,12},{9,13},{10,... | collective-permute-start | bytes 122888 | tf_op jit(solution)/shard_map/ppermute | solution.py:17
  167.2 12.4 %collective-permute-start.27 = (f32[80,128]{1,0:T(8,128)S(1)}, f32[80,128]{1,0:T(8,128)S(1)}, u32[]{:S(2)}, u32[]{:S(2)}) collective-permute-start(f32[80,128]{1,0:T(8,128)S(1)} %add_add_fusion.1), channel_id=1, source_target_pairs={{0,6},{1,7},{2,4},{3,5},{4,2},{5,3},{6,0},{7,1},{8,14},{9,15},{10,... | collective-permute-start | bytes 122888 | tf_op jit(solution)/shard_map/ppermute | solution.py:17
  167.8 12.4 %collective-permute-start.25 = (f32[80,128]{1,0:T(8,128)S(1)}, f32[80,128]{1,0:T(8,128)}, u32[]{:S(2)}, u32[]{:S(2)}) collective-permute-start(f32[80,128]{1,0:T(8,128)S(1)} %add_add_fusion.1), channel_id=1, source_target_pairs={{0,2},{1,3},{2,0},{3,1},{4,6},{5,7},{6,4},{7,5},{8,10},{9,11},{10,... | collective-permute-start | bytes 122888 | tf_op jit(solution)/shard_map/ppermute | solution.py:17
  171.8 11.2 %collective-permute-start.34 = (bf16[48,8,64]{2,1,0:T(8,128)(2,1)}, bf16[48,8,64]{2,1,0:T(8,128)(2,1)S(1)}, u32[]{:S(2)}, u32[]{:S(2)}) collective-permute-start(bf16[48,8,64]{2,1,0:T(8,128)(2,1)} %copy.111), channel_id=1, source_target_pairs={{0,1},{1,2},{2,3},{3,4},{4,5},{5,6},{6,7},{8,9},{9,10},{10,11},{11... | collective-permute-start | bytes 147464 | tf_op jit(solution)/shard_map/ppermute | solution.py:25
  176.9 9.0 %collective-permute-start.33 = (bf16[48,8,64]{2,1,0:T(8,128)(2,1)S(1)}, bf16[48,8,64]{2,1,0:T(8,128)(2,1)}, u32[]{:S(2)}, u32[]{:S(2)}) collective-permute-start(bf16[48,8,64]{2,1,0:T(8,128)(2,1)S(1)} %copy.107), channel_id=1, source_target_pairs={{1,0},{2,1},{3,2},{4,3},{5,4},{6,5},{7,6},{9,8},{10,9},{11,10},{12... | collective-permute-start | bytes 147464 | tf_op jit(solution)/shard_map/ppermute | solution.py:28
  181.0 13.9 %collective-permute-start.30 = (f32[80,128]{1,0:T(8,128)S(1)}, f32[80,128]{1,0:T(8,128)S(1)}, u32[]{:S(2)}, u32[]{:S(2)}) collective-permute-start(f32[80,128]{1,0:T(8,128)S(1)} %add_add_fusion), channel_id=1, source_target_pairs={{0,24},{1,25},{2,26},{3,27},{4,28},{5,29},{6,30},{7,31},{8,16},{9,... | collective-permute-start | bytes 122888 | tf_op jit(solution)/shard_map/ppermute | solution.py:17
  181.1 13.8 %collective-permute-start.29 = (f32[80,128]{1,0:T(8,128)S(1)}, f32[80,128]{1,0:T(8,128)S(1)}, u32[]{:S(2)}, u32[]{:S(2)}) collective-permute-start(f32[80,128]{1,0:T(8,128)S(1)} %add_add_fusion), channel_id=1, source_target_pairs={{0,16},{1,17},{2,18},{3,19},{4,20},{5,21},{6,22},{7,23},{8,24},{9,... | collective-permute-start | bytes 122888 | tf_op jit(solution)/shard_map/ppermute | solution.py:17
  181.2 13.7 %collective-permute-start.28 = (f32[80,128]{1,0:T(8,128)S(1)}, f32[80,128]{1,0:T(8,128)}, u32[]{:S(2)}, u32[]{:S(2)}) collective-permute-start(f32[80,128]{1,0:T(8,128)S(1)} %add_add_fusion), channel_id=1, source_target_pairs={{0,8},{1,9},{2,10},{3,11},{4,12},{5,13},{6,14},{7,15},{8,0},{9,1},... | collective-permute-start | bytes 122888 | tf_op jit(solution)/shard_map/ppermute | solution.py:17
  (18 other events, 20.4 us)

commit v2 on v1

v2 whole, which is shorter than its diff:
```python
import jax
import jax.numpy as jnp
from jax import lax
from jax.experimental import pallas as pl
from jax.experimental.pallas import tpu as pltpu
from jax.sharding import PartitionSpec as P

STEP = 8
GRID = ("row", "col")
F32, BF16 = jnp.float32, jnp.bfloat16
LANES = 128
FAR_BELOW = -1e30
VMEM = pl.BlockSpec(memory_space=pltpu.VMEM)
SMEM = pl.BlockSpec(memory_space=pltpu.SMEM)


def run(body, outs, args, scratch=(), scalars=0, micros=3):
    return pl.pallas_call(
        body,
        out_shape=outs,
        in_specs=[SMEM] * scalars + [VMEM] * (len(args) - scalars),
        out_specs=[VMEM] * len(outs),
        scratch_shapes=list(scratch),
        compiler_params=pltpu.CompilerParams(vmem_limit_bytes=48 * 1024 * 1024),
        cost_estimate=pl.CostEstimate(
            flops=0, bytes_accessed=int(micros * 3.6e6), transcendentals=0
        ),
    )(*args)


def shape(dims, kind):
    return jax.ShapeDtypeStruct(dims, kind)


def send(block, target):
    nrow, ncol = lax.axis_size("row"), lax.axis_size("col")
    pairs = []
    for r in range(nrow):
        for c in range(ncol):
            r2, c2 = target(r, c)
            pairs.append((r * ncol + c, r2 * ncol + c2))
    return lax.ppermute(block, GRID, pairs)


def shifted(block, axis, forward):
    count = lax.axis_size(axis)
    pairs = [(i, i + 1) for i in range(count - 1)]
    return lax.ppermute(block, axis, pairs if forward else [(b, a) for a, b in pairs])


def activate_kernel(feat, act, top, bottom):
    rows = feat.shape[0]

    def step(i, carry):
        v = feat[i].astype(F32)
        near = v * (1.0 + v * (0.5 + v * (1.0 / 6.0 + v * (1.0 / 24.0))))
        low = jnp.where(v > -0.03, near, jnp.exp(jnp.minimum(v, 0.0)) - 1.0)
        act[i] = jnp.where(v > 0, v, low).astype(BF16)
        return carry

    lax.fori_loop(0, rows, step, 0)
    top[...] = act[:STEP]
    bottom[...] = act[rows - STEP :]


def row_of(own, up, down, at):
    rows = own.shape[0]
    if at < STEP:
        return up[at]
    if at < STEP + rows:
        return own[at - STEP]
    return down[at - STEP - rows]


def pack_kernel(own, up, down, first, last):
    chans = own.shape[1]
    lane = lax.broadcasted_iota(jnp.int32, (chans, LANES), 1) // STEP
    for group in range(first.shape[0]):
        low = jnp.zeros((chans, LANES), F32)
        high = jnp.zeros((chans, LANES), F32)
        for slot in range(16):
            x = row_of(own, up, down, group * 16 + slot).astype(F32)
            here = lane == slot
            low = jnp.where(here, pltpu.roll(x, (STEP * slot) % LANES, 1), low)
            high = jnp.where(here, pltpu.roll(x, (STEP * slot + STEP) % LANES, 1), high)
        first[group] = low.astype(BF16)
        last[group] = high.astype(BF16)


def spread_columns(own, up, down, left, right, wide):
    chans = own.shape[1]
    lane = lax.broadcasted_iota(jnp.int32, (chans, LANES), 1)
    for group in range(left.shape[0]):
        from_left = left[group].astype(F32)
        from_right = right[group].astype(F32)
        for slot in range(16):
            at = group * 16 + slot
            middle = row_of(own, up, down, at)
            x = middle.astype(F32)
            before = jnp.where(
                lane < STEP,
                pltpu.roll(from_left, (LANES - STEP * slot) % LANES, 1),
                pltpu.roll(x, STEP, 1),
            )
            after = jnp.where(
                lane >= LANES - STEP,
                pltpu.roll(from_right, (2 * LANES - STEP - STEP * slot) % LANES, 1),
                pltpu.roll(x, LANES - STEP, 1),
            )
            wide[at, 0:chans] = before.astype(BF16)
            wide[at, chans : 2 * chans] = middle
            wide[at, 2 * chans : 3 * chans] = after.astype(BF16)


def windows(wide, i):
    return jnp.concatenate([wide[i], wide[i + STEP], wide[i + 2 * STEP]], axis=0)


def pair_windows(wide, i):
    return jnp.concatenate([windows(wide, i), windows(wide, i + 1)], axis=1)


def forward_kernel(
    place, act, up, down, left, right, feat, weight, labels, valid,
    wide, mixed, pay0, pay1, pay2, pay3, turned,
):
    rows, chans = act.shape[0], act.shape[1]
    part = rows
    pays = (pay0, pay1, pay2, pay3)
    spread_columns(act, up, down, left, right, wide)
    kernel = weight[...].astype(F32).T.astype(BF16)

    def step(p, carry):
        i = 2 * p
        out = jnp.dot(kernel, pair_windows(wide, i), preferred_element_type=F32)
        for d in range(2):
            total = feat[i + d].astype(F32) + out[:, d * LANES : (d + 1) * LANES]
            low = total.astype(BF16)
            mixed[i + d] = low
            turned[pl.ds(pl.multiple_of((i + d) * LANES, LANES), LANES), :] = low.astype(F32).T
        return carry

    lax.fori_loop(0, rows // 2, step, 0)
    turned[rows * LANES :, :] = jnp.concatenate(
        [labels[...].astype(F32).T, valid[...].astype(F32).T], axis=1
    )
    half = part // 2

    def pack(j, carry):
        for s in range(4):
            base = j * LANES + (place[0] ^ s) * part
            low = turned[pl.ds(pl.multiple_of(base, 16), half), :]
            high = turned[pl.ds(pl.multiple_of(base + half, 16), half), :]
            pays[s][pl.ds(pl.multiple_of(j * half, 16), half), :] = jnp.concatenate(
                [low, high], axis=1
            ).astype(BF16)
        return carry

    lax.fori_loop(0, rows + 1, pack, 0)


def softmax_kernel(
    place, got0, got1, got2, got3, mixed, head, labels, valid,
    grad, head_sum, bias_sum, loss_sum, cells, lab, lab_t, val, val_t,
):
    rows, chans = mixed.shape[0], mixed.shape[1]
    bins = head.shape[0]
    half = rows // 2
    size = rows * half
    lab[...] = labels[...].astype(F32)
    val[...] = valid[...].astype(F32)
    notes = []
    for s, got in enumerate((got0, got1, got2, got3)):
        q = place[0] ^ s
        cells[pl.ds(pl.multiple_of(q * size, size), size), :] = got[:size, :].astype(F32)
        cells[pl.ds(pl.multiple_of(4 * size + q * half, half), half), :] = got[size:, :].astype(F32)
    notes = [cells[4 * size + q * half : 4 * size + (q + 1) * half, :] for q in range(4)]
    for top in range(2):
        base = top * 2 * rows
        lab_t[top * half : (top + 1) * half, :] = jnp.concatenate(
            [n[:, base : base + rows] for n in notes], axis=1
        )
        val_t[top * half : (top + 1) * half, :] = jnp.concatenate(
            [n[:, base + rows : base + 2 * rows] for n in notes], axis=1
        )
    lane = lax.broadcasted_iota(jnp.int32, (bins, LANES), 1)
    plain = jnp.where(lane < chans, head[...], 0.0)
    both = jnp.concatenate([plain, pltpu.roll(plain, chans, 1)], axis=0).astype(BF16)
    single = plain[:, :chans]
    thrice = jnp.concatenate([single, single, single], axis=0).T.astype(BF16)
    single = single.astype(BF16)
    bias = head[:, chans : chans + 1]
    bin_ids = lax.broadcasted_iota(jnp.int32, (bins, LANES), 0).astype(F32)
    head_sum[...] = jnp.zeros_like(head_sum)
    bias_sum[...] = jnp.zeros_like(bias_sum)
    loss_sum[...] = jnp.zeros_like(loss_sum)

    def step(i, carry):
        other = cells[pl.ds(i, LANES, stride=half), :].astype(BF16)
        logits_t = lax.dot_general(both, other, (((1,), (1,)), ((), ())), preferred_element_type=F32)
        pair = jnp.concatenate([mixed[i], mixed[i + half]], axis=1)
        logits = jnp.dot(single, pair, preferred_element_type=F32)
        pieces = []
        for d in range(2):
            at = pl.ds(i + d * half, 1)
            own = logits[:, d * LANES : (d + 1) * LANES] + bias
            far = logits_t[d * bins : (d + 1) * bins] + bias
            sym = 0.5 * (own + far)
            peak = jnp.max(sym, axis=0, keepdims=True)
            raised = jnp.exp(sym - peak)
            total = jnp.sum(raised, axis=0, keepdims=True)
            lse = peak + jnp.log(total)
            hot = bin_ids == lab[at, :]
            hot_t = bin_ids == lab_t[at, :]
            mask, mask_t = val[at, :], val_t[at, :]
            picked = jnp.sum(jnp.where(hot, sym, 0.0), axis=0, keepdims=True)
            loss_sum[...] += mask * (lse - picked)
            share = raised * ((mask + mask_t) / total)
            pieces.append(share - jnp.where(hot, mask, 0.0) - jnp.where(hot_t, mask_t, 0.0))
        bias_sum[...] += pieces[0] + pieces[1]
        g = jnp.concatenate(pieces, axis=1)
        first = g.astype(BF16).astype(F32)
        rest = g - first
        second = rest.astype(BF16).astype(F32)
        split = jnp.concatenate([first, second, rest - second], axis=0).astype(BF16)
        out = jnp.dot(thrice, split, preferred_element_type=F32)
        grad[i] = out[:, :LANES]
        grad[i + half] = out[:, LANES:]
        head_sum[...] += lax.dot_general(
            split, pair, (((1,), (1,)), ((), ())), preferred_element_type=F32
        )
        return carry

    lax.fori_loop(0, half, step, 0)


def scale_of(count):
    return 0.5 / jnp.maximum(count[0:1, 0:1], 1.0)


def kernel_grad_kernel(
    place, count, grad, wide, head_sum, bias_sum, loss_sum,
    low, top, bottom, out0, out1, out2, out3, total, sheet,
):
    rows, chans = grad.shape[0], grad.shape[1]
    bins = bias_sum.shape[0]
    scale = scale_of(count)
    total[...] = jnp.zeros_like(total)

    def step(p, carry):
        i = 2 * p
        a = (grad[i] * scale).astype(BF16)
        b = (grad[i + 1] * scale).astype(BF16)
        low[i] = a
        low[i + 1] = b
        total[...] += lax.dot_general(
            pair_windows(wide, i),
            jnp.concatenate([a, b], axis=1),
            (((1,), (1,)), ((), ())),
            preferred_element_type=F32,
        )
        return carry

    lax.fori_loop(0, rows // 2, step, 0)
    top[...] = low[:STEP]
    bottom[...] = low[rows - STEP :]
    half = total.shape[0] // 2
    sheet[...] = jnp.zeros_like(sheet)
    sheet[:half, :] = jnp.concatenate([total[:half], total[half:]], axis=1)
    h = (head_sum[:bins] + head_sum[bins : 2 * bins] + head_sum[2 * bins :]) * scale
    b = jnp.sum(bias_sum[...], axis=1, keepdims=True) * scale
    loss = jnp.sum(loss_sum[...], axis=1, keepdims=True)
    lane = lax.broadcasted_iota(jnp.int32, (bins, chans), 1)
    extra = jnp.where(lane == 0, b, jnp.where(lane == 1, loss, 0.0))
    sheet[half : half + bins, :] = jnp.concatenate([h, extra], axis=1)
    quarter = sheet.shape[0] // 4
    for s, out in enumerate((out0, out1, out2, out3)):
        out[...] = sheet[pl.ds(pl.multiple_of((place[0] ^ s) * quarter, 8), quarter), :]


def backward_kernel(count, low, up, down, left, right, grad, feat, weight, out, wide):
    rows, chans = grad.shape[0], grad.shape[1]
    scale = scale_of(count)
    spread_columns(low, up, down, left, right, wide)
    taps = weight.shape[0] // chans
    kernel = jnp.concatenate(
        [weight[(taps - 1 - t) * chans : (taps - t) * chans, :].astype(F32) for t in range(taps)],
        axis=1,
    ).astype(BF16)

    def step(p, carry):
        i = 2 * p
        back = jnp.dot(kernel, pair_windows(wide, i), preferred_element_type=F32)
        for d in range(2):
            v = feat[i + d].astype(F32)
            slope = jnp.where(v > 0, 1.0, jnp.exp(jnp.minimum(v, 0.0)))
            out[i + d] = (
                grad[i + d] * scale + slope * back[:, d * LANES : (d + 1) * LANES]
            ).astype(BF16)
        return carry

    lax.fori_loop(0, rows // 2, step, 0)


def finish_kernel(place, got0, got1, got2, got3, kernel_grad, tail, sheet):
    quarter = got0.shape[0]
    for s, got in enumerate((got0, got1, got2, got3)):
        sheet[pl.ds(pl.multiple_of((place[0] ^ s) * quarter, 8), quarter), :] = got[...]
    half, chans = kernel_grad.shape[0] // 2, kernel_grad.shape[1]
    kernel_grad[:half, :] = sheet[:half, :chans]
    kernel_grad[half:, :] = sheet[:half, chans:]
    tail[...] = sheet[half : half + tail.shape[0], :]


def borders(own, top, bottom):
    rows, chans, _ = own.shape
    up = shifted(bottom, "row", True)
    down = shifted(top, "row", False)
    groups = (rows + 2 * STEP) // 16
    first, last = run(
        pack_kernel, [shape((groups, chans, LANES), BF16)] * 2, (own, up, down), micros=1
    )
    left = shifted(last, "col", True)
    right = shifted(first, "col", False)
    return up, down, left, right


def partners(stage):
    if stage < 2:
        return lambda m: lambda r, c: (r ^ (m << (2 * stage)), c)
    if stage == 2:
        return lambda m: lambda r, c: (r ^ ((m & 1) << 4), c ^ (m >> 1))
    return lambda m: lambda r, c: (r, c ^ (m << 1))


def total_small(value):
    for bit in range(5):
        value = value + send(value, lambda r, c: (r ^ (1 << bit), c))
    for bit in range(3):
        value = value + send(value, lambda r, c: (r, c ^ (1 << bit)))
    return value


def total_quarters(quarters):
    near = partners(0)
    a, b, c, d = quarters
    part = (a + send(b, near(1))) + (send(c, near(2)) + send(d, near(3)))
    for stage in (1, 2, 3):
        to = partners(stage)
        part = (part + send(part, to(1))) + (send(part, to(2)) + send(part, to(3)))
    return [part] + [send(part, near(m)) for m in (1, 2, 3)]


def per_device(features, conv_weight, head_weight, head_bias, labels, valid):
    rows, cols, chans = features.shape
    bins = head_weight.shape[1]
    parts = cols // rows
    place = (lax.axis_index("row") % parts).astype(jnp.int32).reshape(1)
    feat = features.transpose(0, 2, 1)
    weight = conv_weight.reshape(-1, chans)
    tall = -(-bins // 8) * 8
    head = jnp.concatenate(
        [
            jnp.pad(head_weight.T.astype(F32), ((0, tall - bins), (0, 0))),
            jnp.pad(head_bias, (0, tall - bins), constant_values=FAR_BELOW)[:, None],
            jnp.zeros((tall, LANES - chans - 1), F32),
        ],
        axis=1,
    )
    counted = jnp.full((8, LANES), jnp.sum(valid.astype(F32)))
    tile = (rows, chans, LANES)
    edge = (STEP, chans, LANES)
    act, top, bottom = run(
        activate_kernel, [shape(tile, BF16), shape(edge, BF16), shape(edge, BF16)], (feat,), micros=1
    )
    around = borders(act, top, bottom)
    count = total_small(counted)
    length = (rows + 1) * rows // 2
    wide, mixed, *pays = run(
        forward_kernel,
        [shape((rows + 2 * STEP, 3 * chans, LANES), BF16), shape(tile, BF16)]
        + [shape((length, LANES), BF16)] * 4,
        (place, act, *around, feat, weight, labels, valid),
        scratch=[pltpu.VMEM(((rows + 1) * LANES, chans), F32)],
        scalars=1,
        micros=5,
    )
    got = [
        send(pays[s], lambda r, c: (parts * c + (r % parts ^ s), r // parts)) for s in range(parts)
    ]
    grad, head_sum, bias_sum, loss_sum = run(
        softmax_kernel,
        [
            shape(tile, F32),
            shape((3 * tall, chans), F32),
            shape((tall, LANES), F32),
            shape((1, LANES), F32),
        ],
        (place, *got, mixed, head, labels, valid),
        scratch=[pltpu.VMEM((length * 4, LANES), F32)] + [pltpu.VMEM((rows, LANES), F32)] * 4,
        scalars=1,
        micros=5,
    )
    half = 9 * chans // 2
    lines = -(-(half + tall) // 32) * 32
    low, top, bottom, *quarters = run(
        kernel_grad_kernel,
        [shape(tile, BF16), shape(edge, BF16), shape(edge, BF16)]
        + [shape((lines // 4, LANES), F32)] * 4,
        (place, count, grad, wide, head_sum, bias_sum, loss_sum),
        scratch=[pltpu.VMEM((9 * chans, chans), F32), pltpu.VMEM((lines, LANES), F32)],
        scalars=1,
        micros=3,
    )
    sums = total_quarters(quarters)
    around = borders(low, top, bottom)
    (grad_features,) = run(
        backward_kernel,
        [shape(tile, BF16)],
        (count, low, *around, grad, feat, weight),
        scratch=[pltpu.VMEM((rows + 2 * STEP, 3 * chans, LANES), BF16)],
        micros=4,
    )
    kernel_grad, tail = run(
        finish_kernel,
        [shape((9 * chans, chans), F32), shape((tall, LANES), F32)],
        (place, *sums),
        scratch=[pltpu.VMEM((lines, LANES), F32)],
        scalars=1,
        micros=1,
    )
    loss = tail[0, chans + 1] / jnp.maximum(count[0, 0], 1.0)
    return (
        loss,
        grad_features.transpose(0, 2, 1),
        kernel_grad.reshape(conv_weight.shape),
        tail[:bins, :chans].T,
        tail[:bins, chans],
    )


def solution(mesh):
    placed = (P("row", "col", None), P(), P(), P(), P("row", "col"), P("row", "col"))
    return jax.shard_map(
        per_device,
        mesh=mesh,
        in_specs=placed,
        out_specs=(P(), P("row", "col", None), P(), P(), P()),
        check_vma=False,
    )
```

time: 202 us -> 171 us (0.85)
  Pallas kernels: 0 us -> 26.7 us
  local copies, waits for them, and re-layouts: 31.8 us -> 8.3 us
  waiting for transfers between devices: 61.5 us -> 40.7 us
  matrix products: 15.3 us -> 0 us
  starting transfers between devices: 74.2 us -> 86.1 us
  other arithmetic: 13.5 us -> 3.48 us
    pallas_call x0 -> x8, Pallas kernels: none -> 26.7 us  [run(): pl.pallas_call(body, out_shape=outs, in_specs=[SMEM] * scalars + [VMEM] *...]
    dot_general x31 -> x0, matrix products: 15.3 us -> none  [the longest x18 5.58 us: taps_product(): jnp.dot(window.reshape(-1, width), kernel, preferred_element_type=jnp.flo...]
    ppermute x27, starting transfers between devices: 44 us -> 55.3 us  [send(): return lax.ppermute(block, GRID, pairs)]
    ppermute x8, waiting for transfers between devices: 10.8 us -> 0.22 us  [shifted(): lax.ppermute(block, axis, pairs if forward else [(b, a) for a, b in pairs])]
    ppermute x27, waiting for transfers between devices: 50.8 us -> 40.4 us  [send(): return lax.ppermute(block, GRID, pairs)]
    reshape x13 -> x0, local copies, waits for them, and re-layouts: 7.04 us -> none  [the longest x1 1.79 us: mirror(): mix.reshape(parts, split, 128)]
    concatenate x5 -> x1, other arithmetic: 4.6 us -> 0.08 us  [per_device(): jnp.concatenate([jnp.pad(head_weight.T.astype(F32), ((0, tall - bins), (0...]
    unnamed x70 -> x12, local copies, waits for them, and re-layouts: 8.54 us -> 4.43 us
  transfers between devices with their start and end apart: 35 -> 35, of which waited for: 20 -> 12; matrix products, arithmetic and copies ran while one was open for 8% -> 2% of each run, Pallas kernels for 0% -> 9%
where the time goes in v2:
time: 171 us; the launch traced here: 169 us
  starting transfers between devices  86.1 us (50%)
  waiting for transfers between devices  40.7 us (24%)
  Pallas kernels  26.7 us (16%)
  local copies, waits for them, and re-layouts  8.3 us (5%)
  other arithmetic  3.48 us (2%)
  between operations  3.4 us (2%)
    ppermute x27, starting transfers between devices, send(): return lax.ppermute(block, GRID, pairs)  55.3 us
    ppermute x27, waiting for transfers between devices, send(): return lax.ppermute(block, GRID, pairs)  40.4 us
    ppermute x8, starting transfers between devices, shifted(): lax.ppermute(block, axis, pairs if forward else [(b, a) for a, b in pairs])  30.8 us
    pallas_call x8, Pallas kernels, run(): pl.pallas_call(body, out_shape=outs, in_specs=[SMEM] * scalars + [VMEM] *...  26.7 us
    unnamed x12, local copies, waits for them, and re-layouts  4.43 us
  transfers between devices with their start and end apart: 35, of which 12 were waited for; matrix products, arithmetic and copies ran while one was open for 2% of the time, Pallas kernels for 9%

profile of v2, /device:TPU:24, one launch (start us, length us, event | category | flops | bytes accessed | tf_op | source)
XLA Modules:
  0.0 168.7 jit_solution(6479971152999827460)
XLA Ops:
  0.6 1.3 convert_reduce_fusion
  2.7 1.2 collective-permute-done
  4.5 2.0 %collective-permute-start.1 = (f32[8,128]{1,0:T(8,128)S(1)}, f32[8,128]{1,0:T(8,128)S(1)}, u32[]{:S(2)}, u32[]{:S(2)}) collective-permute-start(f32[8,128]{1,0:T(8,128)S(1)} %broadcast_add_fusion), channel_id=1, source_target_pairs={{0,16},{1,17},{2,18},{3,19},{4,20},{5,21},{6,22},{7,23},{8,24},{9,... | collective-permute-start | bytes 12296 | tf_op jit(solution)/shard_map/ppermute | solution.py:42
  6.5 1.0 copy-done
  7.6 0.8 shard_map.101
  8.4 1.9 %collective-permute-start.8 = (bf16[8,64,128]{2,1,0:T(8,128)(2,1)S(1)}, bf16[8,64,128]{2,1,0:T(8,128)(2,1)S(1)}, u32[]{:S(2)}, u32[]{:S(2)}) collective-permute-start(bf16[8,64,128]{2,1,0:T(8,128)(2,1)S(1)} %get-tuple-element.32), channel_id=1, source_target_pairs={{0,8},{8,16},{16,24},{24,32},{32,40},{40,48},{48,56},{56,64},{64,7... | collective-permute-start | bytes 393224 | tf_op jit(solution)/shard_map/ppermute | solution.py:48
  10.3 6.5 %collective-permute-start.9 = (bf16[8,64,128]{2,1,0:T(8,128)(2,1)S(1)}, bf16[8,64,128]{2,1,0:T(8,128)(2,1)S(1)}, u32[]{:S(2)}, u32[]{:S(2)}) collective-permute-start(bf16[8,64,128]{2,1,0:T(8,128)(2,1)S(1)} %get-tuple-element.33), channel_id=1, source_target_pairs={{8,0},{16,8},{24,16},{32,24},{40,32},{48,40},{56,48},{64,56},{72,6... | collective-permute-start | bytes 393224 | tf_op jit(solution)/shard_map/ppermute | solution.py:48
  18.0 4.1 %collective-permute-done.2 = f32[8,128]{1,0:T(8,128)S(1)} collective-permute-done((f32[8,128]{1,0:T(8,128)S(1)}, f32[8,128]{1,0:T(8,128)S(1)}, u32[]{:S(2)}, u32[]{:S(2)}) %collective-permute-start.2) | collective-permute-done | bytes 4128 | tf_op jit(solution)/shard_map/ppermute | solution.py:42
  22.1 4.6 %collective-permute-start.3 = (f32[8,128]{1,0:T(8,128)S(1)}, f32[8,128]{1,0:T(8,128)S(1)}, u32[]{:S(2)}, u32[]{:S(2)}) collective-permute-start(f32[8,128]{1,0:T(8,128)S(1)} %add.71), channel_id=1, source_target_pairs={{0,64},{1,65},{2,66},{3,67},{4,68},{5,69},{6,70},{7,71},{8,72},{9,... | collective-permute-start | bytes 12296 | tf_op jit(solution)/shard_map/ppermute | solution.py:42
  26.7 2.9 %collective-permute-done.3 = f32[8,128]{1,0:T(8,128)S(1)} collective-permute-done((f32[8,128]{1,0:T(8,128)S(1)}, f32[8,128]{1,0:T(8,128)S(1)}, u32[]{:S(2)}, u32[]{:S(2)}) %collective-permute-start.3) | collective-permute-done | bytes 4128 | tf_op jit(solution)/shard_map/ppermute | solution.py:42
  29.6 3.6 %collective-permute-done.4 = f32[8,128]{1,0:T(8,128)S(1)} collective-permute-done((f32[8,128]{1,0:T(8,128)S(1)}, f32[8,128]{1,0:T(8,128)S(1)}, u32[]{:S(2)}, u32[]{:S(2)}) %collective-permute-start.4) | collective-permute-done | bytes 4128 | tf_op jit(solution)/shard_map/ppermute | solution.py:42
  33.3 0.9 collective-permute-start.5
  34.2 0.7 pad_convert_fusion
  34.9 3.5 %collective-permute-done.5 = f32[8,128]{1,0:T(8,128)S(1)} collective-permute-done((f32[8,128]{1,0:T(8,128)S(1)}, f32[8,128]{1,0:T(8,128)S(1)}, u32[]{:S(2)}, u32[]{:S(2)}) %collective-permute-start.5) | collective-permute-done | bytes 4128 | tf_op jit(solution)/shard_map/ppermute | solution.py:42
  38.4 1.5 collective-permute-start.6
  40.3 2.8 %collective-permute-start.10 = (bf16[3,64,128]{2,1,0:T(8,128)(2,1)S(1)}, bf16[3,64,128]{2,1,0:T(8,128)(2,1)S(1)}, u32[]{:S(2)}, u32[]{:S(2)}) collective-permute-start(bf16[3,64,128]{2,1,0:T(8,128)(2,1)S(1)} %get-tuple-element.34), channel_id=1, source_target_pairs={{0,1},{1,2},{2,3},{3,4},{4,5},{5,6},{6,7},{8,9},{9,10},{10,11},{11... | collective-permute-start | bytes 147464 | tf_op jit(solution)/shard_map/ppermute | solution.py:48
  43.2 4.5 %collective-permute-start.11 = (bf16[3,64,128]{2,1,0:T(8,128)(2,1)S(1)}, bf16[3,64,128]{2,1,0:T(8,128)(2,1)S(1)}, u32[]{:S(2)}, u32[]{:S(2)}) collective-permute-start(bf16[3,64,128]{2,1,0:T(8,128)(2,1)S(1)} %get-tuple-element.35), channel_id=1, source_target_pairs={{1,0},{2,1},{3,2},{4,3},{5,4},{6,5},{7,6},{9,8},{10,9},{11,10},{12... | collective-permute-start | bytes 147464 | tf_op jit(solution)/shard_map/ppermute | solution.py:48
  48.5 2.8 %collective-permute-start.7 = (f32[8,128]{1,0:T(8,128)S(1)}, f32[8,128]{1,0:T(8,128)S(1)}, u32[]{:S(2)}, u32[]{:S(2)}) collective-permute-start(f32[8,128]{1,0:T(8,128)S(1)} %add.75), channel_id=1, source_target_pairs={{0,4},{1,5},{2,6},{3,7},{4,0},{5,1},{6,2},{7,3},{8,12},{9,13},{10,... | collective-permute-start | bytes 12296 | tf_op jit(solution)/shard_map/ppermute | solution.py:42
  51.5 1.0 copy-done.1
  52.6 0.9 copy-done.3
  53.5 0.7 copy-done.4
  54.2 0.7 copy-done.5
  54.9 8.0 %shard_map.103 = (bf16[48,192,128]{2,1,0:T(8,128)(2,1)S(1)}, bf16[32,64,128]{2,1,0:T(8,128)(2,1)S(1)}, bf16[528,128]{1,0:T(8,128)(2,1)S(1)}, bf16[528,128]{1,0:T...) custom-call(s32[1]{0:T(128)} %bitcast.place, ...), custom_call_target="tpu_custom_call" | custom-call | bytes 18000000 | tf_op jit(solution)/shard_map/pallas_call | solution.py:18
  63.0 5.5 %collective-permute-start.12 = (bf16[528,128]{1,0:T(8,128)(2,1)S(1)}, bf16[528,128]{1,0:T(8,128)(2,1)S(1)}, u32[]{:S(2)}, u32[]{:S(2)}) collective-permute-start(bf16[528,128]{1,0:T(8,128)(2,1)S(1)} %get-tuple-element.36), channel_id=1, source_target_pairs={{0,0},{1,32},{2,64},{3,96},{4,128},{5,160},{6,192},{7,224},{8,8},{... | collective-permute-start | bytes 405512 | tf_op jit(solution)/shard_map/ppermute | solution.py:42
  68.6 2.4 %collective-permute-start.14 = (bf16[528,128]{1,0:T(8,128)(2,1)S(1)}, bf16[528,128]{1,0:T(8,128)(2,1)S(1)}, u32[]{:S(2)}, u32[]{:S(2)}) collective-permute-start(bf16[528,128]{1,0:T(8,128)(2,1)S(1)} %get-tuple-element.38), channel_id=1, source_target_pairs={{0,16},{1,48},{2,80},{3,112},{4,144},{5,176},{6,208},{7,240},{8,24... | collective-permute-start | bytes 405512 | tf_op jit(solution)/shard_map/ppermute | solution.py:42
  71.0 9.2 %collective-permute-start.15 = (bf16[528,128]{1,0:T(8,128)(2,1)S(1)}, bf16[528,128]{1,0:T(8,128)(2,1)S(1)}, u32[]{:S(2)}, u32[]{:S(2)}) collective-permute-start(bf16[528,128]{1,0:T(8,128)(2,1)S(1)} %get-tuple-element.39), channel_id=1, source_target_pairs={{0,24},{1,56},{2,88},{3,120},{4,152},{5,184},{6,216},{7,248},{8,16... | collective-permute-start | bytes 405512 | tf_op jit(solution)/shard_map/ppermute | solution.py:42
  80.3 14.5 %collective-permute-done.12.got0 = bf16[528,128]{1,0:T(8,128)(2,1)S(1)} collective-permute-done((bf16[528,128]{1,0:T(8,128)(2,1)S(1)}, bf16[528,128]{1,0:T(8,128)(2,1)S(1)}, u32[]{:S(2)}, u32[]{:S(2)}) %collective-permute-start.12) | collective-permute-done | bytes 135200 | tf_op jit(solution)/shard_map/ppermute | solution.py:42
  94.7 1.1 collective-permute-done.13.got1
  95.8 6.9 %shard_map.104 = (f32[32,64,128]{2,1,0:T(8,128)S(1)}, f32[120,64]{1,0:T(8,128)S(1)}, f32[40,128]{1,0:T(8,128)S(1)}, f32[1,128]{1,0:T(1,128)S(1)}) custom-call(s32[1]{0:T(128)} %bitcast.place, bf16[528,128]{1,0:T(8,128)(2,1)S(1)} %collective-permute-done.12.got0, bf16[528,128]{1,0:T(8,128)(2,1)S(1)} %collective-permute-done.13.got1, ...), custom_call_target="tpu_custom_call" | custom-call | bytes 18000000 | tf_op jit(solution)/shard_map/pallas_call | solution.py:18
  102.7 4.4 %shard_map.105 = (bf16[32,64,128]{2,1,0:T(8,128)(2,1)S(1)}, bf16[8,64,128]{2,1,0:T(8,128)(2,1)S(1)}, bf16[8,64,128]{2,1,0:T(8,128)(2,1)S(1)}, f32[88,128]{1,0:T(...) custom-call(s32[1]{0:T(128)} %bitcast.place, f32[8,128]{1,0:T(8,128)S(1)} %add.76.count, ...), custom_call_target="tpu_custom_call" | custom-call | bytes 10800000 | tf_op jit(solution)/shard_map/pallas_call | solution.py:18
  107.2 1.7 %collective-permute-start.16 = (f32[88,128]{1,0:T(8,128)S(1)}, f32[88,128]{1,0:T(8,128)S(1)}, u32[]{:S(2)}, u32[]{:S(2)}) collective-permute-start(f32[88,128]{1,0:T(8,128)S(1)} %get-tuple-element.47), channel_id=1, source_target_pairs={{0,8},{1,9},{2,10},{3,11},{4,12},{5,13},{6,14},{7,15},{8,0},{9,1},... | collective-permute-start | bytes 135176 | tf_op jit(solution)/shard_map/ppermute | solution.py:42
  108.9 5.4 %collective-permute-start.17 = (f32[88,128]{1,0:T(8,128)S(1)}, f32[88,128]{1,0:T(8,128)S(1)}, u32[]{:S(2)}, u32[]{:S(2)}) collective-permute-start(f32[88,128]{1,0:T(8,128)S(1)} %get-tuple-element.48), channel_id=1, source_target_pairs={{0,16},{1,17},{2,18},{3,19},{4,20},{5,21},{6,22},{7,23},{8,24},{9,... | collective-permute-start | bytes 135176 | tf_op jit(solution)/shard_map/ppermute | solution.py:42
  114.4 2.0 %collective-permute-done.17 = f32[88,128]{1,0:T(8,128)S(1)} collective-permute-done((f32[88,128]{1,0:T(8,128)S(1)}, f32[88,128]{1,0:T(8,128)S(1)}, u32[]{:S(2)}, u32[]{:S(2)}) %collective-permute-start.17) | collective-permute-done | bytes 45088 | tf_op jit(solution)/shard_map/ppermute | solution.py:42
  116.4 1.9 %collective-permute-done.18 = f32[88,128]{1,0:T(8,128)S(1)} collective-permute-done((f32[88,128]{1,0:T(8,128)S(1)}, f32[88,128]{1,0:T(8,128)S(1)}, u32[]{:S(2)}, u32[]{:S(2)}) %collective-permute-start.18) | collective-permute-done | bytes 45088 | tf_op jit(solution)/shard_map/ppermute | solution.py:42
  118.4 6.2 %collective-permute-start.20 = (f32[88,128]{1,0:T(8,128)S(1)}, f32[88,128]{1,0:T(8,128)S(1)}, u32[]{:S(2)}, u32[]{:S(2)}) collective-permute-start(f32[88,128]{1,0:T(8,128)S(1)} %add_add_fusion.3), channel_id=1, source_target_pairs={{0,64},{1,65},{2,66},{3,67},{4,68},{5,69},{6,70},{7,71},{8,72},{9,... | collective-permute-start | bytes 135176 | tf_op jit(solution)/shard_map/ppermute | solution.py:42
  125.1 2.7 %collective-permute-done.20 = f32[88,128]{1,0:T(8,128)S(1)} collective-permute-done((f32[88,128]{1,0:T(8,128)S(1)}, f32[88,128]{1,0:T(8,128)S(1)}, u32[]{:S(2)}, u32[]{:S(2)}) %collective-permute-start.20) | collective-permute-done | bytes 45088 | tf_op jit(solution)/shard_map/ppermute | solution.py:42
  127.8 3.0 %collective-permute-done.21 = f32[88,128]{1,0:T(8,128)S(1)} collective-permute-done((f32[88,128]{1,0:T(8,128)S(1)}, f32[88,128]{1,0:T(8,128)S(1)}, u32[]{:S(2)}, u32[]{:S(2)}) %collective-permute-start.21) | collective-permute-done | bytes 45088 | tf_op jit(solution)/shard_map/ppermute | solution.py:42
  131.1 4.3 %collective-permute-start.23 = (f32[88,128]{1,0:T(8,128)S(1)}, f32[88,128]{1,0:T(8,128)S(1)}, u32[]{:S(2)}, u32[]{:S(2)}) collective-permute-start(f32[88,128]{1,0:T(8,128)S(1)} %add_add_fusion.2), channel_id=1, source_target_pairs={{0,1},{1,0},{2,3},{3,2},{4,5},{5,4},{6,7},{7,6},{8,9},{9,8},{10,11... | collective-permute-start | bytes 135176 | tf_op jit(solution)/shard_map/ppermute | solution.py:42
  135.8 1.9 %collective-permute-start.31 = (bf16[8,64,128]{2,1,0:T(8,128)(2,1)S(1)}, bf16[8,64,128]{2,1,0:T(8,128)(2,1)S(1)}, u32[]{:S(2)}, u32[]{:S(2)}) collective-permute-start(bf16[8,64,128]{2,1,0:T(8,128)(2,1)S(1)} %get-tuple-element.52), channel_id=1, source_target_pairs={{0,8},{8,16},{16,24},{24,32},{32,40},{40,48},{48,56},{56,64},{64,7... | collective-permute-start | bytes 393224 | tf_op jit(solution)/shard_map/ppermute | solution.py:48
  137.7 5.8 %collective-permute-start.32 = (bf16[8,64,128]{2,1,0:T(8,128)(2,1)S(1)}, bf16[8,64,128]{2,1,0:T(8,128)(2,1)S(1)}, u32[]{:S(2)}, u32[]{:S(2)}) collective-permute-start(bf16[8,64,128]{2,1,0:T(8,128)(2,1)S(1)} %get-tuple-element.53), channel_id=1, source_target_pairs={{8,0},{16,8},{24,16},{32,24},{40,32},{48,40},{56,48},{64,56},{72,6... | collective-permute-start | bytes 393224 | tf_op jit(solution)/shard_map/ppermute | solution.py:48
  143.5 2.0 %collective-permute-start.25 = (f32[88,128]{1,0:T(8,128)S(1)}, f32[88,128]{1,0:T(8,128)S(1)}, u32[]{:S(2)}, u32[]{:S(2)}) collective-permute-start(f32[88,128]{1,0:T(8,128)S(1)} %add_add_fusion.1), channel_id=1, source_target_pairs={{0,2},{1,3},{2,0},{3,1},{4,6},{5,7},{6,4},{7,5},{8,10},{9,11},{10,... | collective-permute-start | bytes 135176 | tf_op jit(solution)/shard_map/ppermute | solution.py:42
  145.5 2.8 %collective-permute-start.27 = (f32[88,128]{1,0:T(8,128)S(1)}, f32[88,128]{1,0:T(8,128)S(1)}, u32[]{:S(2)}, u32[]{:S(2)}) collective-permute-start(f32[88,128]{1,0:T(8,128)S(1)} %add_add_fusion.1), channel_id=1, source_target_pairs={{0,6},{1,7},{2,4},{3,5},{4,2},{5,3},{6,0},{7,1},{8,14},{9,15},{10,... | collective-permute-start | bytes 135176 | tf_op jit(solution)/shard_map/ppermute | solution.py:42
  148.8 1.9 %collective-permute-start.33 = (bf16[3,64,128]{2,1,0:T(8,128)(2,1)S(1)}, bf16[3,64,128]{2,1,0:T(8,128)(2,1)S(1)}, u32[]{:S(2)}, u32[]{:S(2)}) collective-permute-start(bf16[3,64,128]{2,1,0:T(8,128)(2,1)S(1)} %get-tuple-element.54), channel_id=1, source_target_pairs={{0,1},{1,2},{2,3},{3,4},{4,5},{5,6},{6,7},{8,9},{9,10},{10,11},{11... | collective-permute-start | bytes 147464 | tf_op jit(solution)/shard_map/ppermute | solution.py:48
  150.7 5.4 %collective-permute-start.34 = (bf16[3,64,128]{2,1,0:T(8,128)(2,1)S(1)}, bf16[3,64,128]{2,1,0:T(8,128)(2,1)S(1)}, u32[]{:S(2)}, u32[]{:S(2)}) collective-permute-start(bf16[3,64,128]{2,1,0:T(8,128)(2,1)S(1)} %get-tuple-element.55), channel_id=1, source_target_pairs={{1,0},{2,1},{3,2},{4,3},{5,4},{6,5},{7,6},{9,8},{10,9},{11,10},{12... | collective-permute-start | bytes 147464 | tf_op jit(solution)/shard_map/ppermute | solution.py:48
  156.4 1.8 %collective-permute-start.30 = (f32[88,128]{1,0:T(8,128)S(1)}, f32[88,128]{1,0:T(8,128)S(1)}, u32[]{:S(2)}, u32[]{:S(2)}) collective-permute-start(f32[88,128]{1,0:T(8,128)S(1)} %add_add_fusion.got0), channel_id=1, source_target_pairs={{0,24},{1,25},{2,26},{3,27},{4,28},{5,29},{6,30},{7,31},{8,16},{9,... | collective-permute-start | bytes 135176 | tf_op jit(solution)/shard_map/ppermute | solution.py:42
  159.4 4.8 %shard_map.108 = bf16[32,64,128]{2,1,0:T(8,128)(2,1)} custom-call(f32[8,128]{1,0:T(8,128)S(1)} %add.76.count, bf16[32,64,128]{2,1,0:T(8,128)(2,1)S(1)} %get-tuple-element.51.own.low, bf16[8,64,128]{2,1,0:T(8,128)(2,1)S(1)} %collective-permute-done.31.up, bf16[8,64,128]{2,1,0:T(8,128)(2,1)S(1)} %collective-permute-done.32.down, ...), custom_call_target="tpu_custom_call" | custom-call | bytes 14400000 | tf_op jit(solution)/shard_map/pallas_call | solution.py:18
  164.2 0.8 shard_map.106
  166.2 0.7 slice_reduce_fusion
  (66 shorter events, 7.9 us)
Async XLA Ops:
  2.6 1.3 collective-permute-start
  4.5 12.3 %collective-permute-start.1 = (f32[8,128]{1,0:T(8,128)S(1)}, f32[8,128]{1,0:T(8,128)S(1)}, u32[]{:S(2)}, u32[]{:S(2)}) collective-permute-start(f32[8,128]{1,0:T(8,128)S(1)} %broadcast_add_fusion), channel_id=1, source_target_pairs={{0,16},{1,17},{2,18},{3,19},{4,20},{5,21},{6,22},{7,23},{8,24},{9,... | collective-permute-start | bytes 12296 | tf_op jit(solution)/shard_map/ppermute | solution.py:42
  6.5 1.0 copy-start
  8.4 31.5 %collective-permute-start.8 = (bf16[8,64,128]{2,1,0:T(8,128)(2,1)S(1)}, bf16[8,64,128]{2,1,0:T(8,128)(2,1)S(1)}, u32[]{:S(2)}, u32[]{:S(2)}) collective-permute-start(bf16[8,64,128]{2,1,0:T(8,128)(2,1)S(1)} %get-tuple-element.32), channel_id=1, source_target_pairs={{0,8},{8,16},{16,24},{24,32},{32,40},{40,48},{48,56},{56,64},{64,7... | collective-permute-start | bytes 393224 | tf_op jit(solution)/shard_map/ppermute | solution.py:48
  10.3 29.5 %collective-permute-start.9 = (bf16[8,64,128]{2,1,0:T(8,128)(2,1)S(1)}, bf16[8,64,128]{2,1,0:T(8,128)(2,1)S(1)}, u32[]{:S(2)}, u32[]{:S(2)}) collective-permute-start(bf16[8,64,128]{2,1,0:T(8,128)(2,1)S(1)} %get-tuple-element.33), channel_id=1, source_target_pairs={{8,0},{16,8},{24,16},{32,24},{40,32},{48,40},{56,48},{64,56},{72,6... | collective-permute-start | bytes 393224 | tf_op jit(solution)/shard_map/ppermute | solution.py:48
  17.5 4.6 %collective-permute-start.2 = (f32[8,128]{1,0:T(8,128)S(1)}, f32[8,128]{1,0:T(8,128)S(1)}, u32[]{:S(2)}, u32[]{:S(2)}) collective-permute-start(f32[8,128]{1,0:T(8,128)S(1)} %fusion), channel_id=1, source_target_pairs={{0,32},{1,33},{2,34},{3,35},{4,36},{5,37},{6,38},{7,39},{8,40},{9,... | collective-permute-start | bytes 12296 | tf_op jit(solution)/shard_map/ppermute | solution.py:42
  22.1 7.5 %collective-permute-start.3 = (f32[8,128]{1,0:T(8,128)S(1)}, f32[8,128]{1,0:T(8,128)S(1)}, u32[]{:S(2)}, u32[]{:S(2)}) collective-permute-start(f32[8,128]{1,0:T(8,128)S(1)} %add.71), channel_id=1, source_target_pairs={{0,64},{1,65},{2,66},{3,67},{4,68},{5,69},{6,70},{7,71},{8,72},{9,... | collective-permute-start | bytes 12296 | tf_op jit(solution)/shard_map/ppermute | solution.py:42
  29.6 3.6 %collective-permute-start.4 = (f32[8,128]{1,0:T(8,128)S(1)}, f32[8,128]{1,0:T(8,128)S(1)}, u32[]{:S(2)}, u32[]{:S(2)}) collective-permute-start(f32[8,128]{1,0:T(8,128)S(1)} %add.72), channel_id=1, source_target_pairs={{0,128},{1,129},{2,130},{3,131},{4,132},{5,133},{6,134},{7,135},{8... | collective-permute-start | bytes 12296 | tf_op jit(solution)/shard_map/ppermute | solution.py:42
  33.3 5.1 %collective-permute-start.5 = (f32[8,128]{1,0:T(8,128)S(1)}, f32[8,128]{1,0:T(8,128)S(1)}, u32[]{:S(2)}, u32[]{:S(2)}) collective-permute-start(f32[8,128]{1,0:T(8,128)S(1)} %add.73), channel_id=1, source_target_pairs={{0,1},{1,0},{2,3},{3,2},{4,5},{5,4},{6,7},{7,6},{8,9},{9,8},{10,11... | collective-permute-start | bytes 12296 | tf_op jit(solution)/shard_map/ppermute | solution.py:42
  38.4 10.2 %collective-permute-start.6 = (f32[8,128]{1,0:T(8,128)S(1)}, f32[8,128]{1,0:T(8,128)S(1)}, u32[]{:S(2)}, u32[]{:S(2)}) collective-permute-start(f32[8,128]{1,0:T(8,128)S(1)} %add.74), channel_id=1, source_target_pairs={{0,2},{1,3},{2,0},{3,1},{4,6},{5,7},{6,4},{7,5},{8,10},{9,11},{10,... | collective-permute-start | bytes 12296 | tf_op jit(solution)/shard_map/ppermute | solution.py:42
  40.3 11.0 %collective-permute-start.10 = (bf16[3,64,128]{2,1,0:T(8,128)(2,1)S(1)}, bf16[3,64,128]{2,1,0:T(8,128)(2,1)S(1)}, u32[]{:S(2)}, u32[]{:S(2)}) collective-permute-start(bf16[3,64,128]{2,1,0:T(8,128)(2,1)S(1)} %get-tuple-element.34), channel_id=1, source_target_pairs={{0,1},{1,2},{2,3},{3,4},{4,5},{5,6},{6,7},{8,9},{9,10},{10,11},{11... | collective-permute-start | bytes 147464 | tf_op jit(solution)/shard_map/ppermute | solution.py:48
  43.2 8.4 %collective-permute-start.11 = (bf16[3,64,128]{2,1,0:T(8,128)(2,1)S(1)}, bf16[3,64,128]{2,1,0:T(8,128)(2,1)S(1)}, u32[]{:S(2)}, u32[]{:S(2)}) collective-permute-start(bf16[3,64,128]{2,1,0:T(8,128)(2,1)S(1)} %get-tuple-element.35), channel_id=1, source_target_pairs={{1,0},{2,1},{3,2},{4,3},{5,4},{6,5},{7,6},{9,8},{10,9},{11,10},{12... | collective-permute-start | bytes 147464 | tf_op jit(solution)/shard_map/ppermute | solution.py:48
  48.5 31.7 %collective-permute-start.7 = (f32[8,128]{1,0:T(8,128)S(1)}, f32[8,128]{1,0:T(8,128)S(1)}, u32[]{:S(2)}, u32[]{:S(2)}) collective-permute-start(f32[8,128]{1,0:T(8,128)S(1)} %add.75), channel_id=1, source_target_pairs={{0,4},{1,5},{2,6},{3,7},{4,0},{5,1},{6,2},{7,3},{8,12},{9,13},{10,... | collective-permute-start | bytes 12296 | tf_op jit(solution)/shard_map/ppermute | solution.py:42
  51.5 1.0 copy-start.1
  52.6 0.9 copy-start.3
  53.5 0.7 copy-start.4
  54.2 0.7 copy-start.5
  63.0 31.8 %collective-permute-start.12 = (bf16[528,128]{1,0:T(8,128)(2,1)S(1)}, bf16[528,128]{1,0:T(8,128)(2,1)S(1)}, u32[]{:S(2)}, u32[]{:S(2)}) collective-permute-start(bf16[528,128]{1,0:T(8,128)(2,1)S(1)} %get-tuple-element.36), channel_id=1, source_target_pairs={{0,0},{1,32},{2,64},{3,96},{4,128},{5,160},{6,192},{7,224},{8,8},{... | collective-permute-start | bytes 405512 | tf_op jit(solution)/shard_map/ppermute | solution.py:42
  68.5 27.3 %collective-permute-start.13 = (bf16[528,128]{1,0:T(8,128)(2,1)S(1)}, bf16[528,128]{1,0:T(8,128)(2,1)S(1)}, u32[]{:S(2)}, u32[]{:S(2)}) collective-permute-start(bf16[528,128]{1,0:T(8,128)(2,1)S(1)} %get-tuple-element.37), channel_id=1, source_target_pairs={{0,8},{1,40},{2,72},{3,104},{4,136},{5,168},{6,200},{7,232},{8,0},... | collective-permute-start | bytes 405512 | tf_op jit(solution)/shard_map/ppermute | solution.py:42
  68.6 27.2 %collective-permute-start.14 = (bf16[528,128]{1,0:T(8,128)(2,1)S(1)}, bf16[528,128]{1,0:T(8,128)(2,1)S(1)}, u32[]{:S(2)}, u32[]{:S(2)}) collective-permute-start(bf16[528,128]{1,0:T(8,128)(2,1)S(1)} %get-tuple-element.38), channel_id=1, source_target_pairs={{0,16},{1,48},{2,80},{3,112},{4,144},{5,176},{6,208},{7,240},{8,24... | collective-permute-start | bytes 405512 | tf_op jit(solution)/shard_map/ppermute | solution.py:42
  71.0 24.8 %collective-permute-start.15 = (bf16[528,128]{1,0:T(8,128)(2,1)S(1)}, bf16[528,128]{1,0:T(8,128)(2,1)S(1)}, u32[]{:S(2)}, u32[]{:S(2)}) collective-permute-start(bf16[528,128]{1,0:T(8,128)(2,1)S(1)} %get-tuple-element.39), channel_id=1, source_target_pairs={{0,24},{1,56},{2,88},{3,120},{4,152},{5,184},{6,216},{7,248},{8,16... | collective-permute-start | bytes 405512 | tf_op jit(solution)/shard_map/ppermute | solution.py:42
  102.7 56.6 %copy-start.2 = (bf16[32,128,64]{1,2,0:T(8,128)(2,1)S(1)}, bf16[32,128,64]{1,2,0:T(8,128)(2,1)}, u32[]{:S(2)}) copy-start(bf16[32,128,64]{1,2,0:T(8,128)(2,1)} %param.6) | copy-start | bytes 1572868
  107.2 7.2 %collective-permute-start.16 = (f32[88,128]{1,0:T(8,128)S(1)}, f32[88,128]{1,0:T(8,128)S(1)}, u32[]{:S(2)}, u32[]{:S(2)}) collective-permute-start(f32[88,128]{1,0:T(8,128)S(1)} %get-tuple-element.47), channel_id=1, source_target_pairs={{0,8},{1,9},{2,10},{3,11},{4,12},{5,13},{6,14},{7,15},{8,0},{9,1},... | collective-permute-start | bytes 135176 | tf_op jit(solution)/shard_map/ppermute | solution.py:42
  108.9 7.5 %collective-permute-start.17 = (f32[88,128]{1,0:T(8,128)S(1)}, f32[88,128]{1,0:T(8,128)S(1)}, u32[]{:S(2)}, u32[]{:S(2)}) collective-permute-start(f32[88,128]{1,0:T(8,128)S(1)} %get-tuple-element.48), channel_id=1, source_target_pairs={{0,16},{1,17},{2,18},{3,19},{4,20},{5,21},{6,22},{7,23},{8,24},{9,... | collective-permute-start | bytes 135176 | tf_op jit(solution)/shard_map/ppermute | solution.py:42
  114.4 4.0 %collective-permute-start.18 = (f32[88,128]{1,0:T(8,128)S(1)}, f32[88,128]{1,0:T(8,128)S(1)}, u32[]{:S(2)}, u32[]{:S(2)}) collective-permute-start(f32[88,128]{1,0:T(8,128)S(1)} %get-tuple-element.49), channel_id=1, source_target_pairs={{0,24},{1,25},{2,26},{3,27},{4,28},{5,29},{6,30},{7,31},{8,16},{9,... | collective-permute-start | bytes 135176 | tf_op jit(solution)/shard_map/ppermute | solution.py:42
  118.3 6.8 %collective-permute-start.19 = (f32[88,128]{1,0:T(8,128)S(1)}, f32[88,128]{1,0:T(8,128)S(1)}, u32[]{:S(2)}, u32[]{:S(2)}) collective-permute-start(f32[88,128]{1,0:T(8,128)S(1)} %add_add_fusion.3), channel_id=1, source_target_pairs={{0,32},{1,33},{2,34},{3,35},{4,36},{5,37},{6,38},{7,39},{8,40},{9,... | collective-permute-start | bytes 135176 | tf_op jit(solution)/shard_map/ppermute | solution.py:42
  118.4 9.4 %collective-permute-start.20 = (f32[88,128]{1,0:T(8,128)S(1)}, f32[88,128]{1,0:T(8,128)S(1)}, u32[]{:S(2)}, u32[]{:S(2)}) collective-permute-start(f32[88,128]{1,0:T(8,128)S(1)} %add_add_fusion.3), channel_id=1, source_target_pairs={{0,64},{1,65},{2,66},{3,67},{4,68},{5,69},{6,70},{7,71},{8,72},{9,... | collective-permute-start | bytes 135176 | tf_op jit(solution)/shard_map/ppermute | solution.py:42
  124.7 6.2 %collective-permute-start.21 = (f32[88,128]{1,0:T(8,128)S(1)}, f32[88,128]{1,0:T(8,128)S(1)}, u32[]{:S(2)}, u32[]{:S(2)}) collective-permute-start(f32[88,128]{1,0:T(8,128)S(1)} %add_add_fusion.3), channel_id=1, source_target_pairs={{0,96},{1,97},{2,98},{3,99},{4,100},{5,101},{6,102},{7,103},{8,104... | collective-permute-start | bytes 135176 | tf_op jit(solution)/shard_map/ppermute | solution.py:42
  130.8 12.6 %collective-permute-start.22 = (f32[88,128]{1,0:T(8,128)S(1)}, f32[88,128]{1,0:T(8,128)S(1)}, u32[]{:S(2)}, u32[]{:S(2)}) collective-permute-start(f32[88,128]{1,0:T(8,128)S(1)} %add_add_fusion.2), channel_id=1, source_target_pairs={{0,128},{1,129},{2,130},{3,131},{4,132},{5,133},{6,134},{7,135},{8... | collective-permute-start | bytes 135176 | tf_op jit(solution)/shard_map/ppermute | solution.py:42
  131.1 12.4 %collective-permute-start.23 = (f32[88,128]{1,0:T(8,128)S(1)}, f32[88,128]{1,0:T(8,128)S(1)}, u32[]{:S(2)}, u32[]{:S(2)}) collective-permute-start(f32[88,128]{1,0:T(8,128)S(1)} %add_add_fusion.2), channel_id=1, source_target_pairs={{0,1},{1,0},{2,3},{3,2},{4,5},{5,4},{6,7},{7,6},{8,9},{9,8},{10,11... | collective-permute-start | bytes 135176 | tf_op jit(solution)/shard_map/ppermute | solution.py:42
  135.4 8.1 %collective-permute-start.24 = (f32[88,128]{1,0:T(8,128)S(1)}, f32[88,128]{1,0:T(8,128)S(1)}, u32[]{:S(2)}, u32[]{:S(2)}) collective-permute-start(f32[88,128]{1,0:T(8,128)S(1)} %add_add_fusion.2), channel_id=1, source_target_pairs={{0,129},{1,128},{2,131},{3,130},{4,133},{5,132},{6,135},{7,134},{8... | collective-permute-start | bytes 135176 | tf_op jit(solution)/shard_map/ppermute | solution.py:42
  135.8 12.5 %collective-permute-start.31 = (bf16[8,64,128]{2,1,0:T(8,128)(2,1)S(1)}, bf16[8,64,128]{2,1,0:T(8,128)(2,1)S(1)}, u32[]{:S(2)}, u32[]{:S(2)}) collective-permute-start(bf16[8,64,128]{2,1,0:T(8,128)(2,1)S(1)} %get-tuple-element.52), channel_id=1, source_target_pairs={{0,8},{8,16},{16,24},{24,32},{32,40},{40,48},{48,56},{56,64},{64,7... | collective-permute-start | bytes 393224 | tf_op jit(solution)/shard_map/ppermute | solution.py:48
  137.7 10.6 %collective-permute-start.32 = (bf16[8,64,128]{2,1,0:T(8,128)(2,1)S(1)}, bf16[8,64,128]{2,1,0:T(8,128)(2,1)S(1)}, u32[]{:S(2)}, u32[]{:S(2)}) collective-permute-start(bf16[8,64,128]{2,1,0:T(8,128)(2,1)S(1)} %get-tuple-element.53), channel_id=1, source_target_pairs={{8,0},{16,8},{24,16},{32,24},{40,32},{48,40},{56,48},{64,56},{72,6... | collective-permute-start | bytes 393224 | tf_op jit(solution)/shard_map/ppermute | solution.py:48
  143.5 12.6 %collective-permute-start.25 = (f32[88,128]{1,0:T(8,128)S(1)}, f32[88,128]{1,0:T(8,128)S(1)}, u32[]{:S(2)}, u32[]{:S(2)}) collective-permute-start(f32[88,128]{1,0:T(8,128)S(1)} %add_add_fusion.1), channel_id=1, source_target_pairs={{0,2},{1,3},{2,0},{3,1},{4,6},{5,7},{6,4},{7,5},{8,10},{9,11},{10,... | collective-permute-start | bytes 135176 | tf_op jit(solution)/shard_map/ppermute | solution.py:42
  145.5 10.6 %collective-permute-start.26 = (f32[88,128]{1,0:T(8,128)S(1)}, f32[88,128]{1,0:T(8,128)S(1)}, u32[]{:S(2)}, u32[]{:S(2)}) collective-permute-start(f32[88,128]{1,0:T(8,128)S(1)} %add_add_fusion.1), channel_id=1, source_target_pairs={{0,4},{1,5},{2,6},{3,7},{4,0},{5,1},{6,2},{7,3},{8,12},{9,13},{10,... | collective-permute-start | bytes 135176 | tf_op jit(solution)/shard_map/ppermute | solution.py:42
  145.5 10.7 %collective-permute-start.27 = (f32[88,128]{1,0:T(8,128)S(1)}, f32[88,128]{1,0:T(8,128)S(1)}, u32[]{:S(2)}, u32[]{:S(2)}) collective-permute-start(f32[88,128]{1,0:T(8,128)S(1)} %add_add_fusion.1), channel_id=1, source_target_pairs={{0,6},{1,7},{2,4},{3,5},{4,2},{5,3},{6,0},{7,1},{8,14},{9,15},{10,... | collective-permute-start | bytes 135176 | tf_op jit(solution)/shard_map/ppermute | solution.py:42
  148.8 10.5 %collective-permute-start.33 = (bf16[3,64,128]{2,1,0:T(8,128)(2,1)S(1)}, bf16[3,64,128]{2,1,0:T(8,128)(2,1)S(1)}, u32[]{:S(2)}, u32[]{:S(2)}) collective-permute-start(bf16[3,64,128]{2,1,0:T(8,128)(2,1)S(1)} %get-tuple-element.54), channel_id=1, source_target_pairs={{0,1},{1,2},{2,3},{3,4},{4,5},{5,6},{6,7},{8,9},{9,10},{10,11},{11... | collective-permute-start | bytes 147464 | tf_op jit(solution)/shard_map/ppermute | solution.py:48
  150.7 8.6 %collective-permute-start.34 = (bf16[3,64,128]{2,1,0:T(8,128)(2,1)S(1)}, bf16[3,64,128]{2,1,0:T(8,128)(2,1)S(1)}, u32[]{:S(2)}, u32[]{:S(2)}) collective-permute-start(bf16[3,64,128]{2,1,0:T(8,128)(2,1)S(1)} %get-tuple-element.55), channel_id=1, source_target_pairs={{1,0},{2,1},{3,2},{4,3},{5,4},{6,5},{7,6},{9,8},{10,9},{11,10},{12... | collective-permute-start | bytes 147464 | tf_op jit(solution)/shard_map/ppermute | solution.py:48
  156.2 7.9 %collective-permute-start.28 = (f32[88,128]{1,0:T(8,128)S(1)}, f32[88,128]{1,0:T(8,128)S(1)}, u32[]{:S(2)}, u32[]{:S(2)}) collective-permute-start(f32[88,128]{1,0:T(8,128)S(1)} %add_add_fusion.got0), channel_id=1, source_target_pairs={{0,8},{1,9},{2,10},{3,11},{4,12},{5,13},{6,14},{7,15},{8,0},{9,1},... | collective-permute-start | bytes 135176 | tf_op jit(solution)/shard_map/ppermute | solution.py:42
  156.3 7.9 %collective-permute-start.29 = (f32[88,128]{1,0:T(8,128)S(1)}, f32[88,128]{1,0:T(8,128)S(1)}, u32[]{:S(2)}, u32[]{:S(2)}) collective-permute-start(f32[88,128]{1,0:T(8,128)S(1)} %add_add_fusion.got0), channel_id=1, source_target_pairs={{0,16},{1,17},{2,18},{3,19},{4,20},{5,21},{6,22},{7,23},{8,24},{9,... | collective-permute-start | bytes 135176 | tf_op jit(solution)/shard_map/ppermute | solution.py:42
  156.4 7.8 %collective-permute-start.30 = (f32[88,128]{1,0:T(8,128)S(1)}, f32[88,128]{1,0:T(8,128)S(1)}, u32[]{:S(2)}, u32[]{:S(2)}) collective-permute-start(f32[88,128]{1,0:T(8,128)S(1)} %add_add_fusion.got0), channel_id=1, source_target_pairs={{0,24},{1,25},{2,26},{3,27},{4,28},{5,29},{6,30},{7,31},{8,16},{9,... | collective-permute-start | bytes 135176 | tf_op jit(solution)/shard_map/ppermute | solution.py:42

commit v3 on v2

--- a/solution.py
+++ b/solution.py
@@ -367,6 +367,7 @@
         ],
         axis=1,
     )
+    turns = jnp.where(labels[0, 0] >= 0, 1, 0).astype(jnp.int32)
     counted = jnp.full((8, LANES), jnp.sum(valid.astype(F32)))
     tile = (rows, chans, LANES)
     edge = (STEP, chans, LANES)
@@ -374,7 +375,6 @@
         activate_kernel, [shape(tile, BF16), shape(edge, BF16), shape(edge, BF16)], (feat,), micros=1
     )
     around = borders(act, top, bottom)
-    count = total_small(counted)
     length = (rows + 1) * rows // 2
     wide, mixed, *pays = run(
         forward_kernel,
@@ -388,6 +388,13 @@
     got = [
         send(pays[s], lambda r, c: (parts * c + (r % parts ^ s), r // parts)) for s in range(parts)
     ]
+    counted, mixed = lax.optimization_barrier((counted, mixed))
+    count = lax.while_loop(
+        lambda state: state[0] < turns,
+        lambda state: (state[0] + 1, total_small(state[1])),
+        (jnp.int32(0), counted),
+    )[1]
+    got, count = lax.optimization_barrier((got, count))
     grad, head_sum, bias_sum, loss_sum = run(
         softmax_kernel,
         [

time: 171 us -> 177 us (1.035)
  local copies, waits for them, and re-layouts: 8.3 us -> 13.9 us
  starting transfers between devices: 86.1 us -> 81.9 us
  waiting for transfers between devices: 40.7 us -> 44.5 us
    ppermute x8, waiting for transfers between devices: 0.22 us -> 6.88 us  [shifted(): lax.ppermute(block, axis, pairs if forward else [(b, a) for a, b in pairs])]
    ppermute x27, starting transfers between devices: 55.3 us -> 50.3 us  [send(): return lax.ppermute(block, GRID, pairs)]
    unnamed x12 -> x30, local copies, waits for them, and re-layouts: 4.43 us -> 8.89 us
    ppermute x27, waiting for transfers between devices: 40.4 us -> 37.6 us  [send(): return lax.ppermute(block, GRID, pairs)]
  transfers between devices with their start and end apart: 35 -> 35, of which waited for: 12 -> 16; matrix products, arithmetic and copies ran while one was open for 2% -> 3% of each run, Pallas kernels for 9% -> 3%
where the time goes in v3:
time: 177 us; the launch traced here: 176 us
  starting transfers between devices  81.9 us (46%)
  waiting for transfers between devices  44.5 us (25%)
  Pallas kernels  28.4 us (16%)
  local copies, waits for them, and re-layouts  13.9 us (8%)
  between operations  4.04 us (2%)
  other arithmetic  2.81 us (2%)
    ppermute x27, starting transfers between devices, send(): return lax.ppermute(block, GRID, pairs)  50.3 us
    ppermute x27, waiting for transfers between devices, send(): return lax.ppermute(block, GRID, pairs)  37.6 us
    ppermute x8, starting transfers between devices, shifted(): lax.ppermute(block, axis, pairs if forward else [(b, a) for a, b in pairs])  31.7 us
    pallas_call x8, Pallas kernels, run(): pl.pallas_call(body, out_shape=outs, in_specs=[SMEM] * scalars + [VMEM] *...  28.4 us
    unnamed x30, local copies, waits for them, and re-layouts  8.89 us
    ppermute x8, waiting for transfers between devices, shifted(): lax.ppermute(block, axis, pairs if forward else [(b, a) for a, b in pairs])  6.88 us
  transfers between devices with their start and end apart: 35, of which 16 were waited for; matrix products, arithmetic and copies ran while one was open for 3% of the time, Pallas kernels for 3%

profile of v3, /device:TPU:24, one launch (start us, length us, event | category | flops | bytes accessed | tf_op | source)
XLA Modules:
  0.0 175.6 jit_solution(18276618591132287623)
XLA Ops:
  0.6 1.0 copy-done
  2.5 1.9 %collective-permute-start.8 = (bf16[8,64,128]{2,1,0:T(8,128)(2,1)S(1)}, bf16[8,64,128]{2,1,0:T(8,128)(2,1)S(1)}, u32[]{:S(2)}, u32[]{:S(2)}) collective-permute-start(bf16[8,64,128]{2,1,0:T(8,128)(2,1)S(1)} %get-tuple-element.57), channel_id=1, source_target_pairs={{0,8},{8,16},{16,24},{24,32},{32,40},{40,48},{48,56},{56,64},{64,7... | collective-permute-start | bytes 393224 | tf_op jit(solution)/shard_map/ppermute | solution.py:48
  4.4 7.4 %collective-permute-start.9 = (bf16[8,64,128]{2,1,0:T(8,128)(2,1)S(1)}, bf16[8,64,128]{2,1,0:T(8,128)(2,1)S(1)}, u32[]{:S(2)}, u32[]{:S(2)}) collective-permute-start(bf16[8,64,128]{2,1,0:T(8,128)(2,1)S(1)} %get-tuple-element.58), channel_id=1, source_target_pairs={{8,0},{16,8},{24,16},{32,24},{40,32},{48,40},{56,48},{64,56},{72,6... | collective-permute-start | bytes 393224 | tf_op jit(solution)/shard_map/ppermute | solution.py:48
  11.8 1.3 pad_convert_fusion
  13.1 1.2 collective-permute-done.9.down
  14.8 3.8 %collective-permute-start.10 = (bf16[3,64,128]{2,1,0:T(8,128)(2,1)S(1)}, bf16[3,64,128]{2,1,0:T(8,128)(2,1)S(1)}, u32[]{:S(2)}, u32[]{:S(2)}) collective-permute-start(bf16[3,64,128]{2,1,0:T(8,128)(2,1)S(1)} %get-tuple-element.59), channel_id=1, source_target_pairs={{0,1},{1,2},{2,3},{3,4},{4,5},{5,6},{6,7},{8,9},{9,10},{10,11},{11... | collective-permute-start | bytes 147464 | tf_op jit(solution)/shard_map/ppermute | solution.py:48
  18.6 3.6 %collective-permute-start.11 = (bf16[3,64,128]{2,1,0:T(8,128)(2,1)S(1)}, bf16[3,64,128]{2,1,0:T(8,128)(2,1)S(1)}, u32[]{:S(2)}, u32[]{:S(2)}) collective-permute-start(bf16[3,64,128]{2,1,0:T(8,128)(2,1)S(1)} %get-tuple-element.60), channel_id=1, source_target_pairs={{1,0},{2,1},{3,2},{4,3},{5,4},{6,5},{7,6},{9,8},{10,9},{11,10},{12... | collective-permute-start | bytes 147464 | tf_op jit(solution)/shard_map/ppermute | solution.py:48
  24.2 2.7 %collective-permute-done.11.right = bf16[3,64,128]{2,1,0:T(8,128)(2,1)S(1)} collective-permute-done((bf16[3,64,128]{2,1,0:T(8,128)(2,1)S(1)}, bf16[3,64,128]{2,1,0:T(8,128)(2,1)S(1)}, u32[]{:S(2)}, u32[]{:S(2)}) %collective-permute-start.11) | collective-permute-done | bytes 49184 | tf_op jit(solution)/shard_map/ppermute | solution.py:48
  27.6 1.0 copy-done.1
  28.6 0.9 copy-done.3
  29.5 0.9 copy-done.6
  33.5 8.8 %shard_map.103 = (bf16[48,192,128]{2,1,0:T(8,128)(2,1)S(1)}, bf16[32,64,128]{2,1,0:T(8,128)(2,1)S(1)}, bf16[528,128]{1,0:T(8,128)(2,1)}, bf16[528,128]{1,0:T(8,1...) custom-call(s32[1]{0:T(128)} %bitcast.place, bf16[32,64,128]{2,1,0:T(8,128)(2,1)S(1)} %get-tuple-element.56.own.act, ...), custom_call_target="tpu_custom_call" | custom-call | bytes 18000000 | tf_op jit(solution)/shard_map/pallas_call | solution.py:18
  42.3 4.0 %collective-permute-start.12 = (bf16[528,128]{1,0:T(8,128)(2,1)}, bf16[528,128]{1,0:T(8,128)(2,1)S(1)}, u32[]{:S(2)}, u32[]{:S(2)}) collective-permute-start(bf16[528,128]{1,0:T(8,128)(2,1)} %get-tuple-element.61), channel_id=1, source_target_pairs={{0,0},{1,32},{2,64},{3,96},{4,128},{5,160},{6,192},{7,224},{8,8},{... | collective-permute-start | bytes 405512 | tf_op jit(solution)/shard_map/ppermute | solution.py:42
  46.3 2.1 %collective-permute-start.13 = (bf16[528,128]{1,0:T(8,128)(2,1)}, bf16[528,128]{1,0:T(8,128)(2,1)S(1)}, u32[]{:S(2)}, u32[]{:S(2)}) collective-permute-start(bf16[528,128]{1,0:T(8,128)(2,1)} %get-tuple-element.62), channel_id=1, source_target_pairs={{0,8},{1,40},{2,72},{3,104},{4,136},{5,168},{6,200},{7,232},{8,0},... | collective-permute-start | bytes 405512 | tf_op jit(solution)/shard_map/ppermute | solution.py:42
  48.3 9.3 %collective-permute-start.14 = (bf16[528,128]{1,0:T(8,128)(2,1)}, bf16[528,128]{1,0:T(8,128)(2,1)S(1)}, u32[]{:S(2)}, u32[]{:S(2)}) collective-permute-start(bf16[528,128]{1,0:T(8,128)(2,1)} %get-tuple-element.63), channel_id=1, source_target_pairs={{0,16},{1,48},{2,80},{3,112},{4,144},{5,176},{6,208},{7,240},{8,24... | collective-permute-start | bytes 405512 | tf_op jit(solution)/shard_map/ppermute | solution.py:42
  57.6 1.9 %collective-permute-start.15 = (bf16[528,128]{1,0:T(8,128)(2,1)}, bf16[528,128]{1,0:T(8,128)(2,1)}, u32[]{:S(2)}, u32[]{:S(2)}) collective-permute-start(bf16[528,128]{1,0:T(8,128)(2,1)} %get-tuple-element.64), channel_id=1, source_target_pairs={{0,24},{1,56},{2,88},{3,120},{4,152},{5,184},{6,216},{7,248},{8,16... | collective-permute-start | bytes 405512 | tf_op jit(solution)/shard_map/ppermute | solution.py:42
  62.7 41.6 %while.10 = (s32[]{:T(128)}, f32[8,128]{1,0:T(8,128)S(1)}, s32[]{:T(128)}, s32[]{:T(128)}) while((s32[]{:T(128)}, f32[8,128]{1,0:T(8,128)S(1)}, s32[]{:T(128)}, s32[]{:T(128)}) %tuple.26), condition=%wide.region_2.3_spmd, body=%wide.region_1.2_spmd.sunk | while | flops 8194 | bytes 229749 | solution.py:392
  62.9 1.2 collective-permute-done
  64.0 9.3 %collective-permute-done.1 = f32[8,128]{1,0:T(8,128)S(1)} collective-permute-done((f32[8,128]{1,0:T(8,128)S(1)}, f32[8,128]{1,0:T(8,128)S(1)}, u32[]{:S(2)}, u32[]{:S(2)}) %collective-permute-start.1) | collective-permute-done | bytes 4128 | tf_op jit(solution)/shard_map/while/body/ppermute | solution.py:42
  73.3 4.5 %collective-permute-done.2 = f32[8,128]{1,0:T(8,128)S(1)} collective-permute-done((f32[8,128]{1,0:T(8,128)S(1)}, f32[8,128]{1,0:T(8,128)S(1)}, u32[]{:S(2)}, u32[]{:S(2)}) %collective-permute-start.2) | collective-permute-done | bytes 4128 | tf_op jit(solution)/shard_map/while/body/ppermute | solution.py:42
  77.8 1.9 %collective-permute-start.3 = (f32[8,128]{1,0:T(8,128)S(1)}, f32[8,128]{1,0:T(8,128)S(1)}, u32[]{:S(2)}, u32[]{:S(2)}) collective-permute-start(f32[8,128]{1,0:T(8,128)S(1)} %add.109), channel_id=1, source_target_pairs={{0,64},{1,65},{2,66},{3,67},{4,68},{5,69},{6,70},{7,71},{8,72},{9,... | collective-permute-start | bytes 12296 | tf_op jit(solution)/shard_map/while/body/ppermute | solution.py:42
  79.7 5.7 %collective-permute-done.3 = f32[8,128]{1,0:T(8,128)S(1)} collective-permute-done((f32[8,128]{1,0:T(8,128)S(1)}, f32[8,128]{1,0:T(8,128)S(1)}, u32[]{:S(2)}, u32[]{:S(2)}) %collective-permute-start.3) | collective-permute-done | bytes 4128 | tf_op jit(solution)/shard_map/while/body/ppermute | solution.py:42
  85.4 3.6 %collective-permute-done.4 = f32[8,128]{1,0:T(8,128)S(1)} collective-permute-done((f32[8,128]{1,0:T(8,128)S(1)}, f32[8,128]{1,0:T(8,128)S(1)}, u32[]{:S(2)}, u32[]{:S(2)}) %collective-permute-start.4) | collective-permute-done | bytes 4128 | tf_op jit(solution)/shard_map/while/body/ppermute | solution.py:42
  89.0 4.5 %collective-permute-start.5 = (f32[8,128]{1,0:T(8,128)S(1)}, f32[8,128]{1,0:T(8,128)S(1)}, u32[]{:S(2)}, u32[]{:S(2)}) collective-permute-start(f32[8,128]{1,0:T(8,128)S(1)} %add.111), channel_id=1, source_target_pairs={{0,1},{1,0},{2,3},{3,2},{4,5},{5,4},{6,7},{7,6},{8,9},{9,8},{10,11... | collective-permute-start | bytes 12296 | tf_op jit(solution)/shard_map/while/body/ppermute | solution.py:42
  93.5 1.6 collective-permute-done.5
  95.0 2.6 %collective-permute-start.6 = (f32[8,128]{1,0:T(8,128)S(1)}, f32[8,128]{1,0:T(8,128)S(1)}, u32[]{:S(2)}, u32[]{:S(2)}) collective-permute-start(f32[8,128]{1,0:T(8,128)S(1)} %add.112), channel_id=1, source_target_pairs={{0,2},{1,3},{2,0},{3,1},{4,6},{5,7},{6,4},{7,5},{8,10},{9,11},{10,... | collective-permute-start | bytes 12296 | tf_op jit(solution)/shard_map/while/body/ppermute | solution.py:42
  97.7 1.6 collective-permute-done.6
  99.3 3.3 %collective-permute-start.7 = (f32[8,128]{1,0:T(8,128)S(1)}, f32[8,128]{1,0:T(8,128)S(1)}, u32[]{:S(2)}, u32[]{:S(2)}) collective-permute-start(f32[8,128]{1,0:T(8,128)S(1)} %add.113), channel_id=1, source_target_pairs={{0,4},{1,5},{2,6},{3,7},{4,0},{5,1},{6,2},{7,3},{8,12},{9,13},{10,... | collective-permute-start | bytes 12296 | tf_op jit(solution)/shard_map/while/body/ppermute | solution.py:42
  102.5 1.8 %collective-permute-done.7 = f32[8,128]{1,0:T(8,128)S(1)} collective-permute-done((f32[8,128]{1,0:T(8,128)S(1)}, f32[8,128]{1,0:T(8,128)S(1)}, u32[]{:S(2)}, u32[]{:S(2)}) %collective-permute-start.7) | collective-permute-done | bytes 4128 | tf_op jit(solution)/shard_map/while/body/ppermute | solution.py:42
  105.1 7.8 %shard_map.104 = (f32[32,64,128]{2,1,0:T(8,128)S(1)}, f32[120,64]{1,0:T(8,128)S(1)}, f32[40,128]{1,0:T(8,128)S(1)}, f32[1,128]{1,0:T(1,128)S(1)}) custom-call(s32[1]{0:T(128)} %bitcast.place, bf16[528,128]{1,0:T(8,128)(2,1)S(1)} %collective-permute-done.12.got0, bf16[528,128]{1,0:T(8,128)(2,1)S(1)} %collective-permute-done.13.got1, ...), custom_call_target="tpu_custom_call" | custom-call | bytes 18000000 | tf_op jit(solution)/shard_map/pallas_call | solution.py:18
  113.0 4.4 %shard_map.105 = (bf16[32,64,128]{2,1,0:T(8,128)(2,1)S(1)}, bf16[8,64,128]{2,1,0:T(8,128)(2,1)S(1)}, bf16[8,64,128]{2,1,0:T(8,128)(2,1)S(1)}, f32[88,128]{1,0:T(...) custom-call(s32[1]{0:T(128)} %bitcast.place, ...), custom_call_target="tpu_custom_call" | custom-call | bytes 10800000 | tf_op jit(solution)/shard_map/pallas_call | solution.py:18
  117.5 4.0 %collective-permute-start.17 = (f32[88,128]{1,0:T(8,128)S(1)}, f32[88,128]{1,0:T(8,128)S(1)}, u32[]{:S(2)}, u32[]{:S(2)}) collective-permute-start(f32[88,128]{1,0:T(8,128)S(1)} %get-tuple-element.81), channel_id=1, source_target_pairs={{0,16},{1,17},{2,18},{3,19},{4,20},{5,21},{6,22},{7,23},{8,24},{9,... | collective-permute-start | bytes 135176 | tf_op jit(solution)/shard_map/ppermute | solution.py:42
  121.7 1.8 %collective-permute-done.17 = f32[88,128]{1,0:T(8,128)S(1)} collective-permute-done((f32[88,128]{1,0:T(8,128)S(1)}, f32[88,128]{1,0:T(8,128)S(1)}, u32[]{:S(2)}, u32[]{:S(2)}) %collective-permute-start.17) | collective-permute-done | bytes 45088 | tf_op jit(solution)/shard_map/ppermute | solution.py:42
  123.5 1.4 collective-permute-done.18
  125.0 4.1 %collective-permute-start.20 = (f32[88,128]{1,0:T(8,128)S(1)}, f32[88,128]{1,0:T(8,128)S(1)}, u32[]{:S(2)}, u32[]{:S(2)}) collective-permute-start(f32[88,128]{1,0:T(8,128)S(1)} %add_add_fusion.3), channel_id=1, source_target_pairs={{0,64},{1,65},{2,66},{3,67},{4,68},{5,69},{6,70},{7,71},{8,72},{9,... | collective-permute-start | bytes 135176 | tf_op jit(solution)/shard_map/ppermute | solution.py:42
  129.1 3.0 %collective-permute-start.21 = (f32[88,128]{1,0:T(8,128)S(1)}, f32[88,128]{1,0:T(8,128)S(1)}, u32[]{:S(2)}, u32[]{:S(2)}) collective-permute-start(f32[88,128]{1,0:T(8,128)S(1)} %add_add_fusion.3), channel_id=1, source_target_pairs={{0,96},{1,97},{2,98},{3,99},{4,100},{5,101},{6,102},{7,103},{8,104... | collective-permute-start | bytes 135176 | tf_op jit(solution)/shard_map/ppermute | solution.py:42
  133.2 2.1 %collective-permute-done.21 = f32[88,128]{1,0:T(8,128)S(1)} collective-permute-done((f32[88,128]{1,0:T(8,128)S(1)}, f32[88,128]{1,0:T(8,128)S(1)}, u32[]{:S(2)}, u32[]{:S(2)}) %collective-permute-start.21) | collective-permute-done | bytes 45088 | tf_op jit(solution)/shard_map/ppermute | solution.py:42
  135.2 2.2 %collective-permute-done.19 = f32[88,128]{1,0:T(8,128)S(1)} collective-permute-done((f32[88,128]{1,0:T(8,128)S(1)}, f32[88,128]{1,0:T(8,128)S(1)}, u32[]{:S(2)}, u32[]{:S(2)}) %collective-permute-start.19) | collective-permute-done | bytes 45088 | tf_op jit(solution)/shard_map/ppermute | solution.py:42
  137.6 2.7 %collective-permute-start.24 = (f32[88,128]{1,0:T(8,128)S(1)}, f32[88,128]{1,0:T(8,128)S(1)}, u32[]{:S(2)}, u32[]{:S(2)}) collective-permute-start(f32[88,128]{1,0:T(8,128)S(1)} %add_add_fusion.2), channel_id=1, source_target_pairs={{0,129},{1,128},{2,131},{3,130},{4,133},{5,132},{6,135},{7,134},{8... | collective-permute-start | bytes 135176 | tf_op jit(solution)/shard_map/ppermute | solution.py:42
  141.0 1.9 %collective-permute-start.31 = (bf16[8,64,128]{2,1,0:T(8,128)(2,1)S(1)}, bf16[8,64,128]{2,1,0:T(8,128)(2,1)S(1)}, u32[]{:S(2)}, u32[]{:S(2)}) collective-permute-start(bf16[8,64,128]{2,1,0:T(8,128)(2,1)S(1)} %get-tuple-element.85), channel_id=1, source_target_pairs={{0,8},{8,16},{16,24},{24,32},{32,40},{40,48},{48,56},{56,64},{64,7... | collective-permute-start | bytes 393224 | tf_op jit(solution)/shard_map/ppermute | solution.py:48
  143.0 5.8 %collective-permute-start.32 = (bf16[8,64,128]{2,1,0:T(8,128)(2,1)S(1)}, bf16[8,64,128]{2,1,0:T(8,128)(2,1)S(1)}, u32[]{:S(2)}, u32[]{:S(2)}) collective-permute-start(bf16[8,64,128]{2,1,0:T(8,128)(2,1)S(1)} %get-tuple-element.86), channel_id=1, source_target_pairs={{8,0},{16,8},{24,16},{32,24},{40,32},{48,40},{56,48},{64,56},{72,6... | collective-permute-start | bytes 393224 | tf_op jit(solution)/shard_map/ppermute | solution.py:48
  148.8 1.0 collective-permute-start.26
  149.8 2.0 %collective-permute-start.27 = (f32[88,128]{1,0:T(8,128)S(1)}, f32[88,128]{1,0:T(8,128)S(1)}, u32[]{:S(2)}, u32[]{:S(2)}) collective-permute-start(f32[88,128]{1,0:T(8,128)S(1)} %add_add_fusion.1), channel_id=1, source_target_pairs={{0,6},{1,7},{2,4},{3,5},{4,2},{5,3},{6,0},{7,1},{8,14},{9,15},{10,... | collective-permute-start | bytes 135176 | tf_op jit(solution)/shard_map/ppermute | solution.py:42
  152.8 5.1 %collective-permute-start.33 = (bf16[3,64,128]{2,1,0:T(8,128)(2,1)S(1)}, bf16[3,64,128]{2,1,0:T(8,128)(2,1)S(1)}, u32[]{:S(2)}, u32[]{:S(2)}) collective-permute-start(bf16[3,64,128]{2,1,0:T(8,128)(2,1)S(1)} %get-tuple-element.87), channel_id=1, source_target_pairs={{0,1},{1,2},{2,3},{3,4},{4,5},{5,6},{6,7},{8,9},{9,10},{10,11},{11... | collective-permute-start | bytes 147464 | tf_op jit(solution)/shard_map/ppermute | solution.py:48
  157.9 2.3 %collective-permute-start.34 = (bf16[3,64,128]{2,1,0:T(8,128)(2,1)S(1)}, bf16[3,64,128]{2,1,0:T(8,128)(2,1)S(1)}, u32[]{:S(2)}, u32[]{:S(2)}) collective-permute-start(bf16[3,64,128]{2,1,0:T(8,128)(2,1)S(1)} %get-tuple-element.88), channel_id=1, source_target_pairs={{1,0},{2,1},{3,2},{4,3},{5,4},{6,5},{7,6},{9,8},{10,9},{11,10},{12... | collective-permute-start | bytes 147464 | tf_op jit(solution)/shard_map/ppermute | solution.py:48
  160.4 1.8 %collective-permute-start.30 = (f32[88,128]{1,0:T(8,128)S(1)}, f32[88,128]{1,0:T(8,128)S(1)}, u32[]{:S(2)}, u32[]{:S(2)}) collective-permute-start(f32[88,128]{1,0:T(8,128)S(1)} %add_add_fusion.got0), channel_id=1, source_target_pairs={{0,24},{1,25},{2,26},{3,27},{4,28},{5,29},{6,30},{7,31},{8,16},{9,... | collective-permute-start | bytes 135176 | tf_op jit(solution)/shard_map/ppermute | solution.py:42
  163.4 2.9 %collective-permute-done.34.right = bf16[3,64,128]{2,1,0:T(8,128)(2,1)S(1)} collective-permute-done((bf16[3,64,128]{2,1,0:T(8,128)(2,1)S(1)}, bf16[3,64,128]{2,1,0:T(8,128)(2,1)S(1)}, u32[]{:S(2)}, u32[]{:S(2)}) %collective-permute-start.34) | collective-permute-done | bytes 49184 | tf_op jit(solution)/shard_map/ppermute | solution.py:48
  166.3 4.8 %shard_map.108 = bf16[32,64,128]{2,1,0:T(8,128)(2,1)} custom-call(f32[8,128]{1,0:T(8,128)S(1)} %get-tuple-element.68.count, bf16[32,64,128]{2,1,0:T(8,128)(2,1)S(1)} %get-tuple-element.84.own.low, bf16[8,64,128]{2,1,0:T(8,128)(2,1)S(1)} %collective-permute-done.31.up, bf16[8,64,128]{2,1,0:T(8,128)(2,1)S(1)} %collective-permute-done.32.down, ...), custom_call_target="tpu_custom_call" | custom-call | bytes 14400000 | tf_op jit(solution)/shard_map/pallas_call | solution.py:18
  (86 shorter events, 17.2 us)
Async XLA Ops:
  0.6 1.0 copy-start
  1.7 102.7 %copy-start.8 = (s32[32,128]{1,0:T(8,128)S(1)}, s32[32,128]{1,0:T(8,128)}, u32[]{:S(2)}) copy-start(s32[32,128]{1,0:T(8,128)} %valid.3) | copy-start | bytes 49156
  2.5 10.6 %collective-permute-start.8 = (bf16[8,64,128]{2,1,0:T(8,128)(2,1)S(1)}, bf16[8,64,128]{2,1,0:T(8,128)(2,1)S(1)}, u32[]{:S(2)}, u32[]{:S(2)}) collective-permute-start(bf16[8,64,128]{2,1,0:T(8,128)(2,1)S(1)} %get-tuple-element.57), channel_id=1, source_target_pairs={{0,8},{8,16},{16,24},{24,32},{32,40},{40,48},{48,56},{56,64},{64,7... | collective-permute-start | bytes 393224 | tf_op jit(solution)/shard_map/ppermute | solution.py:48
  4.4 9.9 %collective-permute-start.9 = (bf16[8,64,128]{2,1,0:T(8,128)(2,1)S(1)}, bf16[8,64,128]{2,1,0:T(8,128)(2,1)S(1)}, u32[]{:S(2)}, u32[]{:S(2)}) collective-permute-start(bf16[8,64,128]{2,1,0:T(8,128)(2,1)S(1)} %get-tuple-element.58), channel_id=1, source_target_pairs={{8,0},{16,8},{24,16},{32,24},{40,32},{48,40},{56,48},{64,56},{72,6... | collective-permute-start | bytes 393224 | tf_op jit(solution)/shard_map/ppermute | solution.py:48
  14.3 13.2 %copy-start.5 = (bf16[8,64,128]{2,1,0:T(8,128)(2,1)}, bf16[8,64,128]{2,1,0:T(8,128)(2,1)S(1)}, u32[]{:S(2)}) copy-start(bf16[8,64,128]{2,1,0:T(8,128)(2,1)S(1)} %collective-permute-done.9.down) | copy-start | bytes 393220
  14.8 8.8 %collective-permute-start.10 = (bf16[3,64,128]{2,1,0:T(8,128)(2,1)S(1)}, bf16[3,64,128]{2,1,0:T(8,128)(2,1)S(1)}, u32[]{:S(2)}, u32[]{:S(2)}) collective-permute-start(bf16[3,64,128]{2,1,0:T(8,128)(2,1)S(1)} %get-tuple-element.59), channel_id=1, source_target_pairs={{0,1},{1,2},{2,3},{3,4},{4,5},{5,6},{6,7},{8,9},{9,10},{10,11},{11... | collective-permute-start | bytes 147464 | tf_op jit(solution)/shard_map/ppermute | solution.py:48
  18.6 8.4 %collective-permute-start.11 = (bf16[3,64,128]{2,1,0:T(8,128)(2,1)S(1)}, bf16[3,64,128]{2,1,0:T(8,128)(2,1)S(1)}, u32[]{:S(2)}, u32[]{:S(2)}) collective-permute-start(bf16[3,64,128]{2,1,0:T(8,128)(2,1)S(1)} %get-tuple-element.60), channel_id=1, source_target_pairs={{1,0},{2,1},{3,2},{4,3},{5,4},{6,5},{7,6},{9,8},{10,9},{11,10},{12... | collective-permute-start | bytes 147464 | tf_op jit(solution)/shard_map/ppermute | solution.py:48
  27.6 1.0 copy-start.1
  28.6 0.9 copy-start.3
  29.5 0.9 copy-start.6
  30.4 0.7 copy-start.7
  31.1 0.7 copy-start.9
  31.9 0.8 copy-start.12
  32.7 0.8 copy-start.14
  42.3 62.1 %collective-permute-start.12 = (bf16[528,128]{1,0:T(8,128)(2,1)}, bf16[528,128]{1,0:T(8,128)(2,1)S(1)}, u32[]{:S(2)}, u32[]{:S(2)}) collective-permute-start(bf16[528,128]{1,0:T(8,128)(2,1)} %get-tuple-element.61), channel_id=1, source_target_pairs={{0,0},{1,32},{2,64},{3,96},{4,128},{5,160},{6,192},{7,224},{8,8},{... | collective-permute-start | bytes 405512 | tf_op jit(solution)/shard_map/ppermute | solution.py:42
  46.3 58.1 %collective-permute-start.13 = (bf16[528,128]{1,0:T(8,128)(2,1)}, bf16[528,128]{1,0:T(8,128)(2,1)S(1)}, u32[]{:S(2)}, u32[]{:S(2)}) collective-permute-start(bf16[528,128]{1,0:T(8,128)(2,1)} %get-tuple-element.62), channel_id=1, source_target_pairs={{0,8},{1,40},{2,72},{3,104},{4,136},{5,168},{6,200},{7,232},{8,0},... | collective-permute-start | bytes 405512 | tf_op jit(solution)/shard_map/ppermute | solution.py:42
  48.3 56.1 %collective-permute-start.14 = (bf16[528,128]{1,0:T(8,128)(2,1)}, bf16[528,128]{1,0:T(8,128)(2,1)S(1)}, u32[]{:S(2)}, u32[]{:S(2)}) collective-permute-start(bf16[528,128]{1,0:T(8,128)(2,1)} %get-tuple-element.63), channel_id=1, source_target_pairs={{0,16},{1,48},{2,80},{3,112},{4,144},{5,176},{6,208},{7,240},{8,24... | collective-permute-start | bytes 405512 | tf_op jit(solution)/shard_map/ppermute | solution.py:42
  57.6 46.8 %collective-permute-start.15 = (bf16[528,128]{1,0:T(8,128)(2,1)}, bf16[528,128]{1,0:T(8,128)(2,1)}, u32[]{:S(2)}, u32[]{:S(2)}) collective-permute-start(bf16[528,128]{1,0:T(8,128)(2,1)} %get-tuple-element.64), channel_id=1, source_target_pairs={{0,24},{1,56},{2,88},{3,120},{4,152},{5,184},{6,216},{7,248},{8,16... | collective-permute-start | bytes 405512 | tf_op jit(solution)/shard_map/ppermute | solution.py:42
  62.8 1.3 collective-permute-start
  64.0 9.3 %collective-permute-start.1 = (f32[8,128]{1,0:T(8,128)S(1)}, f32[8,128]{1,0:T(8,128)S(1)}, u32[]{:S(2)}, u32[]{:S(2)}) collective-permute-start(f32[8,128]{1,0:T(8,128)S(1)} %add.107), channel_id=1, source_target_pairs={{0,16},{1,17},{2,18},{3,19},{4,20},{5,21},{6,22},{7,23},{8,24},{9,... | collective-permute-start | bytes 12296 | tf_op jit(solution)/shard_map/while/body/ppermute | solution.py:42
  73.3 4.5 %collective-permute-start.2 = (f32[8,128]{1,0:T(8,128)S(1)}, f32[8,128]{1,0:T(8,128)S(1)}, u32[]{:S(2)}, u32[]{:S(2)}) collective-permute-start(f32[8,128]{1,0:T(8,128)S(1)} %add.108), channel_id=1, source_target_pairs={{0,32},{1,33},{2,34},{3,35},{4,36},{5,37},{6,38},{7,39},{8,40},{9,... | collective-permute-start | bytes 12296 | tf_op jit(solution)/shard_map/while/body/ppermute | solution.py:42
  77.8 7.5 %collective-permute-start.3 = (f32[8,128]{1,0:T(8,128)S(1)}, f32[8,128]{1,0:T(8,128)S(1)}, u32[]{:S(2)}, u32[]{:S(2)}) collective-permute-start(f32[8,128]{1,0:T(8,128)S(1)} %add.109), channel_id=1, source_target_pairs={{0,64},{1,65},{2,66},{3,67},{4,68},{5,69},{6,70},{7,71},{8,72},{9,... | collective-permute-start | bytes 12296 | tf_op jit(solution)/shard_map/while/body/ppermute | solution.py:42
  85.4 3.6 %collective-permute-start.4 = (f32[8,128]{1,0:T(8,128)S(1)}, f32[8,128]{1,0:T(8,128)S(1)}, u32[]{:S(2)}, u32[]{:S(2)}) collective-permute-start(f32[8,128]{1,0:T(8,128)S(1)} %add.110), channel_id=1, source_target_pairs={{0,128},{1,129},{2,130},{3,131},{4,132},{5,133},{6,134},{7,135},{8... | collective-permute-start | bytes 12296 | tf_op jit(solution)/shard_map/while/body/ppermute | solution.py:42
  89.0 6.1 %collective-permute-start.5 = (f32[8,128]{1,0:T(8,128)S(1)}, f32[8,128]{1,0:T(8,128)S(1)}, u32[]{:S(2)}, u32[]{:S(2)}) collective-permute-start(f32[8,128]{1,0:T(8,128)S(1)} %add.111), channel_id=1, source_target_pairs={{0,1},{1,0},{2,3},{3,2},{4,5},{5,4},{6,7},{7,6},{8,9},{9,8},{10,11... | collective-permute-start | bytes 12296 | tf_op jit(solution)/shard_map/while/body/ppermute | solution.py:42
  95.0 4.2 %collective-permute-start.6 = (f32[8,128]{1,0:T(8,128)S(1)}, f32[8,128]{1,0:T(8,128)S(1)}, u32[]{:S(2)}, u32[]{:S(2)}) collective-permute-start(f32[8,128]{1,0:T(8,128)S(1)} %add.112), channel_id=1, source_target_pairs={{0,2},{1,3},{2,0},{3,1},{4,6},{5,7},{6,4},{7,5},{8,10},{9,11},{10,... | collective-permute-start | bytes 12296 | tf_op jit(solution)/shard_map/while/body/ppermute | solution.py:42
  99.3 5.1 %collective-permute-start.7 = (f32[8,128]{1,0:T(8,128)S(1)}, f32[8,128]{1,0:T(8,128)S(1)}, u32[]{:S(2)}, u32[]{:S(2)}) collective-permute-start(f32[8,128]{1,0:T(8,128)S(1)} %add.113), channel_id=1, source_target_pairs={{0,4},{1,5},{2,6},{3,7},{4,0},{5,1},{6,2},{7,3},{8,12},{9,13},{10,... | collective-permute-start | bytes 12296 | tf_op jit(solution)/shard_map/while/body/ppermute | solution.py:42
  104.4 0.7 copy-start.10
  113.0 53.3 %copy-start.2 = (bf16[32,128,64]{1,2,0:T(8,128)(2,1)S(1)}, bf16[32,128,64]{1,2,0:T(8,128)(2,1)}, u32[]{:S(2)}) copy-start(bf16[32,128,64]{1,2,0:T(8,128)(2,1)} %param.8) | copy-start | bytes 1572868
  113.0 53.3 %copy-start.4 = (bf16[3,3,64,64]{3,2,1,0:T(8,128)(2,1)S(1)}, bf16[3,3,64,64]{3,2,1,0:T(8,128)(2,1)}, u32[]{:S(2)}) copy-start(bf16[3,3,64,64]{3,2,1,0:T(8,128)(2,1)} %param.9) | copy-start | bytes 221188
  117.5 6.0 %collective-permute-start.17 = (f32[88,128]{1,0:T(8,128)S(1)}, f32[88,128]{1,0:T(8,128)S(1)}, u32[]{:S(2)}, u32[]{:S(2)}) collective-permute-start(f32[88,128]{1,0:T(8,128)S(1)} %get-tuple-element.81), channel_id=1, source_target_pairs={{0,16},{1,17},{2,18},{3,19},{4,20},{5,21},{6,22},{7,23},{8,24},{9,... | collective-permute-start | bytes 135176 | tf_op jit(solution)/shard_map/ppermute | solution.py:42
  121.5 3.5 %collective-permute-start.18 = (f32[88,128]{1,0:T(8,128)S(1)}, f32[88,128]{1,0:T(8,128)S(1)}, u32[]{:S(2)}, u32[]{:S(2)}) collective-permute-start(f32[88,128]{1,0:T(8,128)S(1)} %get-tuple-element.82), channel_id=1, source_target_pairs={{0,24},{1,25},{2,26},{3,27},{4,28},{5,29},{6,30},{7,31},{8,16},{9,... | collective-permute-start | bytes 135176 | tf_op jit(solution)/shard_map/ppermute | solution.py:42
  121.5 3.5 %collective-permute-start.16 = (f32[88,128]{1,0:T(8,128)S(1)}, f32[88,128]{1,0:T(8,128)S(1)}, u32[]{:S(2)}, u32[]{:S(2)}) collective-permute-start(f32[88,128]{1,0:T(8,128)S(1)} %get-tuple-element.80), channel_id=1, source_target_pairs={{0,8},{1,9},{2,10},{3,11},{4,12},{5,13},{6,14},{7,15},{8,0},{9,1},... | collective-permute-start | bytes 135176 | tf_op jit(solution)/shard_map/ppermute | solution.py:42
  125.0 8.2 %collective-permute-start.20 = (f32[88,128]{1,0:T(8,128)S(1)}, f32[88,128]{1,0:T(8,128)S(1)}, u32[]{:S(2)}, u32[]{:S(2)}) collective-permute-start(f32[88,128]{1,0:T(8,128)S(1)} %add_add_fusion.3), channel_id=1, source_target_pairs={{0,64},{1,65},{2,66},{3,67},{4,68},{5,69},{6,70},{7,71},{8,72},{9,... | collective-permute-start | bytes 135176 | tf_op jit(solution)/shard_map/ppermute | solution.py:42
  129.1 6.2 %collective-permute-start.21 = (f32[88,128]{1,0:T(8,128)S(1)}, f32[88,128]{1,0:T(8,128)S(1)}, u32[]{:S(2)}, u32[]{:S(2)}) collective-permute-start(f32[88,128]{1,0:T(8,128)S(1)} %add_add_fusion.3), channel_id=1, source_target_pairs={{0,96},{1,97},{2,98},{3,99},{4,100},{5,101},{6,102},{7,103},{8,104... | collective-permute-start | bytes 135176 | tf_op jit(solution)/shard_map/ppermute | solution.py:42
  132.0 5.4 %collective-permute-start.19 = (f32[88,128]{1,0:T(8,128)S(1)}, f32[88,128]{1,0:T(8,128)S(1)}, u32[]{:S(2)}, u32[]{:S(2)}) collective-permute-start(f32[88,128]{1,0:T(8,128)S(1)} %add_add_fusion.3), channel_id=1, source_target_pairs={{0,32},{1,33},{2,34},{3,35},{4,36},{5,37},{6,38},{7,39},{8,40},{9,... | collective-permute-start | bytes 135176 | tf_op jit(solution)/shard_map/ppermute | solution.py:42
  137.5 11.3 %collective-permute-start.23 = (f32[88,128]{1,0:T(8,128)S(1)}, f32[88,128]{1,0:T(8,128)S(1)}, u32[]{:S(2)}, u32[]{:S(2)}) collective-permute-start(f32[88,128]{1,0:T(8,128)S(1)} %add_add_fusion.2), channel_id=1, source_target_pairs={{0,1},{1,0},{2,3},{3,2},{4,5},{5,4},{6,7},{7,6},{8,9},{9,8},{10,11... | collective-permute-start | bytes 135176 | tf_op jit(solution)/shard_map/ppermute | solution.py:42
  137.6 11.2 %collective-permute-start.24 = (f32[88,128]{1,0:T(8,128)S(1)}, f32[88,128]{1,0:T(8,128)S(1)}, u32[]{:S(2)}, u32[]{:S(2)}) collective-permute-start(f32[88,128]{1,0:T(8,128)S(1)} %add_add_fusion.2), channel_id=1, source_target_pairs={{0,129},{1,128},{2,131},{3,130},{4,133},{5,132},{6,135},{7,134},{8... | collective-permute-start | bytes 135176 | tf_op jit(solution)/shard_map/ppermute | solution.py:42
  140.2 8.5 %collective-permute-start.22 = (f32[88,128]{1,0:T(8,128)S(1)}, f32[88,128]{1,0:T(8,128)S(1)}, u32[]{:S(2)}, u32[]{:S(2)}) collective-permute-start(f32[88,128]{1,0:T(8,128)S(1)} %add_add_fusion.2), channel_id=1, source_target_pairs={{0,128},{1,129},{2,130},{3,131},{4,132},{5,133},{6,134},{7,135},{8... | collective-permute-start | bytes 135176 | tf_op jit(solution)/shard_map/ppermute | solution.py:42
  141.0 11.3 %collective-permute-start.31 = (bf16[8,64,128]{2,1,0:T(8,128)(2,1)S(1)}, bf16[8,64,128]{2,1,0:T(8,128)(2,1)S(1)}, u32[]{:S(2)}, u32[]{:S(2)}) collective-permute-start(bf16[8,64,128]{2,1,0:T(8,128)(2,1)S(1)} %get-tuple-element.85), channel_id=1, source_target_pairs={{0,8},{8,16},{16,24},{24,32},{32,40},{40,48},{48,56},{56,64},{64,7... | collective-permute-start | bytes 393224 | tf_op jit(solution)/shard_map/ppermute | solution.py:48
  143.0 9.4 %collective-permute-start.32 = (bf16[8,64,128]{2,1,0:T(8,128)(2,1)S(1)}, bf16[8,64,128]{2,1,0:T(8,128)(2,1)S(1)}, u32[]{:S(2)}, u32[]{:S(2)}) collective-permute-start(bf16[8,64,128]{2,1,0:T(8,128)(2,1)S(1)} %get-tuple-element.86), channel_id=1, source_target_pairs={{8,0},{16,8},{24,16},{32,24},{40,32},{48,40},{56,48},{64,56},{72,6... | collective-permute-start | bytes 393224 | tf_op jit(solution)/shard_map/ppermute | solution.py:48
  148.8 11.4 %collective-permute-start.26 = (f32[88,128]{1,0:T(8,128)S(1)}, f32[88,128]{1,0:T(8,128)S(1)}, u32[]{:S(2)}, u32[]{:S(2)}) collective-permute-start(f32[88,128]{1,0:T(8,128)S(1)} %add_add_fusion.1), channel_id=1, source_target_pairs={{0,4},{1,5},{2,6},{3,7},{4,0},{5,1},{6,2},{7,3},{8,12},{9,13},{10,... | collective-permute-start | bytes 135176 | tf_op jit(solution)/shard_map/ppermute | solution.py:42
  149.8 10.4 %collective-permute-start.27 = (f32[88,128]{1,0:T(8,128)S(1)}, f32[88,128]{1,0:T(8,128)S(1)}, u32[]{:S(2)}, u32[]{:S(2)}) collective-permute-start(f32[88,128]{1,0:T(8,128)S(1)} %add_add_fusion.1), channel_id=1, source_target_pairs={{0,6},{1,7},{2,4},{3,5},{4,2},{5,3},{6,0},{7,1},{8,14},{9,15},{10,... | collective-permute-start | bytes 135176 | tf_op jit(solution)/shard_map/ppermute | solution.py:42
  151.8 8.4 %collective-permute-start.25 = (f32[88,128]{1,0:T(8,128)S(1)}, f32[88,128]{1,0:T(8,128)S(1)}, u32[]{:S(2)}, u32[]{:S(2)}) collective-permute-start(f32[88,128]{1,0:T(8,128)S(1)} %add_add_fusion.1), channel_id=1, source_target_pairs={{0,2},{1,3},{2,0},{3,1},{4,6},{5,7},{6,4},{7,5},{8,10},{9,11},{10,... | collective-permute-start | bytes 135176 | tf_op jit(solution)/shard_map/ppermute | solution.py:42
  152.8 10.5 %collective-permute-start.33 = (bf16[3,64,128]{2,1,0:T(8,128)(2,1)S(1)}, bf16[3,64,128]{2,1,0:T(8,128)(2,1)S(1)}, u32[]{:S(2)}, u32[]{:S(2)}) collective-permute-start(bf16[3,64,128]{2,1,0:T(8,128)(2,1)S(1)} %get-tuple-element.87), channel_id=1, source_target_pairs={{0,1},{1,2},{2,3},{3,4},{4,5},{5,6},{6,7},{8,9},{9,10},{10,11},{11... | collective-permute-start | bytes 147464 | tf_op jit(solution)/shard_map/ppermute | solution.py:48
  157.9 8.4 %collective-permute-start.34 = (bf16[3,64,128]{2,1,0:T(8,128)(2,1)S(1)}, bf16[3,64,128]{2,1,0:T(8,128)(2,1)S(1)}, u32[]{:S(2)}, u32[]{:S(2)}) collective-permute-start(bf16[3,64,128]{2,1,0:T(8,128)(2,1)S(1)} %get-tuple-element.88), channel_id=1, source_target_pairs={{1,0},{2,1},{3,2},{4,3},{5,4},{6,5},{7,6},{9,8},{10,9},{11,10},{12... | collective-permute-start | bytes 147464 | tf_op jit(solution)/shard_map/ppermute | solution.py:48
  160.2 10.9 %collective-permute-start.28 = (f32[88,128]{1,0:T(8,128)S(1)}, f32[88,128]{1,0:T(8,128)S(1)}, u32[]{:S(2)}, u32[]{:S(2)}) collective-permute-start(f32[88,128]{1,0:T(8,128)S(1)} %add_add_fusion.got0), channel_id=1, source_target_pairs={{0,8},{1,9},{2,10},{3,11},{4,12},{5,13},{6,14},{7,15},{8,0},{9,1},... | collective-permute-start | bytes 135176 | tf_op jit(solution)/shard_map/ppermute | solution.py:42
  160.3 10.8 %collective-permute-start.29 = (f32[88,128]{1,0:T(8,128)S(1)}, f32[88,128]{1,0:T(8,128)S(1)}, u32[]{:S(2)}, u32[]{:S(2)}) collective-permute-start(f32[88,128]{1,0:T(8,128)S(1)} %add_add_fusion.got0), channel_id=1, source_target_pairs={{0,16},{1,17},{2,18},{3,19},{4,20},{5,21},{6,22},{7,23},{8,24},{9,... | collective-permute-start | bytes 135176 | tf_op jit(solution)/shard_map/ppermute | solution.py:42
  160.4 10.7 %collective-permute-start.30 = (f32[88,128]{1,0:T(8,128)S(1)}, f32[88,128]{1,0:T(8,128)S(1)}, u32[]{:S(2)}, u32[]{:S(2)}) collective-permute-start(f32[88,128]{1,0:T(8,128)S(1)} %add_add_fusion.got0), channel_id=1, source_target_pairs={{0,24},{1,25},{2,26},{3,27},{4,28},{5,29},{6,30},{7,31},{8,16},{9,... | collective-permute-start | bytes 135176 | tf_op jit(solution)/shard_map/ppermute | solution.py:42
  (2 other events, 1.2 us)

commit v4 on v2

--- a/solution.py
+++ b/solution.py
@@ -48,7 +48,7 @@
     return lax.ppermute(block, axis, pairs if forward else [(b, a) for a, b in pairs])
 
 
-def activate_kernel(feat, act, top, bottom):
+def activate_kernel(feat, valid, act, top, bottom, counted):
     rows = feat.shape[0]
 
     def step(i, carry):
@@ -61,6 +61,8 @@
     lax.fori_loop(0, rows, step, 0)
     top[...] = act[:STEP]
     bottom[...] = act[rows - STEP :]
+    lines = jnp.sum(valid[...].astype(F32), axis=0, keepdims=True)
+    counted[...] = jnp.broadcast_to(jnp.sum(lines, axis=1, keepdims=True), counted.shape)
 
 
 def row_of(own, up, down, at):
@@ -160,16 +162,13 @@
 
 
 def softmax_kernel(
-    place, got0, got1, got2, got3, mixed, head, labels, valid,
-    grad, head_sum, bias_sum, loss_sum, cells, lab, lab_t, val, val_t,
+    place, got0, got1, got2, got3, mixed, head, head_bias, labels, valid,
+    grad, head_sum, bias_sum, loss_sum, cells, lab, lab_t, val, val_t, padded_head,
 ):
     rows, chans = mixed.shape[0], mixed.shape[1]
-    bins = head.shape[0]
+    bins, real = padded_head.shape[0], head.shape[0]
     half = rows // 2
     size = rows * half
-    lab[...] = labels[...].astype(F32)
-    val[...] = valid[...].astype(F32)
-    notes = []
     for s, got in enumerate((got0, got1, got2, got3)):
         q = place[0] ^ s
         cells[pl.ds(pl.multiple_of(q * size, size), size), :] = got[:size, :].astype(F32)
@@ -183,13 +182,21 @@
         val_t[top * half : (top + 1) * half, :] = jnp.concatenate(
             [n[:, base + rows : base + 2 * rows] for n in notes], axis=1
         )
-    lane = lax.broadcasted_iota(jnp.int32, (bins, LANES), 1)
-    plain = jnp.where(lane < chans, head[...], 0.0)
-    both = jnp.concatenate([plain, pltpu.roll(plain, chans, 1)], axis=0).astype(BF16)
-    single = plain[:, :chans]
+    padded_head[...] = jnp.zeros_like(padded_head)
+    padded_head[:real, :] = head[...].astype(F32)
+    single = padded_head[...]
+    blank = jnp.zeros_like(single)
+    both = jnp.concatenate(
+        [jnp.concatenate([single, blank], axis=1), jnp.concatenate([blank, single], axis=1)], axis=0
+    ).astype(BF16)
     thrice = jnp.concatenate([single, single, single], axis=0).T.astype(BF16)
     single = single.astype(BF16)
-    bias = head[:, chans : chans + 1]
+    line = lax.broadcasted_iota(jnp.int32, (bins, real), 0)
+    across = lax.broadcasted_iota(jnp.int32, (bins, real), 1)
+    bias = jnp.sum(jnp.where(line == across, head_bias[...], 0.0), axis=1, keepdims=True)
+    bias = jnp.where(lax.broadcasted_iota(jnp.int32, (bins, 1), 0) < real, bias, FAR_BELOW)
+    lab[...] = labels[...].astype(F32)
+    val[...] = valid[...].astype(F32)
     bin_ids = lax.broadcasted_iota(jnp.int32, (bins, LANES), 0).astype(F32)
     head_sum[...] = jnp.zeros_like(head_sum)
     bias_sum[...] = jnp.zeros_like(bias_sum)
@@ -268,11 +275,10 @@
     sheet[...] = jnp.zeros_like(sheet)
     sheet[:half, :] = jnp.concatenate([total[:half], total[half:]], axis=1)
     h = (head_sum[:bins] + head_sum[bins : 2 * bins] + head_sum[2 * bins :]) * scale
-    b = jnp.sum(bias_sum[...], axis=1, keepdims=True) * scale
-    loss = jnp.sum(loss_sum[...], axis=1, keepdims=True)
-    lane = lax.broadcasted_iota(jnp.int32, (bins, chans), 1)
-    extra = jnp.where(lane == 0, b, jnp.where(lane == 1, loss, 0.0))
-    sheet[half : half + bins, :] = jnp.concatenate([h, extra], axis=1)
+    sheet[half : half + bins, :chans] = h
+    note = half + bins
+    sheet[note : note + 1, :bins] = jnp.sum(bias_sum[...].T, axis=0, keepdims=True) * scale
+    sheet[note + 1 : note + 2, :1] = jnp.sum(loss_sum[...], axis=1, keepdims=True)
     quarter = sheet.shape[0] // 4
     for s, out in enumerate((out0, out1, out2, out3)):
         out[...] = sheet[pl.ds(pl.multiple_of((place[0] ^ s) * quarter, 8), quarter), :]
@@ -302,14 +308,20 @@
     lax.fori_loop(0, rows // 2, step, 0)
 
 
-def finish_kernel(place, got0, got1, got2, got3, kernel_grad, tail, sheet):
+def finish_kernel(
+    place, count, got0, got1, got2, got3, kernel_grad, head_grad, bias_grad, loss, sheet
+):
     quarter = got0.shape[0]
     for s, got in enumerate((got0, got1, got2, got3)):
         sheet[pl.ds(pl.multiple_of((place[0] ^ s) * quarter, 8), quarter), :] = got[...]
     half, chans = kernel_grad.shape[0] // 2, kernel_grad.shape[1]
+    bins = head_grad.shape[0]
     kernel_grad[:half, :] = sheet[:half, :chans]
     kernel_grad[half:, :] = sheet[:half, chans:]
-    tail[...] = sheet[half : half + tail.shape[0], :]
+    head_grad[...] = sheet[half : half + bins, :chans]
+    note = half + -(-bins // 8) * 8
+    bias_grad[...] = sheet[note : note + 1, :bins]
+    loss[...] = sheet[note + 1 : note + 2, :1] / jnp.maximum(count[0:1, 0:1], 1.0)
 
 
 def borders(own, top, bottom):
@@ -318,7 +330,7 @@
     down = shifted(top, "row", False)
     groups = (rows + 2 * STEP) // 16
     first, last = run(
-        pack_kernel, [shape((groups, chans, LANES), BF16)] * 2, (own, up, down), micros=1
+        pack_kernel, [shape((groups, chans, LANES), BF16)] * 2, (own, up, down), micros=8
     )
     left = shifted(last, "col", True)
     right = shifted(first, "col", False)
@@ -334,11 +346,21 @@
 
 
 def total_small(value):
-    for bit in range(5):
-        value = value + send(value, lambda r, c: (r ^ (1 << bit), c))
-    for bit in range(3):
-        value = value + send(value, lambda r, c: (r, c ^ (1 << bit)))
+    for stage in range(4):
+        to = partners(stage)
+        value = (value + send(value, to(1))) + (send(value, to(2)) + send(value, to(3)))
     return value
+
+
+def mirrored(pays, parts):
+    got = []
+    for s, block in enumerate(pays):
+        bits = (2, 6, 0, 0)[s]
+        owner = lambda r, c: (parts * c + (r % parts ^ s), r // parts)
+        if bits:
+            block = send(block, lambda r, c: (r, c ^ bits))
+        got.append(send(block, lambda r, c: owner(r, c ^ bits)))
+    return got
 
 
 def total_quarters(quarters):
@@ -359,22 +381,17 @@
     feat = features.transpose(0, 2, 1)
     weight = conv_weight.reshape(-1, chans)
     tall = -(-bins // 8) * 8
-    head = jnp.concatenate(
-        [
-            jnp.pad(head_weight.T.astype(F32), ((0, tall - bins), (0, 0))),
-            jnp.pad(head_bias, (0, tall - bins), constant_values=FAR_BELOW)[:, None],
-            jnp.zeros((tall, LANES - chans - 1), F32),
-        ],
-        axis=1,
-    )
-    counted = jnp.full((8, LANES), jnp.sum(valid.astype(F32)))
     tile = (rows, chans, LANES)
     edge = (STEP, chans, LANES)
-    act, top, bottom = run(
-        activate_kernel, [shape(tile, BF16), shape(edge, BF16), shape(edge, BF16)], (feat,), micros=1
+    act, top, bottom, counted = run(
+        activate_kernel,
+        [shape(tile, BF16), shape(edge, BF16), shape(edge, BF16), shape((8, LANES), F32)],
+        (feat, valid),
+        micros=1,
     )
     around = borders(act, top, bottom)
     count = total_small(counted)
+    count, act = lax.optimization_barrier((count, act))
     length = (rows + 1) * rows // 2
     wide, mixed, *pays = run(
         forward_kernel,
@@ -385,9 +402,7 @@
         scalars=1,
         micros=5,
     )
-    got = [
-        send(pays[s], lambda r, c: (parts * c + (r % parts ^ s), r // parts)) for s in range(parts)
-    ]
+    got = mirrored(pays, parts)
     grad, head_sum, bias_sum, loss_sum = run(
         softmax_kernel,
         [
@@ -396,13 +411,15 @@
             shape((tall, LANES), F32),
             shape((1, LANES), F32),
         ],
-        (place, *got, mixed, head, labels, valid),
-        scratch=[pltpu.VMEM((length * 4, LANES), F32)] + [pltpu.VMEM((rows, LANES), F32)] * 4,
+        (place, *got, mixed, head_weight.T, head_bias.reshape(1, bins), labels, valid),
+        scratch=[pltpu.VMEM((length * 4, LANES), F32)]
+        + [pltpu.VMEM((rows, LANES), F32)] * 4
+        + [pltpu.VMEM((tall, chans), F32)],
         scalars=1,
         micros=5,
     )
     half = 9 * chans // 2
-    lines = -(-(half + tall) // 32) * 32
+    lines = -(-(half + tall + 8) // 32) * 32
     low, top, bottom, *quarters = run(
         kernel_grad_kernel,
         [shape(tile, BF16), shape(edge, BF16), shape(edge, BF16)]
@@ -421,21 +438,25 @@
         scratch=[pltpu.VMEM((rows + 2 * STEP, 3 * chans, LANES), BF16)],
         micros=4,
     )
-    kernel_grad, tail = run(
+    kernel_grad, head_grad, bias_grad, loss = run(
         finish_kernel,
-        [shape((9 * chans, chans), F32), shape((tall, LANES), F32)],
-        (place, *sums),
+        [
+            shape((9 * chans, chans), F32),
+            shape((bins, chans), F32),
+            shape((1, bins), F32),
+            shape((1, 1), F32),
+        ],
+        (place, count, *sums),
         scratch=[pltpu.VMEM((lines, LANES), F32)],
         scalars=1,
         micros=1,
     )
-    loss = tail[0, chans + 1] / jnp.maximum(count[0, 0], 1.0)
     return (
-        loss,
+        loss.reshape(()),
         grad_features.transpose(0, 2, 1),
         kernel_grad.reshape(conv_weight.shape),
-        tail[:bins, :chans].T,
-        tail[:bins, chans],
+        head_grad.T,
+        bias_grad.reshape(bins),
     )
 
 

time: 171 us -> 157 us (0.918)
  other arithmetic: 3.48 us -> 0.09 us
  local copies, waits for them, and re-layouts: 8.3 us -> 5.16 us
  between operations: 3.4 us -> 0.94 us
  waiting for transfers between devices: 40.7 us -> 38.3 us
    ppermute x27 -> x33, waiting for transfers between devices: 40.4 us -> 30 us  [send(): return lax.ppermute(block, GRID, pairs)]
    ppermute x8, waiting for transfers between devices: 0.22 us -> 8.32 us  [shifted(): lax.ppermute(block, axis, pairs if forward else [(b, a) for a, b in pairs])]
    slice x3 -> x0, local copies, waits for them, and re-layouts: 1.78 us -> none  [the longest x2 1.09 us: per_device(): loss = tail[0, chans + 1] / jnp.maximum(count[0, 0], 1.0)]
    unnamed x12 -> x18, local copies, waits for them, and re-layouts: 4.43 us -> 5.16 us
    ppermute x27 -> x33, starting transfers between devices: 55.3 us -> 55 us  [send(): return lax.ppermute(block, GRID, pairs)]
  transfers between devices with their start and end apart: 35 -> 41, of which waited for: 12 -> 12; matrix products, arithmetic and copies ran while one was open for 2% -> 0% of each run, Pallas kernels for 9% -> 4%
where the time goes in v4:
time: 157 us; the launch traced here: 156 us
  starting transfers between devices  85 us (54%)
  waiting for transfers between devices  38.3 us (24%)
  Pallas kernels  26.8 us (17%)
  local copies, waits for them, and re-layouts  5.16 us (3%)
    ppermute x33, starting transfers between devices, send(): return lax.ppermute(block, GRID, pairs)  55 us
    ppermute x8, starting transfers between devices, shifted(): lax.ppermute(block, axis, pairs if forward else [(b, a) for a, b in pairs])  30 us
    ppermute x33, waiting for transfers between devices, send(): return lax.ppermute(block, GRID, pairs)  30 us
    pallas_call x8, Pallas kernels, run(): pl.pallas_call(body, out_shape=outs, in_specs=[SMEM] * scalars + [VMEM] *...  26.8 us
    ppermute x8, waiting for transfers between devices, shifted(): lax.ppermute(block, axis, pairs if forward else [(b, a) for a, b in pairs])  8.32 us
    unnamed x18, local copies, waits for them, and re-layouts  5.16 us
  transfers between devices with their start and end apart: 41, of which 12 were waited for; matrix products, arithmetic and copies ran while one was open for 0% of the time, Pallas kernels for 4%

profile of v4, /device:TPU:24, one launch (start us, length us, event | category | flops | bytes accessed | tf_op | source)
XLA Modules:
  0.0 156.2 jit_solution(17747161303391744825)
XLA Ops:
  0.7 1.0 copy-done
  2.4 0.9 shard_map.101
  3.3 1.4 collective-permute-start.2
  5.4 1.0 collective-permute-done.2
  6.4 1.9 %collective-permute-done.1 = f32[8,128]{1,0:T(8,128)S(1)} collective-permute-done((f32[8,128]{1,0:T(8,128)S(1)}, f32[8,128]{1,0:T(8,128)S(1)}, u32[]{:S(2)}, u32[]{:S(2)}) %collective-permute-start.1) | collective-permute-done | bytes 4128 | tf_op jit(solution)/shard_map/ppermute | solution.py:42
  8.3 5.5 %collective-permute-start.5 = (f32[8,128]{1,0:T(8,128)S(1)}, f32[8,128]{1,0:T(8,128)S(1)}, u32[]{:S(2)}, u32[]{:S(2)}) collective-permute-start(f32[8,128]{1,0:T(8,128)S(1)} %add_add_fusion.7), channel_id=1, source_target_pairs={{0,96},{1,97},{2,98},{3,99},{4,100},{5,101},{6,102},{7,103},{8,104... | collective-permute-start | bytes 12296 | tf_op jit(solution)/shard_map/ppermute | solution.py:42
  13.8 1.4 collective-permute-start.4
  15.2 1.0 collective-permute-start.3
  16.3 5.0 %collective-permute-done.4 = f32[8,128]{1,0:T(8,128)S(1)} collective-permute-done((f32[8,128]{1,0:T(8,128)S(1)}, f32[8,128]{1,0:T(8,128)S(1)}, u32[]{:S(2)}, u32[]{:S(2)}) %collective-permute-start.4) | collective-permute-done | bytes 4128 | tf_op jit(solution)/shard_map/ppermute | solution.py:42
  21.6 2.6 %collective-permute-start.7 = (f32[8,128]{1,0:T(8,128)S(1)}, f32[8,128]{1,0:T(8,128)S(1)}, u32[]{:S(2)}, u32[]{:S(2)}) collective-permute-start(f32[8,128]{1,0:T(8,128)S(1)} %add_add_fusion.6), channel_id=1, source_target_pairs={{0,1},{1,0},{2,3},{3,2},{4,5},{5,4},{6,7},{7,6},{8,9},{9,8},{10,11... | collective-permute-start | bytes 12296 | tf_op jit(solution)/shard_map/ppermute | solution.py:42
  24.2 1.3 collective-permute-start.6
  25.5 1.9 %collective-permute-start.12 = (bf16[8,64,128]{2,1,0:T(8,128)(2,1)S(1)}, bf16[8,64,128]{2,1,0:T(8,128)(2,1)S(1)}, u32[]{:S(2)}, u32[]{:S(2)}) collective-permute-start(bf16[8,64,128]{2,1,0:T(8,128)(2,1)S(1)} %get-tuple-element.40), channel_id=1, source_target_pairs={{0,8},{8,16},{16,24},{24,32},{32,40},{40,48},{48,56},{56,64},{64,7... | collective-permute-start | bytes 393224 | tf_op jit(solution)/shard_map/ppermute | solution.py:48
  27.4 5.8 %collective-permute-start.13 = (bf16[8,64,128]{2,1,0:T(8,128)(2,1)S(1)}, bf16[8,64,128]{2,1,0:T(8,128)(2,1)S(1)}, u32[]{:S(2)}, u32[]{:S(2)}) collective-permute-start(bf16[8,64,128]{2,1,0:T(8,128)(2,1)S(1)} %get-tuple-element.41), channel_id=1, source_target_pairs={{8,0},{16,8},{24,16},{32,24},{40,32},{48,40},{56,48},{64,56},{72,6... | collective-permute-start | bytes 393224 | tf_op jit(solution)/shard_map/ppermute | solution.py:48
  33.2 2.8 %collective-permute-start.11 = (f32[8,128]{1,0:T(8,128)S(1)}, f32[8,128]{1,0:T(8,128)S(1)}, u32[]{:S(2)}, u32[]{:S(2)}) collective-permute-start(f32[8,128]{1,0:T(8,128)S(1)} %add_add_fusion.5), channel_id=1, source_target_pairs={{0,6},{1,7},{2,4},{3,5},{4,2},{5,3},{6,0},{7,1},{8,14},{9,15},{10,... | collective-permute-start | bytes 12296 | tf_op jit(solution)/shard_map/ppermute | solution.py:42
  36.1 0.8 collective-permute-start.10
  37.9 4.1 %collective-permute-start.14 = (bf16[3,64,128]{2,1,0:T(8,128)(2,1)S(1)}, bf16[3,64,128]{2,1,0:T(8,128)(2,1)S(1)}, u32[]{:S(2)}, u32[]{:S(2)}) collective-permute-start(bf16[3,64,128]{2,1,0:T(8,128)(2,1)S(1)} %get-tuple-element.42), channel_id=1, source_target_pairs={{0,1},{1,2},{2,3},{3,4},{4,5},{5,6},{6,7},{8,9},{9,10},{10,11},{11... | collective-permute-start | bytes 147464 | tf_op jit(solution)/shard_map/ppermute | solution.py:48
  41.9 3.3 %collective-permute-start.15 = (bf16[3,64,128]{2,1,0:T(8,128)(2,1)S(1)}, bf16[3,64,128]{2,1,0:T(8,128)(2,1)S(1)}, u32[]{:S(2)}, u32[]{:S(2)}) collective-permute-start(bf16[3,64,128]{2,1,0:T(8,128)(2,1)S(1)} %get-tuple-element.43), channel_id=1, source_target_pairs={{1,0},{2,1},{3,2},{4,3},{5,4},{6,5},{7,6},{9,8},{10,9},{11,10},{12... | collective-permute-start | bytes 147464 | tf_op jit(solution)/shard_map/ppermute | solution.py:48
  45.4 5.0 %collective-permute-done.15.right = bf16[3,64,128]{2,1,0:T(8,128)(2,1)S(1)} collective-permute-done((bf16[3,64,128]{2,1,0:T(8,128)(2,1)S(1)}, bf16[3,64,128]{2,1,0:T(8,128)(2,1)S(1)}, u32[]{:S(2)}, u32[]{:S(2)}) %collective-permute-start.15) | collective-permute-done | bytes 49184 | tf_op jit(solution)/shard_map/ppermute | solution.py:48
  50.3 1.0 copy-done.1
  51.4 0.9 copy-done.3
  53.7 8.0 %shard_map.103 = (bf16[48,192,128]{2,1,0:T(8,128)(2,1)S(1)}, bf16[32,64,128]{2,1,0:T(8,128)(2,1)S(1)}, bf16[528,128]{1,0:T(8,128)(2,1)S(1)}, bf16[528,128]{1,0:T...) custom-call(s32[1]{0:T(128)} %bitcast.place, ...), custom_call_target="tpu_custom_call" | custom-call | bytes 18000000 | tf_op jit(solution)/shard_map/pallas_call | solution.py:18
  61.8 1.5 collective-permute-start.16
  63.3 1.8 %collective-permute-start.18 = (bf16[528,128]{1,0:T(8,128)(2,1)S(1)}, bf16[528,128]{1,0:T(8,128)(2,1)S(1)}, u32[]{:S(2)}, u32[]{:S(2)}) collective-permute-start(bf16[528,128]{1,0:T(8,128)(2,1)S(1)} %get-tuple-element.45), channel_id=1, source_target_pairs={{0,6},{1,7},{2,4},{3,5},{4,2},{5,3},{6,0},{7,1},{8,14},{9,15},{10,... | collective-permute-start | bytes 405512 | tf_op jit(solution)/shard_map/ppermute | solution.py:42
  65.4 2.8 %collective-permute-start.21 = (bf16[528,128]{1,0:T(8,128)(2,1)S(1)}, bf16[528,128]{1,0:T(8,128)(2,1)S(1)}, u32[]{:S(2)}, u32[]{:S(2)}) collective-permute-start(bf16[528,128]{1,0:T(8,128)(2,1)S(1)} %get-tuple-element.47), channel_id=1, source_target_pairs={{0,24},{1,56},{2,88},{3,120},{4,152},{5,184},{6,216},{7,248},{8,16... | collective-permute-start | bytes 405512 | tf_op jit(solution)/shard_map/ppermute | solution.py:42
  68.2 2.1 %collective-permute-start.17 = (bf16[528,128]{1,0:T(8,128)(2,1)S(1)}, bf16[528,128]{1,0:T(8,128)(2,1)S(1)}, u32[]{:S(2)}, u32[]{:S(2)}) collective-permute-start(bf16[528,128]{1,0:T(8,128)(2,1)S(1)} %collective-permute-done.16), channel_id=1, source_target_pairs={{0,64},{1,96},{2,0},{3,32},{4,192},{5,224},{6,128},{7,160},{8,72},... | collective-permute-start | bytes 405512 | tf_op jit(solution)/shard_map/ppermute | solution.py:42
  70.2 7.2 %collective-permute-start.19 = (bf16[528,128]{1,0:T(8,128)(2,1)S(1)}, bf16[528,128]{1,0:T(8,128)(2,1)S(1)}, u32[]{:S(2)}, u32[]{:S(2)}) collective-permute-start(bf16[528,128]{1,0:T(8,128)(2,1)S(1)} %collective-permute-done.18), channel_id=1, source_target_pairs={{0,200},{1,232},{2,136},{3,168},{4,72},{5,104},{6,8},{7,40},{8,192... | collective-permute-start | bytes 405512 | tf_op jit(solution)/shard_map/ppermute | solution.py:42
  77.4 3.5 %collective-permute-done.20.got2 = bf16[528,128]{1,0:T(8,128)(2,1)S(1)} collective-permute-done((bf16[528,128]{1,0:T(8,128)(2,1)S(1)}, bf16[528,128]{1,0:T(8,128)(2,1)S(1)}, u32[]{:S(2)}, u32[]{:S(2)}) %collective-permute-start.20) | collective-permute-done | bytes 135200 | tf_op jit(solution)/shard_map/ppermute | solution.py:42
  81.0 6.7 %collective-permute-done.17.got0 = bf16[528,128]{1,0:T(8,128)(2,1)S(1)} collective-permute-done((bf16[528,128]{1,0:T(8,128)(2,1)S(1)}, bf16[528,128]{1,0:T(8,128)(2,1)S(1)}, u32[]{:S(2)}, u32[]{:S(2)}) %collective-permute-start.17) | collective-permute-done | bytes 135200 | tf_op jit(solution)/shard_map/ppermute | solution.py:42
  87.6 2.9 %collective-permute-done.19.got1 = bf16[528,128]{1,0:T(8,128)(2,1)S(1)} collective-permute-done((bf16[528,128]{1,0:T(8,128)(2,1)S(1)}, bf16[528,128]{1,0:T(8,128)(2,1)S(1)}, u32[]{:S(2)}, u32[]{:S(2)}) %collective-permute-start.19) | collective-permute-done | bytes 135200 | tf_op jit(solution)/shard_map/ppermute | solution.py:42
  90.6 7.0 %shard_map.104 = (f32[32,64,128]{2,1,0:T(8,128)S(1)}, f32[120,64]{1,0:T(8,128)S(1)}, f32[40,128]{1,0:T(8,128)S(1)}, f32[1,128]{1,0:T(1,128)S(1)}) custom-call(s32[1]{0:T(128)} %bitcast.place, bf16[528,128]{1,0:T(8,128)(2,1)S(1)} %collective-permute-done.17.got0, bf16[528,128]{1,0:T(8,128)(2,1)S(1)} %collective-permute-done.19.got1, ...), custom_call_target="tpu_custom_call" | custom-call | bytes 18000000 | tf_op jit(solution)/shard_map/pallas_call | solution.py:18
  97.5 4.4 %shard_map.105 = (bf16[32,64,128]{2,1,0:T(8,128)(2,1)S(1)}, bf16[8,64,128]{2,1,0:T(8,128)(2,1)S(1)}, bf16[8,64,128]{2,1,0:T(8,128)(2,1)S(1)}, f32[88,128]{1,0:T(...) custom-call(s32[1]{0:T(128)} %bitcast.place, f32[8,128]{1,0:T(8,128)S(1)} %add_add_fusion.4.count, ...), custom_call_target="tpu_custom_call" | custom-call | bytes 10800000 | tf_op jit(solution)/shard_map/pallas_call | solution.py:18
  102.4 1.4 collective-permute-start.24
  103.9 2.7 %collective-permute-done.23 = f32[88,128]{1,0:T(8,128)S(1)} collective-permute-done((f32[88,128]{1,0:T(8,128)S(1)}, f32[88,128]{1,0:T(8,128)S(1)}, u32[]{:S(2)}, u32[]{:S(2)}) %collective-permute-start.23) | collective-permute-done | bytes 45088 | tf_op jit(solution)/shard_map/ppermute | solution.py:42
  106.6 4.4 %collective-permute-start.27 = (f32[88,128]{1,0:T(8,128)S(1)}, f32[88,128]{1,0:T(8,128)S(1)}, u32[]{:S(2)}, u32[]{:S(2)}) collective-permute-start(f32[88,128]{1,0:T(8,128)S(1)} %add_add_fusion.3), channel_id=1, source_target_pairs={{0,96},{1,97},{2,98},{3,99},{4,100},{5,101},{6,102},{7,103},{8,104... | collective-permute-start | bytes 135176 | tf_op jit(solution)/shard_map/ppermute | solution.py:42
  111.0 2.8 %collective-permute-start.26 = (f32[88,128]{1,0:T(8,128)S(1)}, f32[88,128]{1,0:T(8,128)S(1)}, u32[]{:S(2)}, u32[]{:S(2)}) collective-permute-start(f32[88,128]{1,0:T(8,128)S(1)} %add_add_fusion.3), channel_id=1, source_target_pairs={{0,64},{1,65},{2,66},{3,67},{4,68},{5,69},{6,70},{7,71},{8,72},{9,... | collective-permute-start | bytes 135176 | tf_op jit(solution)/shard_map/ppermute | solution.py:42
  113.8 5.7 %collective-permute-done.26 = f32[88,128]{1,0:T(8,128)S(1)} collective-permute-done((f32[88,128]{1,0:T(8,128)S(1)}, f32[88,128]{1,0:T(8,128)S(1)}, u32[]{:S(2)}, u32[]{:S(2)}) %collective-permute-start.26) | collective-permute-done | bytes 45088 | tf_op jit(solution)/shard_map/ppermute | solution.py:42
  119.9 4.7 %collective-permute-start.30 = (f32[88,128]{1,0:T(8,128)S(1)}, f32[88,128]{1,0:T(8,128)S(1)}, u32[]{:S(2)}, u32[]{:S(2)}) collective-permute-start(f32[88,128]{1,0:T(8,128)S(1)} %add_add_fusion.2), channel_id=1, source_target_pairs={{0,129},{1,128},{2,131},{3,130},{4,133},{5,132},{6,135},{7,134},{8... | collective-permute-start | bytes 135176 | tf_op jit(solution)/shard_map/ppermute | solution.py:42
  124.6 1.0 collective-permute-start.28
  125.6 1.9 %collective-permute-start.37 = (bf16[8,64,128]{2,1,0:T(8,128)(2,1)S(1)}, bf16[8,64,128]{2,1,0:T(8,128)(2,1)S(1)}, u32[]{:S(2)}, u32[]{:S(2)}) collective-permute-start(bf16[8,64,128]{2,1,0:T(8,128)(2,1)S(1)} %get-tuple-element.60), channel_id=1, source_target_pairs={{0,8},{8,16},{16,24},{24,32},{32,40},{40,48},{48,56},{56,64},{64,7... | collective-permute-start | bytes 393224 | tf_op jit(solution)/shard_map/ppermute | solution.py:48
  127.5 5.8 %collective-permute-start.38 = (bf16[8,64,128]{2,1,0:T(8,128)(2,1)S(1)}, bf16[8,64,128]{2,1,0:T(8,128)(2,1)S(1)}, u32[]{:S(2)}, u32[]{:S(2)}) collective-permute-start(bf16[8,64,128]{2,1,0:T(8,128)(2,1)S(1)} %get-tuple-element.61), channel_id=1, source_target_pairs={{8,0},{16,8},{24,16},{32,24},{40,32},{48,40},{56,48},{64,56},{72,6... | collective-permute-start | bytes 393224 | tf_op jit(solution)/shard_map/ppermute | solution.py:48
  133.3 1.9 %collective-permute-start.33 = (f32[88,128]{1,0:T(8,128)S(1)}, f32[88,128]{1,0:T(8,128)S(1)}, u32[]{:S(2)}, u32[]{:S(2)}) collective-permute-start(f32[88,128]{1,0:T(8,128)S(1)} %add_add_fusion.1), channel_id=1, source_target_pairs={{0,6},{1,7},{2,4},{3,5},{4,2},{5,3},{6,0},{7,1},{8,14},{9,15},{10,... | collective-permute-start | bytes 135176 | tf_op jit(solution)/shard_map/ppermute | solution.py:42
  135.2 1.6 %collective-permute-start.32 = (f32[88,128]{1,0:T(8,128)S(1)}, f32[88,128]{1,0:T(8,128)S(1)}, u32[]{:S(2)}, u32[]{:S(2)}) collective-permute-start(f32[88,128]{1,0:T(8,128)S(1)} %add_add_fusion.1), channel_id=1, source_target_pairs={{0,4},{1,5},{2,6},{3,7},{4,0},{5,1},{6,2},{7,3},{8,12},{9,13},{10,... | collective-permute-start | bytes 135176 | tf_op jit(solution)/shard_map/ppermute | solution.py:42
  138.0 4.2 %collective-permute-start.39 = (bf16[3,64,128]{2,1,0:T(8,128)(2,1)S(1)}, bf16[3,64,128]{2,1,0:T(8,128)(2,1)S(1)}, u32[]{:S(2)}, u32[]{:S(2)}) collective-permute-start(bf16[3,64,128]{2,1,0:T(8,128)(2,1)S(1)} %get-tuple-element.62), channel_id=1, source_target_pairs={{0,1},{1,2},{2,3},{3,4},{4,5},{5,6},{6,7},{8,9},{9,10},{10,11},{11... | collective-permute-start | bytes 147464 | tf_op jit(solution)/shard_map/ppermute | solution.py:48
  142.2 3.1 %collective-permute-start.40 = (bf16[3,64,128]{2,1,0:T(8,128)(2,1)S(1)}, bf16[3,64,128]{2,1,0:T(8,128)(2,1)S(1)}, u32[]{:S(2)}, u32[]{:S(2)}) collective-permute-start(bf16[3,64,128]{2,1,0:T(8,128)(2,1)S(1)} %get-tuple-element.63), channel_id=1, source_target_pairs={{1,0},{2,1},{3,2},{4,3},{5,4},{6,5},{7,6},{9,8},{10,9},{11,10},{12... | collective-permute-start | bytes 147464 | tf_op jit(solution)/shard_map/ppermute | solution.py:48
  145.6 1.7 %collective-permute-start.34 = (f32[88,128]{1,0:T(8,128)S(1)}, f32[88,128]{1,0:T(8,128)S(1)}, u32[]{:S(2)}, u32[]{:S(2)}) collective-permute-start(f32[88,128]{1,0:T(8,128)S(1)} %add_add_fusion.got0), channel_id=1, source_target_pairs={{0,8},{1,9},{2,10},{3,11},{4,12},{5,13},{6,14},{7,15},{8,0},{9,1},... | collective-permute-start | bytes 135176 | tf_op jit(solution)/shard_map/ppermute | solution.py:42
  147.3 3.2 %collective-permute-done.40.right = bf16[3,64,128]{2,1,0:T(8,128)(2,1)S(1)} collective-permute-done((bf16[3,64,128]{2,1,0:T(8,128)(2,1)S(1)}, bf16[3,64,128]{2,1,0:T(8,128)(2,1)S(1)}, u32[]{:S(2)}, u32[]{:S(2)}) %collective-permute-start.40) | collective-permute-done | bytes 49184 | tf_op jit(solution)/shard_map/ppermute | solution.py:48
  150.6 4.8 %shard_map.108 = bf16[32,64,128]{2,1,0:T(8,128)(2,1)} custom-call(f32[8,128]{1,0:T(8,128)S(1)} %add_add_fusion.4.count, bf16[32,64,128]{2,1,0:T(8,128)(2,1)S(1)} %get-tuple-element.59.own.low, bf16[8,64,128]{2,1,0:T(8,128)(2,1)S(1)} %collective-permute-done.37.up, bf16[8,64,128]{2,1,0:T(8,128)(2,1)S(1)} %collective-permute-done.38.down, ...), custom_call_target="tpu_custom_call" | custom-call | bytes 14400000 | tf_op jit(solution)/shard_map/pallas_call | solution.py:18
  155.4 0.8 shard_map.106
  (68 shorter events, 6.9 us)
Async XLA Ops:
  0.6 89.9 %copy-start.8 = (f32[37]{0:T(128)S(1)}, f32[37]{0:T(128)}, u32[]{:S(2)}) copy-start(f32[37]{0:T(128)} %param.9) | copy-start | bytes 448
  0.6 1.0 copy-start
  1.7 0.7 copy-start.4
  2.4 88.2 %copy-start.7 = (bf16[64,37]{0,1:T(8,128)(2,1)S(1)}, bf16[64,37]{0,1:T(8,128)(2,1)}, u32[]{:S(2)}) copy-start(bf16[64,37]{0,1:T(8,128)(2,1)} %param.8) | copy-start | bytes 14212
  3.3 3.0 %collective-permute-start.2 = (f32[8,128]{1,0:T(8,128)S(1)}, f32[8,128]{1,0:T(8,128)S(1)}, u32[]{:S(2)}, u32[]{:S(2)}) collective-permute-start(f32[8,128]{1,0:T(8,128)S(1)} %get-tuple-element.36), channel_id=1, source_target_pairs={{0,24},{1,25},{2,26},{3,27},{4,28},{5,29},{6,30},{7,31},{8,16},{9,... | collective-permute-start | bytes 12296 | tf_op jit(solution)/shard_map/ppermute | solution.py:42
  4.7 3.6 %collective-permute-start.1 = (f32[8,128]{1,0:T(8,128)S(1)}, f32[8,128]{1,0:T(8,128)S(1)}, u32[]{:S(2)}, u32[]{:S(2)}) collective-permute-start(f32[8,128]{1,0:T(8,128)S(1)} %get-tuple-element.36), channel_id=1, source_target_pairs={{0,16},{1,17},{2,18},{3,19},{4,20},{5,21},{6,22},{7,23},{8,24},{9,... | collective-permute-start | bytes 12296 | tf_op jit(solution)/shard_map/ppermute | solution.py:42
  5.4 2.9 %collective-permute-start = (f32[8,128]{1,0:T(8,128)S(1)}, f32[8,128]{1,0:T(8,128)S(1)}, u32[]{:S(2)}, u32[]{:S(2)}) collective-permute-start(f32[8,128]{1,0:T(8,128)S(1)} %get-tuple-element.36), channel_id=1, source_target_pairs={{0,8},{1,9},{2,10},{3,11},{4,12},{5,13},{6,14},{7,15},{8,0},{9,1},... | collective-permute-start | bytes 12296 | tf_op jit(solution)/shard_map/ppermute | solution.py:42
  8.3 8.0 %collective-permute-start.5 = (f32[8,128]{1,0:T(8,128)S(1)}, f32[8,128]{1,0:T(8,128)S(1)}, u32[]{:S(2)}, u32[]{:S(2)}) collective-permute-start(f32[8,128]{1,0:T(8,128)S(1)} %add_add_fusion.7), channel_id=1, source_target_pairs={{0,96},{1,97},{2,98},{3,99},{4,100},{5,101},{6,102},{7,103},{8,104... | collective-permute-start | bytes 12296 | tf_op jit(solution)/shard_map/ppermute | solution.py:42
  13.8 7.5 %collective-permute-start.4 = (f32[8,128]{1,0:T(8,128)S(1)}, f32[8,128]{1,0:T(8,128)S(1)}, u32[]{:S(2)}, u32[]{:S(2)}) collective-permute-start(f32[8,128]{1,0:T(8,128)S(1)} %add_add_fusion.7), channel_id=1, source_target_pairs={{0,64},{1,65},{2,66},{3,67},{4,68},{5,69},{6,70},{7,71},{8,72},{9,... | collective-permute-start | bytes 12296 | tf_op jit(solution)/shard_map/ppermute | solution.py:42
  15.2 6.1 %collective-permute-start.3 = (f32[8,128]{1,0:T(8,128)S(1)}, f32[8,128]{1,0:T(8,128)S(1)}, u32[]{:S(2)}, u32[]{:S(2)}) collective-permute-start(f32[8,128]{1,0:T(8,128)S(1)} %add_add_fusion.7), channel_id=1, source_target_pairs={{0,32},{1,33},{2,34},{3,35},{4,36},{5,37},{6,38},{7,39},{8,40},{9,... | collective-permute-start | bytes 12296 | tf_op jit(solution)/shard_map/ppermute | solution.py:42
  21.3 11.9 %collective-permute-start.8 = (f32[8,128]{1,0:T(8,128)S(1)}, f32[8,128]{1,0:T(8,128)S(1)}, u32[]{:S(2)}, u32[]{:S(2)}) collective-permute-start(f32[8,128]{1,0:T(8,128)S(1)} %add_add_fusion.6), channel_id=1, source_target_pairs={{0,129},{1,128},{2,131},{3,130},{4,133},{5,132},{6,135},{7,134},{8... | collective-permute-start | bytes 12296 | tf_op jit(solution)/shard_map/ppermute | solution.py:42
  21.6 11.6 %collective-permute-start.7 = (f32[8,128]{1,0:T(8,128)S(1)}, f32[8,128]{1,0:T(8,128)S(1)}, u32[]{:S(2)}, u32[]{:S(2)}) collective-permute-start(f32[8,128]{1,0:T(8,128)S(1)} %add_add_fusion.6), channel_id=1, source_target_pairs={{0,1},{1,0},{2,3},{3,2},{4,5},{5,4},{6,7},{7,6},{8,9},{9,8},{10,11... | collective-permute-start | bytes 12296 | tf_op jit(solution)/shard_map/ppermute | solution.py:42
  24.2 9.0 %collective-permute-start.6 = (f32[8,128]{1,0:T(8,128)S(1)}, f32[8,128]{1,0:T(8,128)S(1)}, u32[]{:S(2)}, u32[]{:S(2)}) collective-permute-start(f32[8,128]{1,0:T(8,128)S(1)} %add_add_fusion.6), channel_id=1, source_target_pairs={{0,128},{1,129},{2,130},{3,131},{4,132},{5,133},{6,134},{7,135},{8... | collective-permute-start | bytes 12296 | tf_op jit(solution)/shard_map/ppermute | solution.py:42
  25.5 11.9 %collective-permute-start.12 = (bf16[8,64,128]{2,1,0:T(8,128)(2,1)S(1)}, bf16[8,64,128]{2,1,0:T(8,128)(2,1)S(1)}, u32[]{:S(2)}, u32[]{:S(2)}) collective-permute-start(bf16[8,64,128]{2,1,0:T(8,128)(2,1)S(1)} %get-tuple-element.40), channel_id=1, source_target_pairs={{0,8},{8,16},{16,24},{24,32},{32,40},{40,48},{48,56},{56,64},{64,7... | collective-permute-start | bytes 393224 | tf_op jit(solution)/shard_map/ppermute | solution.py:48
  27.4 10.0 %collective-permute-start.13 = (bf16[8,64,128]{2,1,0:T(8,128)(2,1)S(1)}, bf16[8,64,128]{2,1,0:T(8,128)(2,1)S(1)}, u32[]{:S(2)}, u32[]{:S(2)}) collective-permute-start(bf16[8,64,128]{2,1,0:T(8,128)(2,1)S(1)} %get-tuple-element.41), channel_id=1, source_target_pairs={{8,0},{16,8},{24,16},{32,24},{40,32},{48,40},{56,48},{64,56},{72,6... | collective-permute-start | bytes 393224 | tf_op jit(solution)/shard_map/ppermute | solution.py:48
  33.2 12.0 %collective-permute-start.11 = (f32[8,128]{1,0:T(8,128)S(1)}, f32[8,128]{1,0:T(8,128)S(1)}, u32[]{:S(2)}, u32[]{:S(2)}) collective-permute-start(f32[8,128]{1,0:T(8,128)S(1)} %add_add_fusion.5), channel_id=1, source_target_pairs={{0,6},{1,7},{2,4},{3,5},{4,2},{5,3},{6,0},{7,1},{8,14},{9,15},{10,... | collective-permute-start | bytes 12296 | tf_op jit(solution)/shard_map/ppermute | solution.py:42
  36.1 9.2 %collective-permute-start.10 = (f32[8,128]{1,0:T(8,128)S(1)}, f32[8,128]{1,0:T(8,128)S(1)}, u32[]{:S(2)}, u32[]{:S(2)}) collective-permute-start(f32[8,128]{1,0:T(8,128)S(1)} %add_add_fusion.5), channel_id=1, source_target_pairs={{0,4},{1,5},{2,6},{3,7},{4,0},{5,1},{6,2},{7,3},{8,12},{9,13},{10,... | collective-permute-start | bytes 12296 | tf_op jit(solution)/shard_map/ppermute | solution.py:42
  36.9 8.4 %collective-permute-start.9 = (f32[8,128]{1,0:T(8,128)S(1)}, f32[8,128]{1,0:T(8,128)S(1)}, u32[]{:S(2)}, u32[]{:S(2)}) collective-permute-start(f32[8,128]{1,0:T(8,128)S(1)} %add_add_fusion.5), channel_id=1, source_target_pairs={{0,2},{1,3},{2,0},{3,1},{4,6},{5,7},{6,4},{7,5},{8,10},{9,11},{10,... | collective-permute-start | bytes 12296 | tf_op jit(solution)/shard_map/ppermute | solution.py:42
  37.9 7.5 %collective-permute-start.14 = (bf16[3,64,128]{2,1,0:T(8,128)(2,1)S(1)}, bf16[3,64,128]{2,1,0:T(8,128)(2,1)S(1)}, u32[]{:S(2)}, u32[]{:S(2)}) collective-permute-start(bf16[3,64,128]{2,1,0:T(8,128)(2,1)S(1)} %get-tuple-element.42), channel_id=1, source_target_pairs={{0,1},{1,2},{2,3},{3,4},{4,5},{5,6},{6,7},{8,9},{9,10},{10,11},{11... | collective-permute-start | bytes 147464 | tf_op jit(solution)/shard_map/ppermute | solution.py:48
  41.9 8.4 %collective-permute-start.15 = (bf16[3,64,128]{2,1,0:T(8,128)(2,1)S(1)}, bf16[3,64,128]{2,1,0:T(8,128)(2,1)S(1)}, u32[]{:S(2)}, u32[]{:S(2)}) collective-permute-start(bf16[3,64,128]{2,1,0:T(8,128)(2,1)S(1)} %get-tuple-element.43), channel_id=1, source_target_pairs={{1,0},{2,1},{3,2},{4,3},{5,4},{6,5},{7,6},{9,8},{10,9},{11,10},{12... | collective-permute-start | bytes 147464 | tf_op jit(solution)/shard_map/ppermute | solution.py:48
  50.3 1.0 copy-start.1
  51.4 0.9 copy-start.3
  61.8 6.4 %collective-permute-start.16 = (bf16[528,128]{1,0:T(8,128)(2,1)S(1)}, bf16[528,128]{1,0:T(8,128)(2,1)S(1)}, u32[]{:S(2)}, u32[]{:S(2)}) collective-permute-start(bf16[528,128]{1,0:T(8,128)(2,1)S(1)} %get-tuple-element.44), channel_id=1, source_target_pairs={{0,2},{1,3},{2,0},{3,1},{4,6},{5,7},{6,4},{7,5},{8,10},{9,11},{10,... | collective-permute-start | bytes 405512 | tf_op jit(solution)/shard_map/ppermute | solution.py:42
  63.3 7.0 %collective-permute-start.18 = (bf16[528,128]{1,0:T(8,128)(2,1)S(1)}, bf16[528,128]{1,0:T(8,128)(2,1)S(1)}, u32[]{:S(2)}, u32[]{:S(2)}) collective-permute-start(bf16[528,128]{1,0:T(8,128)(2,1)S(1)} %get-tuple-element.45), channel_id=1, source_target_pairs={{0,6},{1,7},{2,4},{3,5},{4,2},{5,3},{6,0},{7,1},{8,14},{9,15},{10,... | collective-permute-start | bytes 405512 | tf_op jit(solution)/shard_map/ppermute | solution.py:42
  65.1 15.9 %collective-permute-start.20 = (bf16[528,128]{1,0:T(8,128)(2,1)S(1)}, bf16[528,128]{1,0:T(8,128)(2,1)S(1)}, u32[]{:S(2)}, u32[]{:S(2)}) collective-permute-start(bf16[528,128]{1,0:T(8,128)(2,1)S(1)} %get-tuple-element.46), channel_id=1, source_target_pairs={{0,16},{1,48},{2,80},{3,112},{4,144},{5,176},{6,208},{7,240},{8,24... | collective-permute-start | bytes 405512 | tf_op jit(solution)/shard_map/ppermute | solution.py:42
  65.4 15.6 %collective-permute-start.21 = (bf16[528,128]{1,0:T(8,128)(2,1)S(1)}, bf16[528,128]{1,0:T(8,128)(2,1)S(1)}, u32[]{:S(2)}, u32[]{:S(2)}) collective-permute-start(bf16[528,128]{1,0:T(8,128)(2,1)S(1)} %get-tuple-element.47), channel_id=1, source_target_pairs={{0,24},{1,56},{2,88},{3,120},{4,152},{5,184},{6,216},{7,248},{8,16... | collective-permute-start | bytes 405512 | tf_op jit(solution)/shard_map/ppermute | solution.py:42
  68.2 19.5 %collective-permute-start.17 = (bf16[528,128]{1,0:T(8,128)(2,1)S(1)}, bf16[528,128]{1,0:T(8,128)(2,1)S(1)}, u32[]{:S(2)}, u32[]{:S(2)}) collective-permute-start(bf16[528,128]{1,0:T(8,128)(2,1)S(1)} %collective-permute-done.16), channel_id=1, source_target_pairs={{0,64},{1,96},{2,0},{3,32},{4,192},{5,224},{6,128},{7,160},{8,72},... | collective-permute-start | bytes 405512 | tf_op jit(solution)/shard_map/ppermute | solution.py:42
  70.2 20.3 %collective-permute-start.19 = (bf16[528,128]{1,0:T(8,128)(2,1)S(1)}, bf16[528,128]{1,0:T(8,128)(2,1)S(1)}, u32[]{:S(2)}, u32[]{:S(2)}) collective-permute-start(bf16[528,128]{1,0:T(8,128)(2,1)S(1)} %collective-permute-done.18), channel_id=1, source_target_pairs={{0,200},{1,232},{2,136},{3,168},{4,72},{5,104},{6,8},{7,40},{8,192... | collective-permute-start | bytes 405512 | tf_op jit(solution)/shard_map/ppermute | solution.py:42
  97.5 53.0 %copy-start.2 = (bf16[32,128,64]{1,2,0:T(8,128)(2,1)S(1)}, bf16[32,128,64]{1,2,0:T(8,128)(2,1)}, u32[]{:S(2)}) copy-start(bf16[32,128,64]{1,2,0:T(8,128)(2,1)} %param.6) | copy-start | bytes 1572868
  101.9 2.0 %collective-permute-start.22 = (f32[88,128]{1,0:T(8,128)S(1)}, f32[88,128]{1,0:T(8,128)S(1)}, u32[]{:S(2)}, u32[]{:S(2)}) collective-permute-start(f32[88,128]{1,0:T(8,128)S(1)} %get-tuple-element.55), channel_id=1, source_target_pairs={{0,8},{1,9},{2,10},{3,11},{4,12},{5,13},{6,14},{7,15},{8,0},{9,1},... | collective-permute-start | bytes 135176 | tf_op jit(solution)/shard_map/ppermute | solution.py:42
  102.4 4.1 %collective-permute-start.23 = (f32[88,128]{1,0:T(8,128)S(1)}, f32[88,128]{1,0:T(8,128)S(1)}, u32[]{:S(2)}, u32[]{:S(2)}) collective-permute-start(f32[88,128]{1,0:T(8,128)S(1)} %get-tuple-element.56), channel_id=1, source_target_pairs={{0,16},{1,17},{2,18},{3,19},{4,20},{5,21},{6,22},{7,23},{8,24},{9,... | collective-permute-start | bytes 135176 | tf_op jit(solution)/shard_map/ppermute | solution.py:42
  102.4 4.1 %collective-permute-start.24 = (f32[88,128]{1,0:T(8,128)S(1)}, f32[88,128]{1,0:T(8,128)S(1)}, u32[]{:S(2)}, u32[]{:S(2)}) collective-permute-start(f32[88,128]{1,0:T(8,128)S(1)} %get-tuple-element.57), channel_id=1, source_target_pairs={{0,24},{1,25},{2,26},{3,27},{4,28},{5,29},{6,30},{7,31},{8,16},{9,... | collective-permute-start | bytes 135176 | tf_op jit(solution)/shard_map/ppermute | solution.py:42
  106.6 7.2 %collective-permute-start.27 = (f32[88,128]{1,0:T(8,128)S(1)}, f32[88,128]{1,0:T(8,128)S(1)}, u32[]{:S(2)}, u32[]{:S(2)}) collective-permute-start(f32[88,128]{1,0:T(8,128)S(1)} %add_add_fusion.3), channel_id=1, source_target_pairs={{0,96},{1,97},{2,98},{3,99},{4,100},{5,101},{6,102},{7,103},{8,104... | collective-permute-start | bytes 135176 | tf_op jit(solution)/shard_map/ppermute | solution.py:42
  111.0 8.5 %collective-permute-start.26 = (f32[88,128]{1,0:T(8,128)S(1)}, f32[88,128]{1,0:T(8,128)S(1)}, u32[]{:S(2)}, u32[]{:S(2)}) collective-permute-start(f32[88,128]{1,0:T(8,128)S(1)} %add_add_fusion.3), channel_id=1, source_target_pairs={{0,64},{1,65},{2,66},{3,67},{4,68},{5,69},{6,70},{7,71},{8,72},{9,... | collective-permute-start | bytes 135176 | tf_op jit(solution)/shard_map/ppermute | solution.py:42
  113.8 6.1 %collective-permute-start.25 = (f32[88,128]{1,0:T(8,128)S(1)}, f32[88,128]{1,0:T(8,128)S(1)}, u32[]{:S(2)}, u32[]{:S(2)}) collective-permute-start(f32[88,128]{1,0:T(8,128)S(1)} %add_add_fusion.3), channel_id=1, source_target_pairs={{0,32},{1,33},{2,34},{3,35},{4,36},{5,37},{6,38},{7,39},{8,40},{9,... | collective-permute-start | bytes 135176 | tf_op jit(solution)/shard_map/ppermute | solution.py:42
  119.9 13.4 %collective-permute-start.30 = (f32[88,128]{1,0:T(8,128)S(1)}, f32[88,128]{1,0:T(8,128)S(1)}, u32[]{:S(2)}, u32[]{:S(2)}) collective-permute-start(f32[88,128]{1,0:T(8,128)S(1)} %add_add_fusion.2), channel_id=1, source_target_pairs={{0,129},{1,128},{2,131},{3,130},{4,133},{5,132},{6,135},{7,134},{8... | collective-permute-start | bytes 135176 | tf_op jit(solution)/shard_map/ppermute | solution.py:42
  124.6 8.6 %collective-permute-start.29 = (f32[88,128]{1,0:T(8,128)S(1)}, f32[88,128]{1,0:T(8,128)S(1)}, u32[]{:S(2)}, u32[]{:S(2)}) collective-permute-start(f32[88,128]{1,0:T(8,128)S(1)} %add_add_fusion.2), channel_id=1, source_target_pairs={{0,1},{1,0},{2,3},{3,2},{4,5},{5,4},{6,7},{7,6},{8,9},{9,8},{10,11... | collective-permute-start | bytes 135176 | tf_op jit(solution)/shard_map/ppermute | solution.py:42
  124.6 8.7 %collective-permute-start.28 = (f32[88,128]{1,0:T(8,128)S(1)}, f32[88,128]{1,0:T(8,128)S(1)}, u32[]{:S(2)}, u32[]{:S(2)}) collective-permute-start(f32[88,128]{1,0:T(8,128)S(1)} %add_add_fusion.2), channel_id=1, source_target_pairs={{0,128},{1,129},{2,130},{3,131},{4,132},{5,133},{6,134},{7,135},{8... | collective-permute-start | bytes 135176 | tf_op jit(solution)/shard_map/ppermute | solution.py:42
  125.6 11.9 %collective-permute-start.37 = (bf16[8,64,128]{2,1,0:T(8,128)(2,1)S(1)}, bf16[8,64,128]{2,1,0:T(8,128)(2,1)S(1)}, u32[]{:S(2)}, u32[]{:S(2)}) collective-permute-start(bf16[8,64,128]{2,1,0:T(8,128)(2,1)S(1)} %get-tuple-element.60), channel_id=1, source_target_pairs={{0,8},{8,16},{16,24},{24,32},{32,40},{40,48},{48,56},{56,64},{64,7... | collective-permute-start | bytes 393224 | tf_op jit(solution)/shard_map/ppermute | solution.py:48
  127.5 10.0 %collective-permute-start.38 = (bf16[8,64,128]{2,1,0:T(8,128)(2,1)S(1)}, bf16[8,64,128]{2,1,0:T(8,128)(2,1)S(1)}, u32[]{:S(2)}, u32[]{:S(2)}) collective-permute-start(bf16[8,64,128]{2,1,0:T(8,128)(2,1)S(1)} %get-tuple-element.61), channel_id=1, source_target_pairs={{8,0},{16,8},{24,16},{32,24},{40,32},{48,40},{56,48},{64,56},{72,6... | collective-permute-start | bytes 393224 | tf_op jit(solution)/shard_map/ppermute | solution.py:48
  133.3 12.0 %collective-permute-start.33 = (f32[88,128]{1,0:T(8,128)S(1)}, f32[88,128]{1,0:T(8,128)S(1)}, u32[]{:S(2)}, u32[]{:S(2)}) collective-permute-start(f32[88,128]{1,0:T(8,128)S(1)} %add_add_fusion.1), channel_id=1, source_target_pairs={{0,6},{1,7},{2,4},{3,5},{4,2},{5,3},{6,0},{7,1},{8,14},{9,15},{10,... | collective-permute-start | bytes 135176 | tf_op jit(solution)/shard_map/ppermute | solution.py:42
  135.2 10.1 %collective-permute-start.32 = (f32[88,128]{1,0:T(8,128)S(1)}, f32[88,128]{1,0:T(8,128)S(1)}, u32[]{:S(2)}, u32[]{:S(2)}) collective-permute-start(f32[88,128]{1,0:T(8,128)S(1)} %add_add_fusion.1), channel_id=1, source_target_pairs={{0,4},{1,5},{2,6},{3,7},{4,0},{5,1},{6,2},{7,3},{8,12},{9,13},{10,... | collective-permute-start | bytes 135176 | tf_op jit(solution)/shard_map/ppermute | solution.py:42
  136.8 8.6 %collective-permute-start.31 = (f32[88,128]{1,0:T(8,128)S(1)}, f32[88,128]{1,0:T(8,128)S(1)}, u32[]{:S(2)}, u32[]{:S(2)}) collective-permute-start(f32[88,128]{1,0:T(8,128)S(1)} %add_add_fusion.1), channel_id=1, source_target_pairs={{0,2},{1,3},{2,0},{3,1},{4,6},{5,7},{6,4},{7,5},{8,10},{9,11},{10,... | collective-permute-start | bytes 135176 | tf_op jit(solution)/shard_map/ppermute | solution.py:42
  138.0 9.4 %collective-permute-start.39 = (bf16[3,64,128]{2,1,0:T(8,128)(2,1)S(1)}, bf16[3,64,128]{2,1,0:T(8,128)(2,1)S(1)}, u32[]{:S(2)}, u32[]{:S(2)}) collective-permute-start(bf16[3,64,128]{2,1,0:T(8,128)(2,1)S(1)} %get-tuple-element.62), channel_id=1, source_target_pairs={{0,1},{1,2},{2,3},{3,4},{4,5},{5,6},{6,7},{8,9},{9,10},{10,11},{11... | collective-permute-start | bytes 147464 | tf_op jit(solution)/shard_map/ppermute | solution.py:48
  142.2 8.4 %collective-permute-start.40 = (bf16[3,64,128]{2,1,0:T(8,128)(2,1)S(1)}, bf16[3,64,128]{2,1,0:T(8,128)(2,1)S(1)}, u32[]{:S(2)}, u32[]{:S(2)}) collective-permute-start(bf16[3,64,128]{2,1,0:T(8,128)(2,1)S(1)} %get-tuple-element.63), channel_id=1, source_target_pairs={{1,0},{2,1},{3,2},{4,3},{5,4},{6,5},{7,6},{9,8},{10,9},{11,10},{12... | collective-permute-start | bytes 147464 | tf_op jit(solution)/shard_map/ppermute | solution.py:48
  145.4 10.0 %collective-permute-start.36 = (f32[88,128]{1,0:T(8,128)S(1)}, f32[88,128]{1,0:T(8,128)S(1)}, u32[]{:S(2)}, u32[]{:S(2)}) collective-permute-start(f32[88,128]{1,0:T(8,128)S(1)} %add_add_fusion.got0), channel_id=1, source_target_pairs={{0,24},{1,25},{2,26},{3,27},{4,28},{5,29},{6,30},{7,31},{8,16},{9,... | collective-permute-start | bytes 135176 | tf_op jit(solution)/shard_map/ppermute | solution.py:42
  145.5 9.9 %collective-permute-start.35 = (f32[88,128]{1,0:T(8,128)S(1)}, f32[88,128]{1,0:T(8,128)S(1)}, u32[]{:S(2)}, u32[]{:S(2)}) collective-permute-start(f32[88,128]{1,0:T(8,128)S(1)} %add_add_fusion.got0), channel_id=1, source_target_pairs={{0,16},{1,17},{2,18},{3,19},{4,20},{5,21},{6,22},{7,23},{8,24},{9,... | collective-permute-start | bytes 135176 | tf_op jit(solution)/shard_map/ppermute | solution.py:42
  145.6 9.8 %collective-permute-start.34 = (f32[88,128]{1,0:T(8,128)S(1)}, f32[88,128]{1,0:T(8,128)S(1)}, u32[]{:S(2)}, u32[]{:S(2)}) collective-permute-start(f32[88,128]{1,0:T(8,128)S(1)} %add_add_fusion.got0), channel_id=1, source_target_pairs={{0,8},{1,9},{2,10},{3,11},{4,12},{5,13},{6,14},{7,15},{8,0},{9,1},... | collective-permute-start | bytes 135176 | tf_op jit(solution)/shard_map/ppermute | solution.py:42
  (2 other events, 1.4 us)

commit v5 on v4

--- a/solution.py
+++ b/solution.py
@@ -9,6 +9,7 @@
 GRID = ("row", "col")
 F32, BF16 = jnp.float32, jnp.bfloat16
 LANES = 128
+UNROLL = 8
 FAR_BELOW = -1e30
 VMEM = pl.BlockSpec(memory_space=pltpu.VMEM)
 SMEM = pl.BlockSpec(memory_space=pltpu.SMEM)
@@ -48,20 +49,22 @@
     return lax.ppermute(block, axis, pairs if forward else [(b, a) for a, b in pairs])
 
 
-def activate_kernel(feat, valid, act, top, bottom, counted):
+def activate_kernel(feat, valid, act, top, bottom, counted, kept_feat, kept_valid):
     rows = feat.shape[0]
 
     def step(i, carry):
+        kept_feat[i] = feat[i]
         v = feat[i].astype(F32)
         near = v * (1.0 + v * (0.5 + v * (1.0 / 6.0 + v * (1.0 / 24.0))))
         low = jnp.where(v > -0.03, near, jnp.exp(jnp.minimum(v, 0.0)) - 1.0)
         act[i] = jnp.where(v > 0, v, low).astype(BF16)
         return carry
 
-    lax.fori_loop(0, rows, step, 0)
+    lax.fori_loop(0, rows, step, 0, unroll=4)
     top[...] = act[:STEP]
     bottom[...] = act[rows - STEP :]
     lines = jnp.sum(valid[...].astype(F32), axis=0, keepdims=True)
+    kept_valid[...] = valid[...]
     counted[...] = jnp.broadcast_to(jnp.sum(lines, axis=1, keepdims=True), counted.shape)
 
 
@@ -142,7 +145,7 @@
             turned[pl.ds(pl.multiple_of((i + d) * LANES, LANES), LANES), :] = low.astype(F32).T
         return carry
 
-    lax.fori_loop(0, rows // 2, step, 0)
+    lax.fori_loop(0, rows // 2, step, 0, unroll=UNROLL)
     turned[rows * LANES :, :] = jnp.concatenate(
         [labels[...].astype(F32).T, valid[...].astype(F32).T], axis=1
     )
@@ -158,7 +161,7 @@
             ).astype(BF16)
         return carry
 
-    lax.fori_loop(0, rows + 1, pack, 0)
+    lax.fori_loop(0, rows + 1, pack, 0, unroll=3)
 
 
 def softmax_kernel(
@@ -238,7 +241,7 @@
         )
         return carry
 
-    lax.fori_loop(0, half, step, 0)
+    lax.fori_loop(0, half, step, 0, unroll=UNROLL)
 
 
 def scale_of(count):
@@ -268,7 +271,7 @@
         )
         return carry
 
-    lax.fori_loop(0, rows // 2, step, 0)
+    lax.fori_loop(0, rows // 2, step, 0, unroll=UNROLL)
     top[...] = low[:STEP]
     bottom[...] = low[rows - STEP :]
     half = total.shape[0] // 2
@@ -305,7 +308,7 @@
             ).astype(BF16)
         return carry
 
-    lax.fori_loop(0, rows // 2, step, 0)
+    lax.fori_loop(0, rows // 2, step, 0, unroll=UNROLL)
 
 
 def finish_kernel(
@@ -383,9 +386,10 @@
     tall = -(-bins // 8) * 8
     tile = (rows, chans, LANES)
     edge = (STEP, chans, LANES)
-    act, top, bottom, counted = run(
+    act, top, bottom, counted, feat, valid = run(
         activate_kernel,
-        [shape(tile, BF16), shape(edge, BF16), shape(edge, BF16), shape((8, LANES), F32)],
+        [shape(tile, BF16), shape(edge, BF16), shape(edge, BF16), shape((8, LANES), F32)]
+        + [shape(tile, BF16), shape(valid.shape, jnp.int32)],
         (feat, valid),
         micros=1,
     )

time: 157 us -> 143 us (0.911)
  Pallas kernels: 26.8 us -> 15.3 us
  local copies, waits for them, and re-layouts: 5.16 us -> 3.4 us
    pallas_call x8, Pallas kernels: 26.8 us -> 15.3 us  [run(): pl.pallas_call(body, out_shape=outs, in_specs=[SMEM] * scalars + [VMEM] *...]
    unnamed x18 -> x14, local copies, waits for them, and re-layouts: 5.16 us -> 3.4 us
  transfers between devices with their start and end apart: 41 -> 41, of which waited for: 12 -> 12; matrix products, arithmetic and copies ran while one was open for 0% -> 0% of each run, Pallas kernels for 4% -> 3%
where the time goes in v5:
time: 143 us
  starting transfers between devices  85.1 us (60%)
  waiting for transfers between devices  38.2 us (27%)
  Pallas kernels  15.3 us (11%)
  local copies, waits for them, and re-layouts  3.4 us (2%)
    ppermute x33, starting transfers between devices, send(): return lax.ppermute(block, GRID, pairs)  55.1 us
    ppermute x8, starting transfers between devices, shifted(): lax.ppermute(block, axis, pairs if forward else [(b, a) for a, b in pairs])  30 us
    ppermute x33, waiting for transfers between devices, send(): return lax.ppermute(block, GRID, pairs)  29.9 us
    pallas_call x8, Pallas kernels, run(): pl.pallas_call(body, out_shape=outs, in_specs=[SMEM] * scalars + [VMEM] *...  15.3 us
    ppermute x8, waiting for transfers between devices, shifted(): lax.ppermute(block, axis, pairs if forward else [(b, a) for a, b in pairs])  8.26 us
    unnamed x14, local copies, waits for them, and re-layouts  3.4 us
  transfers between devices with their start and end apart: 41, of which 12 were waited for; matrix products, arithmetic and copies ran while one was open for 0% of the time, Pallas kernels for 3%

profile of v5, /device:TPU:24, one launch (start us, length us, event | category | flops | bytes accessed | tf_op | source)
XLA Modules:
  0.0 142.9 jit_solution(13354970635039184384)
XLA Ops:
  0.7 1.0 copy-done.1
  2.4 0.7 shard_map.101
  3.1 1.4 collective-permute-start.2
  5.2 1.0 collective-permute-done.2
  6.2 1.9 %collective-permute-done.1 = f32[8,128]{1,0:T(8,128)S(1)} collective-permute-done((f32[8,128]{1,0:T(8,128)S(1)}, f32[8,128]{1,0:T(8,128)S(1)}, u32[]{:S(2)}, u32[]{:S(2)}) %collective-permute-start.1) | collective-permute-done | bytes 4128 | tf_op jit(solution)/shard_map/ppermute | solution.py:43
  8.1 5.5 %collective-permute-start.5 = (f32[8,128]{1,0:T(8,128)S(1)}, f32[8,128]{1,0:T(8,128)S(1)}, u32[]{:S(2)}, u32[]{:S(2)}) collective-permute-start(f32[8,128]{1,0:T(8,128)S(1)} %add_add_fusion.7), channel_id=1, source_target_pairs={{0,96},{1,97},{2,98},{3,99},{4,100},{5,101},{6,102},{7,103},{8,104... | collective-permute-start | bytes 12296 | tf_op jit(solution)/shard_map/ppermute | solution.py:43
  13.6 1.4 %collective-permute-start.4 = (f32[8,128]{1,0:T(8,128)S(1)}, f32[8,128]{1,0:T(8,128)S(1)}, u32[]{:S(2)}, u32[]{:S(2)}) collective-permute-start(f32[8,128]{1,0:T(8,128)S(1)} %add_add_fusion.7), channel_id=1, source_target_pairs={{0,64},{1,65},{2,66},{3,67},{4,68},{5,69},{6,70},{7,71},{8,72},{9,... | collective-permute-start | bytes 12296 | tf_op jit(solution)/shard_map/ppermute | solution.py:43
  15.1 1.0 collective-permute-start.3
  16.1 5.0 %collective-permute-done.4 = f32[8,128]{1,0:T(8,128)S(1)} collective-permute-done((f32[8,128]{1,0:T(8,128)S(1)}, f32[8,128]{1,0:T(8,128)S(1)}, u32[]{:S(2)}, u32[]{:S(2)}) %collective-permute-start.4) | collective-permute-done | bytes 4128 | tf_op jit(solution)/shard_map/ppermute | solution.py:43
  21.4 2.6 %collective-permute-start.7 = (f32[8,128]{1,0:T(8,128)S(1)}, f32[8,128]{1,0:T(8,128)S(1)}, u32[]{:S(2)}, u32[]{:S(2)}) collective-permute-start(f32[8,128]{1,0:T(8,128)S(1)} %add_add_fusion.6), channel_id=1, source_target_pairs={{0,1},{1,0},{2,3},{3,2},{4,5},{5,4},{6,7},{7,6},{8,9},{9,8},{10,11... | collective-permute-start | bytes 12296 | tf_op jit(solution)/shard_map/ppermute | solution.py:43
  24.0 1.3 collective-permute-start.6
  25.3 1.9 %collective-permute-start.12 = (bf16[8,64,128]{2,1,0:T(8,128)(2,1)S(1)}, bf16[8,64,128]{2,1,0:T(8,128)(2,1)S(1)}, u32[]{:S(2)}, u32[]{:S(2)}) collective-permute-start(bf16[8,64,128]{2,1,0:T(8,128)(2,1)S(1)} %get-tuple-element.42), channel_id=1, source_target_pairs={{0,8},{8,16},{16,24},{24,32},{32,40},{40,48},{48,56},{56,64},{64,7... | collective-permute-start | bytes 393224 | tf_op jit(solution)/shard_map/ppermute | solution.py:49
  27.2 5.8 %collective-permute-start.13 = (bf16[8,64,128]{2,1,0:T(8,128)(2,1)S(1)}, bf16[8,64,128]{2,1,0:T(8,128)(2,1)S(1)}, u32[]{:S(2)}, u32[]{:S(2)}) collective-permute-start(bf16[8,64,128]{2,1,0:T(8,128)(2,1)S(1)} %get-tuple-element.43), channel_id=1, source_target_pairs={{8,0},{16,8},{24,16},{32,24},{40,32},{48,40},{56,48},{64,56},{72,6... | collective-permute-start | bytes 393224 | tf_op jit(solution)/shard_map/ppermute | solution.py:49
  33.0 2.8 %collective-permute-start.11 = (f32[8,128]{1,0:T(8,128)S(1)}, f32[8,128]{1,0:T(8,128)S(1)}, u32[]{:S(2)}, u32[]{:S(2)}) collective-permute-start(f32[8,128]{1,0:T(8,128)S(1)} %add_add_fusion.5), channel_id=1, source_target_pairs={{0,6},{1,7},{2,4},{3,5},{4,2},{5,3},{6,0},{7,1},{8,14},{9,15},{10,... | collective-permute-start | bytes 12296 | tf_op jit(solution)/shard_map/ppermute | solution.py:43
  35.9 0.8 collective-permute-start.10
  37.7 4.1 %collective-permute-start.14 = (bf16[3,64,128]{2,1,0:T(8,128)(2,1)S(1)}, bf16[3,64,128]{2,1,0:T(8,128)(2,1)S(1)}, u32[]{:S(2)}, u32[]{:S(2)}) collective-permute-start(bf16[3,64,128]{2,1,0:T(8,128)(2,1)S(1)} %get-tuple-element.44), channel_id=1, source_target_pairs={{0,1},{1,2},{2,3},{3,4},{4,5},{5,6},{6,7},{8,9},{9,10},{10,11},{11... | collective-permute-start | bytes 147464 | tf_op jit(solution)/shard_map/ppermute | solution.py:49
  41.8 3.3 %collective-permute-start.15 = (bf16[3,64,128]{2,1,0:T(8,128)(2,1)S(1)}, bf16[3,64,128]{2,1,0:T(8,128)(2,1)S(1)}, u32[]{:S(2)}, u32[]{:S(2)}) collective-permute-start(bf16[3,64,128]{2,1,0:T(8,128)(2,1)S(1)} %get-tuple-element.45), channel_id=1, source_target_pairs={{1,0},{2,1},{3,2},{4,3},{5,4},{6,5},{7,6},{9,8},{10,9},{11,10},{12... | collective-permute-start | bytes 147464 | tf_op jit(solution)/shard_map/ppermute | solution.py:49
  45.2 5.0 %collective-permute-done.15.right = bf16[3,64,128]{2,1,0:T(8,128)(2,1)S(1)} collective-permute-done((bf16[3,64,128]{2,1,0:T(8,128)(2,1)S(1)}, bf16[3,64,128]{2,1,0:T(8,128)(2,1)S(1)}, u32[]{:S(2)}, u32[]{:S(2)}) %collective-permute-start.15) | collective-permute-done | bytes 49184 | tf_op jit(solution)/shard_map/ppermute | solution.py:49
  50.2 0.9 copy-done
  51.8 3.3 %shard_map.103 = (bf16[48,192,128]{2,1,0:T(8,128)(2,1)S(1)}, bf16[32,64,128]{2,1,0:T(8,128)(2,1)S(1)}, bf16[528,128]{1,0:T(8,128)(2,1)S(1)}, bf16[528,128]{1,0:T...) custom-call(s32[1]{0:T(128)} %bitcast.place, ...), custom_call_target="tpu_custom_call" | custom-call | bytes 18000000 | tf_op jit(solution)/shard_map/pallas_call | solution.py:19
  55.1 1.6 %collective-permute-start.16 = (bf16[528,128]{1,0:T(8,128)(2,1)S(1)}, bf16[528,128]{1,0:T(8,128)(2,1)S(1)}, u32[]{:S(2)}, u32[]{:S(2)}) collective-permute-start(bf16[528,128]{1,0:T(8,128)(2,1)S(1)} %get-tuple-element.48), channel_id=1, source_target_pairs={{0,2},{1,3},{2,0},{3,1},{4,6},{5,7},{6,4},{7,5},{8,10},{9,11},{10,... | collective-permute-start | bytes 405512 | tf_op jit(solution)/shard_map/ppermute | solution.py:43
  56.7 1.8 %collective-permute-start.18 = (bf16[528,128]{1,0:T(8,128)(2,1)S(1)}, bf16[528,128]{1,0:T(8,128)(2,1)S(1)}, u32[]{:S(2)}, u32[]{:S(2)}) collective-permute-start(bf16[528,128]{1,0:T(8,128)(2,1)S(1)} %get-tuple-element.49), channel_id=1, source_target_pairs={{0,6},{1,7},{2,4},{3,5},{4,2},{5,3},{6,0},{7,1},{8,14},{9,15},{10,... | collective-permute-start | bytes 405512 | tf_op jit(solution)/shard_map/ppermute | solution.py:43
  58.8 2.8 %collective-permute-start.21 = (bf16[528,128]{1,0:T(8,128)(2,1)S(1)}, bf16[528,128]{1,0:T(8,128)(2,1)S(1)}, u32[]{:S(2)}, u32[]{:S(2)}) collective-permute-start(bf16[528,128]{1,0:T(8,128)(2,1)S(1)} %get-tuple-element.51), channel_id=1, source_target_pairs={{0,24},{1,56},{2,88},{3,120},{4,152},{5,184},{6,216},{7,248},{8,16... | collective-permute-start | bytes 405512 | tf_op jit(solution)/shard_map/ppermute | solution.py:43
  61.6 2.1 %collective-permute-start.17 = (bf16[528,128]{1,0:T(8,128)(2,1)S(1)}, bf16[528,128]{1,0:T(8,128)(2,1)S(1)}, u32[]{:S(2)}, u32[]{:S(2)}) collective-permute-start(bf16[528,128]{1,0:T(8,128)(2,1)S(1)} %collective-permute-done.16), channel_id=1, source_target_pairs={{0,64},{1,96},{2,0},{3,32},{4,192},{5,224},{6,128},{7,160},{8,72},... | collective-permute-start | bytes 405512 | tf_op jit(solution)/shard_map/ppermute | solution.py:43
  63.6 7.2 %collective-permute-start.19 = (bf16[528,128]{1,0:T(8,128)(2,1)S(1)}, bf16[528,128]{1,0:T(8,128)(2,1)S(1)}, u32[]{:S(2)}, u32[]{:S(2)}) collective-permute-start(bf16[528,128]{1,0:T(8,128)(2,1)S(1)} %collective-permute-done.18), channel_id=1, source_target_pairs={{0,200},{1,232},{2,136},{3,168},{4,72},{5,104},{6,8},{7,40},{8,192... | collective-permute-start | bytes 405512 | tf_op jit(solution)/shard_map/ppermute | solution.py:43
  70.8 3.5 %collective-permute-done.20.got2 = bf16[528,128]{1,0:T(8,128)(2,1)S(1)} collective-permute-done((bf16[528,128]{1,0:T(8,128)(2,1)S(1)}, bf16[528,128]{1,0:T(8,128)(2,1)S(1)}, u32[]{:S(2)}, u32[]{:S(2)}) %collective-permute-start.20) | collective-permute-done | bytes 135200 | tf_op jit(solution)/shard_map/ppermute | solution.py:43
  74.4 6.7 %collective-permute-done.17.got0 = bf16[528,128]{1,0:T(8,128)(2,1)S(1)} collective-permute-done((bf16[528,128]{1,0:T(8,128)(2,1)S(1)}, bf16[528,128]{1,0:T(8,128)(2,1)S(1)}, u32[]{:S(2)}, u32[]{:S(2)}) %collective-permute-start.17) | collective-permute-done | bytes 135200 | tf_op jit(solution)/shard_map/ppermute | solution.py:43
  81.1 2.9 %collective-permute-done.19.got1 = bf16[528,128]{1,0:T(8,128)(2,1)S(1)} collective-permute-done((bf16[528,128]{1,0:T(8,128)(2,1)S(1)}, bf16[528,128]{1,0:T(8,128)(2,1)S(1)}, u32[]{:S(2)}, u32[]{:S(2)}) %collective-permute-start.19) | collective-permute-done | bytes 135200 | tf_op jit(solution)/shard_map/ppermute | solution.py:43
  84.0 4.3 %shard_map.104 = (f32[32,64,128]{2,1,0:T(8,128)S(1)}, f32[120,64]{1,0:T(8,128)S(1)}, f32[40,128]{1,0:T(8,128)S(1)}, f32[1,128]{1,0:T(1,128)S(1)}) custom-call(s32[1]{0:T(128)} %bitcast.place, bf16[528,128]{1,0:T(8,128)(2,1)S(1)} %collective-permute-done.17.got0, bf16[528,128]{1,0:T(8,128)(2,1)S(1)} %collective-permute-done.19.got1, ...), custom_call_target="tpu_custom_call" | custom-call | bytes 18000000 | tf_op jit(solution)/shard_map/pallas_call | solution.py:19
  88.3 2.3 %shard_map.105 = (bf16[32,64,128]{2,1,0:T(8,128)(2,1)S(1)}, bf16[8,64,128]{2,1,0:T(8,128)(2,1)S(1)}, bf16[8,64,128]{2,1,0:T(8,128)(2,1)S(1)}, f32[88,128]{1,0:T(...) custom-call(s32[1]{0:T(128)} %bitcast.place, f32[8,128]{1,0:T(8,128)S(1)} %add_add_fusion.4.count, ...), custom_call_target="tpu_custom_call" | custom-call | bytes 10800000 | tf_op jit(solution)/shard_map/pallas_call | solution.py:19
  91.1 1.5 %collective-permute-start.24 = (f32[88,128]{1,0:T(8,128)S(1)}, f32[88,128]{1,0:T(8,128)S(1)}, u32[]{:S(2)}, u32[]{:S(2)}) collective-permute-start(f32[88,128]{1,0:T(8,128)S(1)} %get-tuple-element.61), channel_id=1, source_target_pairs={{0,24},{1,25},{2,26},{3,27},{4,28},{5,29},{6,30},{7,31},{8,16},{9,... | collective-permute-start | bytes 135176 | tf_op jit(solution)/shard_map/ppermute | solution.py:43
  92.6 2.7 %collective-permute-done.23 = f32[88,128]{1,0:T(8,128)S(1)} collective-permute-done((f32[88,128]{1,0:T(8,128)S(1)}, f32[88,128]{1,0:T(8,128)S(1)}, u32[]{:S(2)}, u32[]{:S(2)}) %collective-permute-start.23) | collective-permute-done | bytes 45088 | tf_op jit(solution)/shard_map/ppermute | solution.py:43
  95.3 4.4 %collective-permute-start.27 = (f32[88,128]{1,0:T(8,128)S(1)}, f32[88,128]{1,0:T(8,128)S(1)}, u32[]{:S(2)}, u32[]{:S(2)}) collective-permute-start(f32[88,128]{1,0:T(8,128)S(1)} %add_add_fusion.3), channel_id=1, source_target_pairs={{0,96},{1,97},{2,98},{3,99},{4,100},{5,101},{6,102},{7,103},{8,104... | collective-permute-start | bytes 135176 | tf_op jit(solution)/shard_map/ppermute | solution.py:43
  99.6 2.9 %collective-permute-start.26 = (f32[88,128]{1,0:T(8,128)S(1)}, f32[88,128]{1,0:T(8,128)S(1)}, u32[]{:S(2)}, u32[]{:S(2)}) collective-permute-start(f32[88,128]{1,0:T(8,128)S(1)} %add_add_fusion.3), channel_id=1, source_target_pairs={{0,64},{1,65},{2,66},{3,67},{4,68},{5,69},{6,70},{7,71},{8,72},{9,... | collective-permute-start | bytes 135176 | tf_op jit(solution)/shard_map/ppermute | solution.py:43
  102.5 5.7 %collective-permute-done.26 = f32[88,128]{1,0:T(8,128)S(1)} collective-permute-done((f32[88,128]{1,0:T(8,128)S(1)}, f32[88,128]{1,0:T(8,128)S(1)}, u32[]{:S(2)}, u32[]{:S(2)}) %collective-permute-start.26) | collective-permute-done | bytes 45088 | tf_op jit(solution)/shard_map/ppermute | solution.py:43
  108.6 4.8 %collective-permute-start.30 = (f32[88,128]{1,0:T(8,128)S(1)}, f32[88,128]{1,0:T(8,128)S(1)}, u32[]{:S(2)}, u32[]{:S(2)}) collective-permute-start(f32[88,128]{1,0:T(8,128)S(1)} %add_add_fusion.2), channel_id=1, source_target_pairs={{0,129},{1,128},{2,131},{3,130},{4,133},{5,132},{6,135},{7,134},{8... | collective-permute-start | bytes 135176 | tf_op jit(solution)/shard_map/ppermute | solution.py:43
  113.3 1.0 collective-permute-start.28
  114.3 1.9 %collective-permute-start.37 = (bf16[8,64,128]{2,1,0:T(8,128)(2,1)S(1)}, bf16[8,64,128]{2,1,0:T(8,128)(2,1)S(1)}, u32[]{:S(2)}, u32[]{:S(2)}) collective-permute-start(bf16[8,64,128]{2,1,0:T(8,128)(2,1)S(1)} %get-tuple-element.64), channel_id=1, source_target_pairs={{0,8},{8,16},{16,24},{24,32},{32,40},{40,48},{48,56},{56,64},{64,7... | collective-permute-start | bytes 393224 | tf_op jit(solution)/shard_map/ppermute | solution.py:49
  116.2 5.8 %collective-permute-start.38 = (bf16[8,64,128]{2,1,0:T(8,128)(2,1)S(1)}, bf16[8,64,128]{2,1,0:T(8,128)(2,1)S(1)}, u32[]{:S(2)}, u32[]{:S(2)}) collective-permute-start(bf16[8,64,128]{2,1,0:T(8,128)(2,1)S(1)} %get-tuple-element.65), channel_id=1, source_target_pairs={{8,0},{16,8},{24,16},{32,24},{40,32},{48,40},{56,48},{64,56},{72,6... | collective-permute-start | bytes 393224 | tf_op jit(solution)/shard_map/ppermute | solution.py:49
  122.0 1.9 %collective-permute-start.33 = (f32[88,128]{1,0:T(8,128)S(1)}, f32[88,128]{1,0:T(8,128)S(1)}, u32[]{:S(2)}, u32[]{:S(2)}) collective-permute-start(f32[88,128]{1,0:T(8,128)S(1)} %add_add_fusion.1), channel_id=1, source_target_pairs={{0,6},{1,7},{2,4},{3,5},{4,2},{5,3},{6,0},{7,1},{8,14},{9,15},{10,... | collective-permute-start | bytes 135176 | tf_op jit(solution)/shard_map/ppermute | solution.py:43
  123.9 1.6 %collective-permute-start.32 = (f32[88,128]{1,0:T(8,128)S(1)}, f32[88,128]{1,0:T(8,128)S(1)}, u32[]{:S(2)}, u32[]{:S(2)}) collective-permute-start(f32[88,128]{1,0:T(8,128)S(1)} %add_add_fusion.1), channel_id=1, source_target_pairs={{0,4},{1,5},{2,6},{3,7},{4,0},{5,1},{6,2},{7,3},{8,12},{9,13},{10,... | collective-permute-start | bytes 135176 | tf_op jit(solution)/shard_map/ppermute | solution.py:43
  125.5 0.7 collective-permute-start.31
  126.7 4.2 %collective-permute-start.39 = (bf16[3,64,128]{2,1,0:T(8,128)(2,1)S(1)}, bf16[3,64,128]{2,1,0:T(8,128)(2,1)S(1)}, u32[]{:S(2)}, u32[]{:S(2)}) collective-permute-start(bf16[3,64,128]{2,1,0:T(8,128)(2,1)S(1)} %get-tuple-element.66), channel_id=1, source_target_pairs={{0,1},{1,2},{2,3},{3,4},{4,5},{5,6},{6,7},{8,9},{9,10},{10,11},{11... | collective-permute-start | bytes 147464 | tf_op jit(solution)/shard_map/ppermute | solution.py:49
  130.8 3.2 %collective-permute-start.40 = (bf16[3,64,128]{2,1,0:T(8,128)(2,1)S(1)}, bf16[3,64,128]{2,1,0:T(8,128)(2,1)S(1)}, u32[]{:S(2)}, u32[]{:S(2)}) collective-permute-start(bf16[3,64,128]{2,1,0:T(8,128)(2,1)S(1)} %get-tuple-element.67), channel_id=1, source_target_pairs={{1,0},{2,1},{3,2},{4,3},{5,4},{6,5},{7,6},{9,8},{10,9},{11,10},{12... | collective-permute-start | bytes 147464 | tf_op jit(solution)/shard_map/ppermute | solution.py:49
  134.3 1.7 %collective-permute-start.34 = (f32[88,128]{1,0:T(8,128)S(1)}, f32[88,128]{1,0:T(8,128)S(1)}, u32[]{:S(2)}, u32[]{:S(2)}) collective-permute-start(f32[88,128]{1,0:T(8,128)S(1)} %add_add_fusion.got0), channel_id=1, source_target_pairs={{0,8},{1,9},{2,10},{3,11},{4,12},{5,13},{6,14},{7,15},{8,0},{9,1},... | collective-permute-start | bytes 135176 | tf_op jit(solution)/shard_map/ppermute | solution.py:43
  136.0 3.2 %collective-permute-done.40.right = bf16[3,64,128]{2,1,0:T(8,128)(2,1)S(1)} collective-permute-done((bf16[3,64,128]{2,1,0:T(8,128)(2,1)S(1)}, bf16[3,64,128]{2,1,0:T(8,128)(2,1)S(1)}, u32[]{:S(2)}, u32[]{:S(2)}) %collective-permute-start.40) | collective-permute-done | bytes 49184 | tf_op jit(solution)/shard_map/ppermute | solution.py:49
  139.2 2.9 %shard_map.108 = bf16[32,64,128]{2,1,0:T(8,128)(2,1)} custom-call(f32[8,128]{1,0:T(8,128)S(1)} %add_add_fusion.4.count, bf16[32,64,128]{2,1,0:T(8,128)(2,1)S(1)} %get-tuple-element.63.own.low, bf16[8,64,128]{2,1,0:T(8,128)(2,1)S(1)} %collective-permute-done.37.up, bf16[8,64,128]{2,1,0:T(8,128)(2,1)S(1)} %collective-permute-done.38.down, ...), custom_call_target="tpu_custom_call" | custom-call | bytes 14400000 | tf_op jit(solution)/shard_map/pallas_call | solution.py:19
  142.1 0.8 shard_map.106
  (64 shorter events, 5.5 us)
Async XLA Ops:
  0.6 83.4 %copy-start.6 = (f32[37]{0:T(128)S(1)}, f32[37]{0:T(128)}, u32[]{:S(2)}) copy-start(f32[37]{0:T(128)} %param.9) | copy-start | bytes 448
  0.6 1.0 copy-start.1
  1.7 0.7 copy-start.4
  2.4 81.6 %copy-start.3 = (s32[32,128]{1,0:T(8,128)S(1)}, s32[32,128]{1,0:T(8,128)}, u32[]{:S(2)}) copy-start(s32[32,128]{1,0:T(8,128)} %labels.3) | copy-start | bytes 49156
  2.4 81.6 %copy-start.5 = (bf16[64,37]{0,1:T(8,128)(2,1)S(1)}, bf16[64,37]{0,1:T(8,128)(2,1)}, u32[]{:S(2)}) copy-start(bf16[64,37]{0,1:T(8,128)(2,1)} %param.8) | copy-start | bytes 14212
  3.1 3.0 %collective-permute-start.2 = (f32[8,128]{1,0:T(8,128)S(1)}, f32[8,128]{1,0:T(8,128)S(1)}, u32[]{:S(2)}, u32[]{:S(2)}) collective-permute-start(f32[8,128]{1,0:T(8,128)S(1)} %get-tuple-element.38), channel_id=1, source_target_pairs={{0,24},{1,25},{2,26},{3,27},{4,28},{5,29},{6,30},{7,31},{8,16},{9,... | collective-permute-start | bytes 12296 | tf_op jit(solution)/shard_map/ppermute | solution.py:43
  4.5 3.6 %collective-permute-start.1 = (f32[8,128]{1,0:T(8,128)S(1)}, f32[8,128]{1,0:T(8,128)S(1)}, u32[]{:S(2)}, u32[]{:S(2)}) collective-permute-start(f32[8,128]{1,0:T(8,128)S(1)} %get-tuple-element.38), channel_id=1, source_target_pairs={{0,16},{1,17},{2,18},{3,19},{4,20},{5,21},{6,22},{7,23},{8,24},{9,... | collective-permute-start | bytes 12296 | tf_op jit(solution)/shard_map/ppermute | solution.py:43
  5.2 2.9 %collective-permute-start = (f32[8,128]{1,0:T(8,128)S(1)}, f32[8,128]{1,0:T(8,128)S(1)}, u32[]{:S(2)}, u32[]{:S(2)}) collective-permute-start(f32[8,128]{1,0:T(8,128)S(1)} %get-tuple-element.38), channel_id=1, source_target_pairs={{0,8},{1,9},{2,10},{3,11},{4,12},{5,13},{6,14},{7,15},{8,0},{9,1},... | collective-permute-start | bytes 12296 | tf_op jit(solution)/shard_map/ppermute | solution.py:43
  8.1 8.0 %collective-permute-start.5 = (f32[8,128]{1,0:T(8,128)S(1)}, f32[8,128]{1,0:T(8,128)S(1)}, u32[]{:S(2)}, u32[]{:S(2)}) collective-permute-start(f32[8,128]{1,0:T(8,128)S(1)} %add_add_fusion.7), channel_id=1, source_target_pairs={{0,96},{1,97},{2,98},{3,99},{4,100},{5,101},{6,102},{7,103},{8,104... | collective-permute-start | bytes 12296 | tf_op jit(solution)/shard_map/ppermute | solution.py:43
  13.6 7.5 %collective-permute-start.4 = (f32[8,128]{1,0:T(8,128)S(1)}, f32[8,128]{1,0:T(8,128)S(1)}, u32[]{:S(2)}, u32[]{:S(2)}) collective-permute-start(f32[8,128]{1,0:T(8,128)S(1)} %add_add_fusion.7), channel_id=1, source_target_pairs={{0,64},{1,65},{2,66},{3,67},{4,68},{5,69},{6,70},{7,71},{8,72},{9,... | collective-permute-start | bytes 12296 | tf_op jit(solution)/shard_map/ppermute | solution.py:43
  15.1 6.1 %collective-permute-start.3 = (f32[8,128]{1,0:T(8,128)S(1)}, f32[8,128]{1,0:T(8,128)S(1)}, u32[]{:S(2)}, u32[]{:S(2)}) collective-permute-start(f32[8,128]{1,0:T(8,128)S(1)} %add_add_fusion.7), channel_id=1, source_target_pairs={{0,32},{1,33},{2,34},{3,35},{4,36},{5,37},{6,38},{7,39},{8,40},{9,... | collective-permute-start | bytes 12296 | tf_op jit(solution)/shard_map/ppermute | solution.py:43
  21.1 11.9 %collective-permute-start.8 = (f32[8,128]{1,0:T(8,128)S(1)}, f32[8,128]{1,0:T(8,128)S(1)}, u32[]{:S(2)}, u32[]{:S(2)}) collective-permute-start(f32[8,128]{1,0:T(8,128)S(1)} %add_add_fusion.6), channel_id=1, source_target_pairs={{0,129},{1,128},{2,131},{3,130},{4,133},{5,132},{6,135},{7,134},{8... | collective-permute-start | bytes 12296 | tf_op jit(solution)/shard_map/ppermute | solution.py:43
  21.4 11.6 %collective-permute-start.7 = (f32[8,128]{1,0:T(8,128)S(1)}, f32[8,128]{1,0:T(8,128)S(1)}, u32[]{:S(2)}, u32[]{:S(2)}) collective-permute-start(f32[8,128]{1,0:T(8,128)S(1)} %add_add_fusion.6), channel_id=1, source_target_pairs={{0,1},{1,0},{2,3},{3,2},{4,5},{5,4},{6,7},{7,6},{8,9},{9,8},{10,11... | collective-permute-start | bytes 12296 | tf_op jit(solution)/shard_map/ppermute | solution.py:43
  24.0 9.0 %collective-permute-start.6 = (f32[8,128]{1,0:T(8,128)S(1)}, f32[8,128]{1,0:T(8,128)S(1)}, u32[]{:S(2)}, u32[]{:S(2)}) collective-permute-start(f32[8,128]{1,0:T(8,128)S(1)} %add_add_fusion.6), channel_id=1, source_target_pairs={{0,128},{1,129},{2,130},{3,131},{4,132},{5,133},{6,134},{7,135},{8... | collective-permute-start | bytes 12296 | tf_op jit(solution)/shard_map/ppermute | solution.py:43
  25.3 11.9 %collective-permute-start.12 = (bf16[8,64,128]{2,1,0:T(8,128)(2,1)S(1)}, bf16[8,64,128]{2,1,0:T(8,128)(2,1)S(1)}, u32[]{:S(2)}, u32[]{:S(2)}) collective-permute-start(bf16[8,64,128]{2,1,0:T(8,128)(2,1)S(1)} %get-tuple-element.42), channel_id=1, source_target_pairs={{0,8},{8,16},{16,24},{24,32},{32,40},{40,48},{48,56},{56,64},{64,7... | collective-permute-start | bytes 393224 | tf_op jit(solution)/shard_map/ppermute | solution.py:49
  27.2 10.0 %collective-permute-start.13 = (bf16[8,64,128]{2,1,0:T(8,128)(2,1)S(1)}, bf16[8,64,128]{2,1,0:T(8,128)(2,1)S(1)}, u32[]{:S(2)}, u32[]{:S(2)}) collective-permute-start(bf16[8,64,128]{2,1,0:T(8,128)(2,1)S(1)} %get-tuple-element.43), channel_id=1, source_target_pairs={{8,0},{16,8},{24,16},{32,24},{40,32},{48,40},{56,48},{64,56},{72,6... | collective-permute-start | bytes 393224 | tf_op jit(solution)/shard_map/ppermute | solution.py:49
  33.0 12.0 %collective-permute-start.11 = (f32[8,128]{1,0:T(8,128)S(1)}, f32[8,128]{1,0:T(8,128)S(1)}, u32[]{:S(2)}, u32[]{:S(2)}) collective-permute-start(f32[8,128]{1,0:T(8,128)S(1)} %add_add_fusion.5), channel_id=1, source_target_pairs={{0,6},{1,7},{2,4},{3,5},{4,2},{5,3},{6,0},{7,1},{8,14},{9,15},{10,... | collective-permute-start | bytes 12296 | tf_op jit(solution)/shard_map/ppermute | solution.py:43
  35.9 9.2 %collective-permute-start.10 = (f32[8,128]{1,0:T(8,128)S(1)}, f32[8,128]{1,0:T(8,128)S(1)}, u32[]{:S(2)}, u32[]{:S(2)}) collective-permute-start(f32[8,128]{1,0:T(8,128)S(1)} %add_add_fusion.5), channel_id=1, source_target_pairs={{0,4},{1,5},{2,6},{3,7},{4,0},{5,1},{6,2},{7,3},{8,12},{9,13},{10,... | collective-permute-start | bytes 12296 | tf_op jit(solution)/shard_map/ppermute | solution.py:43
  36.7 8.4 %collective-permute-start.9 = (f32[8,128]{1,0:T(8,128)S(1)}, f32[8,128]{1,0:T(8,128)S(1)}, u32[]{:S(2)}, u32[]{:S(2)}) collective-permute-start(f32[8,128]{1,0:T(8,128)S(1)} %add_add_fusion.5), channel_id=1, source_target_pairs={{0,2},{1,3},{2,0},{3,1},{4,6},{5,7},{6,4},{7,5},{8,10},{9,11},{10,... | collective-permute-start | bytes 12296 | tf_op jit(solution)/shard_map/ppermute | solution.py:43
  37.7 7.5 %collective-permute-start.14 = (bf16[3,64,128]{2,1,0:T(8,128)(2,1)S(1)}, bf16[3,64,128]{2,1,0:T(8,128)(2,1)S(1)}, u32[]{:S(2)}, u32[]{:S(2)}) collective-permute-start(bf16[3,64,128]{2,1,0:T(8,128)(2,1)S(1)} %get-tuple-element.44), channel_id=1, source_target_pairs={{0,1},{1,2},{2,3},{3,4},{4,5},{5,6},{6,7},{8,9},{9,10},{10,11},{11... | collective-permute-start | bytes 147464 | tf_op jit(solution)/shard_map/ppermute | solution.py:49
  41.8 8.4 %collective-permute-start.15 = (bf16[3,64,128]{2,1,0:T(8,128)(2,1)S(1)}, bf16[3,64,128]{2,1,0:T(8,128)(2,1)S(1)}, u32[]{:S(2)}, u32[]{:S(2)}) collective-permute-start(bf16[3,64,128]{2,1,0:T(8,128)(2,1)S(1)} %get-tuple-element.45), channel_id=1, source_target_pairs={{1,0},{2,1},{3,2},{4,3},{5,4},{6,5},{7,6},{9,8},{10,9},{11,10},{12... | collective-permute-start | bytes 147464 | tf_op jit(solution)/shard_map/ppermute | solution.py:49
  50.1 0.9 copy-start
  51.1 0.7 copy-start.2
  55.1 6.5 %collective-permute-start.16 = (bf16[528,128]{1,0:T(8,128)(2,1)S(1)}, bf16[528,128]{1,0:T(8,128)(2,1)S(1)}, u32[]{:S(2)}, u32[]{:S(2)}) collective-permute-start(bf16[528,128]{1,0:T(8,128)(2,1)S(1)} %get-tuple-element.48), channel_id=1, source_target_pairs={{0,2},{1,3},{2,0},{3,1},{4,6},{5,7},{6,4},{7,5},{8,10},{9,11},{10,... | collective-permute-start | bytes 405512 | tf_op jit(solution)/shard_map/ppermute | solution.py:43
  56.7 7.0 %collective-permute-start.18 = (bf16[528,128]{1,0:T(8,128)(2,1)S(1)}, bf16[528,128]{1,0:T(8,128)(2,1)S(1)}, u32[]{:S(2)}, u32[]{:S(2)}) collective-permute-start(bf16[528,128]{1,0:T(8,128)(2,1)S(1)} %get-tuple-element.49), channel_id=1, source_target_pairs={{0,6},{1,7},{2,4},{3,5},{4,2},{5,3},{6,0},{7,1},{8,14},{9,15},{10,... | collective-permute-start | bytes 405512 | tf_op jit(solution)/shard_map/ppermute | solution.py:43
  58.5 15.9 %collective-permute-start.20 = (bf16[528,128]{1,0:T(8,128)(2,1)S(1)}, bf16[528,128]{1,0:T(8,128)(2,1)S(1)}, u32[]{:S(2)}, u32[]{:S(2)}) collective-permute-start(bf16[528,128]{1,0:T(8,128)(2,1)S(1)} %get-tuple-element.50), channel_id=1, source_target_pairs={{0,16},{1,48},{2,80},{3,112},{4,144},{5,176},{6,208},{7,240},{8,24... | collective-permute-start | bytes 405512 | tf_op jit(solution)/shard_map/ppermute | solution.py:43
  58.8 15.6 %collective-permute-start.21 = (bf16[528,128]{1,0:T(8,128)(2,1)S(1)}, bf16[528,128]{1,0:T(8,128)(2,1)S(1)}, u32[]{:S(2)}, u32[]{:S(2)}) collective-permute-start(bf16[528,128]{1,0:T(8,128)(2,1)S(1)} %get-tuple-element.51), channel_id=1, source_target_pairs={{0,24},{1,56},{2,88},{3,120},{4,152},{5,184},{6,216},{7,248},{8,16... | collective-permute-start | bytes 405512 | tf_op jit(solution)/shard_map/ppermute | solution.py:43
  61.6 19.5 %collective-permute-start.17 = (bf16[528,128]{1,0:T(8,128)(2,1)S(1)}, bf16[528,128]{1,0:T(8,128)(2,1)S(1)}, u32[]{:S(2)}, u32[]{:S(2)}) collective-permute-start(bf16[528,128]{1,0:T(8,128)(2,1)S(1)} %collective-permute-done.16), channel_id=1, source_target_pairs={{0,64},{1,96},{2,0},{3,32},{4,192},{5,224},{6,128},{7,160},{8,72},... | collective-permute-start | bytes 405512 | tf_op jit(solution)/shard_map/ppermute | solution.py:43
  63.6 20.4 %collective-permute-start.19 = (bf16[528,128]{1,0:T(8,128)(2,1)S(1)}, bf16[528,128]{1,0:T(8,128)(2,1)S(1)}, u32[]{:S(2)}, u32[]{:S(2)}) collective-permute-start(bf16[528,128]{1,0:T(8,128)(2,1)S(1)} %collective-permute-done.18), channel_id=1, source_target_pairs={{0,200},{1,232},{2,136},{3,168},{4,72},{5,104},{6,8},{7,40},{8,192... | collective-permute-start | bytes 405512 | tf_op jit(solution)/shard_map/ppermute | solution.py:43
  90.6 2.0 %collective-permute-start.22 = (f32[88,128]{1,0:T(8,128)S(1)}, f32[88,128]{1,0:T(8,128)S(1)}, u32[]{:S(2)}, u32[]{:S(2)}) collective-permute-start(f32[88,128]{1,0:T(8,128)S(1)} %get-tuple-element.59), channel_id=1, source_target_pairs={{0,8},{1,9},{2,10},{3,11},{4,12},{5,13},{6,14},{7,15},{8,0},{9,1},... | collective-permute-start | bytes 135176 | tf_op jit(solution)/shard_map/ppermute | solution.py:43
  91.1 4.2 %collective-permute-start.23 = (f32[88,128]{1,0:T(8,128)S(1)}, f32[88,128]{1,0:T(8,128)S(1)}, u32[]{:S(2)}, u32[]{:S(2)}) collective-permute-start(f32[88,128]{1,0:T(8,128)S(1)} %get-tuple-element.60), channel_id=1, source_target_pairs={{0,16},{1,17},{2,18},{3,19},{4,20},{5,21},{6,22},{7,23},{8,24},{9,... | collective-permute-start | bytes 135176 | tf_op jit(solution)/shard_map/ppermute | solution.py:43
  91.1 4.2 %collective-permute-start.24 = (f32[88,128]{1,0:T(8,128)S(1)}, f32[88,128]{1,0:T(8,128)S(1)}, u32[]{:S(2)}, u32[]{:S(2)}) collective-permute-start(f32[88,128]{1,0:T(8,128)S(1)} %get-tuple-element.61), channel_id=1, source_target_pairs={{0,24},{1,25},{2,26},{3,27},{4,28},{5,29},{6,30},{7,31},{8,16},{9,... | collective-permute-start | bytes 135176 | tf_op jit(solution)/shard_map/ppermute | solution.py:43
  95.3 7.2 %collective-permute-start.27 = (f32[88,128]{1,0:T(8,128)S(1)}, f32[88,128]{1,0:T(8,128)S(1)}, u32[]{:S(2)}, u32[]{:S(2)}) collective-permute-start(f32[88,128]{1,0:T(8,128)S(1)} %add_add_fusion.3), channel_id=1, source_target_pairs={{0,96},{1,97},{2,98},{3,99},{4,100},{5,101},{6,102},{7,103},{8,104... | collective-permute-start | bytes 135176 | tf_op jit(solution)/shard_map/ppermute | solution.py:43
  99.6 8.5 %collective-permute-start.26 = (f32[88,128]{1,0:T(8,128)S(1)}, f32[88,128]{1,0:T(8,128)S(1)}, u32[]{:S(2)}, u32[]{:S(2)}) collective-permute-start(f32[88,128]{1,0:T(8,128)S(1)} %add_add_fusion.3), channel_id=1, source_target_pairs={{0,64},{1,65},{2,66},{3,67},{4,68},{5,69},{6,70},{7,71},{8,72},{9,... | collective-permute-start | bytes 135176 | tf_op jit(solution)/shard_map/ppermute | solution.py:43
  102.5 6.1 %collective-permute-start.25 = (f32[88,128]{1,0:T(8,128)S(1)}, f32[88,128]{1,0:T(8,128)S(1)}, u32[]{:S(2)}, u32[]{:S(2)}) collective-permute-start(f32[88,128]{1,0:T(8,128)S(1)} %add_add_fusion.3), channel_id=1, source_target_pairs={{0,32},{1,33},{2,34},{3,35},{4,36},{5,37},{6,38},{7,39},{8,40},{9,... | collective-permute-start | bytes 135176 | tf_op jit(solution)/shard_map/ppermute | solution.py:43
  108.6 13.4 %collective-permute-start.30 = (f32[88,128]{1,0:T(8,128)S(1)}, f32[88,128]{1,0:T(8,128)S(1)}, u32[]{:S(2)}, u32[]{:S(2)}) collective-permute-start(f32[88,128]{1,0:T(8,128)S(1)} %add_add_fusion.2), channel_id=1, source_target_pairs={{0,129},{1,128},{2,131},{3,130},{4,133},{5,132},{6,135},{7,134},{8... | collective-permute-start | bytes 135176 | tf_op jit(solution)/shard_map/ppermute | solution.py:43
  113.3 8.6 %collective-permute-start.29 = (f32[88,128]{1,0:T(8,128)S(1)}, f32[88,128]{1,0:T(8,128)S(1)}, u32[]{:S(2)}, u32[]{:S(2)}) collective-permute-start(f32[88,128]{1,0:T(8,128)S(1)} %add_add_fusion.2), channel_id=1, source_target_pairs={{0,1},{1,0},{2,3},{3,2},{4,5},{5,4},{6,7},{7,6},{8,9},{9,8},{10,11... | collective-permute-start | bytes 135176 | tf_op jit(solution)/shard_map/ppermute | solution.py:43
  113.3 8.7 %collective-permute-start.28 = (f32[88,128]{1,0:T(8,128)S(1)}, f32[88,128]{1,0:T(8,128)S(1)}, u32[]{:S(2)}, u32[]{:S(2)}) collective-permute-start(f32[88,128]{1,0:T(8,128)S(1)} %add_add_fusion.2), channel_id=1, source_target_pairs={{0,128},{1,129},{2,130},{3,131},{4,132},{5,133},{6,134},{7,135},{8... | collective-permute-start | bytes 135176 | tf_op jit(solution)/shard_map/ppermute | solution.py:43
  114.3 11.9 %collective-permute-start.37 = (bf16[8,64,128]{2,1,0:T(8,128)(2,1)S(1)}, bf16[8,64,128]{2,1,0:T(8,128)(2,1)S(1)}, u32[]{:S(2)}, u32[]{:S(2)}) collective-permute-start(bf16[8,64,128]{2,1,0:T(8,128)(2,1)S(1)} %get-tuple-element.64), channel_id=1, source_target_pairs={{0,8},{8,16},{16,24},{24,32},{32,40},{40,48},{48,56},{56,64},{64,7... | collective-permute-start | bytes 393224 | tf_op jit(solution)/shard_map/ppermute | solution.py:49
  116.2 10.0 %collective-permute-start.38 = (bf16[8,64,128]{2,1,0:T(8,128)(2,1)S(1)}, bf16[8,64,128]{2,1,0:T(8,128)(2,1)S(1)}, u32[]{:S(2)}, u32[]{:S(2)}) collective-permute-start(bf16[8,64,128]{2,1,0:T(8,128)(2,1)S(1)} %get-tuple-element.65), channel_id=1, source_target_pairs={{8,0},{16,8},{24,16},{32,24},{40,32},{48,40},{56,48},{64,56},{72,6... | collective-permute-start | bytes 393224 | tf_op jit(solution)/shard_map/ppermute | solution.py:49
  122.0 12.0 %collective-permute-start.33 = (f32[88,128]{1,0:T(8,128)S(1)}, f32[88,128]{1,0:T(8,128)S(1)}, u32[]{:S(2)}, u32[]{:S(2)}) collective-permute-start(f32[88,128]{1,0:T(8,128)S(1)} %add_add_fusion.1), channel_id=1, source_target_pairs={{0,6},{1,7},{2,4},{3,5},{4,2},{5,3},{6,0},{7,1},{8,14},{9,15},{10,... | collective-permute-start | bytes 135176 | tf_op jit(solution)/shard_map/ppermute | solution.py:43
  123.9 10.2 %collective-permute-start.32 = (f32[88,128]{1,0:T(8,128)S(1)}, f32[88,128]{1,0:T(8,128)S(1)}, u32[]{:S(2)}, u32[]{:S(2)}) collective-permute-start(f32[88,128]{1,0:T(8,128)S(1)} %add_add_fusion.1), channel_id=1, source_target_pairs={{0,4},{1,5},{2,6},{3,7},{4,0},{5,1},{6,2},{7,3},{8,12},{9,13},{10,... | collective-permute-start | bytes 135176 | tf_op jit(solution)/shard_map/ppermute | solution.py:43
  125.5 8.6 %collective-permute-start.31 = (f32[88,128]{1,0:T(8,128)S(1)}, f32[88,128]{1,0:T(8,128)S(1)}, u32[]{:S(2)}, u32[]{:S(2)}) collective-permute-start(f32[88,128]{1,0:T(8,128)S(1)} %add_add_fusion.1), channel_id=1, source_target_pairs={{0,2},{1,3},{2,0},{3,1},{4,6},{5,7},{6,4},{7,5},{8,10},{9,11},{10,... | collective-permute-start | bytes 135176 | tf_op jit(solution)/shard_map/ppermute | solution.py:43
  126.7 9.4 %collective-permute-start.39 = (bf16[3,64,128]{2,1,0:T(8,128)(2,1)S(1)}, bf16[3,64,128]{2,1,0:T(8,128)(2,1)S(1)}, u32[]{:S(2)}, u32[]{:S(2)}) collective-permute-start(bf16[3,64,128]{2,1,0:T(8,128)(2,1)S(1)} %get-tuple-element.66), channel_id=1, source_target_pairs={{0,1},{1,2},{2,3},{3,4},{4,5},{5,6},{6,7},{8,9},{9,10},{10,11},{11... | collective-permute-start | bytes 147464 | tf_op jit(solution)/shard_map/ppermute | solution.py:49
  130.8 8.4 %collective-permute-start.40 = (bf16[3,64,128]{2,1,0:T(8,128)(2,1)S(1)}, bf16[3,64,128]{2,1,0:T(8,128)(2,1)S(1)}, u32[]{:S(2)}, u32[]{:S(2)}) collective-permute-start(bf16[3,64,128]{2,1,0:T(8,128)(2,1)S(1)} %get-tuple-element.67), channel_id=1, source_target_pairs={{1,0},{2,1},{3,2},{4,3},{5,4},{6,5},{7,6},{9,8},{10,9},{11,10},{12... | collective-permute-start | bytes 147464 | tf_op jit(solution)/shard_map/ppermute | solution.py:49
  134.1 8.0 %collective-permute-start.36 = (f32[88,128]{1,0:T(8,128)S(1)}, f32[88,128]{1,0:T(8,128)S(1)}, u32[]{:S(2)}, u32[]{:S(2)}) collective-permute-start(f32[88,128]{1,0:T(8,128)S(1)} %add_add_fusion.got0), channel_id=1, source_target_pairs={{0,24},{1,25},{2,26},{3,27},{4,28},{5,29},{6,30},{7,31},{8,16},{9,... | collective-permute-start | bytes 135176 | tf_op jit(solution)/shard_map/ppermute | solution.py:43
  134.2 7.9 %collective-permute-start.35 = (f32[88,128]{1,0:T(8,128)S(1)}, f32[88,128]{1,0:T(8,128)S(1)}, u32[]{:S(2)}, u32[]{:S(2)}) collective-permute-start(f32[88,128]{1,0:T(8,128)S(1)} %add_add_fusion.got0), channel_id=1, source_target_pairs={{0,16},{1,17},{2,18},{3,19},{4,20},{5,21},{6,22},{7,23},{8,24},{9,... | collective-permute-start | bytes 135176 | tf_op jit(solution)/shard_map/ppermute | solution.py:43
  134.3 7.8 %collective-permute-start.34 = (f32[88,128]{1,0:T(8,128)S(1)}, f32[88,128]{1,0:T(8,128)S(1)}, u32[]{:S(2)}, u32[]{:S(2)}) collective-permute-start(f32[88,128]{1,0:T(8,128)S(1)} %add_add_fusion.got0), channel_id=1, source_target_pairs={{0,8},{1,9},{2,10},{3,11},{4,12},{5,13},{6,14},{7,15},{8,0},{9,1},... | collective-permute-start | bytes 135176 | tf_op jit(solution)/shard_map/ppermute | solution.py:43

commit v6 on v5

--- a/solution.py
+++ b/solution.py
@@ -10,6 +10,7 @@
 F32, BF16 = jnp.float32, jnp.bfloat16
 LANES = 128
 UNROLL = 8
+SLAB = 64
 FAR_BELOW = -1e30
 VMEM = pl.BlockSpec(memory_space=pltpu.VMEM)
 SMEM = pl.BlockSpec(memory_space=pltpu.SMEM)
@@ -348,22 +349,17 @@
     return lambda m: lambda r, c: (r, c ^ (m << 1))
 
 
-def total_small(value):
-    for stage in range(4):
-        to = partners(stage)
-        value = (value + send(value, to(1))) + (send(value, to(2)) + send(value, to(3)))
-    return value
+def total_columns(value):
+    near = lambda m: lambda r, c: (r, c ^ m)
+    value = value + send(value, near(1))
+    return (value + send(value, near(2))) + (send(value, near(4)) + send(value, near(6)))
 
 
 def mirrored(pays, parts):
-    got = []
-    for s, block in enumerate(pays):
-        bits = (2, 6, 0, 0)[s]
-        owner = lambda r, c: (parts * c + (r % parts ^ s), r // parts)
-        if bits:
-            block = send(block, lambda r, c: (r, c ^ bits))
-        got.append(send(block, lambda r, c: owner(r, c ^ bits)))
-    return got
+    bits = (2, 6, 0, 0)
+    half = [send(pays[s], lambda r, c: (r, c ^ bits[s])) if bits[s] else pays[s] for s in range(4)]
+    owner = lambda s: lambda r, c: (parts * (c ^ bits[s]) + (r % parts ^ s), r // parts)
+    return half, [send(half[s], owner(s)) for s in range(4)]
 
 
 def total_quarters(quarters):
@@ -394,8 +390,9 @@
         micros=1,
     )
     around = borders(act, top, bottom)
-    count = total_small(counted)
-    count, act = lax.optimization_barrier((count, act))
+    gathered = lax.all_gather(
+        jnp.broadcast_to(counted[:1], (SLAB, LANES)), "row", axis=0, tiled=True
+    )
     length = (rows + 1) * rows // 2
     wide, mixed, *pays = run(
         forward_kernel,
@@ -406,7 +403,9 @@
         scalars=1,
         micros=5,
     )
-    got = mirrored(pays, parts)
+    half, got = mirrored(pays, parts)
+    _, gathered = lax.optimization_barrier((half[1], gathered))
+    count = total_columns(jnp.sum(gathered.reshape(-1, SLAB, LANES)[:, :8], axis=0))
     grad, head_sum, bias_sum, loss_sum = run(
         softmax_kernel,
         [

time: 143 us -> 172 us (1.20)
  between operations: 0.94 us -> 14.3 us
  local copies, waits for them, and re-layouts: 3.4 us -> 13 us
  waiting for transfers between devices: 38.2 us -> 40.7 us
    ppermute x33 -> x25, waiting for transfers between devices: 29.9 us -> 9.63 us  [send(): return lax.ppermute(block, GRID, pairs)]
    all_gather x0 -> x1, waiting for transfers between devices: none -> 19.9 us  [per_device(): lax.all_gather(jnp.broadcast_to(counted[:1], (SLAB, LANES)), 'row', axis=...]
    unnamed x14 -> x36, local copies, waits for them, and re-layouts: 3.4 us -> 12.4 us
    ppermute x8, waiting for transfers between devices: 8.26 us -> 11.2 us  [shifted(): lax.ppermute(block, axis, pairs if forward else [(b, a) for a, b in pairs])]
    ppermute x33 -> x25, starting transfers between devices: 55.1 us -> 54.8 us  [send(): return lax.ppermute(block, GRID, pairs)]
  transfers between devices with their start and end apart: 41 -> 34, of which waited for: 12 -> 12; matrix products, arithmetic and copies ran while one was open for 0% -> 1% of each run, Pallas kernels for 3% -> 7%
where the time goes in v6:
time: 172 us; the launch traced here: 171 us
  starting transfers between devices  86.5 us (50%)
  waiting for transfers between devices  40.7 us (24%)
  Pallas kernels  15.9 us (9%)
  between operations  14.3 us (8%)
  local copies, waits for them, and re-layouts  13 us (8%)
    ppermute x25, starting transfers between devices, send(): return lax.ppermute(block, GRID, pairs)  54.8 us
    ppermute x8, starting transfers between devices, shifted(): lax.ppermute(block, axis, pairs if forward else [(b, a) for a, b in pairs])  31.7 us
    all_gather x1, waiting for transfers between devices, per_device(): lax.all_gather(jnp.broadcast_to(counted[:1], (SLAB, LANES)), 'row', axis=...  19.9 us
    pallas_call x8, Pallas kernels, run(): pl.pallas_call(body, out_shape=outs, in_specs=[SMEM] * scalars + [VMEM] *...  15.9 us
    unnamed x36, local copies, waits for them, and re-layouts  12.4 us
    ppermute x8, waiting for transfers between devices, shifted(): lax.ppermute(block, axis, pairs if forward else [(b, a) for a, b in pairs])  11.2 us
    ppermute x25, waiting for transfers between devices, send(): return lax.ppermute(block, GRID, pairs)  9.63 us
  transfers between devices with their start and end apart: 34, of which 12 were waited for; matrix products, arithmetic and copies ran while one was open for 1% of the time, Pallas kernels for 7%

profile of v6, /device:TPU:24, one launch (start us, length us, event | category | flops | bytes accessed | tf_op | source)
XLA Modules:
  0.0 171.5 jit_solution(5176267067723943188)
XLA Ops:
  7.2 1.0 copy-done.4
  9.0 0.7 shard_map.101
  10.3 1.9 %collective-permute-start = (bf16[8,64,128]{2,1,0:T(8,128)(2,1)S(1)}, bf16[8,64,128]{2,1,0:T(8,128)(2,1)S(1)}, u32[]{:S(2)}, u32[]{:S(2)}) collective-permute-start(bf16[8,64,128]{2,1,0:T(8,128)(2,1)S(1)} %get-tuple-element.38), channel_id=1, source_target_pairs={{0,8},{8,16},{16,24},{24,32},{32,40},{40,48},{48,56},{56,64},{64,7... | collective-permute-start | bytes 393224 | tf_op jit(solution)/shard_map/ppermute | solution.py:50
  12.3 7.4 %collective-permute-start.1 = (bf16[8,64,128]{2,1,0:T(8,128)(2,1)S(1)}, bf16[8,64,128]{2,1,0:T(8,128)(2,1)S(1)}, u32[]{:S(2)}, u32[]{:S(2)}) collective-permute-start(bf16[8,64,128]{2,1,0:T(8,128)(2,1)S(1)} %get-tuple-element.39), channel_id=1, source_target_pairs={{8,0},{16,8},{24,16},{32,24},{40,32},{48,40},{56,48},{64,56},{72,6... | collective-permute-start | bytes 393224 | tf_op jit(solution)/shard_map/ppermute | solution.py:50
  20.4 1.8 %collective-permute-done.1.down = bf16[8,64,128]{2,1,0:T(8,128)(2,1)S(1)} collective-permute-done((bf16[8,64,128]{2,1,0:T(8,128)(2,1)S(1)}, bf16[8,64,128]{2,1,0:T(8,128)(2,1)S(1)}, u32[]{:S(2)}, u32[]{:S(2)}) %collective-permute-start.1) | collective-permute-done | bytes 131104 | tf_op jit(solution)/shard_map/ppermute | solution.py:50
  23.3 3.8 %collective-permute-start.2 = (bf16[3,64,128]{2,1,0:T(8,128)(2,1)S(1)}, bf16[3,64,128]{2,1,0:T(8,128)(2,1)S(1)}, u32[]{:S(2)}, u32[]{:S(2)}) collective-permute-start(bf16[3,64,128]{2,1,0:T(8,128)(2,1)S(1)} %get-tuple-element.40), channel_id=1, source_target_pairs={{0,1},{1,2},{2,3},{3,4},{4,5},{5,6},{6,7},{8,9},{9,10},{10,11},{11... | collective-permute-start | bytes 147464 | tf_op jit(solution)/shard_map/ppermute | solution.py:50
  27.0 3.6 %collective-permute-start.3 = (bf16[3,64,128]{2,1,0:T(8,128)(2,1)S(1)}, bf16[3,64,128]{2,1,0:T(8,128)(2,1)S(1)}, u32[]{:S(2)}, u32[]{:S(2)}) collective-permute-start(bf16[3,64,128]{2,1,0:T(8,128)(2,1)S(1)} %get-tuple-element.41), channel_id=1, source_target_pairs={{1,0},{2,1},{3,2},{4,3},{5,4},{6,5},{7,6},{9,8},{10,9},{11,10},{12... | collective-permute-start | bytes 147464 | tf_op jit(solution)/shard_map/ppermute | solution.py:50
  31.5 3.9 %collective-permute-done.3.right = bf16[3,64,128]{2,1,0:T(8,128)(2,1)S(1)} collective-permute-done((bf16[3,64,128]{2,1,0:T(8,128)(2,1)S(1)}, bf16[3,64,128]{2,1,0:T(8,128)(2,1)S(1)}, u32[]{:S(2)}, u32[]{:S(2)}) %collective-permute-start.3) | collective-permute-done | bytes 49184 | tf_op jit(solution)/shard_map/ppermute | solution.py:50
  36.1 0.9 copy-done
  37.0 0.9 copy-done.6
  38.6 0.8 copy-done.12
  39.4 0.8 copy-done.14
  40.2 4.0 %shard_map.103 = (bf16[48,192,128]{2,1,0:T(8,128)(2,1)S(1)}, bf16[32,64,128]{2,1,0:T(8,128)(2,1)S(1)}, bf16[528,128]{1,0:T(8,128)(2,1)S(1)}, bf16[528,128]{1,0:T...) custom-call(s32[1]{0:T(128)} %bitcast.place, bf16[32,64,128]{2,1,0:T(8,128)(2,1)S(1)} %get-tuple-element.37.own.act, ...), custom_call_target="tpu_custom_call" | custom-call | bytes 18000000 | tf_op jit(solution)/shard_map/pallas_call | solution.py:20
  44.2 0.8 copy-done.2
  45.0 1.5 collective-permute-start.9
  46.5 1.8 %collective-permute-start.4 = (bf16[528,128]{1,0:T(8,128)(2,1)S(1)}, bf16[528,128]{1,0:T(8,128)(2,1)}, u32[]{:S(2)}, u32[]{:S(2)}) collective-permute-start(bf16[528,128]{1,0:T(8,128)(2,1)S(1)} %get-tuple-element.44), channel_id=1, source_target_pairs={{0,6},{1,7},{2,4},{3,5},{4,2},{5,3},{6,0},{7,1},{8,14},{9,15},{10,... | collective-permute-start | bytes 405512 | tf_op jit(solution)/shard_map/ppermute | solution.py:44
  48.3 1.3 collective-permute-start.12
  49.6 3.1 %collective-permute-start.13 = (bf16[528,128]{1,0:T(8,128)(2,1)}, bf16[528,128]{1,0:T(8,128)(2,1)S(1)}, u32[]{:S(2)}, u32[]{:S(2)}) collective-permute-start(bf16[528,128]{1,0:T(8,128)(2,1)} %get-tuple-element.49), channel_id=1, source_target_pairs={{0,24},{1,56},{2,88},{3,120},{4,152},{5,184},{6,216},{7,248},{8,16... | collective-permute-start | bytes 405512 | tf_op jit(solution)/shard_map/ppermute | solution.py:44
  52.7 6.3 %collective-permute-start.10 = (bf16[528,128]{1,0:T(8,128)(2,1)}, bf16[528,128]{1,0:T(8,128)(2,1)S(1)}, u32[]{:S(2)}, u32[]{:S(2)}) collective-permute-start(bf16[528,128]{1,0:T(8,128)(2,1)} %collective-permute-done.9), channel_id=1, source_target_pairs={{0,64},{1,96},{2,0},{3,32},{4,192},{5,224},{6,128},{7,160},{8,72},... | collective-permute-start | bytes 405512 | tf_op jit(solution)/shard_map/ppermute | solution.py:44
  59.0 4.6 %collective-permute-start.11 = (bf16[528,128]{1,0:T(8,128)(2,1)}, bf16[528,128]{1,0:T(8,128)(2,1)S(1)}, u32[]{:S(2)}, u32[]{:S(2)}) collective-permute-start(bf16[528,128]{1,0:T(8,128)(2,1)} %collective-permute-done.4), channel_id=1, source_target_pairs={{0,200},{1,232},{2,136},{3,168},{4,72},{5,104},{6,8},{7,40},{8,192... | collective-permute-start | bytes 405512 | tf_op jit(solution)/shard_map/ppermute | solution.py:44
  63.6 19.9 %all-gather.2.cloned.1.call-done = f32[2048,128]{1,0:T(8,128)} async-done(((f32[64,128]{1,0:T(8,128)}), f32[2048,128]{1,0:T(8,128)}) %all-gather.2.cloned.1.call-update) | async-done | bytes 1048592 | tf_op jit(solution)/shard_map/all_gather | solution.py:393
  83.5 0.9 slice_reduce_fusion
  84.5 10.7 %collective-permute-start.5 = (f32[8,128]{1,0:T(8,128)S(1)}, f32[8,128]{1,0:T(8,128)S(1)}, u32[]{:S(2)}, u32[]{:S(2)}) collective-permute-start(f32[8,128]{1,0:T(8,128)S(1)} %slice_reduce_fusion), channel_id=1, source_target_pairs={{0,1},{1,0},{2,3},{3,2},{4,5},{5,4},{6,7},{7,6},{8,9},{9,8},{10,11... | collective-permute-start | bytes 12296 | tf_op jit(solution)/shard_map/ppermute | solution.py:44
  95.2 1.6 collective-permute-done.5
  96.8 1.2 collective-permute-start.7
  98.0 1.3 collective-permute-start.8
  99.3 1.0 collective-permute-start.6
  100.3 1.0 copy-done.3
  104.1 4.3 %shard_map.104 = (f32[32,64,128]{2,1,0:T(8,128)S(1)}, f32[120,64]{1,0:T(8,128)S(1)}, f32[40,128]{1,0:T(8,128)S(1)}, f32[1,128]{1,0:T(1,128)S(1)}) custom-call(s32[1]{0:T(128)} %bitcast.place, bf16[528,128]{1,0:T(8,128)(2,1)S(1)} %collective-permute-done.10.got0, bf16[528,128]{1,0:T(8,128)(2,1)S(1)} %collective-permute-done.11.got1, ...), custom_call_target="tpu_custom_call" | custom-call | bytes 18000000 | tf_op jit(solution)/shard_map/pallas_call | solution.py:20
  108.5 2.3 %shard_map.105 = (bf16[32,64,128]{2,1,0:T(8,128)(2,1)S(1)}, bf16[8,64,128]{2,1,0:T(8,128)(2,1)S(1)}, bf16[8,64,128]{2,1,0:T(8,128)(2,1)S(1)}, f32[88,128]{1,0:T(...) custom-call(s32[1]{0:T(128)} %bitcast.place, f32[8,128]{1,0:T(8,128)S(1)} %add_add_fusion.4.count, ...), custom_call_target="tpu_custom_call" | custom-call | bytes 10800000 | tf_op jit(solution)/shard_map/pallas_call | solution.py:20
  110.8 1.8 %collective-permute-start.15 = (f32[88,128]{1,0:T(8,128)S(1)}, f32[88,128]{1,0:T(8,128)S(1)}, u32[]{:S(2)}, u32[]{:S(2)}) collective-permute-start(f32[88,128]{1,0:T(8,128)S(1)} %get-tuple-element.58), channel_id=1, source_target_pairs={{0,16},{1,17},{2,18},{3,19},{4,20},{5,21},{6,22},{7,23},{8,24},{9,... | collective-permute-start | bytes 135176 | tf_op jit(solution)/shard_map/ppermute | solution.py:44
  113.0 1.9 %collective-permute-done.15 = f32[88,128]{1,0:T(8,128)S(1)} collective-permute-done((f32[88,128]{1,0:T(8,128)S(1)}, f32[88,128]{1,0:T(8,128)S(1)}, u32[]{:S(2)}, u32[]{:S(2)}) %collective-permute-start.15) | collective-permute-done | bytes 45088 | tf_op jit(solution)/shard_map/ppermute | solution.py:44
  114.9 1.1 collective-permute-done.16
  116.1 6.9 %collective-permute-start.18 = (f32[88,128]{1,0:T(8,128)S(1)}, f32[88,128]{1,0:T(8,128)S(1)}, u32[]{:S(2)}, u32[]{:S(2)}) collective-permute-start(f32[88,128]{1,0:T(8,128)S(1)} %add_add_fusion.3), channel_id=1, source_target_pairs={{0,64},{1,65},{2,66},{3,67},{4,68},{5,69},{6,70},{7,71},{8,72},{9,... | collective-permute-start | bytes 135176 | tf_op jit(solution)/shard_map/ppermute | solution.py:44
  123.0 1.7 collective-permute-start.19
  125.1 4.3 %collective-permute-done.19 = f32[88,128]{1,0:T(8,128)S(1)} collective-permute-done((f32[88,128]{1,0:T(8,128)S(1)}, f32[88,128]{1,0:T(8,128)S(1)}, u32[]{:S(2)}, u32[]{:S(2)}) %collective-permute-start.19) | collective-permute-done | bytes 45088 | tf_op jit(solution)/shard_map/ppermute | solution.py:44
  129.6 1.8 %collective-permute-start.21 = (f32[88,128]{1,0:T(8,128)S(1)}, f32[88,128]{1,0:T(8,128)S(1)}, u32[]{:S(2)}, u32[]{:S(2)}) collective-permute-start(f32[88,128]{1,0:T(8,128)S(1)} %add_add_fusion.2), channel_id=1, source_target_pairs={{0,1},{1,0},{2,3},{3,2},{4,5},{5,4},{6,7},{7,6},{8,9},{9,8},{10,11... | collective-permute-start | bytes 135176 | tf_op jit(solution)/shard_map/ppermute | solution.py:44
  131.5 2.6 %collective-permute-start.22 = (f32[88,128]{1,0:T(8,128)S(1)}, f32[88,128]{1,0:T(8,128)S(1)}, u32[]{:S(2)}, u32[]{:S(2)}) collective-permute-start(f32[88,128]{1,0:T(8,128)S(1)} %add_add_fusion.2), channel_id=1, source_target_pairs={{0,129},{1,128},{2,131},{3,130},{4,133},{5,132},{6,135},{7,134},{8... | collective-permute-start | bytes 135176 | tf_op jit(solution)/shard_map/ppermute | solution.py:44
  134.1 1.9 %collective-permute-start.29 = (bf16[8,64,128]{2,1,0:T(8,128)(2,1)S(1)}, bf16[8,64,128]{2,1,0:T(8,128)(2,1)S(1)}, u32[]{:S(2)}, u32[]{:S(2)}) collective-permute-start(bf16[8,64,128]{2,1,0:T(8,128)(2,1)S(1)} %get-tuple-element.62), channel_id=1, source_target_pairs={{0,8},{8,16},{16,24},{24,32},{32,40},{40,48},{48,56},{56,64},{64,7... | collective-permute-start | bytes 393224 | tf_op jit(solution)/shard_map/ppermute | solution.py:50
  136.0 5.8 %collective-permute-start.30 = (bf16[8,64,128]{2,1,0:T(8,128)(2,1)S(1)}, bf16[8,64,128]{2,1,0:T(8,128)(2,1)S(1)}, u32[]{:S(2)}, u32[]{:S(2)}) collective-permute-start(bf16[8,64,128]{2,1,0:T(8,128)(2,1)S(1)} %get-tuple-element.63), channel_id=1, source_target_pairs={{8,0},{16,8},{24,16},{32,24},{40,32},{48,40},{56,48},{64,56},{72,6... | collective-permute-start | bytes 393224 | tf_op jit(solution)/shard_map/ppermute | solution.py:50
  141.8 1.6 collective-permute-start.24
  143.4 3.1 %collective-permute-start.25 = (f32[88,128]{1,0:T(8,128)S(1)}, f32[88,128]{1,0:T(8,128)S(1)}, u32[]{:S(2)}, u32[]{:S(2)}) collective-permute-start(f32[88,128]{1,0:T(8,128)S(1)} %add_add_fusion.1), channel_id=1, source_target_pairs={{0,6},{1,7},{2,4},{3,5},{4,2},{5,3},{6,0},{7,1},{8,14},{9,15},{10,... | collective-permute-start | bytes 135176 | tf_op jit(solution)/shard_map/ppermute | solution.py:44
  147.1 5.5 %collective-permute-start.31 = (bf16[3,64,128]{2,1,0:T(8,128)(2,1)S(1)}, bf16[3,64,128]{2,1,0:T(8,128)(2,1)S(1)}, u32[]{:S(2)}, u32[]{:S(2)}) collective-permute-start(bf16[3,64,128]{2,1,0:T(8,128)(2,1)S(1)} %get-tuple-element.64), channel_id=1, source_target_pairs={{0,1},{1,2},{2,3},{3,4},{4,5},{5,6},{6,7},{8,9},{9,10},{10,11},{11... | collective-permute-start | bytes 147464 | tf_op jit(solution)/shard_map/ppermute | solution.py:50
  152.5 1.9 %collective-permute-start.32 = (bf16[3,64,128]{2,1,0:T(8,128)(2,1)S(1)}, bf16[3,64,128]{2,1,0:T(8,128)(2,1)S(1)}, u32[]{:S(2)}, u32[]{:S(2)}) collective-permute-start(bf16[3,64,128]{2,1,0:T(8,128)(2,1)S(1)} %get-tuple-element.65), channel_id=1, source_target_pairs={{1,0},{2,1},{3,2},{4,3},{5,4},{6,5},{7,6},{9,8},{10,9},{11,10},{12... | collective-permute-start | bytes 147464 | tf_op jit(solution)/shard_map/ppermute | solution.py:50
  154.7 1.8 %collective-permute-start.28 = (f32[88,128]{1,0:T(8,128)S(1)}, f32[88,128]{1,0:T(8,128)S(1)}, u32[]{:S(2)}, u32[]{:S(2)}) collective-permute-start(f32[88,128]{1,0:T(8,128)S(1)} %add_add_fusion.got0), channel_id=1, source_target_pairs={{0,24},{1,25},{2,26},{3,27},{4,28},{5,29},{6,30},{7,31},{8,16},{9,... | collective-permute-start | bytes 135176 | tf_op jit(solution)/shard_map/ppermute | solution.py:44
  156.5 4.4 %collective-permute-done.32.right = bf16[3,64,128]{2,1,0:T(8,128)(2,1)S(1)} collective-permute-done((bf16[3,64,128]{2,1,0:T(8,128)(2,1)S(1)}, bf16[3,64,128]{2,1,0:T(8,128)(2,1)S(1)}, u32[]{:S(2)}, u32[]{:S(2)}) %collective-permute-start.32) | collective-permute-done | bytes 49184 | tf_op jit(solution)/shard_map/ppermute | solution.py:50
  160.9 2.9 %shard_map.108 = bf16[32,64,128]{2,1,0:T(8,128)(2,1)} custom-call(f32[8,128]{1,0:T(8,128)S(1)} %add_add_fusion.4.count, bf16[32,64,128]{2,1,0:T(8,128)(2,1)S(1)} %get-tuple-element.61.own.low, bf16[8,64,128]{2,1,0:T(8,128)(2,1)S(1)} %collective-permute-done.29.up, bf16[8,64,128]{2,1,0:T(8,128)(2,1)S(1)} %collective-permute-done.30.down, ...), custom_call_target="tpu_custom_call" | custom-call | bytes 14400000 | tf_op jit(solution)/shard_map/pallas_call | solution.py:20
  163.8 0.8 shard_map.106
  (74 shorter events, 10.0 us)
Async XLA Ops:
  7.2 76.4 %all-gather.2.cloned.1.call-start = ((), (), s32[]{:S(2)}) async-start(), calls=%async_computation | async-start | bytes 1081344 | tf_op jit(solution)/shard_map/all_gather | solution.py:393
  7.2 1.0 copy-start.4
  8.3 0.7 copy-start.15
  9.7 49.3 %copy-start.9 = (s32[32,128]{1,0:T(8,128)}, s32[32,128]{1,0:T(8,128)S(1)}, u32[]{:S(2)}) copy-start(s32[32,128]{1,0:T(8,128)S(1)} %get-tuple-element.43.valid) | copy-start | bytes 49156
  10.3 10.0 %collective-permute-start = (bf16[8,64,128]{2,1,0:T(8,128)(2,1)S(1)}, bf16[8,64,128]{2,1,0:T(8,128)(2,1)S(1)}, u32[]{:S(2)}, u32[]{:S(2)}) collective-permute-start(bf16[8,64,128]{2,1,0:T(8,128)(2,1)S(1)} %get-tuple-element.38), channel_id=1, source_target_pairs={{0,8},{8,16},{16,24},{24,32},{32,40},{40,48},{48,56},{56,64},{64,7... | collective-permute-start | bytes 393224 | tf_op jit(solution)/shard_map/ppermute | solution.py:50
  12.3 9.9 %collective-permute-start.1 = (bf16[8,64,128]{2,1,0:T(8,128)(2,1)S(1)}, bf16[8,64,128]{2,1,0:T(8,128)(2,1)S(1)}, u32[]{:S(2)}, u32[]{:S(2)}) collective-permute-start(bf16[8,64,128]{2,1,0:T(8,128)(2,1)S(1)} %get-tuple-element.39), channel_id=1, source_target_pairs={{8,0},{16,8},{24,16},{32,24},{40,32},{48,40},{56,48},{64,56},{72,6... | collective-permute-start | bytes 393224 | tf_op jit(solution)/shard_map/ppermute | solution.py:50
  23.3 7.7 %collective-permute-start.2 = (bf16[3,64,128]{2,1,0:T(8,128)(2,1)S(1)}, bf16[3,64,128]{2,1,0:T(8,128)(2,1)S(1)}, u32[]{:S(2)}, u32[]{:S(2)}) collective-permute-start(bf16[3,64,128]{2,1,0:T(8,128)(2,1)S(1)} %get-tuple-element.40), channel_id=1, source_target_pairs={{0,1},{1,2},{2,3},{3,4},{4,5},{5,6},{6,7},{8,9},{9,10},{10,11},{11... | collective-permute-start | bytes 147464 | tf_op jit(solution)/shard_map/ppermute | solution.py:50
  27.0 8.4 %collective-permute-start.3 = (bf16[3,64,128]{2,1,0:T(8,128)(2,1)S(1)}, bf16[3,64,128]{2,1,0:T(8,128)(2,1)S(1)}, u32[]{:S(2)}, u32[]{:S(2)}) collective-permute-start(bf16[3,64,128]{2,1,0:T(8,128)(2,1)S(1)} %get-tuple-element.41), channel_id=1, source_target_pairs={{1,0},{2,1},{3,2},{4,3},{5,4},{6,5},{7,6},{9,8},{10,9},{11,10},{12... | collective-permute-start | bytes 147464 | tf_op jit(solution)/shard_map/ppermute | solution.py:50
  36.1 0.9 copy-start
  37.0 0.9 copy-start.6
  37.9 0.7 copy-start.7
  38.6 0.8 copy-start.12
  39.4 0.8 copy-start.14
  44.2 0.8 copy-start.2
  45.0 7.7 %collective-permute-start.9 = (bf16[528,128]{1,0:T(8,128)(2,1)S(1)}, bf16[528,128]{1,0:T(8,128)(2,1)}, u32[]{:S(2)}, u32[]{:S(2)}) collective-permute-start(bf16[528,128]{1,0:T(8,128)(2,1)S(1)} %get-tuple-element.47), channel_id=1, source_target_pairs={{0,2},{1,3},{2,0},{3,1},{4,6},{5,7},{6,4},{7,5},{8,10},{9,11},{10,... | collective-permute-start | bytes 405512 | tf_op jit(solution)/shard_map/ppermute | solution.py:44
  46.5 12.5 %collective-permute-start.4 = (bf16[528,128]{1,0:T(8,128)(2,1)S(1)}, bf16[528,128]{1,0:T(8,128)(2,1)}, u32[]{:S(2)}, u32[]{:S(2)}) collective-permute-start(bf16[528,128]{1,0:T(8,128)(2,1)S(1)} %get-tuple-element.44), channel_id=1, source_target_pairs={{0,6},{1,7},{2,4},{3,5},{4,2},{5,3},{6,0},{7,1},{8,14},{9,15},{10,... | collective-permute-start | bytes 405512 | tf_op jit(solution)/shard_map/ppermute | solution.py:44
  48.3 49.7 %collective-permute-start.12 = (bf16[528,128]{1,0:T(8,128)(2,1)}, bf16[528,128]{1,0:T(8,128)(2,1)S(1)}, u32[]{:S(2)}, u32[]{:S(2)}) collective-permute-start(bf16[528,128]{1,0:T(8,128)(2,1)} %get-tuple-element.48), channel_id=1, source_target_pairs={{0,16},{1,48},{2,80},{3,112},{4,144},{5,176},{6,208},{7,240},{8,24... | collective-permute-start | bytes 405512 | tf_op jit(solution)/shard_map/ppermute | solution.py:44
  49.6 49.7 %collective-permute-start.13 = (bf16[528,128]{1,0:T(8,128)(2,1)}, bf16[528,128]{1,0:T(8,128)(2,1)S(1)}, u32[]{:S(2)}, u32[]{:S(2)}) collective-permute-start(bf16[528,128]{1,0:T(8,128)(2,1)} %get-tuple-element.49), channel_id=1, source_target_pairs={{0,24},{1,56},{2,88},{3,120},{4,152},{5,184},{6,216},{7,248},{8,16... | collective-permute-start | bytes 405512 | tf_op jit(solution)/shard_map/ppermute | solution.py:44
  52.7 47.6 %collective-permute-start.10 = (bf16[528,128]{1,0:T(8,128)(2,1)}, bf16[528,128]{1,0:T(8,128)(2,1)S(1)}, u32[]{:S(2)}, u32[]{:S(2)}) collective-permute-start(bf16[528,128]{1,0:T(8,128)(2,1)} %collective-permute-done.9), channel_id=1, source_target_pairs={{0,64},{1,96},{2,0},{3,32},{4,192},{5,224},{6,128},{7,160},{8,72},... | collective-permute-start | bytes 405512 | tf_op jit(solution)/shard_map/ppermute | solution.py:44
  59.0 41.3 %collective-permute-start.11 = (bf16[528,128]{1,0:T(8,128)(2,1)}, bf16[528,128]{1,0:T(8,128)(2,1)S(1)}, u32[]{:S(2)}, u32[]{:S(2)}) collective-permute-start(bf16[528,128]{1,0:T(8,128)(2,1)} %collective-permute-done.4), channel_id=1, source_target_pairs={{0,200},{1,232},{2,136},{3,168},{4,72},{5,104},{6,8},{7,40},{8,192... | collective-permute-start | bytes 405512 | tf_op jit(solution)/shard_map/ppermute | solution.py:44
  84.5 12.3 %collective-permute-start.5 = (f32[8,128]{1,0:T(8,128)S(1)}, f32[8,128]{1,0:T(8,128)S(1)}, u32[]{:S(2)}, u32[]{:S(2)}) collective-permute-start(f32[8,128]{1,0:T(8,128)S(1)} %slice_reduce_fusion), channel_id=1, source_target_pairs={{0,1},{1,0},{2,3},{3,2},{4,5},{5,4},{6,7},{7,6},{8,9},{9,8},{10,11... | collective-permute-start | bytes 12296 | tf_op jit(solution)/shard_map/ppermute | solution.py:44
  96.8 11.7 %collective-permute-start.7 = (f32[8,128]{1,0:T(8,128)S(1)}, f32[8,128]{1,0:T(8,128)S(1)}, u32[]{:S(2)}, u32[]{:S(2)}) collective-permute-start(f32[8,128]{1,0:T(8,128)S(1)} %add.53), channel_id=1, source_target_pairs={{0,4},{1,5},{2,6},{3,7},{4,0},{5,1},{6,2},{7,3},{8,12},{9,13},{10,... | collective-permute-start | bytes 12296 | tf_op jit(solution)/shard_map/ppermute | solution.py:44
  98.0 10.5 %collective-permute-start.8 = (f32[8,128]{1,0:T(8,128)S(1)}, f32[8,128]{1,0:T(8,128)S(1)}, u32[]{:S(2)}, u32[]{:S(2)}) collective-permute-start(f32[8,128]{1,0:T(8,128)S(1)} %add.53), channel_id=1, source_target_pairs={{0,6},{1,7},{2,4},{3,5},{4,2},{5,3},{6,0},{7,1},{8,14},{9,15},{10,... | collective-permute-start | bytes 12296 | tf_op jit(solution)/shard_map/ppermute | solution.py:44
  99.3 9.2 %collective-permute-start.6 = (f32[8,128]{1,0:T(8,128)S(1)}, f32[8,128]{1,0:T(8,128)S(1)}, u32[]{:S(2)}, u32[]{:S(2)}) collective-permute-start(f32[8,128]{1,0:T(8,128)S(1)} %add.53), channel_id=1, source_target_pairs={{0,2},{1,3},{2,0},{3,1},{4,6},{5,7},{6,4},{7,5},{8,10},{9,11},{10,... | collective-permute-start | bytes 12296 | tf_op jit(solution)/shard_map/ppermute | solution.py:44
  100.3 1.0 copy-start.3
  101.3 0.7 copy-start.8
  102.1 0.7 copy-start.10
  102.8 0.7 copy-start.16
  108.5 52.4 %copy-start.1 = (bf16[3,3,64,64]{3,2,1,0:T(8,128)(2,1)S(1)}, bf16[3,3,64,64]{3,2,1,0:T(8,128)(2,1)}, u32[]{:S(2)}) copy-start(bf16[3,3,64,64]{3,2,1,0:T(8,128)(2,1)} %param.7) | copy-start | bytes 221188
  110.8 4.1 %collective-permute-start.15 = (f32[88,128]{1,0:T(8,128)S(1)}, f32[88,128]{1,0:T(8,128)S(1)}, u32[]{:S(2)}, u32[]{:S(2)}) collective-permute-start(f32[88,128]{1,0:T(8,128)S(1)} %get-tuple-element.58), channel_id=1, source_target_pairs={{0,16},{1,17},{2,18},{3,19},{4,20},{5,21},{6,22},{7,23},{8,24},{9,... | collective-permute-start | bytes 135176 | tf_op jit(solution)/shard_map/ppermute | solution.py:44
  112.6 3.5 %collective-permute-start.16 = (f32[88,128]{1,0:T(8,128)S(1)}, f32[88,128]{1,0:T(8,128)S(1)}, u32[]{:S(2)}, u32[]{:S(2)}) collective-permute-start(f32[88,128]{1,0:T(8,128)S(1)} %get-tuple-element.59), channel_id=1, source_target_pairs={{0,24},{1,25},{2,26},{3,27},{4,28},{5,29},{6,30},{7,31},{8,16},{9,... | collective-permute-start | bytes 135176 | tf_op jit(solution)/shard_map/ppermute | solution.py:44
  112.6 3.5 %collective-permute-start.14 = (f32[88,128]{1,0:T(8,128)S(1)}, f32[88,128]{1,0:T(8,128)S(1)}, u32[]{:S(2)}, u32[]{:S(2)}) collective-permute-start(f32[88,128]{1,0:T(8,128)S(1)} %get-tuple-element.57), channel_id=1, source_target_pairs={{0,8},{1,9},{2,10},{3,11},{4,12},{5,13},{6,14},{7,15},{8,0},{9,1},... | collective-permute-start | bytes 135176 | tf_op jit(solution)/shard_map/ppermute | solution.py:44
  116.1 9.0 %collective-permute-start.18 = (f32[88,128]{1,0:T(8,128)S(1)}, f32[88,128]{1,0:T(8,128)S(1)}, u32[]{:S(2)}, u32[]{:S(2)}) collective-permute-start(f32[88,128]{1,0:T(8,128)S(1)} %add_add_fusion.3), channel_id=1, source_target_pairs={{0,64},{1,65},{2,66},{3,67},{4,68},{5,69},{6,70},{7,71},{8,72},{9,... | collective-permute-start | bytes 135176 | tf_op jit(solution)/shard_map/ppermute | solution.py:44
  123.0 6.5 %collective-permute-start.19 = (f32[88,128]{1,0:T(8,128)S(1)}, f32[88,128]{1,0:T(8,128)S(1)}, u32[]{:S(2)}, u32[]{:S(2)}) collective-permute-start(f32[88,128]{1,0:T(8,128)S(1)} %add_add_fusion.3), channel_id=1, source_target_pairs={{0,96},{1,97},{2,98},{3,99},{4,100},{5,101},{6,102},{7,103},{8,104... | collective-permute-start | bytes 135176 | tf_op jit(solution)/shard_map/ppermute | solution.py:44
  124.7 4.9 %collective-permute-start.17 = (f32[88,128]{1,0:T(8,128)S(1)}, f32[88,128]{1,0:T(8,128)S(1)}, u32[]{:S(2)}, u32[]{:S(2)}) collective-permute-start(f32[88,128]{1,0:T(8,128)S(1)} %add_add_fusion.3), channel_id=1, source_target_pairs={{0,32},{1,33},{2,34},{3,35},{4,36},{5,37},{6,38},{7,39},{8,40},{9,... | collective-permute-start | bytes 135176 | tf_op jit(solution)/shard_map/ppermute | solution.py:44
  129.6 12.1 %collective-permute-start.21 = (f32[88,128]{1,0:T(8,128)S(1)}, f32[88,128]{1,0:T(8,128)S(1)}, u32[]{:S(2)}, u32[]{:S(2)}) collective-permute-start(f32[88,128]{1,0:T(8,128)S(1)} %add_add_fusion.2), channel_id=1, source_target_pairs={{0,1},{1,0},{2,3},{3,2},{4,5},{5,4},{6,7},{7,6},{8,9},{9,8},{10,11... | collective-permute-start | bytes 135176 | tf_op jit(solution)/shard_map/ppermute | solution.py:44
  131.5 10.3 %collective-permute-start.22 = (f32[88,128]{1,0:T(8,128)S(1)}, f32[88,128]{1,0:T(8,128)S(1)}, u32[]{:S(2)}, u32[]{:S(2)}) collective-permute-start(f32[88,128]{1,0:T(8,128)S(1)} %add_add_fusion.2), channel_id=1, source_target_pairs={{0,129},{1,128},{2,131},{3,130},{4,133},{5,132},{6,135},{7,134},{8... | collective-permute-start | bytes 135176 | tf_op jit(solution)/shard_map/ppermute | solution.py:44
  134.1 7.7 %collective-permute-start.20 = (f32[88,128]{1,0:T(8,128)S(1)}, f32[88,128]{1,0:T(8,128)S(1)}, u32[]{:S(2)}, u32[]{:S(2)}) collective-permute-start(f32[88,128]{1,0:T(8,128)S(1)} %add_add_fusion.2), channel_id=1, source_target_pairs={{0,128},{1,129},{2,130},{3,131},{4,132},{5,133},{6,134},{7,135},{8... | collective-permute-start | bytes 135176 | tf_op jit(solution)/shard_map/ppermute | solution.py:44
  134.1 12.5 %collective-permute-start.29 = (bf16[8,64,128]{2,1,0:T(8,128)(2,1)S(1)}, bf16[8,64,128]{2,1,0:T(8,128)(2,1)S(1)}, u32[]{:S(2)}, u32[]{:S(2)}) collective-permute-start(bf16[8,64,128]{2,1,0:T(8,128)(2,1)S(1)} %get-tuple-element.62), channel_id=1, source_target_pairs={{0,8},{8,16},{16,24},{24,32},{32,40},{40,48},{48,56},{56,64},{64,7... | collective-permute-start | bytes 393224 | tf_op jit(solution)/shard_map/ppermute | solution.py:50
  136.0 10.6 %collective-permute-start.30 = (bf16[8,64,128]{2,1,0:T(8,128)(2,1)S(1)}, bf16[8,64,128]{2,1,0:T(8,128)(2,1)S(1)}, u32[]{:S(2)}, u32[]{:S(2)}) collective-permute-start(bf16[8,64,128]{2,1,0:T(8,128)(2,1)S(1)} %get-tuple-element.63), channel_id=1, source_target_pairs={{8,0},{16,8},{24,16},{32,24},{40,32},{48,40},{56,48},{64,56},{72,6... | collective-permute-start | bytes 393224 | tf_op jit(solution)/shard_map/ppermute | solution.py:50
  141.8 12.6 %collective-permute-start.24 = (f32[88,128]{1,0:T(8,128)S(1)}, f32[88,128]{1,0:T(8,128)S(1)}, u32[]{:S(2)}, u32[]{:S(2)}) collective-permute-start(f32[88,128]{1,0:T(8,128)S(1)} %add_add_fusion.1), channel_id=1, source_target_pairs={{0,4},{1,5},{2,6},{3,7},{4,0},{5,1},{6,2},{7,3},{8,12},{9,13},{10,... | collective-permute-start | bytes 135176 | tf_op jit(solution)/shard_map/ppermute | solution.py:44
  143.4 11.0 %collective-permute-start.25 = (f32[88,128]{1,0:T(8,128)S(1)}, f32[88,128]{1,0:T(8,128)S(1)}, u32[]{:S(2)}, u32[]{:S(2)}) collective-permute-start(f32[88,128]{1,0:T(8,128)S(1)} %add_add_fusion.1), channel_id=1, source_target_pairs={{0,6},{1,7},{2,4},{3,5},{4,2},{5,3},{6,0},{7,1},{8,14},{9,15},{10,... | collective-permute-start | bytes 135176 | tf_op jit(solution)/shard_map/ppermute | solution.py:44
  146.6 7.9 %collective-permute-start.23 = (f32[88,128]{1,0:T(8,128)S(1)}, f32[88,128]{1,0:T(8,128)S(1)}, u32[]{:S(2)}, u32[]{:S(2)}) collective-permute-start(f32[88,128]{1,0:T(8,128)S(1)} %add_add_fusion.1), channel_id=1, source_target_pairs={{0,2},{1,3},{2,0},{3,1},{4,6},{5,7},{6,4},{7,5},{8,10},{9,11},{10,... | collective-permute-start | bytes 135176 | tf_op jit(solution)/shard_map/ppermute | solution.py:44
  147.1 9.4 %collective-permute-start.31 = (bf16[3,64,128]{2,1,0:T(8,128)(2,1)S(1)}, bf16[3,64,128]{2,1,0:T(8,128)(2,1)S(1)}, u32[]{:S(2)}, u32[]{:S(2)}) collective-permute-start(bf16[3,64,128]{2,1,0:T(8,128)(2,1)S(1)} %get-tuple-element.64), channel_id=1, source_target_pairs={{0,1},{1,2},{2,3},{3,4},{4,5},{5,6},{6,7},{8,9},{9,10},{10,11},{11... | collective-permute-start | bytes 147464 | tf_op jit(solution)/shard_map/ppermute | solution.py:50
  152.5 8.4 %collective-permute-start.32 = (bf16[3,64,128]{2,1,0:T(8,128)(2,1)S(1)}, bf16[3,64,128]{2,1,0:T(8,128)(2,1)S(1)}, u32[]{:S(2)}, u32[]{:S(2)}) collective-permute-start(bf16[3,64,128]{2,1,0:T(8,128)(2,1)S(1)} %get-tuple-element.65), channel_id=1, source_target_pairs={{1,0},{2,1},{3,2},{4,3},{5,4},{6,5},{7,6},{9,8},{10,9},{11,10},{12... | collective-permute-start | bytes 147464 | tf_op jit(solution)/shard_map/ppermute | solution.py:50
  154.5 9.3 %collective-permute-start.26 = (f32[88,128]{1,0:T(8,128)S(1)}, f32[88,128]{1,0:T(8,128)S(1)}, u32[]{:S(2)}, u32[]{:S(2)}) collective-permute-start(f32[88,128]{1,0:T(8,128)S(1)} %add_add_fusion.got0), channel_id=1, source_target_pairs={{0,8},{1,9},{2,10},{3,11},{4,12},{5,13},{6,14},{7,15},{8,0},{9,1},... | collective-permute-start | bytes 135176 | tf_op jit(solution)/shard_map/ppermute | solution.py:44
  154.6 9.2 %collective-permute-start.27 = (f32[88,128]{1,0:T(8,128)S(1)}, f32[88,128]{1,0:T(8,128)S(1)}, u32[]{:S(2)}, u32[]{:S(2)}) collective-permute-start(f32[88,128]{1,0:T(8,128)S(1)} %add_add_fusion.got0), channel_id=1, source_target_pairs={{0,16},{1,17},{2,18},{3,19},{4,20},{5,21},{6,22},{7,23},{8,24},{9,... | collective-permute-start | bytes 135176 | tf_op jit(solution)/shard_map/ppermute | solution.py:44
  154.7 9.1 %collective-permute-start.28 = (f32[88,128]{1,0:T(8,128)S(1)}, f32[88,128]{1,0:T(8,128)S(1)}, u32[]{:S(2)}, u32[]{:S(2)}) collective-permute-start(f32[88,128]{1,0:T(8,128)S(1)} %add_add_fusion.got0), channel_id=1, source_target_pairs={{0,24},{1,25},{2,26},{3,27},{4,28},{5,29},{6,30},{7,31},{8,16},{9,... | collective-permute-start | bytes 135176 | tf_op jit(solution)/shard_map/ppermute | solution.py:44
  (4 other events, 2.5 us)
Sparse Core Ops, SparseCore 0:
  10.4 73.0 all-gather.1

commit v7 on v5

--- a/solution.py
+++ b/solution.py
@@ -127,11 +127,11 @@
 
 def forward_kernel(
     place, act, up, down, left, right, feat, weight, labels, valid,
-    wide, mixed, pay0, pay1, pay2, pay3, turned,
+    wide, mixed, pay_near, pay_far, turned,
 ):
     rows, chans = act.shape[0], act.shape[1]
     part = rows
-    pays = (pay0, pay1, pay2, pay3)
+    length = pay_near.shape[0] // 2
     spread_columns(act, up, down, left, right, wide)
     kernel = weight[...].astype(F32).T.astype(BF16)
 
@@ -156,7 +156,8 @@
             base = j * LANES + (place[0] ^ s) * part
             low = turned[pl.ds(pl.multiple_of(base, 16), half), :]
             high = turned[pl.ds(pl.multiple_of(base + half, 16), half), :]
-            pays[s][pl.ds(pl.multiple_of(j * half, 16), half), :] = jnp.concatenate(
+            pay = pay_near if s < 2 else pay_far
+            pay[pl.ds(pl.multiple_of(s % 2 * length + j * half, 16), half), :] = jnp.concatenate(
                 [low, high], axis=1
             ).astype(BF16)
         return carry
@@ -165,17 +166,18 @@
 
 
 def softmax_kernel(
-    place, got0, got1, got2, got3, mixed, head, head_bias, labels, valid,
+    place, near, far, got1, got3, mixed, head, head_bias, labels, valid,
     grad, head_sum, bias_sum, loss_sum, cells, lab, lab_t, val, val_t, padded_head,
 ):
     rows, chans = mixed.shape[0], mixed.shape[1]
     bins, real = padded_head.shape[0], head.shape[0]
     half = rows // 2
     size = rows * half
-    for s, got in enumerate((got0, got1, got2, got3)):
+    length = size + half
+    for s, got in ((0, near), (2, far), (1, got1), (3, got3)):
         q = place[0] ^ s
         cells[pl.ds(pl.multiple_of(q * size, size), size), :] = got[:size, :].astype(F32)
-        cells[pl.ds(pl.multiple_of(4 * size + q * half, half), half), :] = got[size:, :].astype(F32)
+        cells[pl.ds(pl.multiple_of(4 * size + q * half, half), half), :] = got[size:length, :].astype(F32)
     notes = [cells[4 * size + q * half : 4 * size + (q + 1) * half, :] for q in range(4)]
     for top in range(2):
         base = top * 2 * rows
@@ -348,22 +350,20 @@
     return lambda m: lambda r, c: (r, c ^ (m << 1))
 
 
-def total_small(value):
-    for stage in range(4):
+def total_small(value, stages):
+    for stage in stages:
         to = partners(stage)
         value = (value + send(value, to(1))) + (send(value, to(2)) + send(value, to(3)))
     return value
 
 
-def mirrored(pays, parts):
-    got = []
-    for s, block in enumerate(pays):
-        bits = (2, 6, 0, 0)[s]
-        owner = lambda r, c: (parts * c + (r % parts ^ s), r // parts)
-        if bits:
-            block = send(block, lambda r, c: (r, c ^ bits))
-        got.append(send(block, lambda r, c: owner(r, c ^ bits)))
-    return got
+def mirrored(pay_near, pay_far, parts):
+    length = pay_near.shape[0] // 2
+    pay_near = send(pay_near, lambda r, c: (r, c ^ 2))
+    near = send(pay_near, lambda r, c: (parts * (c ^ 2) + r % parts, r // parts))
+    far = send(pay_far, lambda r, c: (parts * c + (r % parts ^ 2), r // parts))
+    mate = lambda r, c: (r ^ 1, c)
+    return pay_near, (near, far, send(near[length:], mate), send(far[length:], mate))
 
 
 def total_quarters(quarters):
@@ -394,19 +394,21 @@
         micros=1,
     )
     around = borders(act, top, bottom)
-    count = total_small(counted)
-    count, act = lax.optimization_barrier((count, act))
+    counted = total_small(counted, (1, 2))
+    counted, act = lax.optimization_barrier((counted, act))
     length = (rows + 1) * rows // 2
-    wide, mixed, *pays = run(
+    wide, mixed, pay_near, pay_far = run(
         forward_kernel,
         [shape((rows + 2 * STEP, 3 * chans, LANES), BF16), shape(tile, BF16)]
-        + [shape((length, LANES), BF16)] * 4,
+        + [shape((2 * length, LANES), BF16)] * 2,
         (place, act, *around, feat, weight, labels, valid),
         scratch=[pltpu.VMEM(((rows + 1) * LANES, chans), F32)],
         scalars=1,
         micros=5,
     )
-    got = mirrored(pays, parts)
+    passed, got = mirrored(pay_near, pay_far, parts)
+    _, counted = lax.optimization_barrier((passed, counted))
+    count = total_small(counted, (3, 0))
     grad, head_sum, bias_sum, loss_sum = run(
         softmax_kernel,
         [

time: 143 us -> 133 us (0.930)
  waiting for transfers between devices: 38.2 us -> 30.4 us
  starting transfers between devices: 85.1 us -> 82.4 us
    ppermute x33 -> x32, waiting for transfers between devices: 29.9 us -> 22.7 us  [send(): return lax.ppermute(block, GRID, pairs)]
    ppermute x33 -> x32, starting transfers between devices: 55.1 us -> 52.4 us  [send(): return lax.ppermute(block, GRID, pairs)]
    unnamed x14 -> x16, local copies, waits for them, and re-layouts: 3.4 us -> 3.4 us
  transfers between devices with their start and end apart: 41 -> 40, of which waited for: 12 -> 12; matrix products, arithmetic and copies ran while one was open for 0% -> 0% of each run, Pallas kernels for 3% -> 3%
where the time goes in v7:
time: 133 us
  starting transfers between devices  82.4 us (62%)
  waiting for transfers between devices  30.4 us (23%)
  Pallas kernels  15.2 us (11%)
  local copies, waits for them, and re-layouts  3.42 us (3%)
    ppermute x32, starting transfers between devices, send(): return lax.ppermute(block, GRID, pairs)  52.4 us
    ppermute x8, starting transfers between devices, shifted(): lax.ppermute(block, axis, pairs if forward else [(b, a) for a, b in pairs])  30 us
    ppermute x32, waiting for transfers between devices, send(): return lax.ppermute(block, GRID, pairs)  22.7 us
    pallas_call x8, Pallas kernels, run(): pl.pallas_call(body, out_shape=outs, in_specs=[SMEM] * scalars + [VMEM] *...  15.2 us
    ppermute x8, waiting for transfers between devices, shifted(): lax.ppermute(block, axis, pairs if forward else [(b, a) for a, b in pairs])  7.72 us
    unnamed x16, local copies, waits for them, and re-layouts  3.4 us
  transfers between devices with their start and end apart: 40, of which 12 were waited for; matrix products, arithmetic and copies ran while one was open for 0% of the time, Pallas kernels for 3%

profile of v7, /device:TPU:24, one launch (start us, length us, event | category | flops | bytes accessed | tf_op | source)
XLA Modules:
  0.0 132.6 jit_solution(10896674088658894629)
XLA Ops:
  0.7 1.0 copy-done.2
  1.7 0.7 copy-done.5
  2.4 0.7 shard_map.101
  3.1 6.3 %collective-permute-start.2 = (f32[8,128]{1,0:T(8,128)S(1)}, f32[8,128]{1,0:T(8,128)S(1)}, u32[]{:S(2)}, u32[]{:S(2)}) collective-permute-start(f32[8,128]{1,0:T(8,128)S(1)} %get-tuple-element.37), channel_id=1, source_target_pairs={{0,96},{1,97},{2,98},{3,99},{4,100},{5,101},{6,102},{7,103},{8,104... | collective-permute-start | bytes 12296 | tf_op jit(solution)/shard_map/ppermute | solution.py:43
  9.4 1.0 collective-permute-start.1
  10.4 1.5 %collective-permute-start = (f32[8,128]{1,0:T(8,128)S(1)}, f32[8,128]{1,0:T(8,128)S(1)}, u32[]{:S(2)}, u32[]{:S(2)}) collective-permute-start(f32[8,128]{1,0:T(8,128)S(1)} %get-tuple-element.37), channel_id=1, source_target_pairs={{0,32},{1,33},{2,34},{3,35},{4,36},{5,37},{6,38},{7,39},{8,40},{9,... | collective-permute-start | bytes 12296 | tf_op jit(solution)/shard_map/ppermute | solution.py:43
  11.9 1.9 %collective-permute-start.6 = (bf16[8,64,128]{2,1,0:T(8,128)(2,1)S(1)}, bf16[8,64,128]{2,1,0:T(8,128)(2,1)S(1)}, u32[]{:S(2)}, u32[]{:S(2)}) collective-permute-start(bf16[8,64,128]{2,1,0:T(8,128)(2,1)S(1)} %get-tuple-element.40), channel_id=1, source_target_pairs={{0,8},{8,16},{16,24},{24,32},{32,40},{40,48},{48,56},{56,64},{64,7... | collective-permute-start | bytes 393224 | tf_op jit(solution)/shard_map/ppermute | solution.py:49
  13.8 5.8 %collective-permute-start.7 = (bf16[8,64,128]{2,1,0:T(8,128)(2,1)S(1)}, bf16[8,64,128]{2,1,0:T(8,128)(2,1)S(1)}, u32[]{:S(2)}, u32[]{:S(2)}) collective-permute-start(bf16[8,64,128]{2,1,0:T(8,128)(2,1)S(1)} %get-tuple-element.41), channel_id=1, source_target_pairs={{8,0},{16,8},{24,16},{32,24},{40,32},{48,40},{56,48},{64,56},{72,6... | collective-permute-start | bytes 393224 | tf_op jit(solution)/shard_map/ppermute | solution.py:49
  19.7 1.3 collective-permute-start.4
  21.1 2.8 %collective-permute-start.3 = (f32[8,128]{1,0:T(8,128)S(1)}, f32[8,128]{1,0:T(8,128)S(1)}, u32[]{:S(2)}, u32[]{:S(2)}) collective-permute-start(f32[8,128]{1,0:T(8,128)S(1)} %add_add_fusion.7), channel_id=1, source_target_pairs={{0,128},{1,129},{2,130},{3,131},{4,132},{5,133},{6,134},{7,135},{8... | collective-permute-start | bytes 12296 | tf_op jit(solution)/shard_map/ppermute | solution.py:43
  24.3 4.1 %collective-permute-start.8 = (bf16[3,64,128]{2,1,0:T(8,128)(2,1)S(1)}, bf16[3,64,128]{2,1,0:T(8,128)(2,1)S(1)}, u32[]{:S(2)}, u32[]{:S(2)}) collective-permute-start(bf16[3,64,128]{2,1,0:T(8,128)(2,1)S(1)} %get-tuple-element.42), channel_id=1, source_target_pairs={{0,1},{1,2},{2,3},{3,4},{4,5},{5,6},{6,7},{8,9},{9,10},{10,11},{11... | collective-permute-start | bytes 147464 | tf_op jit(solution)/shard_map/ppermute | solution.py:49
  28.4 3.3 %collective-permute-start.9 = (bf16[3,64,128]{2,1,0:T(8,128)(2,1)S(1)}, bf16[3,64,128]{2,1,0:T(8,128)(2,1)S(1)}, u32[]{:S(2)}, u32[]{:S(2)}) collective-permute-start(bf16[3,64,128]{2,1,0:T(8,128)(2,1)S(1)} %get-tuple-element.43), channel_id=1, source_target_pairs={{1,0},{2,1},{3,2},{4,3},{5,4},{6,5},{7,6},{9,8},{10,9},{11,10},{12... | collective-permute-start | bytes 147464 | tf_op jit(solution)/shard_map/ppermute | solution.py:49
  31.8 5.0 %collective-permute-done.9.right = bf16[3,64,128]{2,1,0:T(8,128)(2,1)S(1)} collective-permute-done((bf16[3,64,128]{2,1,0:T(8,128)(2,1)S(1)}, bf16[3,64,128]{2,1,0:T(8,128)(2,1)S(1)}, u32[]{:S(2)}, u32[]{:S(2)}) %collective-permute-start.9) | collective-permute-done | bytes 49184 | tf_op jit(solution)/shard_map/ppermute | solution.py:49
  36.7 0.9 copy-done
  37.7 0.7 copy-done.3
  38.4 3.3 %shard_map.103 = (bf16[48,192,128]{2,1,0:T(8,128)(2,1)S(1)}, bf16[32,64,128]{2,1,0:T(8,128)(2,1)S(1)}, bf16[1056,128]{1,0:T(8,128)(2,1)S(1)}, bf16[1056,128]{1,0:T(8,128)(2,1)S(1)}) custom-call(s32[1]{0:T(128)} %bitcast.place, bf16[32,64,128]{2,1,0:T(8,128)(2,1)S(1)} %get-tuple-element.39.own.act, bf16[8,64,128]{2,1,0:T(8,128)(2,1)S(1)} %collective-permute-done.6.up, ...), custom_call_target="tpu_custom_call" | custom-call | bytes 18000000 | tf_op jit(solution)/shard_map/pallas_call | solution.py:19
  41.7 1.6 %collective-permute-start.10 = (bf16[1056,128]{1,0:T(8,128)(2,1)S(1)}, bf16[1056,128]{1,0:T(8,128)(2,1)S(1)}, u32[]{:S(2)}, u32[]{:S(2)}) collective-permute-start(bf16[1056,128]{1,0:T(8,128)(2,1)S(1)} %get-tuple-element.46), channel_id=1, source_target_pairs={{0,2},{1,3},{2,0},{3,1},{4,6},{5,7},{6,4},{7,5},{8,10},{9,11},{10,... | collective-permute-start | bytes 811016 | tf_op jit(solution)/shard_map/ppermute | solution.py:43
  43.3 2.2 %collective-permute-start.18 = (bf16[1056,128]{1,0:T(8,128)(2,1)S(1)}, bf16[1056,128]{1,0:T(8,128)(2,1)S(1)}, u32[]{:S(2)}, u32[]{:S(2)}) collective-permute-start(bf16[1056,128]{1,0:T(8,128)(2,1)S(1)} %get-tuple-element.49), channel_id=1, source_target_pairs={{0,16},{1,48},{2,80},{3,112},{4,144},{5,176},{6,208},{7,240},{8,24... | collective-permute-start | bytes 811016 | tf_op jit(solution)/shard_map/ppermute | solution.py:43
  45.5 2.8 %collective-permute-done.10 = bf16[1056,128]{1,0:T(8,128)(2,1)S(1)} collective-permute-done((bf16[1056,128]{1,0:T(8,128)(2,1)S(1)}, bf16[1056,128]{1,0:T(8,128)(2,1)S(1)}, u32[]{:S(2)}, u32[]{:S(2)}) %collective-permute-start.10) | collective-permute-done | bytes 270368 | tf_op jit(solution)/shard_map/ppermute | solution.py:43
  48.2 4.3 %collective-permute-start.17 = (bf16[1056,128]{1,0:T(8,128)(2,1)S(1)}, bf16[1056,128]{1,0:T(8,128)(2,1)S(1)}, u32[]{:S(2)}, u32[]{:S(2)}) collective-permute-start(bf16[1056,128]{1,0:T(8,128)(2,1)S(1)} %collective-permute-done.10), channel_id=1, source_target_pairs={{0,64},{1,96},{2,0},{3,32},{4,192},{5,224},{6,128},{7,160},{8,72},... | collective-permute-start | bytes 811016 | tf_op jit(solution)/shard_map/ppermute | solution.py:43
  52.5 0.6 collective-permute-start.12
  53.1 3.5 %collective-permute-start.11 = (f32[8,128]{1,0:T(8,128)S(1)}, f32[8,128]{1,0:T(8,128)S(1)}, u32[]{:S(2)}, u32[]{:S(2)}) collective-permute-start(f32[8,128]{1,0:T(8,128)S(1)} %add_add_fusion.6), channel_id=1, source_target_pairs={{0,2},{1,3},{2,0},{3,1},{4,6},{5,7},{6,4},{7,5},{8,10},{9,11},{10,... | collective-permute-start | bytes 12296 | tf_op jit(solution)/shard_map/ppermute | solution.py:43
  56.6 0.7 collective-permute-done.13
  57.7 0.6 collective-permute-done.11
  58.5 2.9 %collective-permute-start.15 = (f32[8,128]{1,0:T(8,128)S(1)}, f32[8,128]{1,0:T(8,128)S(1)}, u32[]{:S(2)}, u32[]{:S(2)}) collective-permute-start(f32[8,128]{1,0:T(8,128)S(1)} %add_add_fusion.5), channel_id=1, source_target_pairs={{0,16},{1,17},{2,18},{3,19},{4,20},{5,21},{6,22},{7,23},{8,24},{9,... | collective-permute-start | bytes 12296 | tf_op jit(solution)/shard_map/ppermute | solution.py:43
  61.4 0.6 collective-permute-start.20
  62.0 8.9 %collective-permute-done.17.near = bf16[1056,128]{1,0:T(8,128)(2,1)S(1)} collective-permute-done((bf16[1056,128]{1,0:T(8,128)(2,1)S(1)}, bf16[1056,128]{1,0:T(8,128)(2,1)S(1)}, u32[]{:S(2)}, u32[]{:S(2)}) %collective-permute-start.17) | collective-permute-done | bytes 270368 | tf_op jit(solution)/shard_map/ppermute | solution.py:43
  71.2 1.3 collective-permute-done.19.got1
  72.5 4.3 %shard_map.104 = (f32[32,64,128]{2,1,0:T(8,128)S(1)}, f32[120,64]{1,0:T(8,128)S(1)}, f32[40,128]{1,0:T(8,128)S(1)}, f32[1,128]{1,0:T(1,128)S(1)}) custom-call(s32[1]{0:T(128)} %bitcast.place, bf16[1056,128]{1,0:T(8,128)(2,1)S(1)} %collective-permute-done.17.near, bf16[1056,128]{1,0:T(8,128)(2,1)S(1)} %collective-permute-done.18.far, ...), custom_call_target="tpu_custom_call" | custom-call | bytes 18000000 | tf_op jit(solution)/shard_map/pallas_call | solution.py:19
  76.8 2.3 %shard_map.105 = (bf16[32,64,128]{2,1,0:T(8,128)(2,1)S(1)}, bf16[8,64,128]{2,1,0:T(8,128)(2,1)S(1)}, bf16[8,64,128]{2,1,0:T(8,128)(2,1)S(1)}, f32[88,128]{1,0:T(...) custom-call(s32[1]{0:T(128)} %bitcast.place, f32[8,128]{1,0:T(8,128)S(1)} %add_add_fusion.4.count, ...), custom_call_target="tpu_custom_call" | custom-call | bytes 10800000 | tf_op jit(solution)/shard_map/pallas_call | solution.py:19
  79.3 1.7 %collective-permute-start.23 = (f32[88,128]{1,0:T(8,128)S(1)}, f32[88,128]{1,0:T(8,128)S(1)}, u32[]{:S(2)}, u32[]{:S(2)}) collective-permute-start(f32[88,128]{1,0:T(8,128)S(1)} %get-tuple-element.59), channel_id=1, source_target_pairs={{0,24},{1,25},{2,26},{3,27},{4,28},{5,29},{6,30},{7,31},{8,16},{9,... | collective-permute-start | bytes 135176 | tf_op jit(solution)/shard_map/ppermute | solution.py:43
  81.1 2.7 %collective-permute-done.22 = f32[88,128]{1,0:T(8,128)S(1)} collective-permute-done((f32[88,128]{1,0:T(8,128)S(1)}, f32[88,128]{1,0:T(8,128)S(1)}, u32[]{:S(2)}, u32[]{:S(2)}) %collective-permute-start.22) | collective-permute-done | bytes 45088 | tf_op jit(solution)/shard_map/ppermute | solution.py:43
  83.8 6.2 %collective-permute-start.26 = (f32[88,128]{1,0:T(8,128)S(1)}, f32[88,128]{1,0:T(8,128)S(1)}, u32[]{:S(2)}, u32[]{:S(2)}) collective-permute-start(f32[88,128]{1,0:T(8,128)S(1)} %add_add_fusion.3), channel_id=1, source_target_pairs={{0,96},{1,97},{2,98},{3,99},{4,100},{5,101},{6,102},{7,103},{8,104... | collective-permute-start | bytes 135176 | tf_op jit(solution)/shard_map/ppermute | solution.py:43
  89.9 4.8 %collective-permute-start.25 = (f32[88,128]{1,0:T(8,128)S(1)}, f32[88,128]{1,0:T(8,128)S(1)}, u32[]{:S(2)}, u32[]{:S(2)}) collective-permute-start(f32[88,128]{1,0:T(8,128)S(1)} %add_add_fusion.3), channel_id=1, source_target_pairs={{0,64},{1,65},{2,66},{3,67},{4,68},{5,69},{6,70},{7,71},{8,72},{9,... | collective-permute-start | bytes 135176 | tf_op jit(solution)/shard_map/ppermute | solution.py:43
  94.8 3.8 %collective-permute-done.25 = f32[88,128]{1,0:T(8,128)S(1)} collective-permute-done((f32[88,128]{1,0:T(8,128)S(1)}, f32[88,128]{1,0:T(8,128)S(1)}, u32[]{:S(2)}, u32[]{:S(2)}) %collective-permute-start.25) | collective-permute-done | bytes 45088 | tf_op jit(solution)/shard_map/ppermute | solution.py:43
  98.5 1.7 %collective-permute-done.24 = f32[88,128]{1,0:T(8,128)S(1)} collective-permute-done((f32[88,128]{1,0:T(8,128)S(1)}, f32[88,128]{1,0:T(8,128)S(1)}, u32[]{:S(2)}, u32[]{:S(2)}) %collective-permute-start.24) | collective-permute-done | bytes 45088 | tf_op jit(solution)/shard_map/ppermute | solution.py:43
  100.3 4.1 %collective-permute-start.28 = (f32[88,128]{1,0:T(8,128)S(1)}, f32[88,128]{1,0:T(8,128)S(1)}, u32[]{:S(2)}, u32[]{:S(2)}) collective-permute-start(f32[88,128]{1,0:T(8,128)S(1)} %add_add_fusion.2), channel_id=1, source_target_pairs={{0,1},{1,0},{2,3},{3,2},{4,5},{5,4},{6,7},{7,6},{8,9},{9,8},{10,11... | collective-permute-start | bytes 135176 | tf_op jit(solution)/shard_map/ppermute | solution.py:43
  104.5 1.9 %collective-permute-start.36 = (bf16[8,64,128]{2,1,0:T(8,128)(2,1)S(1)}, bf16[8,64,128]{2,1,0:T(8,128)(2,1)S(1)}, u32[]{:S(2)}, u32[]{:S(2)}) collective-permute-start(bf16[8,64,128]{2,1,0:T(8,128)(2,1)S(1)} %get-tuple-element.62), channel_id=1, source_target_pairs={{0,8},{8,16},{16,24},{24,32},{32,40},{40,48},{48,56},{56,64},{64,7... | collective-permute-start | bytes 393224 | tf_op jit(solution)/shard_map/ppermute | solution.py:49
  106.4 5.8 %collective-permute-start.37 = (bf16[8,64,128]{2,1,0:T(8,128)(2,1)S(1)}, bf16[8,64,128]{2,1,0:T(8,128)(2,1)S(1)}, u32[]{:S(2)}, u32[]{:S(2)}) collective-permute-start(bf16[8,64,128]{2,1,0:T(8,128)(2,1)S(1)} %get-tuple-element.63), channel_id=1, source_target_pairs={{8,0},{16,8},{24,16},{32,24},{40,32},{48,40},{56,48},{64,56},{72,6... | collective-permute-start | bytes 393224 | tf_op jit(solution)/shard_map/ppermute | solution.py:49
  112.2 3.0 %collective-permute-start.32 = (f32[88,128]{1,0:T(8,128)S(1)}, f32[88,128]{1,0:T(8,128)S(1)}, u32[]{:S(2)}, u32[]{:S(2)}) collective-permute-start(f32[88,128]{1,0:T(8,128)S(1)} %add_add_fusion.1), channel_id=1, source_target_pairs={{0,6},{1,7},{2,4},{3,5},{4,2},{5,3},{6,0},{7,1},{8,14},{9,15},{10,... | collective-permute-start | bytes 135176 | tf_op jit(solution)/shard_map/ppermute | solution.py:43
  115.2 1.2 collective-permute-start.30
  116.4 0.5 shard_map.107
  116.9 3.6 %collective-permute-start.38 = (bf16[3,64,128]{2,1,0:T(8,128)(2,1)S(1)}, bf16[3,64,128]{2,1,0:T(8,128)(2,1)S(1)}, u32[]{:S(2)}, u32[]{:S(2)}) collective-permute-start(bf16[3,64,128]{2,1,0:T(8,128)(2,1)S(1)} %get-tuple-element.64), channel_id=1, source_target_pairs={{0,1},{1,2},{2,3},{3,4},{4,5},{5,6},{6,7},{8,9},{9,10},{10,11},{11... | collective-permute-start | bytes 147464 | tf_op jit(solution)/shard_map/ppermute | solution.py:49
  120.5 3.7 %collective-permute-start.39 = (bf16[3,64,128]{2,1,0:T(8,128)(2,1)S(1)}, bf16[3,64,128]{2,1,0:T(8,128)(2,1)S(1)}, u32[]{:S(2)}, u32[]{:S(2)}) collective-permute-start(bf16[3,64,128]{2,1,0:T(8,128)(2,1)S(1)} %get-tuple-element.65), channel_id=1, source_target_pairs={{1,0},{2,1},{3,2},{4,3},{5,4},{6,5},{7,6},{9,8},{10,9},{11,10},{12... | collective-permute-start | bytes 147464 | tf_op jit(solution)/shard_map/ppermute | solution.py:49
  124.5 1.7 %collective-permute-start.33 = (f32[88,128]{1,0:T(8,128)S(1)}, f32[88,128]{1,0:T(8,128)S(1)}, u32[]{:S(2)}, u32[]{:S(2)}) collective-permute-start(f32[88,128]{1,0:T(8,128)S(1)} %add_add_fusion.got0), channel_id=1, source_target_pairs={{0,8},{1,9},{2,10},{3,11},{4,12},{5,13},{6,14},{7,15},{8,0},{9,1},... | collective-permute-start | bytes 135176 | tf_op jit(solution)/shard_map/ppermute | solution.py:43
  126.2 2.6 %collective-permute-done.39.right = bf16[3,64,128]{2,1,0:T(8,128)(2,1)S(1)} collective-permute-done((bf16[3,64,128]{2,1,0:T(8,128)(2,1)S(1)}, bf16[3,64,128]{2,1,0:T(8,128)(2,1)S(1)}, u32[]{:S(2)}, u32[]{:S(2)}) %collective-permute-start.39) | collective-permute-done | bytes 49184 | tf_op jit(solution)/shard_map/ppermute | solution.py:49
  128.9 2.9 %shard_map.108 = bf16[32,64,128]{2,1,0:T(8,128)(2,1)} custom-call(f32[8,128]{1,0:T(8,128)S(1)} %add_add_fusion.4.count, bf16[32,64,128]{2,1,0:T(8,128)(2,1)S(1)} %get-tuple-element.61.own.low, bf16[8,64,128]{2,1,0:T(8,128)(2,1)S(1)} %collective-permute-done.36.up, bf16[8,64,128]{2,1,0:T(8,128)(2,1)S(1)} %collective-permute-done.37.down, ...), custom_call_target="tpu_custom_call" | custom-call | bytes 14400000 | tf_op jit(solution)/shard_map/pallas_call | solution.py:19
  131.8 0.8 shard_map.106
  (66 shorter events, 2.1 us)
Async XLA Ops:
  0.6 71.8 %copy-start.7 = (f32[37]{0:T(128)S(1)}, f32[37]{0:T(128)}, u32[]{:S(2)}) copy-start(f32[37]{0:T(128)} %param.9) | copy-start | bytes 448
  0.6 1.0 copy-start.2
  1.7 0.7 copy-start.5
  2.4 70.1 %copy-start.4 = (s32[32,128]{1,0:T(8,128)S(1)}, s32[32,128]{1,0:T(8,128)}, u32[]{:S(2)}) copy-start(s32[32,128]{1,0:T(8,128)} %labels.3) | copy-start | bytes 49156
  2.4 70.1 %copy-start.6 = (bf16[64,37]{0,1:T(8,128)(2,1)S(1)}, bf16[64,37]{0,1:T(8,128)(2,1)}, u32[]{:S(2)}) copy-start(bf16[64,37]{0,1:T(8,128)(2,1)} %param.8) | copy-start | bytes 14212
  3.1 16.5 %collective-permute-start.2 = (f32[8,128]{1,0:T(8,128)S(1)}, f32[8,128]{1,0:T(8,128)S(1)}, u32[]{:S(2)}, u32[]{:S(2)}) collective-permute-start(f32[8,128]{1,0:T(8,128)S(1)} %get-tuple-element.37), channel_id=1, source_target_pairs={{0,96},{1,97},{2,98},{3,99},{4,100},{5,101},{6,102},{7,103},{8,104... | collective-permute-start | bytes 12296 | tf_op jit(solution)/shard_map/ppermute | solution.py:43
  9.4 10.2 %collective-permute-start.1 = (f32[8,128]{1,0:T(8,128)S(1)}, f32[8,128]{1,0:T(8,128)S(1)}, u32[]{:S(2)}, u32[]{:S(2)}) collective-permute-start(f32[8,128]{1,0:T(8,128)S(1)} %get-tuple-element.37), channel_id=1, source_target_pairs={{0,64},{1,65},{2,66},{3,67},{4,68},{5,69},{6,70},{7,71},{8,72},{9,... | collective-permute-start | bytes 12296 | tf_op jit(solution)/shard_map/ppermute | solution.py:43
  10.4 9.2 %collective-permute-start = (f32[8,128]{1,0:T(8,128)S(1)}, f32[8,128]{1,0:T(8,128)S(1)}, u32[]{:S(2)}, u32[]{:S(2)}) collective-permute-start(f32[8,128]{1,0:T(8,128)S(1)} %get-tuple-element.37), channel_id=1, source_target_pairs={{0,32},{1,33},{2,34},{3,35},{4,36},{5,37},{6,38},{7,39},{8,40},{9,... | collective-permute-start | bytes 12296 | tf_op jit(solution)/shard_map/ppermute | solution.py:43
  11.9 11.9 %collective-permute-start.6 = (bf16[8,64,128]{2,1,0:T(8,128)(2,1)S(1)}, bf16[8,64,128]{2,1,0:T(8,128)(2,1)S(1)}, u32[]{:S(2)}, u32[]{:S(2)}) collective-permute-start(bf16[8,64,128]{2,1,0:T(8,128)(2,1)S(1)} %get-tuple-element.40), channel_id=1, source_target_pairs={{0,8},{8,16},{16,24},{24,32},{32,40},{40,48},{48,56},{56,64},{64,7... | collective-permute-start | bytes 393224 | tf_op jit(solution)/shard_map/ppermute | solution.py:49
  13.8 10.0 %collective-permute-start.7 = (bf16[8,64,128]{2,1,0:T(8,128)(2,1)S(1)}, bf16[8,64,128]{2,1,0:T(8,128)(2,1)S(1)}, u32[]{:S(2)}, u32[]{:S(2)}) collective-permute-start(bf16[8,64,128]{2,1,0:T(8,128)(2,1)S(1)} %get-tuple-element.41), channel_id=1, source_target_pairs={{8,0},{16,8},{24,16},{32,24},{40,32},{48,40},{56,48},{64,56},{72,6... | collective-permute-start | bytes 393224 | tf_op jit(solution)/shard_map/ppermute | solution.py:49
  19.6 12.0 %collective-permute-start.5 = (f32[8,128]{1,0:T(8,128)S(1)}, f32[8,128]{1,0:T(8,128)S(1)}, u32[]{:S(2)}, u32[]{:S(2)}) collective-permute-start(f32[8,128]{1,0:T(8,128)S(1)} %add_add_fusion.7), channel_id=1, source_target_pairs={{0,129},{1,128},{2,131},{3,130},{4,133},{5,132},{6,135},{7,134},{8... | collective-permute-start | bytes 12296 | tf_op jit(solution)/shard_map/ppermute | solution.py:43
  19.7 11.9 %collective-permute-start.4 = (f32[8,128]{1,0:T(8,128)S(1)}, f32[8,128]{1,0:T(8,128)S(1)}, u32[]{:S(2)}, u32[]{:S(2)}) collective-permute-start(f32[8,128]{1,0:T(8,128)S(1)} %add_add_fusion.7), channel_id=1, source_target_pairs={{0,1},{1,0},{2,3},{3,2},{4,5},{5,4},{6,7},{7,6},{8,9},{9,8},{10,11... | collective-permute-start | bytes 12296 | tf_op jit(solution)/shard_map/ppermute | solution.py:43
  21.1 10.6 %collective-permute-start.3 = (f32[8,128]{1,0:T(8,128)S(1)}, f32[8,128]{1,0:T(8,128)S(1)}, u32[]{:S(2)}, u32[]{:S(2)}) collective-permute-start(f32[8,128]{1,0:T(8,128)S(1)} %add_add_fusion.7), channel_id=1, source_target_pairs={{0,128},{1,129},{2,130},{3,131},{4,132},{5,133},{6,134},{7,135},{8... | collective-permute-start | bytes 12296 | tf_op jit(solution)/shard_map/ppermute | solution.py:43
  24.3 7.5 %collective-permute-start.8 = (bf16[3,64,128]{2,1,0:T(8,128)(2,1)S(1)}, bf16[3,64,128]{2,1,0:T(8,128)(2,1)S(1)}, u32[]{:S(2)}, u32[]{:S(2)}) collective-permute-start(bf16[3,64,128]{2,1,0:T(8,128)(2,1)S(1)} %get-tuple-element.42), channel_id=1, source_target_pairs={{0,1},{1,2},{2,3},{3,4},{4,5},{5,6},{6,7},{8,9},{9,10},{10,11},{11... | collective-permute-start | bytes 147464 | tf_op jit(solution)/shard_map/ppermute | solution.py:49
  28.4 8.4 %collective-permute-start.9 = (bf16[3,64,128]{2,1,0:T(8,128)(2,1)S(1)}, bf16[3,64,128]{2,1,0:T(8,128)(2,1)S(1)}, u32[]{:S(2)}, u32[]{:S(2)}) collective-permute-start(bf16[3,64,128]{2,1,0:T(8,128)(2,1)S(1)} %get-tuple-element.43), channel_id=1, source_target_pairs={{1,0},{2,1},{3,2},{4,3},{5,4},{6,5},{7,6},{9,8},{10,9},{11,10},{12... | collective-permute-start | bytes 147464 | tf_op jit(solution)/shard_map/ppermute | solution.py:49
  36.7 0.9 copy-start
  37.7 0.7 copy-start.3
  41.7 6.5 %collective-permute-start.10 = (bf16[1056,128]{1,0:T(8,128)(2,1)S(1)}, bf16[1056,128]{1,0:T(8,128)(2,1)S(1)}, u32[]{:S(2)}, u32[]{:S(2)}) collective-permute-start(bf16[1056,128]{1,0:T(8,128)(2,1)S(1)} %get-tuple-element.46), channel_id=1, source_target_pairs={{0,2},{1,3},{2,0},{3,1},{4,6},{5,7},{6,4},{7,5},{8,10},{9,11},{10,... | collective-permute-start | bytes 811016 | tf_op jit(solution)/shard_map/ppermute | solution.py:43
  43.3 18.1 %collective-permute-start.18 = (bf16[1056,128]{1,0:T(8,128)(2,1)S(1)}, bf16[1056,128]{1,0:T(8,128)(2,1)S(1)}, u32[]{:S(2)}, u32[]{:S(2)}) collective-permute-start(bf16[1056,128]{1,0:T(8,128)(2,1)S(1)} %get-tuple-element.49), channel_id=1, source_target_pairs={{0,16},{1,48},{2,80},{3,112},{4,144},{5,176},{6,208},{7,240},{8,24... | collective-permute-start | bytes 811016 | tf_op jit(solution)/shard_map/ppermute | solution.py:43
  48.2 22.6 %collective-permute-start.17 = (bf16[1056,128]{1,0:T(8,128)(2,1)S(1)}, bf16[1056,128]{1,0:T(8,128)(2,1)S(1)}, u32[]{:S(2)}, u32[]{:S(2)}) collective-permute-start(bf16[1056,128]{1,0:T(8,128)(2,1)S(1)} %collective-permute-done.10), channel_id=1, source_target_pairs={{0,64},{1,96},{2,0},{3,32},{4,192},{5,224},{6,128},{7,160},{8,72},... | collective-permute-start | bytes 811016 | tf_op jit(solution)/shard_map/ppermute | solution.py:43
  52.5 4.8 %collective-permute-start.13 = (f32[8,128]{1,0:T(8,128)S(1)}, f32[8,128]{1,0:T(8,128)S(1)}, u32[]{:S(2)}, u32[]{:S(2)}) collective-permute-start(f32[8,128]{1,0:T(8,128)S(1)} %add_add_fusion.6), channel_id=1, source_target_pairs={{0,6},{1,7},{2,4},{3,5},{4,2},{5,3},{6,0},{7,1},{8,14},{9,15},{10,... | collective-permute-start | bytes 12296 | tf_op jit(solution)/shard_map/ppermute | solution.py:43
  52.5 5.1 %collective-permute-start.12 = (f32[8,128]{1,0:T(8,128)S(1)}, f32[8,128]{1,0:T(8,128)S(1)}, u32[]{:S(2)}, u32[]{:S(2)}) collective-permute-start(f32[8,128]{1,0:T(8,128)S(1)} %add_add_fusion.6), channel_id=1, source_target_pairs={{0,4},{1,5},{2,6},{3,7},{4,0},{5,1},{6,2},{7,3},{8,12},{9,13},{10,... | collective-permute-start | bytes 12296 | tf_op jit(solution)/shard_map/ppermute | solution.py:43
  53.1 5.1 %collective-permute-start.11 = (f32[8,128]{1,0:T(8,128)S(1)}, f32[8,128]{1,0:T(8,128)S(1)}, u32[]{:S(2)}, u32[]{:S(2)}) collective-permute-start(f32[8,128]{1,0:T(8,128)S(1)} %add_add_fusion.6), channel_id=1, source_target_pairs={{0,2},{1,3},{2,0},{3,1},{4,6},{5,7},{6,4},{7,5},{8,10},{9,11},{10,... | collective-permute-start | bytes 12296 | tf_op jit(solution)/shard_map/ppermute | solution.py:43
  58.3 12.9 %collective-permute-start.16 = (f32[8,128]{1,0:T(8,128)S(1)}, f32[8,128]{1,0:T(8,128)S(1)}, u32[]{:S(2)}, u32[]{:S(2)}) collective-permute-start(f32[8,128]{1,0:T(8,128)S(1)} %add_add_fusion.5), channel_id=1, source_target_pairs={{0,24},{1,25},{2,26},{3,27},{4,28},{5,29},{6,30},{7,31},{8,16},{9,... | collective-permute-start | bytes 12296 | tf_op jit(solution)/shard_map/ppermute | solution.py:43
  58.5 12.7 %collective-permute-start.15 = (f32[8,128]{1,0:T(8,128)S(1)}, f32[8,128]{1,0:T(8,128)S(1)}, u32[]{:S(2)}, u32[]{:S(2)}) collective-permute-start(f32[8,128]{1,0:T(8,128)S(1)} %add_add_fusion.5), channel_id=1, source_target_pairs={{0,16},{1,17},{2,18},{3,19},{4,20},{5,21},{6,22},{7,23},{8,24},{9,... | collective-permute-start | bytes 12296 | tf_op jit(solution)/shard_map/ppermute | solution.py:43
  61.4 9.8 %collective-permute-start.14 = (f32[8,128]{1,0:T(8,128)S(1)}, f32[8,128]{1,0:T(8,128)S(1)}, u32[]{:S(2)}, u32[]{:S(2)}) collective-permute-start(f32[8,128]{1,0:T(8,128)S(1)} %add_add_fusion.5), channel_id=1, source_target_pairs={{0,8},{1,9},{2,10},{3,11},{4,12},{5,13},{6,14},{7,15},{8,0},{9,1},... | collective-permute-start | bytes 12296 | tf_op jit(solution)/shard_map/ppermute | solution.py:43
  61.4 9.8 %collective-permute-start.20 = (bf16[528,128]{1,0:T(8,128)(2,1)S(1)}, bf16[528,128]{1,0:T(8,128)(2,1)S(1)}, u32[]{:S(2)}, u32[]{:S(2)}) collective-permute-start(bf16[528,128]{1,0:T(8,128)(2,1)S(1)} %slice.9), channel_id=1, source_target_pairs={{0,8},{1,9},{2,10},{3,11},{4,12},{5,13},{6,14},{7,15},{8,0},{9,1},... | collective-permute-start | bytes 405512 | tf_op jit(solution)/shard_map/ppermute | solution.py:43
  70.8 1.6 %collective-permute-start.19 = (bf16[528,128]{1,0:T(8,128)(2,1)S(1)}, bf16[528,128]{1,0:T(8,128)(2,1)S(1)}, u32[]{:S(2)}, u32[]{:S(2)}) collective-permute-start(bf16[528,128]{1,0:T(8,128)(2,1)S(1)} %slice.8), channel_id=1, source_target_pairs={{0,8},{1,9},{2,10},{3,11},{4,12},{5,13},{6,14},{7,15},{8,0},{9,1},... | collective-permute-start | bytes 405512 | tf_op jit(solution)/shard_map/ppermute | solution.py:43
  76.8 52.1 %copy-start.1 = (bf16[3,3,64,64]{3,2,1,0:T(8,128)(2,1)S(1)}, bf16[3,3,64,64]{3,2,1,0:T(8,128)(2,1)}, u32[]{:S(2)}) copy-start(bf16[3,3,64,64]{3,2,1,0:T(8,128)(2,1)} %param.7) | copy-start | bytes 221188
  79.1 2.0 %collective-permute-start.21 = (f32[88,128]{1,0:T(8,128)S(1)}, f32[88,128]{1,0:T(8,128)S(1)}, u32[]{:S(2)}, u32[]{:S(2)}) collective-permute-start(f32[88,128]{1,0:T(8,128)S(1)} %get-tuple-element.57), channel_id=1, source_target_pairs={{0,8},{1,9},{2,10},{3,11},{4,12},{5,13},{6,14},{7,15},{8,0},{9,1},... | collective-permute-start | bytes 135176 | tf_op jit(solution)/shard_map/ppermute | solution.py:43
  79.3 4.4 %collective-permute-start.22 = (f32[88,128]{1,0:T(8,128)S(1)}, f32[88,128]{1,0:T(8,128)S(1)}, u32[]{:S(2)}, u32[]{:S(2)}) collective-permute-start(f32[88,128]{1,0:T(8,128)S(1)} %get-tuple-element.58), channel_id=1, source_target_pairs={{0,16},{1,17},{2,18},{3,19},{4,20},{5,21},{6,22},{7,23},{8,24},{9,... | collective-permute-start | bytes 135176 | tf_op jit(solution)/shard_map/ppermute | solution.py:43
  79.3 4.4 %collective-permute-start.23 = (f32[88,128]{1,0:T(8,128)S(1)}, f32[88,128]{1,0:T(8,128)S(1)}, u32[]{:S(2)}, u32[]{:S(2)}) collective-permute-start(f32[88,128]{1,0:T(8,128)S(1)} %get-tuple-element.59), channel_id=1, source_target_pairs={{0,24},{1,25},{2,26},{3,27},{4,28},{5,29},{6,30},{7,31},{8,16},{9,... | collective-permute-start | bytes 135176 | tf_op jit(solution)/shard_map/ppermute | solution.py:43
  83.8 11.0 %collective-permute-start.26 = (f32[88,128]{1,0:T(8,128)S(1)}, f32[88,128]{1,0:T(8,128)S(1)}, u32[]{:S(2)}, u32[]{:S(2)}) collective-permute-start(f32[88,128]{1,0:T(8,128)S(1)} %add_add_fusion.3), channel_id=1, source_target_pairs={{0,96},{1,97},{2,98},{3,99},{4,100},{5,101},{6,102},{7,103},{8,104... | collective-permute-start | bytes 135176 | tf_op jit(solution)/shard_map/ppermute | solution.py:43
  89.9 8.6 %collective-permute-start.25 = (f32[88,128]{1,0:T(8,128)S(1)}, f32[88,128]{1,0:T(8,128)S(1)}, u32[]{:S(2)}, u32[]{:S(2)}) collective-permute-start(f32[88,128]{1,0:T(8,128)S(1)} %add_add_fusion.3), channel_id=1, source_target_pairs={{0,64},{1,65},{2,66},{3,67},{4,68},{5,69},{6,70},{7,71},{8,72},{9,... | collective-permute-start | bytes 135176 | tf_op jit(solution)/shard_map/ppermute | solution.py:43
  94.8 5.5 %collective-permute-start.24 = (f32[88,128]{1,0:T(8,128)S(1)}, f32[88,128]{1,0:T(8,128)S(1)}, u32[]{:S(2)}, u32[]{:S(2)}) collective-permute-start(f32[88,128]{1,0:T(8,128)S(1)} %add_add_fusion.3), channel_id=1, source_target_pairs={{0,32},{1,33},{2,34},{3,35},{4,36},{5,37},{6,38},{7,39},{8,40},{9,... | collective-permute-start | bytes 135176 | tf_op jit(solution)/shard_map/ppermute | solution.py:43
  100.2 11.9 %collective-permute-start.29 = (f32[88,128]{1,0:T(8,128)S(1)}, f32[88,128]{1,0:T(8,128)S(1)}, u32[]{:S(2)}, u32[]{:S(2)}) collective-permute-start(f32[88,128]{1,0:T(8,128)S(1)} %add_add_fusion.2), channel_id=1, source_target_pairs={{0,129},{1,128},{2,131},{3,130},{4,133},{5,132},{6,135},{7,134},{8... | collective-permute-start | bytes 135176 | tf_op jit(solution)/shard_map/ppermute | solution.py:43
  100.3 11.8 %collective-permute-start.28 = (f32[88,128]{1,0:T(8,128)S(1)}, f32[88,128]{1,0:T(8,128)S(1)}, u32[]{:S(2)}, u32[]{:S(2)}) collective-permute-start(f32[88,128]{1,0:T(8,128)S(1)} %add_add_fusion.2), channel_id=1, source_target_pairs={{0,1},{1,0},{2,3},{3,2},{4,5},{5,4},{6,7},{7,6},{8,9},{9,8},{10,11... | collective-permute-start | bytes 135176 | tf_op jit(solution)/shard_map/ppermute | solution.py:43
  104.5 7.7 %collective-permute-start.27 = (f32[88,128]{1,0:T(8,128)S(1)}, f32[88,128]{1,0:T(8,128)S(1)}, u32[]{:S(2)}, u32[]{:S(2)}) collective-permute-start(f32[88,128]{1,0:T(8,128)S(1)} %add_add_fusion.2), channel_id=1, source_target_pairs={{0,128},{1,129},{2,130},{3,131},{4,132},{5,133},{6,134},{7,135},{8... | collective-permute-start | bytes 135176 | tf_op jit(solution)/shard_map/ppermute | solution.py:43
  104.5 11.9 %collective-permute-start.36 = (bf16[8,64,128]{2,1,0:T(8,128)(2,1)S(1)}, bf16[8,64,128]{2,1,0:T(8,128)(2,1)S(1)}, u32[]{:S(2)}, u32[]{:S(2)}) collective-permute-start(bf16[8,64,128]{2,1,0:T(8,128)(2,1)S(1)} %get-tuple-element.62), channel_id=1, source_target_pairs={{0,8},{8,16},{16,24},{24,32},{32,40},{40,48},{48,56},{56,64},{64,7... | collective-permute-start | bytes 393224 | tf_op jit(solution)/shard_map/ppermute | solution.py:49
  106.4 10.0 %collective-permute-start.37 = (bf16[8,64,128]{2,1,0:T(8,128)(2,1)S(1)}, bf16[8,64,128]{2,1,0:T(8,128)(2,1)S(1)}, u32[]{:S(2)}, u32[]{:S(2)}) collective-permute-start(bf16[8,64,128]{2,1,0:T(8,128)(2,1)S(1)} %get-tuple-element.63), channel_id=1, source_target_pairs={{8,0},{16,8},{24,16},{32,24},{40,32},{48,40},{56,48},{64,56},{72,6... | collective-permute-start | bytes 393224 | tf_op jit(solution)/shard_map/ppermute | solution.py:49
  112.2 12.0 %collective-permute-start.32 = (f32[88,128]{1,0:T(8,128)S(1)}, f32[88,128]{1,0:T(8,128)S(1)}, u32[]{:S(2)}, u32[]{:S(2)}) collective-permute-start(f32[88,128]{1,0:T(8,128)S(1)} %add_add_fusion.1), channel_id=1, source_target_pairs={{0,6},{1,7},{2,4},{3,5},{4,2},{5,3},{6,0},{7,1},{8,14},{9,15},{10,... | collective-permute-start | bytes 135176 | tf_op jit(solution)/shard_map/ppermute | solution.py:43
  115.2 9.0 %collective-permute-start.31 = (f32[88,128]{1,0:T(8,128)S(1)}, f32[88,128]{1,0:T(8,128)S(1)}, u32[]{:S(2)}, u32[]{:S(2)}) collective-permute-start(f32[88,128]{1,0:T(8,128)S(1)} %add_add_fusion.1), channel_id=1, source_target_pairs={{0,4},{1,5},{2,6},{3,7},{4,0},{5,1},{6,2},{7,3},{8,12},{9,13},{10,... | collective-permute-start | bytes 135176 | tf_op jit(solution)/shard_map/ppermute | solution.py:43
  115.2 9.0 %collective-permute-start.30 = (f32[88,128]{1,0:T(8,128)S(1)}, f32[88,128]{1,0:T(8,128)S(1)}, u32[]{:S(2)}, u32[]{:S(2)}) collective-permute-start(f32[88,128]{1,0:T(8,128)S(1)} %add_add_fusion.1), channel_id=1, source_target_pairs={{0,2},{1,3},{2,0},{3,1},{4,6},{5,7},{6,4},{7,5},{8,10},{9,11},{10,... | collective-permute-start | bytes 135176 | tf_op jit(solution)/shard_map/ppermute | solution.py:43
  116.9 9.4 %collective-permute-start.38 = (bf16[3,64,128]{2,1,0:T(8,128)(2,1)S(1)}, bf16[3,64,128]{2,1,0:T(8,128)(2,1)S(1)}, u32[]{:S(2)}, u32[]{:S(2)}) collective-permute-start(bf16[3,64,128]{2,1,0:T(8,128)(2,1)S(1)} %get-tuple-element.64), channel_id=1, source_target_pairs={{0,1},{1,2},{2,3},{3,4},{4,5},{5,6},{6,7},{8,9},{9,10},{10,11},{11... | collective-permute-start | bytes 147464 | tf_op jit(solution)/shard_map/ppermute | solution.py:49
  120.5 8.4 %collective-permute-start.39 = (bf16[3,64,128]{2,1,0:T(8,128)(2,1)S(1)}, bf16[3,64,128]{2,1,0:T(8,128)(2,1)S(1)}, u32[]{:S(2)}, u32[]{:S(2)}) collective-permute-start(bf16[3,64,128]{2,1,0:T(8,128)(2,1)S(1)} %get-tuple-element.65), channel_id=1, source_target_pairs={{1,0},{2,1},{3,2},{4,3},{5,4},{6,5},{7,6},{9,8},{10,9},{11,10},{12... | collective-permute-start | bytes 147464 | tf_op jit(solution)/shard_map/ppermute | solution.py:49
  124.3 7.5 %collective-permute-start.35 = (f32[88,128]{1,0:T(8,128)S(1)}, f32[88,128]{1,0:T(8,128)S(1)}, u32[]{:S(2)}, u32[]{:S(2)}) collective-permute-start(f32[88,128]{1,0:T(8,128)S(1)} %add_add_fusion.got0), channel_id=1, source_target_pairs={{0,24},{1,25},{2,26},{3,27},{4,28},{5,29},{6,30},{7,31},{8,16},{9,... | collective-permute-start | bytes 135176 | tf_op jit(solution)/shard_map/ppermute | solution.py:43
  124.4 7.4 %collective-permute-start.34 = (f32[88,128]{1,0:T(8,128)S(1)}, f32[88,128]{1,0:T(8,128)S(1)}, u32[]{:S(2)}, u32[]{:S(2)}) collective-permute-start(f32[88,128]{1,0:T(8,128)S(1)} %add_add_fusion.got0), channel_id=1, source_target_pairs={{0,16},{1,17},{2,18},{3,19},{4,20},{5,21},{6,22},{7,23},{8,24},{9,... | collective-permute-start | bytes 135176 | tf_op jit(solution)/shard_map/ppermute | solution.py:43
  124.5 7.3 %collective-permute-start.33 = (f32[88,128]{1,0:T(8,128)S(1)}, f32[88,128]{1,0:T(8,128)S(1)}, u32[]{:S(2)}, u32[]{:S(2)}) collective-permute-start(f32[88,128]{1,0:T(8,128)S(1)} %add_add_fusion.got0), channel_id=1, source_target_pairs={{0,8},{1,9},{2,10},{3,11},{4,12},{5,13},{6,14},{7,15},{8,0},{9,1},... | collective-permute-start | bytes 135176 | tf_op jit(solution)/shard_map/ppermute | solution.py:43

commit v8 on v7

--- a/solution.py
+++ b/solution.py
@@ -43,13 +43,14 @@
     return lax.ppermute(block, GRID, pairs)
 
 
-def shifted(block, axis, forward):
+def swapped(to_mate, to_other, axis):
     count = lax.axis_size(axis)
-    pairs = [(i, i + 1) for i in range(count - 1)]
-    return lax.ppermute(block, axis, pairs if forward else [(b, a) for a, b in pairs])
-
-
-def activate_kernel(feat, valid, act, top, bottom, counted, kept_feat, kept_valid):
+    mates = [(i, i ^ 1) for i in range(count)]
+    others = [(i, i + 1 if i % 2 else i - 1) for i in range(1, count - 1)]
+    return lax.ppermute(to_mate, axis, mates), lax.ppermute(to_other, axis, others)
+
+
+def activate_kernel(place, feat, valid, act, mate, other, counted, kept_feat, kept_valid):
     rows = feat.shape[0]
 
     def step(i, carry):
@@ -61,46 +62,64 @@
         return carry
 
     lax.fori_loop(0, rows, step, 0, unroll=4)
-    top[...] = act[:STEP]
-    bottom[...] = act[rows - STEP :]
+    share_edges(place, act, mate, other)
     lines = jnp.sum(valid[...].astype(F32), axis=0, keepdims=True)
     kept_valid[...] = valid[...]
     counted[...] = jnp.broadcast_to(jnp.sum(lines, axis=1, keepdims=True), counted.shape)
 
 
-def row_of(own, up, down, at):
+def share_edges(place, own, mate, other):
+    last = own.shape[0] - STEP
+    low = (1 - place[0] % 2) * last
+    mate[...] = own[pl.ds(low, STEP)]
+    other[...] = own[pl.ds(last - low, STEP)]
+
+
+def settle_edges(place, mate, other, edges):
+    odd = place[0] % 2
+    edges[pl.ds((1 - odd) * STEP, STEP)] = mate[...]
+    edges[pl.ds(odd * STEP, STEP)] = other[...]
+
+
+def row_of(own, edges, at):
     rows = own.shape[0]
     if at < STEP:
-        return up[at]
+        return edges[at]
     if at < STEP + rows:
         return own[at - STEP]
-    return down[at - STEP - rows]
-
-
-def pack_kernel(own, up, down, first, last):
+    return edges[at - rows]
+
+
+def pack_kernel(place, own, mate, other, to_mate, to_other, edges, sides):
     chans = own.shape[1]
     lane = lax.broadcasted_iota(jnp.int32, (chans, LANES), 1) // STEP
-    for group in range(first.shape[0]):
+    settle_edges(place, mate, other, edges)
+    for group in range(sides.shape[1]):
         low = jnp.zeros((chans, LANES), F32)
         high = jnp.zeros((chans, LANES), F32)
         for slot in range(16):
-            x = row_of(own, up, down, group * 16 + slot).astype(F32)
+            x = row_of(own, edges, group * 16 + slot).astype(F32)
             here = lane == slot
             low = jnp.where(here, pltpu.roll(x, (STEP * slot) % LANES, 1), low)
             high = jnp.where(here, pltpu.roll(x, (STEP * slot + STEP) % LANES, 1), high)
-        first[group] = low.astype(BF16)
-        last[group] = high.astype(BF16)
-
-
-def spread_columns(own, up, down, left, right, wide):
+        sides[0, group] = low.astype(BF16)
+        sides[1, group] = high.astype(BF16)
+    to_mate[...] = sides[1 - (place[0] // 4)]
+    to_other[...] = sides[(place[0] // 4)]
+
+
+def spread_columns(place, own, mate, other, side_mate, side_other, edges, sides, wide):
     chans = own.shape[1]
     lane = lax.broadcasted_iota(jnp.int32, (chans, LANES), 1)
-    for group in range(left.shape[0]):
-        from_left = left[group].astype(F32)
-        from_right = right[group].astype(F32)
+    settle_edges(place, mate, other, edges)
+    sides[1 - (place[0] // 4)] = side_mate[...]
+    sides[(place[0] // 4)] = side_other[...]
+    for group in range(sides.shape[1]):
+        from_left = sides[0, group].astype(F32)
+        from_right = sides[1, group].astype(F32)
         for slot in range(16):
             at = group * 16 + slot
-            middle = row_of(own, up, down, at)
+            middle = row_of(own, edges, at)
             x = middle.astype(F32)
             before = jnp.where(
                 lane < STEP,
@@ -126,13 +145,13 @@
 
 
 def forward_kernel(
-    place, act, up, down, left, right, feat, weight, labels, valid,
-    wide, mixed, pay_near, pay_far, turned,
+    place, act, mate, other, side_mate, side_other, feat, weight, labels, valid,
+    wide, mixed, pay_near, pay_far, turned, edges, sides,
 ):
     rows, chans = act.shape[0], act.shape[1]
     part = rows
     length = pay_near.shape[0] // 2
-    spread_columns(act, up, down, left, right, wide)
+    spread_columns(place, act, mate, other, side_mate, side_other, edges, sides, wide)
     kernel = weight[...].astype(F32).T.astype(BF16)
 
     def step(p, carry):
@@ -153,7 +172,7 @@
 
     def pack(j, carry):
         for s in range(4):
-            base = j * LANES + (place[0] ^ s) * part
+            base = j * LANES + (place[0] % 4 ^ s) * part
             low = turned[pl.ds(pl.multiple_of(base, 16), half), :]
             high = turned[pl.ds(pl.multiple_of(base + half, 16), half), :]
             pay = pay_near if s < 2 else pay_far
@@ -175,7 +194,7 @@
     size = rows * half
     length = size + half
     for s, got in ((0, near), (2, far), (1, got1), (3, got3)):
-        q = place[0] ^ s
+        q = place[0] % 4 ^ s
         cells[pl.ds(pl.multiple_of(q * size, size), size), :] = got[:size, :].astype(F32)
         cells[pl.ds(pl.multiple_of(4 * size + q * half, half), half), :] = got[size:length, :].astype(F32)
     notes = [cells[4 * size + q * half : 4 * size + (q + 1) * half, :] for q in range(4)]
@@ -252,7 +271,7 @@
 
 def kernel_grad_kernel(
     place, count, grad, wide, head_sum, bias_sum, loss_sum,
-    low, top, bottom, out0, out1, out2, out3, total, sheet,
+    low, mate, other, out0, out1, out2, out3, total, sheet,
 ):
     rows, chans = grad.shape[0], grad.shape[1]
     bins = bias_sum.shape[0]
@@ -274,8 +293,7 @@
         return carry
 
     lax.fori_loop(0, rows // 2, step, 0, unroll=UNROLL)
-    top[...] = low[:STEP]
-    bottom[...] = low[rows - STEP :]
+    share_edges(place, low, mate, other)
     half = total.shape[0] // 2
     sheet[...] = jnp.zeros_like(sheet)
     sheet[:half, :] = jnp.concatenate([total[:half], total[half:]], axis=1)
@@ -286,13 +304,15 @@
     sheet[note + 1 : note + 2, :1] = jnp.sum(loss_sum[...], axis=1, keepdims=True)
     quarter = sheet.shape[0] // 4
     for s, out in enumerate((out0, out1, out2, out3)):
-        out[...] = sheet[pl.ds(pl.multiple_of((place[0] ^ s) * quarter, 8), quarter), :]
-
-
-def backward_kernel(count, low, up, down, left, right, grad, feat, weight, out, wide):
+        out[...] = sheet[pl.ds(pl.multiple_of((place[0] % 4 ^ s) * quarter, 8), quarter), :]
+
+
+def backward_kernel(
+    place, count, low, mate, other, side_mate, side_other, grad, feat, weight, out, wide, edges, sides
+):
     rows, chans = grad.shape[0], grad.shape[1]
     scale = scale_of(count)
-    spread_columns(low, up, down, left, right, wide)
+    spread_columns(place, low, mate, other, side_mate, side_other, edges, sides, wide)
     taps = weight.shape[0] // chans
     kernel = jnp.concatenate(
         [weight[(taps - 1 - t) * chans : (taps - t) * chans, :].astype(F32) for t in range(taps)],
@@ -318,7 +338,7 @@
 ):
     quarter = got0.shape[0]
     for s, got in enumerate((got0, got1, got2, got3)):
-        sheet[pl.ds(pl.multiple_of((place[0] ^ s) * quarter, 8), quarter), :] = got[...]
+        sheet[pl.ds(pl.multiple_of((place[0] % 4 ^ s) * quarter, 8), quarter), :] = got[...]
     half, chans = kernel_grad.shape[0] // 2, kernel_grad.shape[1]
     bins = head_grad.shape[0]
     kernel_grad[:half, :] = sheet[:half, :chans]
@@ -329,17 +349,27 @@
     loss[...] = sheet[note + 1 : note + 2, :1] / jnp.maximum(count[0:1, 0:1], 1.0)
 
 
-def borders(own, top, bottom):
+def border_buffers(rows, chans):
+    groups = (rows + 2 * STEP) // 16
+    return [
+        pltpu.VMEM((2 * STEP, chans, LANES), BF16),
+        pltpu.VMEM((2, groups, chans, LANES), BF16),
+    ]
+
+
+def borders(place, own, mate, other):
     rows, chans, _ = own.shape
-    up = shifted(bottom, "row", True)
-    down = shifted(top, "row", False)
+    edges = swapped(mate, other, "row")
     groups = (rows + 2 * STEP) // 16
-    first, last = run(
-        pack_kernel, [shape((groups, chans, LANES), BF16)] * 2, (own, up, down), micros=8
-    )
-    left = shifted(last, "col", True)
-    right = shifted(first, "col", False)
-    return up, down, left, right
+    sides = run(
+        pack_kernel,
+        [shape((groups, chans, LANES), BF16)] * 2,
+        (place, own, *edges),
+        scratch=border_buffers(rows, chans),
+        scalars=1,
+        micros=8,
+    )
+    return *edges, *swapped(*sides, "col")
 
 
 def partners(stage):
@@ -380,20 +410,22 @@
     rows, cols, chans = features.shape
     bins = head_weight.shape[1]
     parts = cols // rows
-    place = (lax.axis_index("row") % parts).astype(jnp.int32).reshape(1)
+    place = lax.axis_index("row") % parts + 4 * (lax.axis_index("col") % 2)
+    place = place.astype(jnp.int32).reshape(1)
     feat = features.transpose(0, 2, 1)
     weight = conv_weight.reshape(-1, chans)
     tall = -(-bins // 8) * 8
     tile = (rows, chans, LANES)
     edge = (STEP, chans, LANES)
-    act, top, bottom, counted, feat, valid = run(
+    act, mate, other, counted, feat, valid = run(
         activate_kernel,
         [shape(tile, BF16), shape(edge, BF16), shape(edge, BF16), shape((8, LANES), F32)]
         + [shape(tile, BF16), shape(valid.shape, jnp.int32)],
-        (feat, valid),
+        (place, feat, valid),
+        scalars=1,
         micros=1,
     )
-    around = borders(act, top, bottom)
+    around = borders(place, act, mate, other)
     counted = total_small(counted, (1, 2))
     counted, act = lax.optimization_barrier((counted, act))
     length = (rows + 1) * rows // 2
@@ -402,7 +434,7 @@
         [shape((rows + 2 * STEP, 3 * chans, LANES), BF16), shape(tile, BF16)]
         + [shape((2 * length, LANES), BF16)] * 2,
         (place, act, *around, feat, weight, labels, valid),
-        scratch=[pltpu.VMEM(((rows + 1) * LANES, chans), F32)],
+        scratch=[pltpu.VMEM(((rows + 1) * LANES, chans), F32)] + border_buffers(rows, chans),
         scalars=1,
         micros=5,
     )
@@ -426,7 +458,7 @@
     )
     half = 9 * chans // 2
     lines = -(-(half + tall + 8) // 32) * 32
-    low, top, bottom, *quarters = run(
+    low, mate, other, *quarters = run(
         kernel_grad_kernel,
         [shape(tile, BF16), shape(edge, BF16), shape(edge, BF16)]
         + [shape((lines // 4, LANES), F32)] * 4,
@@ -436,12 +468,14 @@
         micros=3,
     )
     sums = total_quarters(quarters)
-    around = borders(low, top, bottom)
+    around = borders(place, low, mate, other)
     (grad_features,) = run(
         backward_kernel,
         [shape(tile, BF16)],
-        (count, low, *around, grad, feat, weight),
-        scratch=[pltpu.VMEM((rows + 2 * STEP, 3 * chans, LANES), BF16)],
+        (place, count, low, *around, grad, feat, weight),
+        scratch=[pltpu.VMEM((rows + 2 * STEP, 3 * chans, LANES), BF16)]
+        + border_buffers(rows, chans),
+        scalars=1,
         micros=4,
     )
     kernel_grad, head_grad, bias_grad, loss = run(

time: 133 us -> 123 us (0.925)
  waiting for transfers between devices: 30.4 us -> 18.4 us
  starting transfers between devices: 82.4 us -> 83.9 us
    ppermute x32, waiting for transfers between devices: 22.7 us -> 13.1 us  [send(): return lax.ppermute(block, GRID, pairs)]
    ppermute x32, starting transfers between devices: 52.4 us -> 61.3 us  [send(): return lax.ppermute(block, GRID, pairs)]
    ppermute x8, starting transfers between devices: 30 us -> 22.6 us  [the longest x4 20.1 us: swapped(): lax.ppermute(to_other, axis, others)]
    ppermute x8, waiting for transfers between devices: 7.72 us -> 5.28 us  [the longest x4 5.27 us: swapped(): lax.ppermute(to_other, axis, others)]
  transfers between devices with their start and end apart: 40 -> 40, of which waited for: 12 -> 10; matrix products, arithmetic and copies ran while one was open for 0% -> 0% of each run, Pallas kernels for 3% -> 3%
where the time goes in v8:
time: 123 us; the launch traced here: 122 us
  starting transfers between devices  83.9 us (68%)
  waiting for transfers between devices  18.4 us (15%)
  Pallas kernels  15.4 us (13%)
  local copies, waits for them, and re-layouts  3.42 us (3%)
    ppermute x32, starting transfers between devices, send(): return lax.ppermute(block, GRID, pairs)  61.3 us
    ppermute x4, starting transfers between devices, swapped(): lax.ppermute(to_other, axis, others)  20.1 us
    pallas_call x8, Pallas kernels, run(): pl.pallas_call(body, out_shape=outs, in_specs=[SMEM] * scalars + [VMEM] *...  15.4 us
    ppermute x32, waiting for transfers between devices, send(): return lax.ppermute(block, GRID, pairs)  13.1 us
    ppermute x4, waiting for transfers between devices, swapped(): lax.ppermute(to_other, axis, others)  5.27 us
    unnamed x16, local copies, waits for them, and re-layouts  3.4 us
    ppermute x4, starting transfers between devices, swapped(): lax.ppermute(to_mate, axis, mates)  2.5 us
  transfers between devices with their start and end apart: 40, of which 10 were waited for; matrix products, arithmetic and copies ran while one was open for 0% of the time, Pallas kernels for 3%

profile of v8, /device:TPU:24, one launch (start us, length us, event | category | flops | bytes accessed | tf_op | source)
XLA Modules:
  0.0 122.3 jit_solution(5200827137757037234)
XLA Ops:
  0.7 1.0 copy-done.2
  1.7 0.7 copy-done.5
  2.4 0.7 shard_map.101
  3.1 6.3 %collective-permute-start.2 = (f32[8,128]{1,0:T(8,128)S(1)}, f32[8,128]{1,0:T(8,128)S(1)}, u32[]{:S(2)}, u32[]{:S(2)}) collective-permute-start(f32[8,128]{1,0:T(8,128)S(1)} %get-tuple-element.37), channel_id=1, source_target_pairs={{0,96},{1,97},{2,98},{3,99},{4,100},{5,101},{6,102},{7,103},{8,104... | collective-permute-start | bytes 12296 | tf_op jit(solution)/shard_map/ppermute | solution.py:43
  9.5 1.0 collective-permute-start.1
  10.5 1.5 %collective-permute-start = (f32[8,128]{1,0:T(8,128)S(1)}, f32[8,128]{1,0:T(8,128)S(1)}, u32[]{:S(2)}, u32[]{:S(2)}) collective-permute-start(f32[8,128]{1,0:T(8,128)S(1)} %get-tuple-element.37), channel_id=1, source_target_pairs={{0,32},{1,33},{2,34},{3,35},{4,36},{5,37},{6,38},{7,39},{8,40},{9,... | collective-permute-start | bytes 12296 | tf_op jit(solution)/shard_map/ppermute | solution.py:43
  11.9 5.8 %collective-permute-start.7 = (bf16[8,64,128]{2,1,0:T(8,128)(2,1)S(1)}, bf16[8,64,128]{2,1,0:T(8,128)(2,1)S(1)}, u32[]{:S(2)}, u32[]{:S(2)}) collective-permute-start(bf16[8,64,128]{2,1,0:T(8,128)(2,1)S(1)} %get-tuple-element.41), channel_id=1, source_target_pairs={{8,16},{16,8},{24,32},{32,24},{40,48},{48,40},{56,64},{64,56},{72,... | collective-permute-start | bytes 393224 | tf_op jit(solution)/shard_map/ppermute | solution.py:50
  17.9 2.0 %collective-permute-start.4 = (f32[8,128]{1,0:T(8,128)S(1)}, f32[8,128]{1,0:T(8,128)S(1)}, u32[]{:S(2)}, u32[]{:S(2)}) collective-permute-start(f32[8,128]{1,0:T(8,128)S(1)} %add_add_fusion.7), channel_id=1, source_target_pairs={{0,1},{1,0},{2,3},{3,2},{4,5},{5,4},{6,7},{7,6},{8,9},{9,8},{10,11... | collective-permute-start | bytes 12296 | tf_op jit(solution)/shard_map/ppermute | solution.py:43
  19.9 2.1 %collective-permute-start.3 = (f32[8,128]{1,0:T(8,128)S(1)}, f32[8,128]{1,0:T(8,128)S(1)}, u32[]{:S(2)}, u32[]{:S(2)}) collective-permute-start(f32[8,128]{1,0:T(8,128)S(1)} %add_add_fusion.7), channel_id=1, source_target_pairs={{0,128},{1,129},{2,130},{3,131},{4,132},{5,133},{6,134},{7,135},{8... | collective-permute-start | bytes 12296 | tf_op jit(solution)/shard_map/ppermute | solution.py:43
  22.0 0.5 shard_map.102
  22.5 1.0 collective-permute-start.8
  23.5 5.4 %collective-permute-start.9 = (bf16[3,64,128]{2,1,0:T(8,128)(2,1)S(1)}, bf16[3,64,128]{2,1,0:T(8,128)(2,1)S(1)}, u32[]{:S(2)}, u32[]{:S(2)}) collective-permute-start(bf16[3,64,128]{2,1,0:T(8,128)(2,1)S(1)} %get-tuple-element.43), channel_id=1, source_target_pairs={{1,2},{2,1},{3,4},{4,3},{5,6},{6,5},{9,10},{10,9},{11,12},{12,11},... | collective-permute-start | bytes 147464 | tf_op jit(solution)/shard_map/ppermute | solution.py:50
  29.0 2.9 %collective-permute-done.9.side_other = bf16[3,64,128]{2,1,0:T(8,128)(2,1)S(1)} collective-permute-done((bf16[3,64,128]{2,1,0:T(8,128)(2,1)S(1)}, bf16[3,64,128]{2,1,0:T(8,128)(2,1)S(1)}, u32[]{:S(2)}, u32[]{:S(2)}) %collective-permute-start.9) | collective-permute-done | bytes 49184 | tf_op jit(solution)/shard_map/ppermute | solution.py:50
  31.9 0.9 copy-done
  32.8 0.7 copy-done.3
  33.5 3.4 %shard_map.103 = (bf16[48,192,128]{2,1,0:T(8,128)(2,1)S(1)}, bf16[32,64,128]{2,1,0:T(8,128)(2,1)S(1)}, bf16[1056,128]{1,0:T(8,128)(2,1)S(1)}, bf16[1056,128]{1,0:T(8,128)(2,1)S(1)}) custom-call(s32[1]{0:T(128)} %bitcast.place, bf16[32,64,128]{2,1,0:T(8,128)(2,1)S(1)} %get-tuple-element.39.own.act, bf16[8,64,128]{2,1,0:T(8,128)(2,1)S(1)} %collective-permute-done.6.mate, ...), custom_call_target="tpu_custom_call" | custom-call | bytes 18000000 | tf_op jit(solution)/shard_map/pallas_call | solution.py:19
  36.9 1.6 %collective-permute-start.10 = (bf16[1056,128]{1,0:T(8,128)(2,1)S(1)}, bf16[1056,128]{1,0:T(8,128)(2,1)S(1)}, u32[]{:S(2)}, u32[]{:S(2)}) collective-permute-start(bf16[1056,128]{1,0:T(8,128)(2,1)S(1)} %get-tuple-element.46), channel_id=1, source_target_pairs={{0,2},{1,3},{2,0},{3,1},{4,6},{5,7},{6,4},{7,5},{8,10},{9,11},{10,... | collective-permute-start | bytes 811016 | tf_op jit(solution)/shard_map/ppermute | solution.py:43
  38.5 5.2 %collective-permute-start.18 = (bf16[1056,128]{1,0:T(8,128)(2,1)S(1)}, bf16[1056,128]{1,0:T(8,128)(2,1)S(1)}, u32[]{:S(2)}, u32[]{:S(2)}) collective-permute-start(bf16[1056,128]{1,0:T(8,128)(2,1)S(1)} %get-tuple-element.49), channel_id=1, source_target_pairs={{0,16},{1,48},{2,80},{3,112},{4,144},{5,176},{6,208},{7,240},{8,24... | collective-permute-start | bytes 811016 | tf_op jit(solution)/shard_map/ppermute | solution.py:43
  43.7 5.5 %collective-permute-start.17 = (bf16[1056,128]{1,0:T(8,128)(2,1)S(1)}, bf16[1056,128]{1,0:T(8,128)(2,1)S(1)}, u32[]{:S(2)}, u32[]{:S(2)}) collective-permute-start(bf16[1056,128]{1,0:T(8,128)(2,1)S(1)} %collective-permute-done.10), channel_id=1, source_target_pairs={{0,64},{1,96},{2,0},{3,32},{4,192},{5,224},{6,128},{7,160},{8,72},... | collective-permute-start | bytes 811016 | tf_op jit(solution)/shard_map/ppermute | solution.py:43
  49.3 1.3 %collective-permute-start.12 = (f32[8,128]{1,0:T(8,128)S(1)}, f32[8,128]{1,0:T(8,128)S(1)}, u32[]{:S(2)}, u32[]{:S(2)}) collective-permute-start(f32[8,128]{1,0:T(8,128)S(1)} %add_add_fusion.6), channel_id=1, source_target_pairs={{0,4},{1,5},{2,6},{3,7},{4,0},{5,1},{6,2},{7,3},{8,12},{9,13},{10,... | collective-permute-start | bytes 12296 | tf_op jit(solution)/shard_map/ppermute | solution.py:43
  50.6 2.7 %collective-permute-start.11 = (f32[8,128]{1,0:T(8,128)S(1)}, f32[8,128]{1,0:T(8,128)S(1)}, u32[]{:S(2)}, u32[]{:S(2)}) collective-permute-start(f32[8,128]{1,0:T(8,128)S(1)} %add_add_fusion.6), channel_id=1, source_target_pairs={{0,2},{1,3},{2,0},{3,1},{4,6},{5,7},{6,4},{7,5},{8,10},{9,11},{10,... | collective-permute-start | bytes 12296 | tf_op jit(solution)/shard_map/ppermute | solution.py:43
  53.3 0.7 collective-permute-done.13
  54.4 0.5 collective-permute-done.11
  54.9 0.6 collective-permute-start.16
  55.6 2.6 %collective-permute-start.15 = (f32[8,128]{1,0:T(8,128)S(1)}, f32[8,128]{1,0:T(8,128)S(1)}, u32[]{:S(2)}, u32[]{:S(2)}) collective-permute-start(f32[8,128]{1,0:T(8,128)S(1)} %add_add_fusion.5), channel_id=1, source_target_pairs={{0,16},{1,17},{2,18},{3,19},{4,20},{5,21},{6,22},{7,23},{8,24},{9,... | collective-permute-start | bytes 12296 | tf_op jit(solution)/shard_map/ppermute | solution.py:43
  58.2 0.8 collective-permute-start.20
  59.0 1.2 collective-permute-done.17.near
  60.4 1.3 %collective-permute-done.19.got1 = bf16[528,128]{1,0:T(8,128)(2,1)S(1)} collective-permute-done((bf16[528,128]{1,0:T(8,128)(2,1)S(1)}, bf16[528,128]{1,0:T(8,128)(2,1)S(1)}, u32[]{:S(2)}, u32[]{:S(2)}) %collective-permute-start.19) | collective-permute-done | bytes 135200 | tf_op jit(solution)/shard_map/ppermute | solution.py:43
  61.7 4.3 %shard_map.104 = (f32[32,64,128]{2,1,0:T(8,128)S(1)}, f32[120,64]{1,0:T(8,128)S(1)}, f32[40,128]{1,0:T(8,128)S(1)}, f32[1,128]{1,0:T(1,128)S(1)}) custom-call(s32[1]{0:T(128)} %bitcast.place, bf16[1056,128]{1,0:T(8,128)(2,1)S(1)} %collective-permute-done.17.near, bf16[1056,128]{1,0:T(8,128)(2,1)S(1)} %collective-permute-done.18.far, ...), custom_call_target="tpu_custom_call" | custom-call | bytes 18000000 | tf_op jit(solution)/shard_map/pallas_call | solution.py:19
  66.0 2.3 %shard_map.105 = (bf16[32,64,128]{2,1,0:T(8,128)(2,1)S(1)}, bf16[8,64,128]{2,1,0:T(8,128)(2,1)S(1)}, bf16[8,64,128]{2,1,0:T(8,128)(2,1)S(1)}, f32[88,128]{1,0:T(...) custom-call(s32[1]{0:T(128)} %bitcast.place, f32[8,128]{1,0:T(8,128)S(1)} %add_add_fusion.4.count, ...), custom_call_target="tpu_custom_call" | custom-call | bytes 10800000 | tf_op jit(solution)/shard_map/pallas_call | solution.py:19
  68.5 0.5 collective-permute-start.22
  69.1 1.2 collective-permute-start.23
  70.3 2.8 %collective-permute-done.22 = f32[88,128]{1,0:T(8,128)S(1)} collective-permute-done((f32[88,128]{1,0:T(8,128)S(1)}, f32[88,128]{1,0:T(8,128)S(1)}, u32[]{:S(2)}, u32[]{:S(2)}) %collective-permute-start.22) | collective-permute-done | bytes 45088 | tf_op jit(solution)/shard_map/ppermute | solution.py:43
  73.0 12.9 %collective-permute-start.26 = (f32[88,128]{1,0:T(8,128)S(1)}, f32[88,128]{1,0:T(8,128)S(1)}, u32[]{:S(2)}, u32[]{:S(2)}) collective-permute-start(f32[88,128]{1,0:T(8,128)S(1)} %add_add_fusion.3), channel_id=1, source_target_pairs={{0,96},{1,97},{2,98},{3,99},{4,100},{5,101},{6,102},{7,103},{8,104... | collective-permute-start | bytes 135176 | tf_op jit(solution)/shard_map/ppermute | solution.py:43
  85.9 2.2 %collective-permute-start.25 = (f32[88,128]{1,0:T(8,128)S(1)}, f32[88,128]{1,0:T(8,128)S(1)}, u32[]{:S(2)}, u32[]{:S(2)}) collective-permute-start(f32[88,128]{1,0:T(8,128)S(1)} %add_add_fusion.3), channel_id=1, source_target_pairs={{0,64},{1,65},{2,66},{3,67},{4,68},{5,69},{6,70},{7,71},{8,72},{9,... | collective-permute-start | bytes 135176 | tf_op jit(solution)/shard_map/ppermute | solution.py:43
  88.4 6.1 %collective-permute-done.25 = f32[88,128]{1,0:T(8,128)S(1)} collective-permute-done((f32[88,128]{1,0:T(8,128)S(1)}, f32[88,128]{1,0:T(8,128)S(1)}, u32[]{:S(2)}, u32[]{:S(2)}) %collective-permute-start.25) | collective-permute-done | bytes 45088 | tf_op jit(solution)/shard_map/ppermute | solution.py:43
  94.9 4.1 %collective-permute-start.28 = (f32[88,128]{1,0:T(8,128)S(1)}, f32[88,128]{1,0:T(8,128)S(1)}, u32[]{:S(2)}, u32[]{:S(2)}) collective-permute-start(f32[88,128]{1,0:T(8,128)S(1)} %add_add_fusion.2), channel_id=1, source_target_pairs={{0,1},{1,0},{2,3},{3,2},{4,5},{5,4},{6,7},{7,6},{8,9},{9,8},{10,11... | collective-permute-start | bytes 135176 | tf_op jit(solution)/shard_map/ppermute | solution.py:43
  99.0 4.9 %collective-permute-start.37 = (bf16[8,64,128]{2,1,0:T(8,128)(2,1)S(1)}, bf16[8,64,128]{2,1,0:T(8,128)(2,1)S(1)}, u32[]{:S(2)}, u32[]{:S(2)}) collective-permute-start(bf16[8,64,128]{2,1,0:T(8,128)(2,1)S(1)} %get-tuple-element.63), channel_id=1, source_target_pairs={{8,16},{16,8},{24,32},{32,24},{40,48},{48,40},{56,64},{64,56},{72,... | collective-permute-start | bytes 393224 | tf_op jit(solution)/shard_map/ppermute | solution.py:50
  104.0 1.5 %collective-permute-start.32 = (f32[88,128]{1,0:T(8,128)S(1)}, f32[88,128]{1,0:T(8,128)S(1)}, u32[]{:S(2)}, u32[]{:S(2)}) collective-permute-start(f32[88,128]{1,0:T(8,128)S(1)} %add_add_fusion.1), channel_id=1, source_target_pairs={{0,6},{1,7},{2,4},{3,5},{4,2},{5,3},{6,0},{7,1},{8,14},{9,15},{10,... | collective-permute-start | bytes 135176 | tf_op jit(solution)/shard_map/ppermute | solution.py:43
  105.5 1.1 collective-permute-start.31
  106.7 1.5 %collective-permute-start.30 = (f32[88,128]{1,0:T(8,128)S(1)}, f32[88,128]{1,0:T(8,128)S(1)}, u32[]{:S(2)}, u32[]{:S(2)}) collective-permute-start(f32[88,128]{1,0:T(8,128)S(1)} %add_add_fusion.1), channel_id=1, source_target_pairs={{0,2},{1,3},{2,0},{3,1},{4,6},{5,7},{6,4},{7,5},{8,10},{9,11},{10,... | collective-permute-start | bytes 135176 | tf_op jit(solution)/shard_map/ppermute | solution.py:43
  108.2 0.5 shard_map.107
  108.7 1.5 %collective-permute-start.38 = (bf16[3,64,128]{2,1,0:T(8,128)(2,1)S(1)}, bf16[3,64,128]{2,1,0:T(8,128)(2,1)S(1)}, u32[]{:S(2)}, u32[]{:S(2)}) collective-permute-start(bf16[3,64,128]{2,1,0:T(8,128)(2,1)S(1)} %get-tuple-element.64), channel_id=1, source_target_pairs={{0,1},{1,0},{2,3},{3,2},{4,5},{5,4},{6,7},{7,6},{8,9},{9,8},{10,11... | collective-permute-start | bytes 147464 | tf_op jit(solution)/shard_map/ppermute | solution.py:50
  110.2 4.0 %collective-permute-start.39 = (bf16[3,64,128]{2,1,0:T(8,128)(2,1)S(1)}, bf16[3,64,128]{2,1,0:T(8,128)(2,1)S(1)}, u32[]{:S(2)}, u32[]{:S(2)}) collective-permute-start(bf16[3,64,128]{2,1,0:T(8,128)(2,1)S(1)} %get-tuple-element.65), channel_id=1, source_target_pairs={{1,2},{2,1},{3,4},{4,3},{5,6},{6,5},{9,10},{10,9},{11,12},{12,11},... | collective-permute-start | bytes 147464 | tf_op jit(solution)/shard_map/ppermute | solution.py:50
  114.4 1.7 %collective-permute-start.33 = (f32[88,128]{1,0:T(8,128)S(1)}, f32[88,128]{1,0:T(8,128)S(1)}, u32[]{:S(2)}, u32[]{:S(2)}) collective-permute-start(f32[88,128]{1,0:T(8,128)S(1)} %add_add_fusion.got0), channel_id=1, source_target_pairs={{0,8},{1,9},{2,10},{3,11},{4,12},{5,13},{6,14},{7,15},{8,0},{9,1},... | collective-permute-start | bytes 135176 | tf_op jit(solution)/shard_map/ppermute | solution.py:43
  116.2 2.4 %collective-permute-done.39.side_other = bf16[3,64,128]{2,1,0:T(8,128)(2,1)S(1)} collective-permute-done((bf16[3,64,128]{2,1,0:T(8,128)(2,1)S(1)}, bf16[3,64,128]{2,1,0:T(8,128)(2,1)S(1)}, u32[]{:S(2)}, u32[]{:S(2)}) %collective-permute-start.39) | collective-permute-done | bytes 49184 | tf_op jit(solution)/shard_map/ppermute | solution.py:50
  118.5 2.9 %shard_map.108 = bf16[32,64,128]{2,1,0:T(8,128)(2,1)} custom-call(s32[1]{0:T(128)} %bitcast.place, f32[8,128]{1,0:T(8,128)S(1)} %add_add_fusion.4.count, bf16[32,64,128]{2,1,0:T(8,128)(2,1)S(1)} %get-tuple-element.61.own.low, bf16[8,64,128]{2,1,0:T(8,128)(2,1)S(1)} %collective-permute-done.36.mate, bf16[8,64,128]{2,1,0:T(8,128)(2,1)S(1)} %collective-permute-done.37.other, ...), custom_call_target="tpu_custom_call" | custom-call | bytes 14400000 | tf_op jit(solution)/shard_map/pallas_call | solution.py:19
  121.5 0.8 shard_map.106
  (66 shorter events, 1.9 us)
Async XLA Ops:
  0.6 61.0 %copy-start.4 = (s32[32,128]{1,0:T(8,128)S(1)}, s32[32,128]{1,0:T(8,128)}, u32[]{:S(2)}) copy-start(s32[32,128]{1,0:T(8,128)} %labels.3) | copy-start | bytes 49156
  0.6 61.0 %copy-start.7 = (f32[37]{0:T(128)S(1)}, f32[37]{0:T(128)}, u32[]{:S(2)}) copy-start(f32[37]{0:T(128)} %param.9) | copy-start | bytes 448
  0.7 61.0 %copy-start.6 = (bf16[64,37]{0,1:T(8,128)(2,1)S(1)}, bf16[64,37]{0,1:T(8,128)(2,1)}, u32[]{:S(2)}) copy-start(bf16[64,37]{0,1:T(8,128)(2,1)} %param.8) | copy-start | bytes 14212
  0.7 1.0 copy-start.2
  1.7 0.7 copy-start.5
  3.1 14.6 %collective-permute-start.2 = (f32[8,128]{1,0:T(8,128)S(1)}, f32[8,128]{1,0:T(8,128)S(1)}, u32[]{:S(2)}, u32[]{:S(2)}) collective-permute-start(f32[8,128]{1,0:T(8,128)S(1)} %get-tuple-element.37), channel_id=1, source_target_pairs={{0,96},{1,97},{2,98},{3,99},{4,100},{5,101},{6,102},{7,103},{8,104... | collective-permute-start | bytes 12296 | tf_op jit(solution)/shard_map/ppermute | solution.py:43
  9.5 8.3 %collective-permute-start.1 = (f32[8,128]{1,0:T(8,128)S(1)}, f32[8,128]{1,0:T(8,128)S(1)}, u32[]{:S(2)}, u32[]{:S(2)}) collective-permute-start(f32[8,128]{1,0:T(8,128)S(1)} %get-tuple-element.37), channel_id=1, source_target_pairs={{0,64},{1,65},{2,66},{3,67},{4,68},{5,69},{6,70},{7,71},{8,72},{9,... | collective-permute-start | bytes 12296 | tf_op jit(solution)/shard_map/ppermute | solution.py:43
  10.5 7.3 %collective-permute-start = (f32[8,128]{1,0:T(8,128)S(1)}, f32[8,128]{1,0:T(8,128)S(1)}, u32[]{:S(2)}, u32[]{:S(2)}) collective-permute-start(f32[8,128]{1,0:T(8,128)S(1)} %get-tuple-element.37), channel_id=1, source_target_pairs={{0,32},{1,33},{2,34},{3,35},{4,36},{5,37},{6,38},{7,39},{8,40},{9,... | collective-permute-start | bytes 12296 | tf_op jit(solution)/shard_map/ppermute | solution.py:43
  11.9 10.0 %collective-permute-start.6 = (bf16[8,64,128]{2,1,0:T(8,128)(2,1)S(1)}, bf16[8,64,128]{2,1,0:T(8,128)(2,1)S(1)}, u32[]{:S(2)}, u32[]{:S(2)}) collective-permute-start(bf16[8,64,128]{2,1,0:T(8,128)(2,1)S(1)} %get-tuple-element.40), channel_id=1, source_target_pairs={{0,8},{8,0},{16,24},{24,16},{32,40},{40,32},{48,56},{56,48},{64,72... | collective-permute-start | bytes 393224 | tf_op jit(solution)/shard_map/ppermute | solution.py:50
  11.9 10.0 %collective-permute-start.7 = (bf16[8,64,128]{2,1,0:T(8,128)(2,1)S(1)}, bf16[8,64,128]{2,1,0:T(8,128)(2,1)S(1)}, u32[]{:S(2)}, u32[]{:S(2)}) collective-permute-start(bf16[8,64,128]{2,1,0:T(8,128)(2,1)S(1)} %get-tuple-element.41), channel_id=1, source_target_pairs={{8,16},{16,8},{24,32},{32,24},{40,48},{48,40},{56,64},{64,56},{72,... | collective-permute-start | bytes 393224 | tf_op jit(solution)/shard_map/ppermute | solution.py:50
  17.8 11.1 %collective-permute-start.5 = (f32[8,128]{1,0:T(8,128)S(1)}, f32[8,128]{1,0:T(8,128)S(1)}, u32[]{:S(2)}, u32[]{:S(2)}) collective-permute-start(f32[8,128]{1,0:T(8,128)S(1)} %add_add_fusion.7), channel_id=1, source_target_pairs={{0,129},{1,128},{2,131},{3,130},{4,133},{5,132},{6,135},{7,134},{8... | collective-permute-start | bytes 12296 | tf_op jit(solution)/shard_map/ppermute | solution.py:43
  17.9 11.0 %collective-permute-start.4 = (f32[8,128]{1,0:T(8,128)S(1)}, f32[8,128]{1,0:T(8,128)S(1)}, u32[]{:S(2)}, u32[]{:S(2)}) collective-permute-start(f32[8,128]{1,0:T(8,128)S(1)} %add_add_fusion.7), channel_id=1, source_target_pairs={{0,1},{1,0},{2,3},{3,2},{4,5},{5,4},{6,7},{7,6},{8,9},{9,8},{10,11... | collective-permute-start | bytes 12296 | tf_op jit(solution)/shard_map/ppermute | solution.py:43
  19.9 9.0 %collective-permute-start.3 = (f32[8,128]{1,0:T(8,128)S(1)}, f32[8,128]{1,0:T(8,128)S(1)}, u32[]{:S(2)}, u32[]{:S(2)}) collective-permute-start(f32[8,128]{1,0:T(8,128)S(1)} %add_add_fusion.7), channel_id=1, source_target_pairs={{0,128},{1,129},{2,130},{3,131},{4,132},{5,133},{6,134},{7,135},{8... | collective-permute-start | bytes 12296 | tf_op jit(solution)/shard_map/ppermute | solution.py:43
  22.5 6.5 %collective-permute-start.8 = (bf16[3,64,128]{2,1,0:T(8,128)(2,1)S(1)}, bf16[3,64,128]{2,1,0:T(8,128)(2,1)S(1)}, u32[]{:S(2)}, u32[]{:S(2)}) collective-permute-start(bf16[3,64,128]{2,1,0:T(8,128)(2,1)S(1)} %get-tuple-element.42), channel_id=1, source_target_pairs={{0,1},{1,0},{2,3},{3,2},{4,5},{5,4},{6,7},{7,6},{8,9},{9,8},{10,11... | collective-permute-start | bytes 147464 | tf_op jit(solution)/shard_map/ppermute | solution.py:50
  23.5 8.4 %collective-permute-start.9 = (bf16[3,64,128]{2,1,0:T(8,128)(2,1)S(1)}, bf16[3,64,128]{2,1,0:T(8,128)(2,1)S(1)}, u32[]{:S(2)}, u32[]{:S(2)}) collective-permute-start(bf16[3,64,128]{2,1,0:T(8,128)(2,1)S(1)} %get-tuple-element.43), channel_id=1, source_target_pairs={{1,2},{2,1},{3,4},{4,3},{5,6},{6,5},{9,10},{10,9},{11,12},{12,11},... | collective-permute-start | bytes 147464 | tf_op jit(solution)/shard_map/ppermute | solution.py:50
  31.9 0.9 copy-start
  32.8 0.7 copy-start.3
  36.9 6.8 %collective-permute-start.10 = (bf16[1056,128]{1,0:T(8,128)(2,1)S(1)}, bf16[1056,128]{1,0:T(8,128)(2,1)S(1)}, u32[]{:S(2)}, u32[]{:S(2)}) collective-permute-start(bf16[1056,128]{1,0:T(8,128)(2,1)S(1)} %get-tuple-element.46), channel_id=1, source_target_pairs={{0,2},{1,3},{2,0},{3,1},{4,6},{5,7},{6,4},{7,5},{8,10},{9,11},{10,... | collective-permute-start | bytes 811016 | tf_op jit(solution)/shard_map/ppermute | solution.py:43
  38.5 19.7 %collective-permute-start.18 = (bf16[1056,128]{1,0:T(8,128)(2,1)S(1)}, bf16[1056,128]{1,0:T(8,128)(2,1)S(1)}, u32[]{:S(2)}, u32[]{:S(2)}) collective-permute-start(bf16[1056,128]{1,0:T(8,128)(2,1)S(1)} %get-tuple-element.49), channel_id=1, source_target_pairs={{0,16},{1,48},{2,80},{3,112},{4,144},{5,176},{6,208},{7,240},{8,24... | collective-permute-start | bytes 811016 | tf_op jit(solution)/shard_map/ppermute | solution.py:43
  43.7 16.5 %collective-permute-start.17 = (bf16[1056,128]{1,0:T(8,128)(2,1)S(1)}, bf16[1056,128]{1,0:T(8,128)(2,1)S(1)}, u32[]{:S(2)}, u32[]{:S(2)}) collective-permute-start(bf16[1056,128]{1,0:T(8,128)(2,1)S(1)} %collective-permute-done.10), channel_id=1, source_target_pairs={{0,64},{1,96},{2,0},{3,32},{4,192},{5,224},{6,128},{7,160},{8,72},... | collective-permute-start | bytes 811016 | tf_op jit(solution)/shard_map/ppermute | solution.py:43
  49.2 4.8 %collective-permute-start.13 = (f32[8,128]{1,0:T(8,128)S(1)}, f32[8,128]{1,0:T(8,128)S(1)}, u32[]{:S(2)}, u32[]{:S(2)}) collective-permute-start(f32[8,128]{1,0:T(8,128)S(1)} %add_add_fusion.6), channel_id=1, source_target_pairs={{0,6},{1,7},{2,4},{3,5},{4,2},{5,3},{6,0},{7,1},{8,14},{9,15},{10,... | collective-permute-start | bytes 12296 | tf_op jit(solution)/shard_map/ppermute | solution.py:43
  49.3 5.1 %collective-permute-start.12 = (f32[8,128]{1,0:T(8,128)S(1)}, f32[8,128]{1,0:T(8,128)S(1)}, u32[]{:S(2)}, u32[]{:S(2)}) collective-permute-start(f32[8,128]{1,0:T(8,128)S(1)} %add_add_fusion.6), channel_id=1, source_target_pairs={{0,4},{1,5},{2,6},{3,7},{4,0},{5,1},{6,2},{7,3},{8,12},{9,13},{10,... | collective-permute-start | bytes 12296 | tf_op jit(solution)/shard_map/ppermute | solution.py:43
  50.6 4.3 %collective-permute-start.11 = (f32[8,128]{1,0:T(8,128)S(1)}, f32[8,128]{1,0:T(8,128)S(1)}, u32[]{:S(2)}, u32[]{:S(2)}) collective-permute-start(f32[8,128]{1,0:T(8,128)S(1)} %add_add_fusion.6), channel_id=1, source_target_pairs={{0,2},{1,3},{2,0},{3,1},{4,6},{5,7},{6,4},{7,5},{8,10},{9,11},{10,... | collective-permute-start | bytes 12296 | tf_op jit(solution)/shard_map/ppermute | solution.py:43
  54.9 5.4 %collective-permute-start.16 = (f32[8,128]{1,0:T(8,128)S(1)}, f32[8,128]{1,0:T(8,128)S(1)}, u32[]{:S(2)}, u32[]{:S(2)}) collective-permute-start(f32[8,128]{1,0:T(8,128)S(1)} %add_add_fusion.5), channel_id=1, source_target_pairs={{0,24},{1,25},{2,26},{3,27},{4,28},{5,29},{6,30},{7,31},{8,16},{9,... | collective-permute-start | bytes 12296 | tf_op jit(solution)/shard_map/ppermute | solution.py:43
  55.6 4.7 %collective-permute-start.15 = (f32[8,128]{1,0:T(8,128)S(1)}, f32[8,128]{1,0:T(8,128)S(1)}, u32[]{:S(2)}, u32[]{:S(2)}) collective-permute-start(f32[8,128]{1,0:T(8,128)S(1)} %add_add_fusion.5), channel_id=1, source_target_pairs={{0,16},{1,17},{2,18},{3,19},{4,20},{5,21},{6,22},{7,23},{8,24},{9,... | collective-permute-start | bytes 12296 | tf_op jit(solution)/shard_map/ppermute | solution.py:43
  58.2 2.1 %collective-permute-start.14 = (f32[8,128]{1,0:T(8,128)S(1)}, f32[8,128]{1,0:T(8,128)S(1)}, u32[]{:S(2)}, u32[]{:S(2)}) collective-permute-start(f32[8,128]{1,0:T(8,128)S(1)} %add_add_fusion.5), channel_id=1, source_target_pairs={{0,8},{1,9},{2,10},{3,11},{4,12},{5,13},{6,14},{7,15},{8,0},{9,1},... | collective-permute-start | bytes 12296 | tf_op jit(solution)/shard_map/ppermute | solution.py:43
  58.2 2.1 %collective-permute-start.20 = (bf16[528,128]{1,0:T(8,128)(2,1)S(1)}, bf16[528,128]{1,0:T(8,128)(2,1)S(1)}, u32[]{:S(2)}, u32[]{:S(2)}) collective-permute-start(bf16[528,128]{1,0:T(8,128)(2,1)S(1)} %slice.9), channel_id=1, source_target_pairs={{0,8},{1,9},{2,10},{3,11},{4,12},{5,13},{6,14},{7,15},{8,0},{9,1},... | collective-permute-start | bytes 405512 | tf_op jit(solution)/shard_map/ppermute | solution.py:43
  60.2 1.4 %collective-permute-start.19 = (bf16[528,128]{1,0:T(8,128)(2,1)S(1)}, bf16[528,128]{1,0:T(8,128)(2,1)S(1)}, u32[]{:S(2)}, u32[]{:S(2)}) collective-permute-start(bf16[528,128]{1,0:T(8,128)(2,1)S(1)} %slice.8), channel_id=1, source_target_pairs={{0,8},{1,9},{2,10},{3,11},{4,12},{5,13},{6,14},{7,15},{8,0},{9,1},... | collective-permute-start | bytes 405512 | tf_op jit(solution)/shard_map/ppermute | solution.py:43
  66.0 52.5 %copy-start.1 = (bf16[3,3,64,64]{3,2,1,0:T(8,128)(2,1)S(1)}, bf16[3,3,64,64]{3,2,1,0:T(8,128)(2,1)}, u32[]{:S(2)}) copy-start(bf16[3,3,64,64]{3,2,1,0:T(8,128)(2,1)} %param.7) | copy-start | bytes 221188
  68.3 2.0 %collective-permute-start.21 = (f32[88,128]{1,0:T(8,128)S(1)}, f32[88,128]{1,0:T(8,128)S(1)}, u32[]{:S(2)}, u32[]{:S(2)}) collective-permute-start(f32[88,128]{1,0:T(8,128)S(1)} %get-tuple-element.57), channel_id=1, source_target_pairs={{0,8},{1,9},{2,10},{3,11},{4,12},{5,13},{6,14},{7,15},{8,0},{9,1},... | collective-permute-start | bytes 135176 | tf_op jit(solution)/shard_map/ppermute | solution.py:43
  68.5 4.5 %collective-permute-start.22 = (f32[88,128]{1,0:T(8,128)S(1)}, f32[88,128]{1,0:T(8,128)S(1)}, u32[]{:S(2)}, u32[]{:S(2)}) collective-permute-start(f32[88,128]{1,0:T(8,128)S(1)} %get-tuple-element.58), channel_id=1, source_target_pairs={{0,16},{1,17},{2,18},{3,19},{4,20},{5,21},{6,22},{7,23},{8,24},{9,... | collective-permute-start | bytes 135176 | tf_op jit(solution)/shard_map/ppermute | solution.py:43
  69.1 4.0 %collective-permute-start.23 = (f32[88,128]{1,0:T(8,128)S(1)}, f32[88,128]{1,0:T(8,128)S(1)}, u32[]{:S(2)}, u32[]{:S(2)}) collective-permute-start(f32[88,128]{1,0:T(8,128)S(1)} %get-tuple-element.59), channel_id=1, source_target_pairs={{0,24},{1,25},{2,26},{3,27},{4,28},{5,29},{6,30},{7,31},{8,16},{9,... | collective-permute-start | bytes 135176 | tf_op jit(solution)/shard_map/ppermute | solution.py:43
  73.0 15.3 %collective-permute-start.26 = (f32[88,128]{1,0:T(8,128)S(1)}, f32[88,128]{1,0:T(8,128)S(1)}, u32[]{:S(2)}, u32[]{:S(2)}) collective-permute-start(f32[88,128]{1,0:T(8,128)S(1)} %add_add_fusion.3), channel_id=1, source_target_pairs={{0,96},{1,97},{2,98},{3,99},{4,100},{5,101},{6,102},{7,103},{8,104... | collective-permute-start | bytes 135176 | tf_op jit(solution)/shard_map/ppermute | solution.py:43
  85.9 8.6 %collective-permute-start.25 = (f32[88,128]{1,0:T(8,128)S(1)}, f32[88,128]{1,0:T(8,128)S(1)}, u32[]{:S(2)}, u32[]{:S(2)}) collective-permute-start(f32[88,128]{1,0:T(8,128)S(1)} %add_add_fusion.3), channel_id=1, source_target_pairs={{0,64},{1,65},{2,66},{3,67},{4,68},{5,69},{6,70},{7,71},{8,72},{9,... | collective-permute-start | bytes 135176 | tf_op jit(solution)/shard_map/ppermute | solution.py:43
  88.1 6.4 %collective-permute-start.24 = (f32[88,128]{1,0:T(8,128)S(1)}, f32[88,128]{1,0:T(8,128)S(1)}, u32[]{:S(2)}, u32[]{:S(2)}) collective-permute-start(f32[88,128]{1,0:T(8,128)S(1)} %add_add_fusion.3), channel_id=1, source_target_pairs={{0,32},{1,33},{2,34},{3,35},{4,36},{5,37},{6,38},{7,39},{8,40},{9,... | collective-permute-start | bytes 135176 | tf_op jit(solution)/shard_map/ppermute | solution.py:43
  94.5 9.4 %collective-permute-start.29 = (f32[88,128]{1,0:T(8,128)S(1)}, f32[88,128]{1,0:T(8,128)S(1)}, u32[]{:S(2)}, u32[]{:S(2)}) collective-permute-start(f32[88,128]{1,0:T(8,128)S(1)} %add_add_fusion.2), channel_id=1, source_target_pairs={{0,129},{1,128},{2,131},{3,130},{4,133},{5,132},{6,135},{7,134},{8... | collective-permute-start | bytes 135176 | tf_op jit(solution)/shard_map/ppermute | solution.py:43
  94.9 9.1 %collective-permute-start.28 = (f32[88,128]{1,0:T(8,128)S(1)}, f32[88,128]{1,0:T(8,128)S(1)}, u32[]{:S(2)}, u32[]{:S(2)}) collective-permute-start(f32[88,128]{1,0:T(8,128)S(1)} %add_add_fusion.2), channel_id=1, source_target_pairs={{0,1},{1,0},{2,3},{3,2},{4,5},{5,4},{6,7},{7,6},{8,9},{9,8},{10,11... | collective-permute-start | bytes 135176 | tf_op jit(solution)/shard_map/ppermute | solution.py:43
  99.0 5.0 %collective-permute-start.27 = (f32[88,128]{1,0:T(8,128)S(1)}, f32[88,128]{1,0:T(8,128)S(1)}, u32[]{:S(2)}, u32[]{:S(2)}) collective-permute-start(f32[88,128]{1,0:T(8,128)S(1)} %add_add_fusion.2), channel_id=1, source_target_pairs={{0,128},{1,129},{2,130},{3,131},{4,132},{5,133},{6,134},{7,135},{8... | collective-permute-start | bytes 135176 | tf_op jit(solution)/shard_map/ppermute | solution.py:43
  99.0 9.2 %collective-permute-start.36 = (bf16[8,64,128]{2,1,0:T(8,128)(2,1)S(1)}, bf16[8,64,128]{2,1,0:T(8,128)(2,1)S(1)}, u32[]{:S(2)}, u32[]{:S(2)}) collective-permute-start(bf16[8,64,128]{2,1,0:T(8,128)(2,1)S(1)} %get-tuple-element.62), channel_id=1, source_target_pairs={{0,8},{8,0},{16,24},{24,16},{32,40},{40,32},{48,56},{56,48},{64,72... | collective-permute-start | bytes 393224 | tf_op jit(solution)/shard_map/ppermute | solution.py:50
  99.0 9.2 %collective-permute-start.37 = (bf16[8,64,128]{2,1,0:T(8,128)(2,1)S(1)}, bf16[8,64,128]{2,1,0:T(8,128)(2,1)S(1)}, u32[]{:S(2)}, u32[]{:S(2)}) collective-permute-start(bf16[8,64,128]{2,1,0:T(8,128)(2,1)S(1)} %get-tuple-element.63), channel_id=1, source_target_pairs={{8,16},{16,8},{24,32},{32,24},{40,48},{48,40},{56,64},{64,56},{72,... | collective-permute-start | bytes 393224 | tf_op jit(solution)/shard_map/ppermute | solution.py:50
  104.0 10.2 %collective-permute-start.32 = (f32[88,128]{1,0:T(8,128)S(1)}, f32[88,128]{1,0:T(8,128)S(1)}, u32[]{:S(2)}, u32[]{:S(2)}) collective-permute-start(f32[88,128]{1,0:T(8,128)S(1)} %add_add_fusion.1), channel_id=1, source_target_pairs={{0,6},{1,7},{2,4},{3,5},{4,2},{5,3},{6,0},{7,1},{8,14},{9,15},{10,... | collective-permute-start | bytes 135176 | tf_op jit(solution)/shard_map/ppermute | solution.py:43
  105.5 8.6 %collective-permute-start.31 = (f32[88,128]{1,0:T(8,128)S(1)}, f32[88,128]{1,0:T(8,128)S(1)}, u32[]{:S(2)}, u32[]{:S(2)}) collective-permute-start(f32[88,128]{1,0:T(8,128)S(1)} %add_add_fusion.1), channel_id=1, source_target_pairs={{0,4},{1,5},{2,6},{3,7},{4,0},{5,1},{6,2},{7,3},{8,12},{9,13},{10,... | collective-permute-start | bytes 135176 | tf_op jit(solution)/shard_map/ppermute | solution.py:43
  106.7 7.5 %collective-permute-start.30 = (f32[88,128]{1,0:T(8,128)S(1)}, f32[88,128]{1,0:T(8,128)S(1)}, u32[]{:S(2)}, u32[]{:S(2)}) collective-permute-start(f32[88,128]{1,0:T(8,128)S(1)} %add_add_fusion.1), channel_id=1, source_target_pairs={{0,2},{1,3},{2,0},{3,1},{4,6},{5,7},{6,4},{7,5},{8,10},{9,11},{10,... | collective-permute-start | bytes 135176 | tf_op jit(solution)/shard_map/ppermute | solution.py:43
  108.7 7.5 %collective-permute-start.38 = (bf16[3,64,128]{2,1,0:T(8,128)(2,1)S(1)}, bf16[3,64,128]{2,1,0:T(8,128)(2,1)S(1)}, u32[]{:S(2)}, u32[]{:S(2)}) collective-permute-start(bf16[3,64,128]{2,1,0:T(8,128)(2,1)S(1)} %get-tuple-element.64), channel_id=1, source_target_pairs={{0,1},{1,0},{2,3},{3,2},{4,5},{5,4},{6,7},{7,6},{8,9},{9,8},{10,11... | collective-permute-start | bytes 147464 | tf_op jit(solution)/shard_map/ppermute | solution.py:50
  110.2 8.4 %collective-permute-start.39 = (bf16[3,64,128]{2,1,0:T(8,128)(2,1)S(1)}, bf16[3,64,128]{2,1,0:T(8,128)(2,1)S(1)}, u32[]{:S(2)}, u32[]{:S(2)}) collective-permute-start(bf16[3,64,128]{2,1,0:T(8,128)(2,1)S(1)} %get-tuple-element.65), channel_id=1, source_target_pairs={{1,2},{2,1},{3,4},{4,3},{5,6},{6,5},{9,10},{10,9},{11,12},{12,11},... | collective-permute-start | bytes 147464 | tf_op jit(solution)/shard_map/ppermute | solution.py:50
  114.2 7.2 %collective-permute-start.35 = (f32[88,128]{1,0:T(8,128)S(1)}, f32[88,128]{1,0:T(8,128)S(1)}, u32[]{:S(2)}, u32[]{:S(2)}) collective-permute-start(f32[88,128]{1,0:T(8,128)S(1)} %add_add_fusion.got0), channel_id=1, source_target_pairs={{0,24},{1,25},{2,26},{3,27},{4,28},{5,29},{6,30},{7,31},{8,16},{9,... | collective-permute-start | bytes 135176 | tf_op jit(solution)/shard_map/ppermute | solution.py:43
  114.3 7.1 %collective-permute-start.34 = (f32[88,128]{1,0:T(8,128)S(1)}, f32[88,128]{1,0:T(8,128)S(1)}, u32[]{:S(2)}, u32[]{:S(2)}) collective-permute-start(f32[88,128]{1,0:T(8,128)S(1)} %add_add_fusion.got0), channel_id=1, source_target_pairs={{0,16},{1,17},{2,18},{3,19},{4,20},{5,21},{6,22},{7,23},{8,24},{9,... | collective-permute-start | bytes 135176 | tf_op jit(solution)/shard_map/ppermute | solution.py:43
  114.4 7.0 %collective-permute-start.33 = (f32[88,128]{1,0:T(8,128)S(1)}, f32[88,128]{1,0:T(8,128)S(1)}, u32[]{:S(2)}, u32[]{:S(2)}) collective-permute-start(f32[88,128]{1,0:T(8,128)S(1)} %add_add_fusion.got0), channel_id=1, source_target_pairs={{0,8},{1,9},{2,10},{3,11},{4,12},{5,13},{6,14},{7,15},{8,0},{9,1},... | collective-permute-start | bytes 135176 | tf_op jit(solution)/shard_map/ppermute | solution.py:43

commit v9 on v8

--- a/solution.py
+++ b/solution.py
@@ -387,13 +387,15 @@
     return value
 
 
-def mirrored(pay_near, pay_far, parts):
+def mirrored(pay_near, pay_far, counted, parts):
     length = pay_near.shape[0] // 2
     pay_near = send(pay_near, lambda r, c: (r, c ^ 2))
+    counted = total_small(counted, (3,))
+    pay_near, pay_far, counted = lax.optimization_barrier((pay_near, pay_far, counted))
     near = send(pay_near, lambda r, c: (parts * (c ^ 2) + r % parts, r // parts))
     far = send(pay_far, lambda r, c: (parts * c + (r % parts ^ 2), r // parts))
     mate = lambda r, c: (r ^ 1, c)
-    return pay_near, (near, far, send(near[length:], mate), send(far[length:], mate))
+    return (near, far, send(near[length:], mate), send(far[length:], mate)), total_small(counted, (0,))
 
 
 def total_quarters(quarters):
@@ -438,9 +440,8 @@
         scalars=1,
         micros=5,
     )
-    passed, got = mirrored(pay_near, pay_far, parts)
-    _, counted = lax.optimization_barrier((passed, counted))
-    count = total_small(counted, (3, 0))
+    _, counted = lax.optimization_barrier((mixed, counted))
+    got, count = mirrored(pay_near, pay_far, counted, parts)
     grad, head_sum, bias_sum, loss_sum = run(
         softmax_kernel,
         [

time: 123 us -> 130 us (1.057)
  waiting for transfers between devices: 18.4 us -> 34.7 us
  starting transfers between devices: 83.9 us -> 74.4 us
    ppermute x32, waiting for transfers between devices: 13.1 us -> 29.4 us  [send(): return lax.ppermute(block, GRID, pairs)]
    ppermute x32, starting transfers between devices: 61.3 us -> 51.2 us  [send(): return lax.ppermute(block, GRID, pairs)]
    ppermute x4, starting transfers between devices: 2.5 us -> 4.06 us  [swapped(): lax.ppermute(to_mate, axis, mates)]
  transfers between devices with their start and end apart: 40 -> 40, of which waited for: 10 -> 14; matrix products, arithmetic and copies ran while one was open for 0% -> 0% of each run, Pallas kernels for 3% -> 3%
where the time goes in v9:
time: 130 us; the launch traced here: 129 us
  starting transfers between devices  74.4 us (57%)
  waiting for transfers between devices  34.7 us (27%)
  Pallas kernels  15.4 us (12%)
  local copies, waits for them, and re-layouts  3.42 us (3%)
    ppermute x32, starting transfers between devices, send(): return lax.ppermute(block, GRID, pairs)  51.2 us
    ppermute x32, waiting for transfers between devices, send(): return lax.ppermute(block, GRID, pairs)  29.4 us
    ppermute x4, starting transfers between devices, swapped(): lax.ppermute(to_other, axis, others)  19.1 us
    pallas_call x8, Pallas kernels, run(): pl.pallas_call(body, out_shape=outs, in_specs=[SMEM] * scalars + [VMEM] *...  15.4 us
    ppermute x4, waiting for transfers between devices, swapped(): lax.ppermute(to_other, axis, others)  5.33 us
    ppermute x4, starting transfers between devices, swapped(): lax.ppermute(to_mate, axis, mates)  4.06 us
    unnamed x16, local copies, waits for them, and re-layouts  3.4 us
  transfers between devices with their start and end apart: 40, of which 14 were waited for; matrix products, arithmetic and copies ran while one was open for 0% of the time, Pallas kernels for 3%

profile of v9, /device:TPU:24, one launch (start us, length us, event | category | flops | bytes accessed | tf_op | source)
XLA Modules:
  0.0 129.0 jit_solution(4518631378269639561)
XLA Ops:
  0.7 1.0 copy-done.2
  1.7 0.7 copy-done.5
  2.4 0.7 shard_map.101
  3.1 6.3 %collective-permute-start.2 = (f32[8,128]{1,0:T(8,128)S(1)}, f32[8,128]{1,0:T(8,128)S(1)}, u32[]{:S(2)}, u32[]{:S(2)}) collective-permute-start(f32[8,128]{1,0:T(8,128)S(1)} %get-tuple-element.40), channel_id=1, source_target_pairs={{0,96},{1,97},{2,98},{3,99},{4,100},{5,101},{6,102},{7,103},{8,104... | collective-permute-start | bytes 12296 | tf_op jit(solution)/shard_map/ppermute | solution.py:43
  9.5 1.0 collective-permute-start.1
  10.5 1.5 %collective-permute-start = (f32[8,128]{1,0:T(8,128)S(1)}, f32[8,128]{1,0:T(8,128)S(1)}, u32[]{:S(2)}, u32[]{:S(2)}) collective-permute-start(f32[8,128]{1,0:T(8,128)S(1)} %get-tuple-element.40), channel_id=1, source_target_pairs={{0,32},{1,33},{2,34},{3,35},{4,36},{5,37},{6,38},{7,39},{8,40},{9,... | collective-permute-start | bytes 12296 | tf_op jit(solution)/shard_map/ppermute | solution.py:43
  11.9 5.8 %collective-permute-start.7 = (bf16[8,64,128]{2,1,0:T(8,128)(2,1)S(1)}, bf16[8,64,128]{2,1,0:T(8,128)(2,1)S(1)}, u32[]{:S(2)}, u32[]{:S(2)}) collective-permute-start(bf16[8,64,128]{2,1,0:T(8,128)(2,1)S(1)} %get-tuple-element.44), channel_id=1, source_target_pairs={{8,16},{16,8},{24,32},{32,24},{40,48},{48,40},{56,64},{64,56},{72,... | collective-permute-start | bytes 393224 | tf_op jit(solution)/shard_map/ppermute | solution.py:50
  17.9 2.0 %collective-permute-start.4 = (f32[8,128]{1,0:T(8,128)S(1)}, f32[8,128]{1,0:T(8,128)S(1)}, u32[]{:S(2)}, u32[]{:S(2)}) collective-permute-start(f32[8,128]{1,0:T(8,128)S(1)} %add_add_fusion.7), channel_id=1, source_target_pairs={{0,1},{1,0},{2,3},{3,2},{4,5},{5,4},{6,7},{7,6},{8,9},{9,8},{10,11... | collective-permute-start | bytes 12296 | tf_op jit(solution)/shard_map/ppermute | solution.py:43
  19.9 2.1 %collective-permute-start.3 = (f32[8,128]{1,0:T(8,128)S(1)}, f32[8,128]{1,0:T(8,128)S(1)}, u32[]{:S(2)}, u32[]{:S(2)}) collective-permute-start(f32[8,128]{1,0:T(8,128)S(1)} %add_add_fusion.7), channel_id=1, source_target_pairs={{0,128},{1,129},{2,130},{3,131},{4,132},{5,133},{6,134},{7,135},{8... | collective-permute-start | bytes 12296 | tf_op jit(solution)/shard_map/ppermute | solution.py:43
  22.5 1.0 collective-permute-start.8
  23.5 5.4 %collective-permute-start.9 = (bf16[3,64,128]{2,1,0:T(8,128)(2,1)S(1)}, bf16[3,64,128]{2,1,0:T(8,128)(2,1)S(1)}, u32[]{:S(2)}, u32[]{:S(2)}) collective-permute-start(bf16[3,64,128]{2,1,0:T(8,128)(2,1)S(1)} %get-tuple-element.46), channel_id=1, source_target_pairs={{1,2},{2,1},{3,4},{4,3},{5,6},{6,5},{9,10},{10,9},{11,12},{12,11},... | collective-permute-start | bytes 147464 | tf_op jit(solution)/shard_map/ppermute | solution.py:50
  29.0 2.9 %collective-permute-done.9.side_other = bf16[3,64,128]{2,1,0:T(8,128)(2,1)S(1)} collective-permute-done((bf16[3,64,128]{2,1,0:T(8,128)(2,1)S(1)}, bf16[3,64,128]{2,1,0:T(8,128)(2,1)S(1)}, u32[]{:S(2)}, u32[]{:S(2)}) %collective-permute-start.9) | collective-permute-done | bytes 49184 | tf_op jit(solution)/shard_map/ppermute | solution.py:50
  31.9 0.9 copy-done
  32.8 0.7 copy-done.3
  33.5 3.4 %shard_map.103 = (bf16[48,192,128]{2,1,0:T(8,128)(2,1)S(1)}, bf16[32,64,128]{2,1,0:T(8,128)(2,1)S(1)}, bf16[1056,128]{1,0:T(8,128)(2,1)S(1)}, bf16[1056,128]{1,0:T(8,128)(2,1)S(1)}) custom-call(s32[1]{0:T(128)} %bitcast.place, bf16[32,64,128]{2,1,0:T(8,128)(2,1)S(1)} %get-tuple-element.42.own.act, bf16[8,64,128]{2,1,0:T(8,128)(2,1)S(1)} %collective-permute-done.6.mate, ...), custom_call_target="tpu_custom_call" | custom-call | bytes 18000000 | tf_op jit(solution)/shard_map/pallas_call | solution.py:19
  36.9 1.6 %collective-permute-start.10 = (bf16[1056,128]{1,0:T(8,128)(2,1)S(1)}, bf16[1056,128]{1,0:T(8,128)(2,1)S(1)}, u32[]{:S(2)}, u32[]{:S(2)}) collective-permute-start(bf16[1056,128]{1,0:T(8,128)(2,1)S(1)} %get-tuple-element.49), channel_id=1, source_target_pairs={{0,2},{1,3},{2,0},{3,1},{4,6},{5,7},{6,4},{7,5},{8,10},{9,11},{10,... | collective-permute-start | bytes 811016 | tf_op jit(solution)/shard_map/ppermute | solution.py:43
  38.5 2.1 %collective-permute-start.13 = (f32[8,128]{1,0:T(8,128)S(1)}, f32[8,128]{1,0:T(8,128)S(1)}, u32[]{:S(2)}, u32[]{:S(2)}) collective-permute-start(f32[8,128]{1,0:T(8,128)S(1)} %add_add_fusion.6), channel_id=1, source_target_pairs={{0,6},{1,7},{2,4},{3,5},{4,2},{5,3},{6,0},{7,1},{8,14},{9,15},{10,... | collective-permute-start | bytes 12296 | tf_op jit(solution)/shard_map/ppermute | solution.py:43
  40.6 0.5 collective-permute-start.12
  41.1 1.5 %collective-permute-start.11 = (f32[8,128]{1,0:T(8,128)S(1)}, f32[8,128]{1,0:T(8,128)S(1)}, u32[]{:S(2)}, u32[]{:S(2)}) collective-permute-start(f32[8,128]{1,0:T(8,128)S(1)} %add_add_fusion.6), channel_id=1, source_target_pairs={{0,2},{1,3},{2,0},{3,1},{4,6},{5,7},{6,4},{7,5},{8,10},{9,11},{10,... | collective-permute-start | bytes 12296 | tf_op jit(solution)/shard_map/ppermute | solution.py:43
  42.6 0.7 collective-permute-done.13
  43.3 2.4 %collective-permute-done.12 = f32[8,128]{1,0:T(8,128)S(1)} collective-permute-done((f32[8,128]{1,0:T(8,128)S(1)}, f32[8,128]{1,0:T(8,128)S(1)}, u32[]{:S(2)}, u32[]{:S(2)}) %collective-permute-start.12) | collective-permute-done | bytes 4128 | tf_op jit(solution)/shard_map/ppermute | solution.py:43
  45.7 4.7 %collective-permute-start.17 = (bf16[1056,128]{1,0:T(8,128)(2,1)S(1)}, bf16[1056,128]{1,0:T(8,128)(2,1)S(1)}, u32[]{:S(2)}, u32[]{:S(2)}) collective-permute-start(bf16[1056,128]{1,0:T(8,128)(2,1)S(1)} %collective-permute-done.10), channel_id=1, source_target_pairs={{0,64},{1,96},{2,0},{3,32},{4,192},{5,224},{6,128},{7,160},{8,72},... | collective-permute-start | bytes 811016 | tf_op jit(solution)/shard_map/ppermute | solution.py:43
  50.4 3.3 %collective-permute-start.18 = (bf16[1056,128]{1,0:T(8,128)(2,1)S(1)}, bf16[1056,128]{1,0:T(8,128)(2,1)S(1)}, u32[]{:S(2)}, u32[]{:S(2)}) collective-permute-start(bf16[1056,128]{1,0:T(8,128)(2,1)S(1)} %get-tuple-element.56), channel_id=1, source_target_pairs={{0,16},{1,48},{2,80},{3,112},{4,144},{5,176},{6,208},{7,240},{8,24... | collective-permute-start | bytes 811016 | tf_op jit(solution)/shard_map/ppermute | solution.py:43
  54.1 1.5 %collective-permute-start.14 = (f32[8,128]{1,0:T(8,128)S(1)}, f32[8,128]{1,0:T(8,128)S(1)}, u32[]{:S(2)}, u32[]{:S(2)}) collective-permute-start(f32[8,128]{1,0:T(8,128)S(1)} %add_add_fusion.5), channel_id=1, source_target_pairs={{0,8},{1,9},{2,10},{3,11},{4,12},{5,13},{6,14},{7,15},{8,0},{9,1},... | collective-permute-start | bytes 12296 | tf_op jit(solution)/shard_map/ppermute | solution.py:43
  55.6 9.7 %collective-permute-done.17.near = bf16[1056,128]{1,0:T(8,128)(2,1)S(1)} collective-permute-done((bf16[1056,128]{1,0:T(8,128)(2,1)S(1)}, bf16[1056,128]{1,0:T(8,128)(2,1)S(1)}, u32[]{:S(2)}, u32[]{:S(2)}) %collective-permute-start.17) | collective-permute-done | bytes 270368 | tf_op jit(solution)/shard_map/ppermute | solution.py:43
  65.6 6.1 %collective-permute-done.18.far = bf16[1056,128]{1,0:T(8,128)(2,1)S(1)} collective-permute-done((bf16[1056,128]{1,0:T(8,128)(2,1)S(1)}, bf16[1056,128]{1,0:T(8,128)(2,1)S(1)}, u32[]{:S(2)}, u32[]{:S(2)}) %collective-permute-start.18) | collective-permute-done | bytes 270368 | tf_op jit(solution)/shard_map/ppermute | solution.py:43
  71.8 0.9 collective-permute-done.16
  73.1 4.3 %shard_map.104 = (f32[32,64,128]{2,1,0:T(8,128)S(1)}, f32[120,64]{1,0:T(8,128)S(1)}, f32[40,128]{1,0:T(8,128)S(1)}, f32[1,128]{1,0:T(1,128)S(1)}) custom-call(s32[1]{0:T(128)} %bitcast.place, bf16[1056,128]{1,0:T(8,128)(2,1)S(1)} %collective-permute-done.17.near, bf16[1056,128]{1,0:T(8,128)(2,1)S(1)} %collective-permute-done.18.far, ...), custom_call_target="tpu_custom_call" | custom-call | bytes 18000000 | tf_op jit(solution)/shard_map/pallas_call | solution.py:19
  77.5 2.3 %shard_map.105 = (bf16[32,64,128]{2,1,0:T(8,128)(2,1)S(1)}, bf16[8,64,128]{2,1,0:T(8,128)(2,1)S(1)}, bf16[8,64,128]{2,1,0:T(8,128)(2,1)S(1)}, f32[88,128]{1,0:T(...) custom-call(s32[1]{0:T(128)} %bitcast.place, f32[8,128]{1,0:T(8,128)S(1)} %add_add_fusion.4.count, ...), custom_call_target="tpu_custom_call" | custom-call | bytes 10800000 | tf_op jit(solution)/shard_map/pallas_call | solution.py:19
  80.0 1.3 collective-permute-start.22
  81.7 2.3 %collective-permute-done.22 = f32[88,128]{1,0:T(8,128)S(1)} collective-permute-done((f32[88,128]{1,0:T(8,128)S(1)}, f32[88,128]{1,0:T(8,128)S(1)}, u32[]{:S(2)}, u32[]{:S(2)}) %collective-permute-start.22) | collective-permute-done | bytes 45088 | tf_op jit(solution)/shard_map/ppermute | solution.py:43
  84.1 1.1 collective-permute-done.23
  85.2 3.2 %collective-permute-start.26 = (f32[88,128]{1,0:T(8,128)S(1)}, f32[88,128]{1,0:T(8,128)S(1)}, u32[]{:S(2)}, u32[]{:S(2)}) collective-permute-start(f32[88,128]{1,0:T(8,128)S(1)} %add_add_fusion.3), channel_id=1, source_target_pairs={{0,96},{1,97},{2,98},{3,99},{4,100},{5,101},{6,102},{7,103},{8,104... | collective-permute-start | bytes 135176 | tf_op jit(solution)/shard_map/ppermute | solution.py:43
  88.4 5.4 %collective-permute-start.25 = (f32[88,128]{1,0:T(8,128)S(1)}, f32[88,128]{1,0:T(8,128)S(1)}, u32[]{:S(2)}, u32[]{:S(2)}) collective-permute-start(f32[88,128]{1,0:T(8,128)S(1)} %add_add_fusion.3), channel_id=1, source_target_pairs={{0,64},{1,65},{2,66},{3,67},{4,68},{5,69},{6,70},{7,71},{8,72},{9,... | collective-permute-start | bytes 135176 | tf_op jit(solution)/shard_map/ppermute | solution.py:43
  93.9 3.0 %collective-permute-done.25 = f32[88,128]{1,0:T(8,128)S(1)} collective-permute-done((f32[88,128]{1,0:T(8,128)S(1)}, f32[88,128]{1,0:T(8,128)S(1)}, u32[]{:S(2)}, u32[]{:S(2)}) %collective-permute-start.25) | collective-permute-done | bytes 45088 | tf_op jit(solution)/shard_map/ppermute | solution.py:43
  96.8 2.2 %collective-permute-done.24 = f32[88,128]{1,0:T(8,128)S(1)} collective-permute-done((f32[88,128]{1,0:T(8,128)S(1)}, f32[88,128]{1,0:T(8,128)S(1)}, u32[]{:S(2)}, u32[]{:S(2)}) %collective-permute-start.24) | collective-permute-done | bytes 45088 | tf_op jit(solution)/shard_map/ppermute | solution.py:43
  99.0 4.2 %collective-permute-start.29 = (f32[88,128]{1,0:T(8,128)S(1)}, f32[88,128]{1,0:T(8,128)S(1)}, u32[]{:S(2)}, u32[]{:S(2)}) collective-permute-start(f32[88,128]{1,0:T(8,128)S(1)} %add_add_fusion.2), channel_id=1, source_target_pairs={{0,129},{1,128},{2,131},{3,130},{4,133},{5,132},{6,135},{7,134},{8... | collective-permute-start | bytes 135176 | tf_op jit(solution)/shard_map/ppermute | solution.py:43
  103.2 1.0 collective-permute-start.27
  104.2 4.0 %collective-permute-start.37 = (bf16[8,64,128]{2,1,0:T(8,128)(2,1)S(1)}, bf16[8,64,128]{2,1,0:T(8,128)(2,1)S(1)}, u32[]{:S(2)}, u32[]{:S(2)}) collective-permute-start(bf16[8,64,128]{2,1,0:T(8,128)(2,1)S(1)} %get-tuple-element.69), channel_id=1, source_target_pairs={{8,16},{16,8},{24,32},{32,24},{40,48},{48,40},{56,64},{64,56},{72,... | collective-permute-start | bytes 393224 | tf_op jit(solution)/shard_map/ppermute | solution.py:50
  108.2 0.6 collective-permute-done.28
  109.1 4.3 %collective-permute-start.31 = (f32[88,128]{1,0:T(8,128)S(1)}, f32[88,128]{1,0:T(8,128)S(1)}, u32[]{:S(2)}, u32[]{:S(2)}) collective-permute-start(f32[88,128]{1,0:T(8,128)S(1)} %add_add_fusion.1), channel_id=1, source_target_pairs={{0,4},{1,5},{2,6},{3,7},{4,0},{5,1},{6,2},{7,3},{8,12},{9,13},{10,... | collective-permute-start | bytes 135176 | tf_op jit(solution)/shard_map/ppermute | solution.py:43
  113.3 0.5 shard_map.107
  113.8 3.0 %collective-permute-start.38 = (bf16[3,64,128]{2,1,0:T(8,128)(2,1)S(1)}, bf16[3,64,128]{2,1,0:T(8,128)(2,1)S(1)}, u32[]{:S(2)}, u32[]{:S(2)}) collective-permute-start(bf16[3,64,128]{2,1,0:T(8,128)(2,1)S(1)} %get-tuple-element.70), channel_id=1, source_target_pairs={{0,1},{1,0},{2,3},{3,2},{4,5},{5,4},{6,7},{7,6},{8,9},{9,8},{10,11... | collective-permute-start | bytes 147464 | tf_op jit(solution)/shard_map/ppermute | solution.py:50
  116.9 3.9 %collective-permute-start.39 = (bf16[3,64,128]{2,1,0:T(8,128)(2,1)S(1)}, bf16[3,64,128]{2,1,0:T(8,128)(2,1)S(1)}, u32[]{:S(2)}, u32[]{:S(2)}) collective-permute-start(bf16[3,64,128]{2,1,0:T(8,128)(2,1)S(1)} %get-tuple-element.71), channel_id=1, source_target_pairs={{1,2},{2,1},{3,4},{4,3},{5,6},{6,5},{9,10},{10,9},{11,12},{12,11},... | collective-permute-start | bytes 147464 | tf_op jit(solution)/shard_map/ppermute | solution.py:50
  121.1 1.7 %collective-permute-start.33 = (f32[88,128]{1,0:T(8,128)S(1)}, f32[88,128]{1,0:T(8,128)S(1)}, u32[]{:S(2)}, u32[]{:S(2)}) collective-permute-start(f32[88,128]{1,0:T(8,128)S(1)} %add_add_fusion.got0), channel_id=1, source_target_pairs={{0,8},{1,9},{2,10},{3,11},{4,12},{5,13},{6,14},{7,15},{8,0},{9,1},... | collective-permute-start | bytes 135176 | tf_op jit(solution)/shard_map/ppermute | solution.py:43
  122.8 2.4 %collective-permute-done.39.side_other = bf16[3,64,128]{2,1,0:T(8,128)(2,1)S(1)} collective-permute-done((bf16[3,64,128]{2,1,0:T(8,128)(2,1)S(1)}, bf16[3,64,128]{2,1,0:T(8,128)(2,1)S(1)}, u32[]{:S(2)}, u32[]{:S(2)}) %collective-permute-start.39) | collective-permute-done | bytes 49184 | tf_op jit(solution)/shard_map/ppermute | solution.py:50
  125.3 2.9 %shard_map.108 = bf16[32,64,128]{2,1,0:T(8,128)(2,1)} custom-call(s32[1]{0:T(128)} %bitcast.place, f32[8,128]{1,0:T(8,128)S(1)} %add_add_fusion.4.count, bf16[32,64,128]{2,1,0:T(8,128)(2,1)S(1)} %get-tuple-element.67.own.low, bf16[8,64,128]{2,1,0:T(8,128)(2,1)S(1)} %collective-permute-done.36.mate, bf16[8,64,128]{2,1,0:T(8,128)(2,1)S(1)} %collective-permute-done.37.other, ...), custom_call_target="tpu_custom_call" | custom-call | bytes 14400000 | tf_op jit(solution)/shard_map/pallas_call | solution.py:19
  128.2 0.8 shard_map.106
  (66 shorter events, 3.2 us)
Async XLA Ops:
  0.6 72.5 %copy-start.4 = (s32[32,128]{1,0:T(8,128)S(1)}, s32[32,128]{1,0:T(8,128)}, u32[]{:S(2)}) copy-start(s32[32,128]{1,0:T(8,128)} %labels.3) | copy-start | bytes 49156
  0.6 72.5 %copy-start.7 = (f32[37]{0:T(128)S(1)}, f32[37]{0:T(128)}, u32[]{:S(2)}) copy-start(f32[37]{0:T(128)} %param.9) | copy-start | bytes 448
  0.7 72.5 %copy-start.6 = (bf16[64,37]{0,1:T(8,128)(2,1)S(1)}, bf16[64,37]{0,1:T(8,128)(2,1)}, u32[]{:S(2)}) copy-start(bf16[64,37]{0,1:T(8,128)(2,1)} %param.8) | copy-start | bytes 14212
  0.7 1.0 copy-start.2
  1.7 0.7 copy-start.5
  3.1 14.6 %collective-permute-start.2 = (f32[8,128]{1,0:T(8,128)S(1)}, f32[8,128]{1,0:T(8,128)S(1)}, u32[]{:S(2)}, u32[]{:S(2)}) collective-permute-start(f32[8,128]{1,0:T(8,128)S(1)} %get-tuple-element.40), channel_id=1, source_target_pairs={{0,96},{1,97},{2,98},{3,99},{4,100},{5,101},{6,102},{7,103},{8,104... | collective-permute-start | bytes 12296 | tf_op jit(solution)/shard_map/ppermute | solution.py:43
  9.5 8.3 %collective-permute-start.1 = (f32[8,128]{1,0:T(8,128)S(1)}, f32[8,128]{1,0:T(8,128)S(1)}, u32[]{:S(2)}, u32[]{:S(2)}) collective-permute-start(f32[8,128]{1,0:T(8,128)S(1)} %get-tuple-element.40), channel_id=1, source_target_pairs={{0,64},{1,65},{2,66},{3,67},{4,68},{5,69},{6,70},{7,71},{8,72},{9,... | collective-permute-start | bytes 12296 | tf_op jit(solution)/shard_map/ppermute | solution.py:43
  10.5 7.3 %collective-permute-start = (f32[8,128]{1,0:T(8,128)S(1)}, f32[8,128]{1,0:T(8,128)S(1)}, u32[]{:S(2)}, u32[]{:S(2)}) collective-permute-start(f32[8,128]{1,0:T(8,128)S(1)} %get-tuple-element.40), channel_id=1, source_target_pairs={{0,32},{1,33},{2,34},{3,35},{4,36},{5,37},{6,38},{7,39},{8,40},{9,... | collective-permute-start | bytes 12296 | tf_op jit(solution)/shard_map/ppermute | solution.py:43
  11.9 10.0 %collective-permute-start.6 = (bf16[8,64,128]{2,1,0:T(8,128)(2,1)S(1)}, bf16[8,64,128]{2,1,0:T(8,128)(2,1)S(1)}, u32[]{:S(2)}, u32[]{:S(2)}) collective-permute-start(bf16[8,64,128]{2,1,0:T(8,128)(2,1)S(1)} %get-tuple-element.43), channel_id=1, source_target_pairs={{0,8},{8,0},{16,24},{24,16},{32,40},{40,32},{48,56},{56,48},{64,72... | collective-permute-start | bytes 393224 | tf_op jit(solution)/shard_map/ppermute | solution.py:50
  11.9 10.0 %collective-permute-start.7 = (bf16[8,64,128]{2,1,0:T(8,128)(2,1)S(1)}, bf16[8,64,128]{2,1,0:T(8,128)(2,1)S(1)}, u32[]{:S(2)}, u32[]{:S(2)}) collective-permute-start(bf16[8,64,128]{2,1,0:T(8,128)(2,1)S(1)} %get-tuple-element.44), channel_id=1, source_target_pairs={{8,16},{16,8},{24,32},{32,24},{40,48},{48,40},{56,64},{64,56},{72,... | collective-permute-start | bytes 393224 | tf_op jit(solution)/shard_map/ppermute | solution.py:50
  17.8 11.1 %collective-permute-start.5 = (f32[8,128]{1,0:T(8,128)S(1)}, f32[8,128]{1,0:T(8,128)S(1)}, u32[]{:S(2)}, u32[]{:S(2)}) collective-permute-start(f32[8,128]{1,0:T(8,128)S(1)} %add_add_fusion.7), channel_id=1, source_target_pairs={{0,129},{1,128},{2,131},{3,130},{4,133},{5,132},{6,135},{7,134},{8... | collective-permute-start | bytes 12296 | tf_op jit(solution)/shard_map/ppermute | solution.py:43
  17.9 11.0 %collective-permute-start.4 = (f32[8,128]{1,0:T(8,128)S(1)}, f32[8,128]{1,0:T(8,128)S(1)}, u32[]{:S(2)}, u32[]{:S(2)}) collective-permute-start(f32[8,128]{1,0:T(8,128)S(1)} %add_add_fusion.7), channel_id=1, source_target_pairs={{0,1},{1,0},{2,3},{3,2},{4,5},{5,4},{6,7},{7,6},{8,9},{9,8},{10,11... | collective-permute-start | bytes 12296 | tf_op jit(solution)/shard_map/ppermute | solution.py:43
  19.9 9.0 %collective-permute-start.3 = (f32[8,128]{1,0:T(8,128)S(1)}, f32[8,128]{1,0:T(8,128)S(1)}, u32[]{:S(2)}, u32[]{:S(2)}) collective-permute-start(f32[8,128]{1,0:T(8,128)S(1)} %add_add_fusion.7), channel_id=1, source_target_pairs={{0,128},{1,129},{2,130},{3,131},{4,132},{5,133},{6,134},{7,135},{8... | collective-permute-start | bytes 12296 | tf_op jit(solution)/shard_map/ppermute | solution.py:43
  22.5 6.5 %collective-permute-start.8 = (bf16[3,64,128]{2,1,0:T(8,128)(2,1)S(1)}, bf16[3,64,128]{2,1,0:T(8,128)(2,1)S(1)}, u32[]{:S(2)}, u32[]{:S(2)}) collective-permute-start(bf16[3,64,128]{2,1,0:T(8,128)(2,1)S(1)} %get-tuple-element.45), channel_id=1, source_target_pairs={{0,1},{1,0},{2,3},{3,2},{4,5},{5,4},{6,7},{7,6},{8,9},{9,8},{10,11... | collective-permute-start | bytes 147464 | tf_op jit(solution)/shard_map/ppermute | solution.py:50
  23.5 8.4 %collective-permute-start.9 = (bf16[3,64,128]{2,1,0:T(8,128)(2,1)S(1)}, bf16[3,64,128]{2,1,0:T(8,128)(2,1)S(1)}, u32[]{:S(2)}, u32[]{:S(2)}) collective-permute-start(bf16[3,64,128]{2,1,0:T(8,128)(2,1)S(1)} %get-tuple-element.46), channel_id=1, source_target_pairs={{1,2},{2,1},{3,4},{4,3},{5,6},{6,5},{9,10},{10,9},{11,12},{12,11},... | collective-permute-start | bytes 147464 | tf_op jit(solution)/shard_map/ppermute | solution.py:50
  31.9 0.9 copy-start
  32.8 0.7 copy-start.3
  36.9 8.8 %collective-permute-start.10 = (bf16[1056,128]{1,0:T(8,128)(2,1)S(1)}, bf16[1056,128]{1,0:T(8,128)(2,1)S(1)}, u32[]{:S(2)}, u32[]{:S(2)}) collective-permute-start(bf16[1056,128]{1,0:T(8,128)(2,1)S(1)} %get-tuple-element.49), channel_id=1, source_target_pairs={{0,2},{1,3},{2,0},{3,1},{4,6},{5,7},{6,4},{7,5},{8,10},{9,11},{10,... | collective-permute-start | bytes 811016 | tf_op jit(solution)/shard_map/ppermute | solution.py:43
  38.5 4.8 %collective-permute-start.13 = (f32[8,128]{1,0:T(8,128)S(1)}, f32[8,128]{1,0:T(8,128)S(1)}, u32[]{:S(2)}, u32[]{:S(2)}) collective-permute-start(f32[8,128]{1,0:T(8,128)S(1)} %add_add_fusion.6), channel_id=1, source_target_pairs={{0,6},{1,7},{2,4},{3,5},{4,2},{5,3},{6,0},{7,1},{8,14},{9,15},{10,... | collective-permute-start | bytes 12296 | tf_op jit(solution)/shard_map/ppermute | solution.py:43
  40.6 5.1 %collective-permute-start.12 = (f32[8,128]{1,0:T(8,128)S(1)}, f32[8,128]{1,0:T(8,128)S(1)}, u32[]{:S(2)}, u32[]{:S(2)}) collective-permute-start(f32[8,128]{1,0:T(8,128)S(1)} %add_add_fusion.6), channel_id=1, source_target_pairs={{0,4},{1,5},{2,6},{3,7},{4,0},{5,1},{6,2},{7,3},{8,12},{9,13},{10,... | collective-permute-start | bytes 12296 | tf_op jit(solution)/shard_map/ppermute | solution.py:43
  41.1 4.6 %collective-permute-start.11 = (f32[8,128]{1,0:T(8,128)S(1)}, f32[8,128]{1,0:T(8,128)S(1)}, u32[]{:S(2)}, u32[]{:S(2)}) collective-permute-start(f32[8,128]{1,0:T(8,128)S(1)} %add_add_fusion.6), channel_id=1, source_target_pairs={{0,2},{1,3},{2,0},{3,1},{4,6},{5,7},{6,4},{7,5},{8,10},{9,11},{10,... | collective-permute-start | bytes 12296 | tf_op jit(solution)/shard_map/ppermute | solution.py:43
  45.7 19.6 %collective-permute-start.17 = (bf16[1056,128]{1,0:T(8,128)(2,1)S(1)}, bf16[1056,128]{1,0:T(8,128)(2,1)S(1)}, u32[]{:S(2)}, u32[]{:S(2)}) collective-permute-start(bf16[1056,128]{1,0:T(8,128)(2,1)S(1)} %collective-permute-done.10), channel_id=1, source_target_pairs={{0,64},{1,96},{2,0},{3,32},{4,192},{5,224},{6,128},{7,160},{8,72},... | collective-permute-start | bytes 811016 | tf_op jit(solution)/shard_map/ppermute | solution.py:43
  50.4 21.2 %collective-permute-start.18 = (bf16[1056,128]{1,0:T(8,128)(2,1)S(1)}, bf16[1056,128]{1,0:T(8,128)(2,1)S(1)}, u32[]{:S(2)}, u32[]{:S(2)}) collective-permute-start(bf16[1056,128]{1,0:T(8,128)(2,1)S(1)} %get-tuple-element.56), channel_id=1, source_target_pairs={{0,16},{1,48},{2,80},{3,112},{4,144},{5,176},{6,208},{7,240},{8,24... | collective-permute-start | bytes 811016 | tf_op jit(solution)/shard_map/ppermute | solution.py:43
  53.8 18.9 %collective-permute-start.16 = (f32[8,128]{1,0:T(8,128)S(1)}, f32[8,128]{1,0:T(8,128)S(1)}, u32[]{:S(2)}, u32[]{:S(2)}) collective-permute-start(f32[8,128]{1,0:T(8,128)S(1)} %add_add_fusion.5), channel_id=1, source_target_pairs={{0,24},{1,25},{2,26},{3,27},{4,28},{5,29},{6,30},{7,31},{8,16},{9,... | collective-permute-start | bytes 12296 | tf_op jit(solution)/shard_map/ppermute | solution.py:43
  53.8 19.0 %collective-permute-start.15 = (f32[8,128]{1,0:T(8,128)S(1)}, f32[8,128]{1,0:T(8,128)S(1)}, u32[]{:S(2)}, u32[]{:S(2)}) collective-permute-start(f32[8,128]{1,0:T(8,128)S(1)} %add_add_fusion.5), channel_id=1, source_target_pairs={{0,16},{1,17},{2,18},{3,19},{4,20},{5,21},{6,22},{7,23},{8,24},{9,... | collective-permute-start | bytes 12296 | tf_op jit(solution)/shard_map/ppermute | solution.py:43
  54.1 18.7 %collective-permute-start.14 = (f32[8,128]{1,0:T(8,128)S(1)}, f32[8,128]{1,0:T(8,128)S(1)}, u32[]{:S(2)}, u32[]{:S(2)}) collective-permute-start(f32[8,128]{1,0:T(8,128)S(1)} %add_add_fusion.5), channel_id=1, source_target_pairs={{0,8},{1,9},{2,10},{3,11},{4,12},{5,13},{6,14},{7,15},{8,0},{9,1},... | collective-permute-start | bytes 12296 | tf_op jit(solution)/shard_map/ppermute | solution.py:43
  65.3 7.5 %collective-permute-start.19 = (bf16[528,128]{1,0:T(8,128)(2,1)S(1)}, bf16[528,128]{1,0:T(8,128)(2,1)S(1)}, u32[]{:S(2)}, u32[]{:S(2)}) collective-permute-start(bf16[528,128]{1,0:T(8,128)(2,1)S(1)} %slice.8), channel_id=1, source_target_pairs={{0,8},{1,9},{2,10},{3,11},{4,12},{5,13},{6,14},{7,15},{8,0},{9,1},... | collective-permute-start | bytes 405512 | tf_op jit(solution)/shard_map/ppermute | solution.py:43
  71.7 1.4 %collective-permute-start.20 = (bf16[528,128]{1,0:T(8,128)(2,1)S(1)}, bf16[528,128]{1,0:T(8,128)(2,1)S(1)}, u32[]{:S(2)}, u32[]{:S(2)}) collective-permute-start(bf16[528,128]{1,0:T(8,128)(2,1)S(1)} %slice.9), channel_id=1, source_target_pairs={{0,8},{1,9},{2,10},{3,11},{4,12},{5,13},{6,14},{7,15},{8,0},{9,1},... | collective-permute-start | bytes 405512 | tf_op jit(solution)/shard_map/ppermute | solution.py:43
  77.5 47.8 %copy-start.1 = (bf16[3,3,64,64]{3,2,1,0:T(8,128)(2,1)S(1)}, bf16[3,3,64,64]{3,2,1,0:T(8,128)(2,1)}, u32[]{:S(2)}) copy-start(bf16[3,3,64,64]{3,2,1,0:T(8,128)(2,1)} %param.7) | copy-start | bytes 221188
  79.8 2.0 %collective-permute-start.21 = (f32[88,128]{1,0:T(8,128)S(1)}, f32[88,128]{1,0:T(8,128)S(1)}, u32[]{:S(2)}, u32[]{:S(2)}) collective-permute-start(f32[88,128]{1,0:T(8,128)S(1)} %get-tuple-element.63), channel_id=1, source_target_pairs={{0,8},{1,9},{2,10},{3,11},{4,12},{5,13},{6,14},{7,15},{8,0},{9,1},... | collective-permute-start | bytes 135176 | tf_op jit(solution)/shard_map/ppermute | solution.py:43
  80.0 4.1 %collective-permute-start.22 = (f32[88,128]{1,0:T(8,128)S(1)}, f32[88,128]{1,0:T(8,128)S(1)}, u32[]{:S(2)}, u32[]{:S(2)}) collective-permute-start(f32[88,128]{1,0:T(8,128)S(1)} %get-tuple-element.64), channel_id=1, source_target_pairs={{0,16},{1,17},{2,18},{3,19},{4,20},{5,21},{6,22},{7,23},{8,24},{9,... | collective-permute-start | bytes 135176 | tf_op jit(solution)/shard_map/ppermute | solution.py:43
  81.3 3.9 %collective-permute-start.23 = (f32[88,128]{1,0:T(8,128)S(1)}, f32[88,128]{1,0:T(8,128)S(1)}, u32[]{:S(2)}, u32[]{:S(2)}) collective-permute-start(f32[88,128]{1,0:T(8,128)S(1)} %get-tuple-element.65), channel_id=1, source_target_pairs={{0,24},{1,25},{2,26},{3,27},{4,28},{5,29},{6,30},{7,31},{8,16},{9,... | collective-permute-start | bytes 135176 | tf_op jit(solution)/shard_map/ppermute | solution.py:43
  85.2 8.7 %collective-permute-start.26 = (f32[88,128]{1,0:T(8,128)S(1)}, f32[88,128]{1,0:T(8,128)S(1)}, u32[]{:S(2)}, u32[]{:S(2)}) collective-permute-start(f32[88,128]{1,0:T(8,128)S(1)} %add_add_fusion.3), channel_id=1, source_target_pairs={{0,96},{1,97},{2,98},{3,99},{4,100},{5,101},{6,102},{7,103},{8,104... | collective-permute-start | bytes 135176 | tf_op jit(solution)/shard_map/ppermute | solution.py:43
  88.4 8.4 %collective-permute-start.25 = (f32[88,128]{1,0:T(8,128)S(1)}, f32[88,128]{1,0:T(8,128)S(1)}, u32[]{:S(2)}, u32[]{:S(2)}) collective-permute-start(f32[88,128]{1,0:T(8,128)S(1)} %add_add_fusion.3), channel_id=1, source_target_pairs={{0,64},{1,65},{2,66},{3,67},{4,68},{5,69},{6,70},{7,71},{8,72},{9,... | collective-permute-start | bytes 135176 | tf_op jit(solution)/shard_map/ppermute | solution.py:43
  93.8 5.1 %collective-permute-start.24 = (f32[88,128]{1,0:T(8,128)S(1)}, f32[88,128]{1,0:T(8,128)S(1)}, u32[]{:S(2)}, u32[]{:S(2)}) collective-permute-start(f32[88,128]{1,0:T(8,128)S(1)} %add_add_fusion.3), channel_id=1, source_target_pairs={{0,32},{1,33},{2,34},{3,35},{4,36},{5,37},{6,38},{7,39},{8,40},{9,... | collective-permute-start | bytes 135176 | tf_op jit(solution)/shard_map/ppermute | solution.py:43
  99.0 9.2 %collective-permute-start.29 = (f32[88,128]{1,0:T(8,128)S(1)}, f32[88,128]{1,0:T(8,128)S(1)}, u32[]{:S(2)}, u32[]{:S(2)}) collective-permute-start(f32[88,128]{1,0:T(8,128)S(1)} %add_add_fusion.2), channel_id=1, source_target_pairs={{0,129},{1,128},{2,131},{3,130},{4,133},{5,132},{6,135},{7,134},{8... | collective-permute-start | bytes 135176 | tf_op jit(solution)/shard_map/ppermute | solution.py:43
  103.2 5.6 %collective-permute-start.28 = (f32[88,128]{1,0:T(8,128)S(1)}, f32[88,128]{1,0:T(8,128)S(1)}, u32[]{:S(2)}, u32[]{:S(2)}) collective-permute-start(f32[88,128]{1,0:T(8,128)S(1)} %add_add_fusion.2), channel_id=1, source_target_pairs={{0,1},{1,0},{2,3},{3,2},{4,5},{5,4},{6,7},{7,6},{8,9},{9,8},{10,11... | collective-permute-start | bytes 135176 | tf_op jit(solution)/shard_map/ppermute | solution.py:43
  103.2 5.6 %collective-permute-start.27 = (f32[88,128]{1,0:T(8,128)S(1)}, f32[88,128]{1,0:T(8,128)S(1)}, u32[]{:S(2)}, u32[]{:S(2)}) collective-permute-start(f32[88,128]{1,0:T(8,128)S(1)} %add_add_fusion.2), channel_id=1, source_target_pairs={{0,128},{1,129},{2,130},{3,131},{4,132},{5,133},{6,134},{7,135},{8... | collective-permute-start | bytes 135176 | tf_op jit(solution)/shard_map/ppermute | solution.py:43
  104.2 9.2 %collective-permute-start.36 = (bf16[8,64,128]{2,1,0:T(8,128)(2,1)S(1)}, bf16[8,64,128]{2,1,0:T(8,128)(2,1)S(1)}, u32[]{:S(2)}, u32[]{:S(2)}) collective-permute-start(bf16[8,64,128]{2,1,0:T(8,128)(2,1)S(1)} %get-tuple-element.68), channel_id=1, source_target_pairs={{0,8},{8,0},{16,24},{24,16},{32,40},{40,32},{48,56},{56,48},{64,72... | collective-permute-start | bytes 393224 | tf_op jit(solution)/shard_map/ppermute | solution.py:50
  104.2 9.2 %collective-permute-start.37 = (bf16[8,64,128]{2,1,0:T(8,128)(2,1)S(1)}, bf16[8,64,128]{2,1,0:T(8,128)(2,1)S(1)}, u32[]{:S(2)}, u32[]{:S(2)}) collective-permute-start(bf16[8,64,128]{2,1,0:T(8,128)(2,1)S(1)} %get-tuple-element.69), channel_id=1, source_target_pairs={{8,16},{16,8},{24,32},{32,24},{40,48},{48,40},{56,64},{64,56},{72,... | collective-permute-start | bytes 393224 | tf_op jit(solution)/shard_map/ppermute | solution.py:50
  108.8 12.0 %collective-permute-start.32 = (f32[88,128]{1,0:T(8,128)S(1)}, f32[88,128]{1,0:T(8,128)S(1)}, u32[]{:S(2)}, u32[]{:S(2)}) collective-permute-start(f32[88,128]{1,0:T(8,128)S(1)} %add_add_fusion.1), channel_id=1, source_target_pairs={{0,6},{1,7},{2,4},{3,5},{4,2},{5,3},{6,0},{7,1},{8,14},{9,15},{10,... | collective-permute-start | bytes 135176 | tf_op jit(solution)/shard_map/ppermute | solution.py:43
  109.1 11.8 %collective-permute-start.31 = (f32[88,128]{1,0:T(8,128)S(1)}, f32[88,128]{1,0:T(8,128)S(1)}, u32[]{:S(2)}, u32[]{:S(2)}) collective-permute-start(f32[88,128]{1,0:T(8,128)S(1)} %add_add_fusion.1), channel_id=1, source_target_pairs={{0,4},{1,5},{2,6},{3,7},{4,0},{5,1},{6,2},{7,3},{8,12},{9,13},{10,... | collective-permute-start | bytes 135176 | tf_op jit(solution)/shard_map/ppermute | solution.py:43
  113.3 7.5 %collective-permute-start.30 = (f32[88,128]{1,0:T(8,128)S(1)}, f32[88,128]{1,0:T(8,128)S(1)}, u32[]{:S(2)}, u32[]{:S(2)}) collective-permute-start(f32[88,128]{1,0:T(8,128)S(1)} %add_add_fusion.1), channel_id=1, source_target_pairs={{0,2},{1,3},{2,0},{3,1},{4,6},{5,7},{6,4},{7,5},{8,10},{9,11},{10,... | collective-permute-start | bytes 135176 | tf_op jit(solution)/shard_map/ppermute | solution.py:43
  113.8 9.0 %collective-permute-start.38 = (bf16[3,64,128]{2,1,0:T(8,128)(2,1)S(1)}, bf16[3,64,128]{2,1,0:T(8,128)(2,1)S(1)}, u32[]{:S(2)}, u32[]{:S(2)}) collective-permute-start(bf16[3,64,128]{2,1,0:T(8,128)(2,1)S(1)} %get-tuple-element.70), channel_id=1, source_target_pairs={{0,1},{1,0},{2,3},{3,2},{4,5},{5,4},{6,7},{7,6},{8,9},{9,8},{10,11... | collective-permute-start | bytes 147464 | tf_op jit(solution)/shard_map/ppermute | solution.py:50
  116.9 8.4 %collective-permute-start.39 = (bf16[3,64,128]{2,1,0:T(8,128)(2,1)S(1)}, bf16[3,64,128]{2,1,0:T(8,128)(2,1)S(1)}, u32[]{:S(2)}, u32[]{:S(2)}) collective-permute-start(bf16[3,64,128]{2,1,0:T(8,128)(2,1)S(1)} %get-tuple-element.71), channel_id=1, source_target_pairs={{1,2},{2,1},{3,4},{4,3},{5,6},{6,5},{9,10},{10,9},{11,12},{12,11},... | collective-permute-start | bytes 147464 | tf_op jit(solution)/shard_map/ppermute | solution.py:50
  120.9 7.3 %collective-permute-start.35 = (f32[88,128]{1,0:T(8,128)S(1)}, f32[88,128]{1,0:T(8,128)S(1)}, u32[]{:S(2)}, u32[]{:S(2)}) collective-permute-start(f32[88,128]{1,0:T(8,128)S(1)} %add_add_fusion.got0), channel_id=1, source_target_pairs={{0,24},{1,25},{2,26},{3,27},{4,28},{5,29},{6,30},{7,31},{8,16},{9,... | collective-permute-start | bytes 135176 | tf_op jit(solution)/shard_map/ppermute | solution.py:43
  121.0 7.2 %collective-permute-start.34 = (f32[88,128]{1,0:T(8,128)S(1)}, f32[88,128]{1,0:T(8,128)S(1)}, u32[]{:S(2)}, u32[]{:S(2)}) collective-permute-start(f32[88,128]{1,0:T(8,128)S(1)} %add_add_fusion.got0), channel_id=1, source_target_pairs={{0,16},{1,17},{2,18},{3,19},{4,20},{5,21},{6,22},{7,23},{8,24},{9,... | collective-permute-start | bytes 135176 | tf_op jit(solution)/shard_map/ppermute | solution.py:43
  121.1 7.1 %collective-permute-start.33 = (f32[88,128]{1,0:T(8,128)S(1)}, f32[88,128]{1,0:T(8,128)S(1)}, u32[]{:S(2)}, u32[]{:S(2)}) collective-permute-start(f32[88,128]{1,0:T(8,128)S(1)} %add_add_fusion.got0), channel_id=1, source_target_pairs={{0,8},{1,9},{2,10},{3,11},{4,12},{5,13},{6,14},{7,15},{8,0},{9,1},... | collective-permute-start | bytes 135176 | tf_op jit(solution)/shard_map/ppermute | solution.py:43

commit v10 on v8

--- a/solution.py
+++ b/solution.py
@@ -9,7 +9,7 @@
 GRID = ("row", "col")
 F32, BF16 = jnp.float32, jnp.bfloat16
 LANES = 128
-UNROLL = 8
+UNROLL = 16
 FAR_BELOW = -1e30
 VMEM = pl.BlockSpec(memory_space=pltpu.VMEM)
 SMEM = pl.BlockSpec(memory_space=pltpu.SMEM)

time: 123 us -> 122 us (level)
  Pallas kernels: 15.4 us -> 13.6 us
    pallas_call x8, Pallas kernels: 15.4 us -> 13.6 us  [run(): pl.pallas_call(body, out_shape=outs, in_specs=[SMEM] * scalars + [VMEM] *...]
where the time goes in v10:
time: 122 us; the launch traced here: 121 us
  starting transfers between devices  83.9 us (69%)
  waiting for transfers between devices  18.5 us (15%)
  Pallas kernels  13.6 us (11%)
  local copies, waits for them, and re-layouts  3.42 us (3%)
    ppermute x32, starting transfers between devices, send(): return lax.ppermute(block, GRID, pairs)  61.4 us
    ppermute x4, starting transfers between devices, swapped(): lax.ppermute(to_other, axis, others)  20.1 us
    pallas_call x8, Pallas kernels, run(): pl.pallas_call(body, out_shape=outs, in_specs=[SMEM] * scalars + [VMEM] *...  13.6 us
    ppermute x32, waiting for transfers between devices, send(): return lax.ppermute(block, GRID, pairs)  13.1 us
    ppermute x4, waiting for transfers between devices, swapped(): lax.ppermute(to_other, axis, others)  5.32 us
    unnamed x16, local copies, waits for them, and re-layouts  3.4 us
    ppermute x4, starting transfers between devices, swapped(): lax.ppermute(to_mate, axis, mates)  2.5 us
  transfers between devices with their start and end apart: 40, of which 10 were waited for; matrix products, arithmetic and copies ran while one was open for 0% of the time, Pallas kernels for 3%

profile of v10, /device:TPU:24, one launch (start us, length us, event | category | flops | bytes accessed | tf_op | source)
XLA Modules:
  0.0 120.5 jit_solution(7675487924169462897)
XLA Ops:
  0.7 1.0 copy-done.2
  1.7 0.7 copy-done.5
  2.4 0.7 shard_map.101
  3.1 6.3 %collective-permute-start.2 = (f32[8,128]{1,0:T(8,128)S(1)}, f32[8,128]{1,0:T(8,128)S(1)}, u32[]{:S(2)}, u32[]{:S(2)}) collective-permute-start(f32[8,128]{1,0:T(8,128)S(1)} %get-tuple-element.37), channel_id=1, source_target_pairs={{0,96},{1,97},{2,98},{3,99},{4,100},{5,101},{6,102},{7,103},{8,104... | collective-permute-start | bytes 12296 | tf_op jit(solution)/shard_map/ppermute | solution.py:43
  9.5 1.0 collective-permute-start.1
  10.5 1.5 %collective-permute-start = (f32[8,128]{1,0:T(8,128)S(1)}, f32[8,128]{1,0:T(8,128)S(1)}, u32[]{:S(2)}, u32[]{:S(2)}) collective-permute-start(f32[8,128]{1,0:T(8,128)S(1)} %get-tuple-element.37), channel_id=1, source_target_pairs={{0,32},{1,33},{2,34},{3,35},{4,36},{5,37},{6,38},{7,39},{8,40},{9,... | collective-permute-start | bytes 12296 | tf_op jit(solution)/shard_map/ppermute | solution.py:43
  11.9 5.8 %collective-permute-start.7 = (bf16[8,64,128]{2,1,0:T(8,128)(2,1)S(1)}, bf16[8,64,128]{2,1,0:T(8,128)(2,1)S(1)}, u32[]{:S(2)}, u32[]{:S(2)}) collective-permute-start(bf16[8,64,128]{2,1,0:T(8,128)(2,1)S(1)} %get-tuple-element.41), channel_id=1, source_target_pairs={{8,16},{16,8},{24,32},{32,24},{40,48},{48,40},{56,64},{64,56},{72,... | collective-permute-start | bytes 393224 | tf_op jit(solution)/shard_map/ppermute | solution.py:50
  17.9 2.0 %collective-permute-start.4 = (f32[8,128]{1,0:T(8,128)S(1)}, f32[8,128]{1,0:T(8,128)S(1)}, u32[]{:S(2)}, u32[]{:S(2)}) collective-permute-start(f32[8,128]{1,0:T(8,128)S(1)} %add_add_fusion.7), channel_id=1, source_target_pairs={{0,1},{1,0},{2,3},{3,2},{4,5},{5,4},{6,7},{7,6},{8,9},{9,8},{10,11... | collective-permute-start | bytes 12296 | tf_op jit(solution)/shard_map/ppermute | solution.py:43
  19.9 2.1 %collective-permute-start.3 = (f32[8,128]{1,0:T(8,128)S(1)}, f32[8,128]{1,0:T(8,128)S(1)}, u32[]{:S(2)}, u32[]{:S(2)}) collective-permute-start(f32[8,128]{1,0:T(8,128)S(1)} %add_add_fusion.7), channel_id=1, source_target_pairs={{0,128},{1,129},{2,130},{3,131},{4,132},{5,133},{6,134},{7,135},{8... | collective-permute-start | bytes 12296 | tf_op jit(solution)/shard_map/ppermute | solution.py:43
  22.0 0.5 shard_map.102
  22.5 1.0 collective-permute-start.8
  23.5 5.4 %collective-permute-start.9 = (bf16[3,64,128]{2,1,0:T(8,128)(2,1)S(1)}, bf16[3,64,128]{2,1,0:T(8,128)(2,1)S(1)}, u32[]{:S(2)}, u32[]{:S(2)}) collective-permute-start(bf16[3,64,128]{2,1,0:T(8,128)(2,1)S(1)} %get-tuple-element.43), channel_id=1, source_target_pairs={{1,2},{2,1},{3,4},{4,3},{5,6},{6,5},{9,10},{10,9},{11,12},{12,11},... | collective-permute-start | bytes 147464 | tf_op jit(solution)/shard_map/ppermute | solution.py:50
  29.0 2.9 %collective-permute-done.9.side_other = bf16[3,64,128]{2,1,0:T(8,128)(2,1)S(1)} collective-permute-done((bf16[3,64,128]{2,1,0:T(8,128)(2,1)S(1)}, bf16[3,64,128]{2,1,0:T(8,128)(2,1)S(1)}, u32[]{:S(2)}, u32[]{:S(2)}) %collective-permute-start.9) | collective-permute-done | bytes 49184 | tf_op jit(solution)/shard_map/ppermute | solution.py:50
  31.9 0.9 copy-done
  32.8 0.7 copy-done.3
  33.5 2.6 %shard_map.103 = (bf16[48,192,128]{2,1,0:T(8,128)(2,1)S(1)}, bf16[32,64,128]{2,1,0:T(8,128)(2,1)S(1)}, bf16[1056,128]{1,0:T(8,128)(2,1)S(1)}, bf16[1056,128]{1,0:T(8,128)(2,1)S(1)}) custom-call(s32[1]{0:T(128)} %bitcast.place, bf16[32,64,128]{2,1,0:T(8,128)(2,1)S(1)} %get-tuple-element.39.own.act, bf16[8,64,128]{2,1,0:T(8,128)(2,1)S(1)} %collective-permute-done.6.mate, ...), custom_call_target="tpu_custom_call" | custom-call | bytes 18000000 | tf_op jit(solution)/shard_map/pallas_call | solution.py:19
  36.1 1.6 %collective-permute-start.10 = (bf16[1056,128]{1,0:T(8,128)(2,1)S(1)}, bf16[1056,128]{1,0:T(8,128)(2,1)S(1)}, u32[]{:S(2)}, u32[]{:S(2)}) collective-permute-start(bf16[1056,128]{1,0:T(8,128)(2,1)S(1)} %get-tuple-element.46), channel_id=1, source_target_pairs={{0,2},{1,3},{2,0},{3,1},{4,6},{5,7},{6,4},{7,5},{8,10},{9,11},{10,... | collective-permute-start | bytes 811016 | tf_op jit(solution)/shard_map/ppermute | solution.py:43
  37.6 5.2 %collective-permute-start.18 = (bf16[1056,128]{1,0:T(8,128)(2,1)S(1)}, bf16[1056,128]{1,0:T(8,128)(2,1)S(1)}, u32[]{:S(2)}, u32[]{:S(2)}) collective-permute-start(bf16[1056,128]{1,0:T(8,128)(2,1)S(1)} %get-tuple-element.49), channel_id=1, source_target_pairs={{0,16},{1,48},{2,80},{3,112},{4,144},{5,176},{6,208},{7,240},{8,24... | collective-permute-start | bytes 811016 | tf_op jit(solution)/shard_map/ppermute | solution.py:43
  42.9 5.5 %collective-permute-start.17 = (bf16[1056,128]{1,0:T(8,128)(2,1)S(1)}, bf16[1056,128]{1,0:T(8,128)(2,1)S(1)}, u32[]{:S(2)}, u32[]{:S(2)}) collective-permute-start(bf16[1056,128]{1,0:T(8,128)(2,1)S(1)} %collective-permute-done.10), channel_id=1, source_target_pairs={{0,64},{1,96},{2,0},{3,32},{4,192},{5,224},{6,128},{7,160},{8,72},... | collective-permute-start | bytes 811016 | tf_op jit(solution)/shard_map/ppermute | solution.py:43
  48.4 1.3 %collective-permute-start.12 = (f32[8,128]{1,0:T(8,128)S(1)}, f32[8,128]{1,0:T(8,128)S(1)}, u32[]{:S(2)}, u32[]{:S(2)}) collective-permute-start(f32[8,128]{1,0:T(8,128)S(1)} %add_add_fusion.6), channel_id=1, source_target_pairs={{0,4},{1,5},{2,6},{3,7},{4,0},{5,1},{6,2},{7,3},{8,12},{9,13},{10,... | collective-permute-start | bytes 12296 | tf_op jit(solution)/shard_map/ppermute | solution.py:43
  49.8 2.7 %collective-permute-start.11 = (f32[8,128]{1,0:T(8,128)S(1)}, f32[8,128]{1,0:T(8,128)S(1)}, u32[]{:S(2)}, u32[]{:S(2)}) collective-permute-start(f32[8,128]{1,0:T(8,128)S(1)} %add_add_fusion.6), channel_id=1, source_target_pairs={{0,2},{1,3},{2,0},{3,1},{4,6},{5,7},{6,4},{7,5},{8,10},{9,11},{10,... | collective-permute-start | bytes 12296 | tf_op jit(solution)/shard_map/ppermute | solution.py:43
  52.5 0.7 collective-permute-done.13
  53.6 0.5 collective-permute-done.11
  54.1 0.7 collective-permute-start.16
  54.8 2.6 %collective-permute-start.15 = (f32[8,128]{1,0:T(8,128)S(1)}, f32[8,128]{1,0:T(8,128)S(1)}, u32[]{:S(2)}, u32[]{:S(2)}) collective-permute-start(f32[8,128]{1,0:T(8,128)S(1)} %add_add_fusion.5), channel_id=1, source_target_pairs={{0,16},{1,17},{2,18},{3,19},{4,20},{5,21},{6,22},{7,23},{8,24},{9,... | collective-permute-start | bytes 12296 | tf_op jit(solution)/shard_map/ppermute | solution.py:43
  57.4 0.8 collective-permute-start.20
  58.1 1.2 collective-permute-done.17.near
  59.5 1.3 %collective-permute-done.19.got1 = bf16[528,128]{1,0:T(8,128)(2,1)S(1)} collective-permute-done((bf16[528,128]{1,0:T(8,128)(2,1)S(1)}, bf16[528,128]{1,0:T(8,128)(2,1)S(1)}, u32[]{:S(2)}, u32[]{:S(2)}) %collective-permute-start.19) | collective-permute-done | bytes 135200 | tf_op jit(solution)/shard_map/ppermute | solution.py:43
  60.8 4.1 %shard_map.104 = (f32[32,64,128]{2,1,0:T(8,128)S(1)}, f32[120,64]{1,0:T(8,128)S(1)}, f32[40,128]{1,0:T(8,128)S(1)}, f32[1,128]{1,0:T(1,128)S(1)}) custom-call(s32[1]{0:T(128)} %bitcast.place, bf16[1056,128]{1,0:T(8,128)(2,1)S(1)} %collective-permute-done.17.near, bf16[1056,128]{1,0:T(8,128)(2,1)S(1)} %collective-permute-done.18.far, ...), custom_call_target="tpu_custom_call" | custom-call | bytes 18000000 | tf_op jit(solution)/shard_map/pallas_call | solution.py:19
  64.9 2.0 %shard_map.105 = (bf16[32,64,128]{2,1,0:T(8,128)(2,1)S(1)}, bf16[8,64,128]{2,1,0:T(8,128)(2,1)S(1)}, bf16[8,64,128]{2,1,0:T(8,128)(2,1)S(1)}, f32[88,128]{1,0:T(...) custom-call(s32[1]{0:T(128)} %bitcast.place, f32[8,128]{1,0:T(8,128)S(1)} %add_add_fusion.4.count, ...), custom_call_target="tpu_custom_call" | custom-call | bytes 10800000 | tf_op jit(solution)/shard_map/pallas_call | solution.py:19
  67.2 0.5 collective-permute-start.22
  67.7 1.2 collective-permute-start.23
  68.9 2.8 %collective-permute-done.22 = f32[88,128]{1,0:T(8,128)S(1)} collective-permute-done((f32[88,128]{1,0:T(8,128)S(1)}, f32[88,128]{1,0:T(8,128)S(1)}, u32[]{:S(2)}, u32[]{:S(2)}) %collective-permute-start.22) | collective-permute-done | bytes 45088 | tf_op jit(solution)/shard_map/ppermute | solution.py:43
  71.7 12.9 %collective-permute-start.26 = (f32[88,128]{1,0:T(8,128)S(1)}, f32[88,128]{1,0:T(8,128)S(1)}, u32[]{:S(2)}, u32[]{:S(2)}) collective-permute-start(f32[88,128]{1,0:T(8,128)S(1)} %add_add_fusion.3), channel_id=1, source_target_pairs={{0,96},{1,97},{2,98},{3,99},{4,100},{5,101},{6,102},{7,103},{8,104... | collective-permute-start | bytes 135176 | tf_op jit(solution)/shard_map/ppermute | solution.py:43
  84.5 2.3 %collective-permute-start.25 = (f32[88,128]{1,0:T(8,128)S(1)}, f32[88,128]{1,0:T(8,128)S(1)}, u32[]{:S(2)}, u32[]{:S(2)}) collective-permute-start(f32[88,128]{1,0:T(8,128)S(1)} %add_add_fusion.3), channel_id=1, source_target_pairs={{0,64},{1,65},{2,66},{3,67},{4,68},{5,69},{6,70},{7,71},{8,72},{9,... | collective-permute-start | bytes 135176 | tf_op jit(solution)/shard_map/ppermute | solution.py:43
  87.0 6.1 %collective-permute-done.25 = f32[88,128]{1,0:T(8,128)S(1)} collective-permute-done((f32[88,128]{1,0:T(8,128)S(1)}, f32[88,128]{1,0:T(8,128)S(1)}, u32[]{:S(2)}, u32[]{:S(2)}) %collective-permute-start.25) | collective-permute-done | bytes 45088 | tf_op jit(solution)/shard_map/ppermute | solution.py:43
  93.6 4.1 %collective-permute-start.28 = (f32[88,128]{1,0:T(8,128)S(1)}, f32[88,128]{1,0:T(8,128)S(1)}, u32[]{:S(2)}, u32[]{:S(2)}) collective-permute-start(f32[88,128]{1,0:T(8,128)S(1)} %add_add_fusion.2), channel_id=1, source_target_pairs={{0,1},{1,0},{2,3},{3,2},{4,5},{5,4},{6,7},{7,6},{8,9},{9,8},{10,11... | collective-permute-start | bytes 135176 | tf_op jit(solution)/shard_map/ppermute | solution.py:43
  97.7 4.9 %collective-permute-start.37 = (bf16[8,64,128]{2,1,0:T(8,128)(2,1)S(1)}, bf16[8,64,128]{2,1,0:T(8,128)(2,1)S(1)}, u32[]{:S(2)}, u32[]{:S(2)}) collective-permute-start(bf16[8,64,128]{2,1,0:T(8,128)(2,1)S(1)} %get-tuple-element.63), channel_id=1, source_target_pairs={{8,16},{16,8},{24,32},{32,24},{40,48},{48,40},{56,64},{64,56},{72,... | collective-permute-start | bytes 393224 | tf_op jit(solution)/shard_map/ppermute | solution.py:50
  102.7 1.5 %collective-permute-start.32 = (f32[88,128]{1,0:T(8,128)S(1)}, f32[88,128]{1,0:T(8,128)S(1)}, u32[]{:S(2)}, u32[]{:S(2)}) collective-permute-start(f32[88,128]{1,0:T(8,128)S(1)} %add_add_fusion.1), channel_id=1, source_target_pairs={{0,6},{1,7},{2,4},{3,5},{4,2},{5,3},{6,0},{7,1},{8,14},{9,15},{10,... | collective-permute-start | bytes 135176 | tf_op jit(solution)/shard_map/ppermute | solution.py:43
  104.2 1.1 collective-permute-start.31
  105.3 1.6 %collective-permute-start.30 = (f32[88,128]{1,0:T(8,128)S(1)}, f32[88,128]{1,0:T(8,128)S(1)}, u32[]{:S(2)}, u32[]{:S(2)}) collective-permute-start(f32[88,128]{1,0:T(8,128)S(1)} %add_add_fusion.1), channel_id=1, source_target_pairs={{0,2},{1,3},{2,0},{3,1},{4,6},{5,7},{6,4},{7,5},{8,10},{9,11},{10,... | collective-permute-start | bytes 135176 | tf_op jit(solution)/shard_map/ppermute | solution.py:43
  106.9 0.5 shard_map.107
  107.4 1.5 %collective-permute-start.38 = (bf16[3,64,128]{2,1,0:T(8,128)(2,1)S(1)}, bf16[3,64,128]{2,1,0:T(8,128)(2,1)S(1)}, u32[]{:S(2)}, u32[]{:S(2)}) collective-permute-start(bf16[3,64,128]{2,1,0:T(8,128)(2,1)S(1)} %get-tuple-element.64), channel_id=1, source_target_pairs={{0,1},{1,0},{2,3},{3,2},{4,5},{5,4},{6,7},{7,6},{8,9},{9,8},{10,11... | collective-permute-start | bytes 147464 | tf_op jit(solution)/shard_map/ppermute | solution.py:50
  108.9 3.9 %collective-permute-start.39 = (bf16[3,64,128]{2,1,0:T(8,128)(2,1)S(1)}, bf16[3,64,128]{2,1,0:T(8,128)(2,1)S(1)}, u32[]{:S(2)}, u32[]{:S(2)}) collective-permute-start(bf16[3,64,128]{2,1,0:T(8,128)(2,1)S(1)} %get-tuple-element.65), channel_id=1, source_target_pairs={{1,2},{2,1},{3,4},{4,3},{5,6},{6,5},{9,10},{10,9},{11,12},{12,11},... | collective-permute-start | bytes 147464 | tf_op jit(solution)/shard_map/ppermute | solution.py:50
  113.1 1.7 %collective-permute-start.33 = (f32[88,128]{1,0:T(8,128)S(1)}, f32[88,128]{1,0:T(8,128)S(1)}, u32[]{:S(2)}, u32[]{:S(2)}) collective-permute-start(f32[88,128]{1,0:T(8,128)S(1)} %add_add_fusion.got0), channel_id=1, source_target_pairs={{0,8},{1,9},{2,10},{3,11},{4,12},{5,13},{6,14},{7,15},{8,0},{9,1},... | collective-permute-start | bytes 135176 | tf_op jit(solution)/shard_map/ppermute | solution.py:43
  114.8 2.4 %collective-permute-done.39.side_other = bf16[3,64,128]{2,1,0:T(8,128)(2,1)S(1)} collective-permute-done((bf16[3,64,128]{2,1,0:T(8,128)(2,1)S(1)}, bf16[3,64,128]{2,1,0:T(8,128)(2,1)S(1)}, u32[]{:S(2)}, u32[]{:S(2)}) %collective-permute-start.39) | collective-permute-done | bytes 49184 | tf_op jit(solution)/shard_map/ppermute | solution.py:50
  117.2 2.4 %shard_map.108 = bf16[32,64,128]{2,1,0:T(8,128)(2,1)} custom-call(s32[1]{0:T(128)} %bitcast.place, f32[8,128]{1,0:T(8,128)S(1)} %add_add_fusion.4.count, bf16[32,64,128]{2,1,0:T(8,128)(2,1)S(1)} %get-tuple-element.61.own.low, bf16[8,64,128]{2,1,0:T(8,128)(2,1)S(1)} %collective-permute-done.36.mate, bf16[8,64,128]{2,1,0:T(8,128)(2,1)S(1)} %collective-permute-done.37.other, ...), custom_call_target="tpu_custom_call" | custom-call | bytes 14400000 | tf_op jit(solution)/shard_map/pallas_call | solution.py:19
  119.7 0.8 shard_map.106
  (66 shorter events, 1.9 us)
Async XLA Ops:
  0.6 60.2 %copy-start.4 = (s32[32,128]{1,0:T(8,128)S(1)}, s32[32,128]{1,0:T(8,128)}, u32[]{:S(2)}) copy-start(s32[32,128]{1,0:T(8,128)} %labels.3) | copy-start | bytes 49156
  0.6 60.2 %copy-start.7 = (f32[37]{0:T(128)S(1)}, f32[37]{0:T(128)}, u32[]{:S(2)}) copy-start(f32[37]{0:T(128)} %param.9) | copy-start | bytes 448
  0.7 60.1 %copy-start.6 = (bf16[64,37]{0,1:T(8,128)(2,1)S(1)}, bf16[64,37]{0,1:T(8,128)(2,1)}, u32[]{:S(2)}) copy-start(bf16[64,37]{0,1:T(8,128)(2,1)} %param.8) | copy-start | bytes 14212
  0.7 1.0 copy-start.2
  1.7 0.7 copy-start.5
  3.1 14.6 %collective-permute-start.2 = (f32[8,128]{1,0:T(8,128)S(1)}, f32[8,128]{1,0:T(8,128)S(1)}, u32[]{:S(2)}, u32[]{:S(2)}) collective-permute-start(f32[8,128]{1,0:T(8,128)S(1)} %get-tuple-element.37), channel_id=1, source_target_pairs={{0,96},{1,97},{2,98},{3,99},{4,100},{5,101},{6,102},{7,103},{8,104... | collective-permute-start | bytes 12296 | tf_op jit(solution)/shard_map/ppermute | solution.py:43
  9.5 8.3 %collective-permute-start.1 = (f32[8,128]{1,0:T(8,128)S(1)}, f32[8,128]{1,0:T(8,128)S(1)}, u32[]{:S(2)}, u32[]{:S(2)}) collective-permute-start(f32[8,128]{1,0:T(8,128)S(1)} %get-tuple-element.37), channel_id=1, source_target_pairs={{0,64},{1,65},{2,66},{3,67},{4,68},{5,69},{6,70},{7,71},{8,72},{9,... | collective-permute-start | bytes 12296 | tf_op jit(solution)/shard_map/ppermute | solution.py:43
  10.5 7.3 %collective-permute-start = (f32[8,128]{1,0:T(8,128)S(1)}, f32[8,128]{1,0:T(8,128)S(1)}, u32[]{:S(2)}, u32[]{:S(2)}) collective-permute-start(f32[8,128]{1,0:T(8,128)S(1)} %get-tuple-element.37), channel_id=1, source_target_pairs={{0,32},{1,33},{2,34},{3,35},{4,36},{5,37},{6,38},{7,39},{8,40},{9,... | collective-permute-start | bytes 12296 | tf_op jit(solution)/shard_map/ppermute | solution.py:43
  11.9 10.0 %collective-permute-start.6 = (bf16[8,64,128]{2,1,0:T(8,128)(2,1)S(1)}, bf16[8,64,128]{2,1,0:T(8,128)(2,1)S(1)}, u32[]{:S(2)}, u32[]{:S(2)}) collective-permute-start(bf16[8,64,128]{2,1,0:T(8,128)(2,1)S(1)} %get-tuple-element.40), channel_id=1, source_target_pairs={{0,8},{8,0},{16,24},{24,16},{32,40},{40,32},{48,56},{56,48},{64,72... | collective-permute-start | bytes 393224 | tf_op jit(solution)/shard_map/ppermute | solution.py:50
  11.9 10.0 %collective-permute-start.7 = (bf16[8,64,128]{2,1,0:T(8,128)(2,1)S(1)}, bf16[8,64,128]{2,1,0:T(8,128)(2,1)S(1)}, u32[]{:S(2)}, u32[]{:S(2)}) collective-permute-start(bf16[8,64,128]{2,1,0:T(8,128)(2,1)S(1)} %get-tuple-element.41), channel_id=1, source_target_pairs={{8,16},{16,8},{24,32},{32,24},{40,48},{48,40},{56,64},{64,56},{72,... | collective-permute-start | bytes 393224 | tf_op jit(solution)/shard_map/ppermute | solution.py:50
  17.8 11.1 %collective-permute-start.5 = (f32[8,128]{1,0:T(8,128)S(1)}, f32[8,128]{1,0:T(8,128)S(1)}, u32[]{:S(2)}, u32[]{:S(2)}) collective-permute-start(f32[8,128]{1,0:T(8,128)S(1)} %add_add_fusion.7), channel_id=1, source_target_pairs={{0,129},{1,128},{2,131},{3,130},{4,133},{5,132},{6,135},{7,134},{8... | collective-permute-start | bytes 12296 | tf_op jit(solution)/shard_map/ppermute | solution.py:43
  17.9 11.0 %collective-permute-start.4 = (f32[8,128]{1,0:T(8,128)S(1)}, f32[8,128]{1,0:T(8,128)S(1)}, u32[]{:S(2)}, u32[]{:S(2)}) collective-permute-start(f32[8,128]{1,0:T(8,128)S(1)} %add_add_fusion.7), channel_id=1, source_target_pairs={{0,1},{1,0},{2,3},{3,2},{4,5},{5,4},{6,7},{7,6},{8,9},{9,8},{10,11... | collective-permute-start | bytes 12296 | tf_op jit(solution)/shard_map/ppermute | solution.py:43
  19.9 9.0 %collective-permute-start.3 = (f32[8,128]{1,0:T(8,128)S(1)}, f32[8,128]{1,0:T(8,128)S(1)}, u32[]{:S(2)}, u32[]{:S(2)}) collective-permute-start(f32[8,128]{1,0:T(8,128)S(1)} %add_add_fusion.7), channel_id=1, source_target_pairs={{0,128},{1,129},{2,130},{3,131},{4,132},{5,133},{6,134},{7,135},{8... | collective-permute-start | bytes 12296 | tf_op jit(solution)/shard_map/ppermute | solution.py:43
  22.5 6.5 %collective-permute-start.8 = (bf16[3,64,128]{2,1,0:T(8,128)(2,1)S(1)}, bf16[3,64,128]{2,1,0:T(8,128)(2,1)S(1)}, u32[]{:S(2)}, u32[]{:S(2)}) collective-permute-start(bf16[3,64,128]{2,1,0:T(8,128)(2,1)S(1)} %get-tuple-element.42), channel_id=1, source_target_pairs={{0,1},{1,0},{2,3},{3,2},{4,5},{5,4},{6,7},{7,6},{8,9},{9,8},{10,11... | collective-permute-start | bytes 147464 | tf_op jit(solution)/shard_map/ppermute | solution.py:50
  23.5 8.4 %collective-permute-start.9 = (bf16[3,64,128]{2,1,0:T(8,128)(2,1)S(1)}, bf16[3,64,128]{2,1,0:T(8,128)(2,1)S(1)}, u32[]{:S(2)}, u32[]{:S(2)}) collective-permute-start(bf16[3,64,128]{2,1,0:T(8,128)(2,1)S(1)} %get-tuple-element.43), channel_id=1, source_target_pairs={{1,2},{2,1},{3,4},{4,3},{5,6},{6,5},{9,10},{10,9},{11,12},{12,11},... | collective-permute-start | bytes 147464 | tf_op jit(solution)/shard_map/ppermute | solution.py:50
  31.9 0.9 copy-start
  32.8 0.7 copy-start.3
  36.1 6.8 %collective-permute-start.10 = (bf16[1056,128]{1,0:T(8,128)(2,1)S(1)}, bf16[1056,128]{1,0:T(8,128)(2,1)S(1)}, u32[]{:S(2)}, u32[]{:S(2)}) collective-permute-start(bf16[1056,128]{1,0:T(8,128)(2,1)S(1)} %get-tuple-element.46), channel_id=1, source_target_pairs={{0,2},{1,3},{2,0},{3,1},{4,6},{5,7},{6,4},{7,5},{8,10},{9,11},{10,... | collective-permute-start | bytes 811016 | tf_op jit(solution)/shard_map/ppermute | solution.py:43
  37.6 19.7 %collective-permute-start.18 = (bf16[1056,128]{1,0:T(8,128)(2,1)S(1)}, bf16[1056,128]{1,0:T(8,128)(2,1)S(1)}, u32[]{:S(2)}, u32[]{:S(2)}) collective-permute-start(bf16[1056,128]{1,0:T(8,128)(2,1)S(1)} %get-tuple-element.49), channel_id=1, source_target_pairs={{0,16},{1,48},{2,80},{3,112},{4,144},{5,176},{6,208},{7,240},{8,24... | collective-permute-start | bytes 811016 | tf_op jit(solution)/shard_map/ppermute | solution.py:43
  42.9 16.5 %collective-permute-start.17 = (bf16[1056,128]{1,0:T(8,128)(2,1)S(1)}, bf16[1056,128]{1,0:T(8,128)(2,1)S(1)}, u32[]{:S(2)}, u32[]{:S(2)}) collective-permute-start(bf16[1056,128]{1,0:T(8,128)(2,1)S(1)} %collective-permute-done.10), channel_id=1, source_target_pairs={{0,64},{1,96},{2,0},{3,32},{4,192},{5,224},{6,128},{7,160},{8,72},... | collective-permute-start | bytes 811016 | tf_op jit(solution)/shard_map/ppermute | solution.py:43
  48.4 4.8 %collective-permute-start.13 = (f32[8,128]{1,0:T(8,128)S(1)}, f32[8,128]{1,0:T(8,128)S(1)}, u32[]{:S(2)}, u32[]{:S(2)}) collective-permute-start(f32[8,128]{1,0:T(8,128)S(1)} %add_add_fusion.6), channel_id=1, source_target_pairs={{0,6},{1,7},{2,4},{3,5},{4,2},{5,3},{6,0},{7,1},{8,14},{9,15},{10,... | collective-permute-start | bytes 12296 | tf_op jit(solution)/shard_map/ppermute | solution.py:43
  48.4 5.1 %collective-permute-start.12 = (f32[8,128]{1,0:T(8,128)S(1)}, f32[8,128]{1,0:T(8,128)S(1)}, u32[]{:S(2)}, u32[]{:S(2)}) collective-permute-start(f32[8,128]{1,0:T(8,128)S(1)} %add_add_fusion.6), channel_id=1, source_target_pairs={{0,4},{1,5},{2,6},{3,7},{4,0},{5,1},{6,2},{7,3},{8,12},{9,13},{10,... | collective-permute-start | bytes 12296 | tf_op jit(solution)/shard_map/ppermute | solution.py:43
  49.8 4.3 %collective-permute-start.11 = (f32[8,128]{1,0:T(8,128)S(1)}, f32[8,128]{1,0:T(8,128)S(1)}, u32[]{:S(2)}, u32[]{:S(2)}) collective-permute-start(f32[8,128]{1,0:T(8,128)S(1)} %add_add_fusion.6), channel_id=1, source_target_pairs={{0,2},{1,3},{2,0},{3,1},{4,6},{5,7},{6,4},{7,5},{8,10},{9,11},{10,... | collective-permute-start | bytes 12296 | tf_op jit(solution)/shard_map/ppermute | solution.py:43
  54.1 5.4 %collective-permute-start.16 = (f32[8,128]{1,0:T(8,128)S(1)}, f32[8,128]{1,0:T(8,128)S(1)}, u32[]{:S(2)}, u32[]{:S(2)}) collective-permute-start(f32[8,128]{1,0:T(8,128)S(1)} %add_add_fusion.5), channel_id=1, source_target_pairs={{0,24},{1,25},{2,26},{3,27},{4,28},{5,29},{6,30},{7,31},{8,16},{9,... | collective-permute-start | bytes 12296 | tf_op jit(solution)/shard_map/ppermute | solution.py:43
  54.8 4.7 %collective-permute-start.15 = (f32[8,128]{1,0:T(8,128)S(1)}, f32[8,128]{1,0:T(8,128)S(1)}, u32[]{:S(2)}, u32[]{:S(2)}) collective-permute-start(f32[8,128]{1,0:T(8,128)S(1)} %add_add_fusion.5), channel_id=1, source_target_pairs={{0,16},{1,17},{2,18},{3,19},{4,20},{5,21},{6,22},{7,23},{8,24},{9,... | collective-permute-start | bytes 12296 | tf_op jit(solution)/shard_map/ppermute | solution.py:43
  57.3 2.1 %collective-permute-start.14 = (f32[8,128]{1,0:T(8,128)S(1)}, f32[8,128]{1,0:T(8,128)S(1)}, u32[]{:S(2)}, u32[]{:S(2)}) collective-permute-start(f32[8,128]{1,0:T(8,128)S(1)} %add_add_fusion.5), channel_id=1, source_target_pairs={{0,8},{1,9},{2,10},{3,11},{4,12},{5,13},{6,14},{7,15},{8,0},{9,1},... | collective-permute-start | bytes 12296 | tf_op jit(solution)/shard_map/ppermute | solution.py:43
  57.4 2.1 %collective-permute-start.20 = (bf16[528,128]{1,0:T(8,128)(2,1)S(1)}, bf16[528,128]{1,0:T(8,128)(2,1)S(1)}, u32[]{:S(2)}, u32[]{:S(2)}) collective-permute-start(bf16[528,128]{1,0:T(8,128)(2,1)S(1)} %slice.9), channel_id=1, source_target_pairs={{0,8},{1,9},{2,10},{3,11},{4,12},{5,13},{6,14},{7,15},{8,0},{9,1},... | collective-permute-start | bytes 405512 | tf_op jit(solution)/shard_map/ppermute | solution.py:43
  59.3 1.4 %collective-permute-start.19 = (bf16[528,128]{1,0:T(8,128)(2,1)S(1)}, bf16[528,128]{1,0:T(8,128)(2,1)S(1)}, u32[]{:S(2)}, u32[]{:S(2)}) collective-permute-start(bf16[528,128]{1,0:T(8,128)(2,1)S(1)} %slice.8), channel_id=1, source_target_pairs={{0,8},{1,9},{2,10},{3,11},{4,12},{5,13},{6,14},{7,15},{8,0},{9,1},... | collective-permute-start | bytes 405512 | tf_op jit(solution)/shard_map/ppermute | solution.py:43
  64.9 52.3 %copy-start.1 = (bf16[3,3,64,64]{3,2,1,0:T(8,128)(2,1)S(1)}, bf16[3,3,64,64]{3,2,1,0:T(8,128)(2,1)}, u32[]{:S(2)}) copy-start(bf16[3,3,64,64]{3,2,1,0:T(8,128)(2,1)} %param.7) | copy-start | bytes 221188
  66.9 2.0 %collective-permute-start.21 = (f32[88,128]{1,0:T(8,128)S(1)}, f32[88,128]{1,0:T(8,128)S(1)}, u32[]{:S(2)}, u32[]{:S(2)}) collective-permute-start(f32[88,128]{1,0:T(8,128)S(1)} %get-tuple-element.57), channel_id=1, source_target_pairs={{0,8},{1,9},{2,10},{3,11},{4,12},{5,13},{6,14},{7,15},{8,0},{9,1},... | collective-permute-start | bytes 135176 | tf_op jit(solution)/shard_map/ppermute | solution.py:43
  67.2 4.5 %collective-permute-start.22 = (f32[88,128]{1,0:T(8,128)S(1)}, f32[88,128]{1,0:T(8,128)S(1)}, u32[]{:S(2)}, u32[]{:S(2)}) collective-permute-start(f32[88,128]{1,0:T(8,128)S(1)} %get-tuple-element.58), channel_id=1, source_target_pairs={{0,16},{1,17},{2,18},{3,19},{4,20},{5,21},{6,22},{7,23},{8,24},{9,... | collective-permute-start | bytes 135176 | tf_op jit(solution)/shard_map/ppermute | solution.py:43
  67.7 4.0 %collective-permute-start.23 = (f32[88,128]{1,0:T(8,128)S(1)}, f32[88,128]{1,0:T(8,128)S(1)}, u32[]{:S(2)}, u32[]{:S(2)}) collective-permute-start(f32[88,128]{1,0:T(8,128)S(1)} %get-tuple-element.59), channel_id=1, source_target_pairs={{0,24},{1,25},{2,26},{3,27},{4,28},{5,29},{6,30},{7,31},{8,16},{9,... | collective-permute-start | bytes 135176 | tf_op jit(solution)/shard_map/ppermute | solution.py:43
  71.7 15.3 %collective-permute-start.26 = (f32[88,128]{1,0:T(8,128)S(1)}, f32[88,128]{1,0:T(8,128)S(1)}, u32[]{:S(2)}, u32[]{:S(2)}) collective-permute-start(f32[88,128]{1,0:T(8,128)S(1)} %add_add_fusion.3), channel_id=1, source_target_pairs={{0,96},{1,97},{2,98},{3,99},{4,100},{5,101},{6,102},{7,103},{8,104... | collective-permute-start | bytes 135176 | tf_op jit(solution)/shard_map/ppermute | solution.py:43
  84.5 8.6 %collective-permute-start.25 = (f32[88,128]{1,0:T(8,128)S(1)}, f32[88,128]{1,0:T(8,128)S(1)}, u32[]{:S(2)}, u32[]{:S(2)}) collective-permute-start(f32[88,128]{1,0:T(8,128)S(1)} %add_add_fusion.3), channel_id=1, source_target_pairs={{0,64},{1,65},{2,66},{3,67},{4,68},{5,69},{6,70},{7,71},{8,72},{9,... | collective-permute-start | bytes 135176 | tf_op jit(solution)/shard_map/ppermute | solution.py:43
  86.8 6.4 %collective-permute-start.24 = (f32[88,128]{1,0:T(8,128)S(1)}, f32[88,128]{1,0:T(8,128)S(1)}, u32[]{:S(2)}, u32[]{:S(2)}) collective-permute-start(f32[88,128]{1,0:T(8,128)S(1)} %add_add_fusion.3), channel_id=1, source_target_pairs={{0,32},{1,33},{2,34},{3,35},{4,36},{5,37},{6,38},{7,39},{8,40},{9,... | collective-permute-start | bytes 135176 | tf_op jit(solution)/shard_map/ppermute | solution.py:43
  93.2 9.4 %collective-permute-start.29 = (f32[88,128]{1,0:T(8,128)S(1)}, f32[88,128]{1,0:T(8,128)S(1)}, u32[]{:S(2)}, u32[]{:S(2)}) collective-permute-start(f32[88,128]{1,0:T(8,128)S(1)} %add_add_fusion.2), channel_id=1, source_target_pairs={{0,129},{1,128},{2,131},{3,130},{4,133},{5,132},{6,135},{7,134},{8... | collective-permute-start | bytes 135176 | tf_op jit(solution)/shard_map/ppermute | solution.py:43
  93.6 9.1 %collective-permute-start.28 = (f32[88,128]{1,0:T(8,128)S(1)}, f32[88,128]{1,0:T(8,128)S(1)}, u32[]{:S(2)}, u32[]{:S(2)}) collective-permute-start(f32[88,128]{1,0:T(8,128)S(1)} %add_add_fusion.2), channel_id=1, source_target_pairs={{0,1},{1,0},{2,3},{3,2},{4,5},{5,4},{6,7},{7,6},{8,9},{9,8},{10,11... | collective-permute-start | bytes 135176 | tf_op jit(solution)/shard_map/ppermute | solution.py:43
  97.7 5.0 %collective-permute-start.27 = (f32[88,128]{1,0:T(8,128)S(1)}, f32[88,128]{1,0:T(8,128)S(1)}, u32[]{:S(2)}, u32[]{:S(2)}) collective-permute-start(f32[88,128]{1,0:T(8,128)S(1)} %add_add_fusion.2), channel_id=1, source_target_pairs={{0,128},{1,129},{2,130},{3,131},{4,132},{5,133},{6,134},{7,135},{8... | collective-permute-start | bytes 135176 | tf_op jit(solution)/shard_map/ppermute | solution.py:43
  97.7 9.2 %collective-permute-start.36 = (bf16[8,64,128]{2,1,0:T(8,128)(2,1)S(1)}, bf16[8,64,128]{2,1,0:T(8,128)(2,1)S(1)}, u32[]{:S(2)}, u32[]{:S(2)}) collective-permute-start(bf16[8,64,128]{2,1,0:T(8,128)(2,1)S(1)} %get-tuple-element.62), channel_id=1, source_target_pairs={{0,8},{8,0},{16,24},{24,16},{32,40},{40,32},{48,56},{56,48},{64,72... | collective-permute-start | bytes 393224 | tf_op jit(solution)/shard_map/ppermute | solution.py:50
  97.7 9.2 %collective-permute-start.37 = (bf16[8,64,128]{2,1,0:T(8,128)(2,1)S(1)}, bf16[8,64,128]{2,1,0:T(8,128)(2,1)S(1)}, u32[]{:S(2)}, u32[]{:S(2)}) collective-permute-start(bf16[8,64,128]{2,1,0:T(8,128)(2,1)S(1)} %get-tuple-element.63), channel_id=1, source_target_pairs={{8,16},{16,8},{24,32},{32,24},{40,48},{48,40},{56,64},{64,56},{72,... | collective-permute-start | bytes 393224 | tf_op jit(solution)/shard_map/ppermute | solution.py:50
  102.7 10.1 %collective-permute-start.32 = (f32[88,128]{1,0:T(8,128)S(1)}, f32[88,128]{1,0:T(8,128)S(1)}, u32[]{:S(2)}, u32[]{:S(2)}) collective-permute-start(f32[88,128]{1,0:T(8,128)S(1)} %add_add_fusion.1), channel_id=1, source_target_pairs={{0,6},{1,7},{2,4},{3,5},{4,2},{5,3},{6,0},{7,1},{8,14},{9,15},{10,... | collective-permute-start | bytes 135176 | tf_op jit(solution)/shard_map/ppermute | solution.py:43
  104.2 8.6 %collective-permute-start.31 = (f32[88,128]{1,0:T(8,128)S(1)}, f32[88,128]{1,0:T(8,128)S(1)}, u32[]{:S(2)}, u32[]{:S(2)}) collective-permute-start(f32[88,128]{1,0:T(8,128)S(1)} %add_add_fusion.1), channel_id=1, source_target_pairs={{0,4},{1,5},{2,6},{3,7},{4,0},{5,1},{6,2},{7,3},{8,12},{9,13},{10,... | collective-permute-start | bytes 135176 | tf_op jit(solution)/shard_map/ppermute | solution.py:43
  105.3 7.5 %collective-permute-start.30 = (f32[88,128]{1,0:T(8,128)S(1)}, f32[88,128]{1,0:T(8,128)S(1)}, u32[]{:S(2)}, u32[]{:S(2)}) collective-permute-start(f32[88,128]{1,0:T(8,128)S(1)} %add_add_fusion.1), channel_id=1, source_target_pairs={{0,2},{1,3},{2,0},{3,1},{4,6},{5,7},{6,4},{7,5},{8,10},{9,11},{10,... | collective-permute-start | bytes 135176 | tf_op jit(solution)/shard_map/ppermute | solution.py:43
  107.4 7.4 %collective-permute-start.38 = (bf16[3,64,128]{2,1,0:T(8,128)(2,1)S(1)}, bf16[3,64,128]{2,1,0:T(8,128)(2,1)S(1)}, u32[]{:S(2)}, u32[]{:S(2)}) collective-permute-start(bf16[3,64,128]{2,1,0:T(8,128)(2,1)S(1)} %get-tuple-element.64), channel_id=1, source_target_pairs={{0,1},{1,0},{2,3},{3,2},{4,5},{5,4},{6,7},{7,6},{8,9},{9,8},{10,11... | collective-permute-start | bytes 147464 | tf_op jit(solution)/shard_map/ppermute | solution.py:50
  108.9 8.4 %collective-permute-start.39 = (bf16[3,64,128]{2,1,0:T(8,128)(2,1)S(1)}, bf16[3,64,128]{2,1,0:T(8,128)(2,1)S(1)}, u32[]{:S(2)}, u32[]{:S(2)}) collective-permute-start(bf16[3,64,128]{2,1,0:T(8,128)(2,1)S(1)} %get-tuple-element.65), channel_id=1, source_target_pairs={{1,2},{2,1},{3,4},{4,3},{5,6},{6,5},{9,10},{10,9},{11,12},{12,11},... | collective-permute-start | bytes 147464 | tf_op jit(solution)/shard_map/ppermute | solution.py:50
  112.9 6.8 %collective-permute-start.35 = (f32[88,128]{1,0:T(8,128)S(1)}, f32[88,128]{1,0:T(8,128)S(1)}, u32[]{:S(2)}, u32[]{:S(2)}) collective-permute-start(f32[88,128]{1,0:T(8,128)S(1)} %add_add_fusion.got0), channel_id=1, source_target_pairs={{0,24},{1,25},{2,26},{3,27},{4,28},{5,29},{6,30},{7,31},{8,16},{9,... | collective-permute-start | bytes 135176 | tf_op jit(solution)/shard_map/ppermute | solution.py:43
  113.0 6.7 %collective-permute-start.34 = (f32[88,128]{1,0:T(8,128)S(1)}, f32[88,128]{1,0:T(8,128)S(1)}, u32[]{:S(2)}, u32[]{:S(2)}) collective-permute-start(f32[88,128]{1,0:T(8,128)S(1)} %add_add_fusion.got0), channel_id=1, source_target_pairs={{0,16},{1,17},{2,18},{3,19},{4,20},{5,21},{6,22},{7,23},{8,24},{9,... | collective-permute-start | bytes 135176 | tf_op jit(solution)/shard_map/ppermute | solution.py:43
  113.1 6.6 %collective-permute-start.33 = (f32[88,128]{1,0:T(8,128)S(1)}, f32[88,128]{1,0:T(8,128)S(1)}, u32[]{:S(2)}, u32[]{:S(2)}) collective-permute-start(f32[88,128]{1,0:T(8,128)S(1)} %add_add_fusion.got0), channel_id=1, source_target_pairs={{0,8},{1,9},{2,10},{3,11},{4,12},{5,13},{6,14},{7,15},{8,0},{9,1},... | collective-permute-start | bytes 135176 | tf_op jit(solution)/shard_map/ppermute | solution.py:43

commit v11 on v10

--- a/solution.py
+++ b/solution.py
@@ -184,9 +184,14 @@
     lax.fori_loop(0, rows + 1, pack, 0, unroll=3)
 
 
-def softmax_kernel(
-    place, near, far, got1, got3, mixed, head, head_bias, labels, valid,
-    grad, head_sum, bias_sum, loss_sum, cells, lab, lab_t, val, val_t, padded_head,
+def scale_of(count):
+    return 0.5 / jnp.maximum(count[0:1, 0:1], 1.0)
+
+
+def gradient_kernel(
+    place, count, near, far, got1, got3, mixed, head, head_bias, labels, valid, wide,
+    grad, low, mate, other, out0, out1, out2, out3,
+    cells, lab, lab_t, val, val_t, padded_head, head_sum, bias_sum, loss_sum, total, sheet,
 ):
     rows, chans = mixed.shape[0], mixed.shape[1]
     bins, real = padded_head.shape[0], head.shape[0]
@@ -225,6 +230,8 @@
     head_sum[...] = jnp.zeros_like(head_sum)
     bias_sum[...] = jnp.zeros_like(bias_sum)
     loss_sum[...] = jnp.zeros_like(loss_sum)
+    total[...] = jnp.zeros_like(total)
+    scale = scale_of(count)
 
     def step(i, carry):
         other = cells[pl.ds(i, LANES, stride=half), :].astype(BF16)
@@ -239,14 +246,14 @@
             sym = 0.5 * (own + far)
             peak = jnp.max(sym, axis=0, keepdims=True)
             raised = jnp.exp(sym - peak)
-            total = jnp.sum(raised, axis=0, keepdims=True)
-            lse = peak + jnp.log(total)
+            mass = jnp.sum(raised, axis=0, keepdims=True)
+            lse = peak + jnp.log(mass)
             hot = bin_ids == lab[at, :]
             hot_t = bin_ids == lab_t[at, :]
             mask, mask_t = val[at, :], val_t[at, :]
             picked = jnp.sum(jnp.where(hot, sym, 0.0), axis=0, keepdims=True)
             loss_sum[...] += mask * (lse - picked)
-            share = raised * ((mask + mask_t) / total)
+            share = raised * ((mask + mask_t) / mass)
             pieces.append(share - jnp.where(hot, mask, 0.0) - jnp.where(hot_t, mask_t, 0.0))
         bias_sum[...] += pieces[0] + pieces[1]
         g = jnp.concatenate(pieces, axis=1)
@@ -257,49 +264,28 @@
         out = jnp.dot(thrice, split, preferred_element_type=F32)
         grad[i] = out[:, :LANES]
         grad[i + half] = out[:, LANES:]
+        rounded = (out * scale).astype(BF16)
+        low[i] = rounded[:, :LANES]
+        low[i + half] = rounded[:, LANES:]
+        total[...] += lax.dot_general(
+            jnp.concatenate([windows(wide, i), windows(wide, i + half)], axis=1),
+            rounded,
+            (((1,), (1,)), ((), ())),
+            preferred_element_type=F32,
+        )
         head_sum[...] += lax.dot_general(
             split, pair, (((1,), (1,)), ((), ())), preferred_element_type=F32
         )
         return carry
 
     lax.fori_loop(0, half, step, 0, unroll=UNROLL)
-
-
-def scale_of(count):
-    return 0.5 / jnp.maximum(count[0:1, 0:1], 1.0)
-
-
-def kernel_grad_kernel(
-    place, count, grad, wide, head_sum, bias_sum, loss_sum,
-    low, mate, other, out0, out1, out2, out3, total, sheet,
-):
-    rows, chans = grad.shape[0], grad.shape[1]
-    bins = bias_sum.shape[0]
-    scale = scale_of(count)
-    total[...] = jnp.zeros_like(total)
-
-    def step(p, carry):
-        i = 2 * p
-        a = (grad[i] * scale).astype(BF16)
-        b = (grad[i + 1] * scale).astype(BF16)
-        low[i] = a
-        low[i + 1] = b
-        total[...] += lax.dot_general(
-            pair_windows(wide, i),
-            jnp.concatenate([a, b], axis=1),
-            (((1,), (1,)), ((), ())),
-            preferred_element_type=F32,
-        )
-        return carry
-
-    lax.fori_loop(0, rows // 2, step, 0, unroll=UNROLL)
     share_edges(place, low, mate, other)
-    half = total.shape[0] // 2
+    upper = total.shape[0] // 2
     sheet[...] = jnp.zeros_like(sheet)
-    sheet[:half, :] = jnp.concatenate([total[:half], total[half:]], axis=1)
+    sheet[:upper, :] = jnp.concatenate([total[:upper], total[upper:]], axis=1)
     h = (head_sum[:bins] + head_sum[bins : 2 * bins] + head_sum[2 * bins :]) * scale
-    sheet[half : half + bins, :chans] = h
-    note = half + bins
+    sheet[upper : upper + bins, :chans] = h
+    note = upper + bins
     sheet[note : note + 1, :bins] = jnp.sum(bias_sum[...].T, axis=0, keepdims=True) * scale
     sheet[note + 1 : note + 2, :1] = jnp.sum(loss_sum[...], axis=1, keepdims=True)
     quarter = sheet.shape[0] // 4
@@ -441,31 +427,25 @@
     passed, got = mirrored(pay_near, pay_far, parts)
     _, counted = lax.optimization_barrier((passed, counted))
     count = total_small(counted, (3, 0))
-    grad, head_sum, bias_sum, loss_sum = run(
-        softmax_kernel,
-        [
-            shape(tile, F32),
-            shape((3 * tall, chans), F32),
-            shape((tall, LANES), F32),
-            shape((1, LANES), F32),
-        ],
-        (place, *got, mixed, head_weight.T, head_bias.reshape(1, bins), labels, valid),
+    half = 9 * chans // 2
+    lines = -(-(half + tall + 8) // 32) * 32
+    grad, low, mate, other, *quarters = run(
+        gradient_kernel,
+        [shape(tile, F32), shape(tile, BF16), shape(edge, BF16), shape(edge, BF16)]
+        + [shape((lines // 4, LANES), F32)] * 4,
+        (place, count, *got, mixed, head_weight.T, head_bias.reshape(1, bins), labels, valid, wide),
         scratch=[pltpu.VMEM((length * 4, LANES), F32)]
         + [pltpu.VMEM((rows, LANES), F32)] * 4
-        + [pltpu.VMEM((tall, chans), F32)],
-        scalars=1,
-        micros=5,
-    )
-    half = 9 * chans // 2
-    lines = -(-(half + tall + 8) // 32) * 32
-    low, mate, other, *quarters = run(
-        kernel_grad_kernel,
-        [shape(tile, BF16), shape(edge, BF16), shape(edge, BF16)]
-        + [shape((lines // 4, LANES), F32)] * 4,
-        (place, count, grad, wide, head_sum, bias_sum, loss_sum),
-        scratch=[pltpu.VMEM((9 * chans, chans), F32), pltpu.VMEM((lines, LANES), F32)],
-        scalars=1,
-        micros=3,
+        + [
+            pltpu.VMEM((tall, chans), F32),
+            pltpu.VMEM((3 * tall, chans), F32),
+            pltpu.VMEM((tall, LANES), F32),
+            pltpu.VMEM((1, LANES), F32),
+            pltpu.VMEM((9 * chans, chans), F32),
+            pltpu.VMEM((lines, LANES), F32),
+        ],
+        scalars=1,
+        micros=6,
     )
     sums = total_quarters(quarters)
     around = borders(place, low, mate, other)

time: 122 us -> 120 us (0.984)
    pallas_call x8 -> x7, Pallas kernels: 13.6 us -> 12.5 us  [run(): pl.pallas_call(body, out_shape=outs, in_specs=[SMEM] * scalars + [VMEM] *...]
    unnamed x16 -> x12, local copies, waits for them, and re-layouts: 3.4 us -> 3.39 us
where the time goes in v11:
time: 120 us; the launch traced here: 119 us
  starting transfers between devices  83.9 us (70%)
  waiting for transfers between devices  18.5 us (15%)
  Pallas kernels  12.5 us (10%)
  local copies, waits for them, and re-layouts  3.41 us (3%)
    ppermute x32, starting transfers between devices, send(): return lax.ppermute(block, GRID, pairs)  61.4 us
    ppermute x4, starting transfers between devices, swapped(): lax.ppermute(to_other, axis, others)  20.1 us
    ppermute x32, waiting for transfers between devices, send(): return lax.ppermute(block, GRID, pairs)  13.2 us
    pallas_call x7, Pallas kernels, run(): pl.pallas_call(body, out_shape=outs, in_specs=[SMEM] * scalars + [VMEM] *...  12.5 us
    ppermute x4, waiting for transfers between devices, swapped(): lax.ppermute(to_other, axis, others)  5.32 us
    unnamed x12, local copies, waits for them, and re-layouts  3.39 us
    ppermute x4, starting transfers between devices, swapped(): lax.ppermute(to_mate, axis, mates)  2.5 us
  transfers between devices with their start and end apart: 40, of which 10 were waited for; matrix products, arithmetic and copies ran while one was open for 0% of the time, Pallas kernels for 3%

profile of v11, /device:TPU:24, one launch (start us, length us, event | category | flops | bytes accessed | tf_op | source)
XLA Modules:
  0.0 119.4 jit_solution(13781363332534996121)
XLA Ops:
  0.7 1.0 copy-done.1
  1.7 0.7 copy-done.3
  2.4 0.7 shard_map.101
  3.1 6.3 %collective-permute-start.2 = (f32[8,128]{1,0:T(8,128)S(1)}, f32[8,128]{1,0:T(8,128)S(1)}, u32[]{:S(2)}, u32[]{:S(2)}) collective-permute-start(f32[8,128]{1,0:T(8,128)S(1)} %get-tuple-element.34), channel_id=1, source_target_pairs={{0,96},{1,97},{2,98},{3,99},{4,100},{5,101},{6,102},{7,103},{8,104... | collective-permute-start | bytes 12296 | tf_op jit(solution)/shard_map/ppermute | solution.py:43
  9.5 1.0 collective-permute-start.1
  10.5 1.5 %collective-permute-start = (f32[8,128]{1,0:T(8,128)S(1)}, f32[8,128]{1,0:T(8,128)S(1)}, u32[]{:S(2)}, u32[]{:S(2)}) collective-permute-start(f32[8,128]{1,0:T(8,128)S(1)} %get-tuple-element.34), channel_id=1, source_target_pairs={{0,32},{1,33},{2,34},{3,35},{4,36},{5,37},{6,38},{7,39},{8,40},{9,... | collective-permute-start | bytes 12296 | tf_op jit(solution)/shard_map/ppermute | solution.py:43
  11.9 5.8 %collective-permute-start.7 = (bf16[8,64,128]{2,1,0:T(8,128)(2,1)S(1)}, bf16[8,64,128]{2,1,0:T(8,128)(2,1)S(1)}, u32[]{:S(2)}, u32[]{:S(2)}) collective-permute-start(bf16[8,64,128]{2,1,0:T(8,128)(2,1)S(1)} %get-tuple-element.38), channel_id=1, source_target_pairs={{8,16},{16,8},{24,32},{32,24},{40,48},{48,40},{56,64},{64,56},{72,... | collective-permute-start | bytes 393224 | tf_op jit(solution)/shard_map/ppermute | solution.py:50
  17.9 2.0 %collective-permute-start.4 = (f32[8,128]{1,0:T(8,128)S(1)}, f32[8,128]{1,0:T(8,128)S(1)}, u32[]{:S(2)}, u32[]{:S(2)}) collective-permute-start(f32[8,128]{1,0:T(8,128)S(1)} %add_add_fusion.7), channel_id=1, source_target_pairs={{0,1},{1,0},{2,3},{3,2},{4,5},{5,4},{6,7},{7,6},{8,9},{9,8},{10,11... | collective-permute-start | bytes 12296 | tf_op jit(solution)/shard_map/ppermute | solution.py:43
  19.9 2.1 %collective-permute-start.3 = (f32[8,128]{1,0:T(8,128)S(1)}, f32[8,128]{1,0:T(8,128)S(1)}, u32[]{:S(2)}, u32[]{:S(2)}) collective-permute-start(f32[8,128]{1,0:T(8,128)S(1)} %add_add_fusion.7), channel_id=1, source_target_pairs={{0,128},{1,129},{2,130},{3,131},{4,132},{5,133},{6,134},{7,135},{8... | collective-permute-start | bytes 12296 | tf_op jit(solution)/shard_map/ppermute | solution.py:43
  22.0 0.5 shard_map.102
  22.5 1.0 collective-permute-start.8
  23.5 5.4 %collective-permute-start.9 = (bf16[3,64,128]{2,1,0:T(8,128)(2,1)S(1)}, bf16[3,64,128]{2,1,0:T(8,128)(2,1)S(1)}, u32[]{:S(2)}, u32[]{:S(2)}) collective-permute-start(bf16[3,64,128]{2,1,0:T(8,128)(2,1)S(1)} %get-tuple-element.40), channel_id=1, source_target_pairs={{1,2},{2,1},{3,4},{4,3},{5,6},{6,5},{9,10},{10,9},{11,12},{12,11},... | collective-permute-start | bytes 147464 | tf_op jit(solution)/shard_map/ppermute | solution.py:50
  29.0 2.9 %collective-permute-done.9.side_other = bf16[3,64,128]{2,1,0:T(8,128)(2,1)S(1)} collective-permute-done((bf16[3,64,128]{2,1,0:T(8,128)(2,1)S(1)}, bf16[3,64,128]{2,1,0:T(8,128)(2,1)S(1)}, u32[]{:S(2)}, u32[]{:S(2)}) %collective-permute-start.9) | collective-permute-done | bytes 49184 | tf_op jit(solution)/shard_map/ppermute | solution.py:50
  31.9 0.9 copy-done
  32.8 0.7 copy-done.2
  33.5 2.5 %shard_map.103 = (bf16[48,192,128]{2,1,0:T(8,128)(2,1)S(1)}, bf16[32,64,128]{2,1,0:T(8,128)(2,1)S(1)}, bf16[1056,128]{1,0:T(8,128)(2,1)S(1)}, bf16[1056,128]{1,0:T(8,128)(2,1)S(1)}) custom-call(s32[1]{0:T(128)} %bitcast.place, bf16[32,64,128]{2,1,0:T(8,128)(2,1)S(1)} %get-tuple-element.36.own.act, bf16[8,64,128]{2,1,0:T(8,128)(2,1)S(1)} %collective-permute-done.6.mate, ...), custom_call_target="tpu_custom_call" | custom-call | bytes 18000000 | tf_op jit(solution)/shard_map/pallas_call | solution.py:19
  36.0 1.6 %collective-permute-start.10 = (bf16[1056,128]{1,0:T(8,128)(2,1)S(1)}, bf16[1056,128]{1,0:T(8,128)(2,1)S(1)}, u32[]{:S(2)}, u32[]{:S(2)}) collective-permute-start(bf16[1056,128]{1,0:T(8,128)(2,1)S(1)} %get-tuple-element.43), channel_id=1, source_target_pairs={{0,2},{1,3},{2,0},{3,1},{4,6},{5,7},{6,4},{7,5},{8,10},{9,11},{10,... | collective-permute-start | bytes 811016 | tf_op jit(solution)/shard_map/ppermute | solution.py:43
  37.6 5.2 %collective-permute-start.18 = (bf16[1056,128]{1,0:T(8,128)(2,1)S(1)}, bf16[1056,128]{1,0:T(8,128)(2,1)S(1)}, u32[]{:S(2)}, u32[]{:S(2)}) collective-permute-start(bf16[1056,128]{1,0:T(8,128)(2,1)S(1)} %get-tuple-element.46), channel_id=1, source_target_pairs={{0,16},{1,48},{2,80},{3,112},{4,144},{5,176},{6,208},{7,240},{8,24... | collective-permute-start | bytes 811016 | tf_op jit(solution)/shard_map/ppermute | solution.py:43
  42.9 5.5 %collective-permute-start.17 = (bf16[1056,128]{1,0:T(8,128)(2,1)S(1)}, bf16[1056,128]{1,0:T(8,128)(2,1)S(1)}, u32[]{:S(2)}, u32[]{:S(2)}) collective-permute-start(bf16[1056,128]{1,0:T(8,128)(2,1)S(1)} %collective-permute-done.10), channel_id=1, source_target_pairs={{0,64},{1,96},{2,0},{3,32},{4,192},{5,224},{6,128},{7,160},{8,72},... | collective-permute-start | bytes 811016 | tf_op jit(solution)/shard_map/ppermute | solution.py:43
  48.4 1.3 %collective-permute-start.12 = (f32[8,128]{1,0:T(8,128)S(1)}, f32[8,128]{1,0:T(8,128)S(1)}, u32[]{:S(2)}, u32[]{:S(2)}) collective-permute-start(f32[8,128]{1,0:T(8,128)S(1)} %add_add_fusion.6), channel_id=1, source_target_pairs={{0,4},{1,5},{2,6},{3,7},{4,0},{5,1},{6,2},{7,3},{8,12},{9,13},{10,... | collective-permute-start | bytes 12296 | tf_op jit(solution)/shard_map/ppermute | solution.py:43
  49.8 2.7 %collective-permute-start.11 = (f32[8,128]{1,0:T(8,128)S(1)}, f32[8,128]{1,0:T(8,128)S(1)}, u32[]{:S(2)}, u32[]{:S(2)}) collective-permute-start(f32[8,128]{1,0:T(8,128)S(1)} %add_add_fusion.6), channel_id=1, source_target_pairs={{0,2},{1,3},{2,0},{3,1},{4,6},{5,7},{6,4},{7,5},{8,10},{9,11},{10,... | collective-permute-start | bytes 12296 | tf_op jit(solution)/shard_map/ppermute | solution.py:43
  52.4 0.7 collective-permute-done.13
  53.1 0.4 collective-permute-done.12
  53.5 0.5 collective-permute-done.11
  54.1 0.7 collective-permute-start.16
  54.7 2.6 %collective-permute-start.15 = (f32[8,128]{1,0:T(8,128)S(1)}, f32[8,128]{1,0:T(8,128)S(1)}, u32[]{:S(2)}, u32[]{:S(2)}) collective-permute-start(f32[8,128]{1,0:T(8,128)S(1)} %add_add_fusion.5), channel_id=1, source_target_pairs={{0,16},{1,17},{2,18},{3,19},{4,20},{5,21},{6,22},{7,23},{8,24},{9,... | collective-permute-start | bytes 12296 | tf_op jit(solution)/shard_map/ppermute | solution.py:43
  57.4 0.8 collective-permute-start.20
  58.1 1.2 collective-permute-done.17.near
  59.5 1.3 %collective-permute-done.19.got1 = bf16[528,128]{1,0:T(8,128)(2,1)S(1)} collective-permute-done((bf16[528,128]{1,0:T(8,128)(2,1)S(1)}, bf16[528,128]{1,0:T(8,128)(2,1)S(1)}, u32[]{:S(2)}, u32[]{:S(2)}) %collective-permute-start.19) | collective-permute-done | bytes 135200 | tf_op jit(solution)/shard_map/ppermute | solution.py:43
  60.8 5.1 %shard_map.104 = (f32[32,64,128]{2,1,0:T(8,128)S(1)}, bf16[32,64,128]{2,1,0:T(8,128)(2,1)S(1)}, bf16[8,64,128]{2,1,0:T(8,128)(2,1)S(1)}, bf16[8,64,128]{2,1,0:T(...) custom-call(s32[1]{0:T(128)} %bitcast.place, ...), custom_call_target="tpu_custom_call" | custom-call | bytes 21600000 | tf_op jit(solution)/shard_map/pallas_call | solution.py:19
  66.1 0.6 collective-permute-start.22
  66.6 1.2 collective-permute-start.23
  67.8 2.8 %collective-permute-done.22 = f32[88,128]{1,0:T(8,128)S(1)} collective-permute-done((f32[88,128]{1,0:T(8,128)S(1)}, f32[88,128]{1,0:T(8,128)S(1)}, u32[]{:S(2)}, u32[]{:S(2)}) %collective-permute-start.22) | collective-permute-done | bytes 45088 | tf_op jit(solution)/shard_map/ppermute | solution.py:43
  70.6 12.8 %collective-permute-start.26 = (f32[88,128]{1,0:T(8,128)S(1)}, f32[88,128]{1,0:T(8,128)S(1)}, u32[]{:S(2)}, u32[]{:S(2)}) collective-permute-start(f32[88,128]{1,0:T(8,128)S(1)} %add_add_fusion.3), channel_id=1, source_target_pairs={{0,96},{1,97},{2,98},{3,99},{4,100},{5,101},{6,102},{7,103},{8,104... | collective-permute-start | bytes 135176 | tf_op jit(solution)/shard_map/ppermute | solution.py:43
  83.4 2.3 %collective-permute-start.25 = (f32[88,128]{1,0:T(8,128)S(1)}, f32[88,128]{1,0:T(8,128)S(1)}, u32[]{:S(2)}, u32[]{:S(2)}) collective-permute-start(f32[88,128]{1,0:T(8,128)S(1)} %add_add_fusion.3), channel_id=1, source_target_pairs={{0,64},{1,65},{2,66},{3,67},{4,68},{5,69},{6,70},{7,71},{8,72},{9,... | collective-permute-start | bytes 135176 | tf_op jit(solution)/shard_map/ppermute | solution.py:43
  85.9 6.1 %collective-permute-done.25 = f32[88,128]{1,0:T(8,128)S(1)} collective-permute-done((f32[88,128]{1,0:T(8,128)S(1)}, f32[88,128]{1,0:T(8,128)S(1)}, u32[]{:S(2)}, u32[]{:S(2)}) %collective-permute-start.25) | collective-permute-done | bytes 45088 | tf_op jit(solution)/shard_map/ppermute | solution.py:43
  92.5 4.2 %collective-permute-start.28 = (f32[88,128]{1,0:T(8,128)S(1)}, f32[88,128]{1,0:T(8,128)S(1)}, u32[]{:S(2)}, u32[]{:S(2)}) collective-permute-start(f32[88,128]{1,0:T(8,128)S(1)} %add_add_fusion.2), channel_id=1, source_target_pairs={{0,1},{1,0},{2,3},{3,2},{4,5},{5,4},{6,7},{7,6},{8,9},{9,8},{10,11... | collective-permute-start | bytes 135176 | tf_op jit(solution)/shard_map/ppermute | solution.py:43
  96.6 4.9 %collective-permute-start.37 = (bf16[8,64,128]{2,1,0:T(8,128)(2,1)S(1)}, bf16[8,64,128]{2,1,0:T(8,128)(2,1)S(1)}, u32[]{:S(2)}, u32[]{:S(2)}) collective-permute-start(bf16[8,64,128]{2,1,0:T(8,128)(2,1)S(1)} %get-tuple-element.56), channel_id=1, source_target_pairs={{8,16},{16,8},{24,32},{32,24},{40,48},{48,40},{56,64},{64,56},{72,... | collective-permute-start | bytes 393224 | tf_op jit(solution)/shard_map/ppermute | solution.py:50
  101.6 1.4 %collective-permute-start.32 = (f32[88,128]{1,0:T(8,128)S(1)}, f32[88,128]{1,0:T(8,128)S(1)}, u32[]{:S(2)}, u32[]{:S(2)}) collective-permute-start(f32[88,128]{1,0:T(8,128)S(1)} %add_add_fusion.1), channel_id=1, source_target_pairs={{0,6},{1,7},{2,4},{3,5},{4,2},{5,3},{6,0},{7,1},{8,14},{9,15},{10,... | collective-permute-start | bytes 135176 | tf_op jit(solution)/shard_map/ppermute | solution.py:43
  103.1 1.2 collective-permute-start.31
  104.2 1.6 %collective-permute-start.30 = (f32[88,128]{1,0:T(8,128)S(1)}, f32[88,128]{1,0:T(8,128)S(1)}, u32[]{:S(2)}, u32[]{:S(2)}) collective-permute-start(f32[88,128]{1,0:T(8,128)S(1)} %add_add_fusion.1), channel_id=1, source_target_pairs={{0,2},{1,3},{2,0},{3,1},{4,6},{5,7},{6,4},{7,5},{8,10},{9,11},{10,... | collective-permute-start | bytes 135176 | tf_op jit(solution)/shard_map/ppermute | solution.py:43
  105.8 0.5 shard_map.106
  106.3 1.5 %collective-permute-start.38 = (bf16[3,64,128]{2,1,0:T(8,128)(2,1)S(1)}, bf16[3,64,128]{2,1,0:T(8,128)(2,1)S(1)}, u32[]{:S(2)}, u32[]{:S(2)}) collective-permute-start(bf16[3,64,128]{2,1,0:T(8,128)(2,1)S(1)} %get-tuple-element.57), channel_id=1, source_target_pairs={{0,1},{1,0},{2,3},{3,2},{4,5},{5,4},{6,7},{7,6},{8,9},{9,8},{10,11... | collective-permute-start | bytes 147464 | tf_op jit(solution)/shard_map/ppermute | solution.py:50
  107.8 3.9 %collective-permute-start.39 = (bf16[3,64,128]{2,1,0:T(8,128)(2,1)S(1)}, bf16[3,64,128]{2,1,0:T(8,128)(2,1)S(1)}, u32[]{:S(2)}, u32[]{:S(2)}) collective-permute-start(bf16[3,64,128]{2,1,0:T(8,128)(2,1)S(1)} %get-tuple-element.58), channel_id=1, source_target_pairs={{1,2},{2,1},{3,4},{4,3},{5,6},{6,5},{9,10},{10,9},{11,12},{12,11},... | collective-permute-start | bytes 147464 | tf_op jit(solution)/shard_map/ppermute | solution.py:50
  112.0 1.7 %collective-permute-start.33 = (f32[88,128]{1,0:T(8,128)S(1)}, f32[88,128]{1,0:T(8,128)S(1)}, u32[]{:S(2)}, u32[]{:S(2)}) collective-permute-start(f32[88,128]{1,0:T(8,128)S(1)} %add_add_fusion.got0), channel_id=1, source_target_pairs={{0,8},{1,9},{2,10},{3,11},{4,12},{5,13},{6,14},{7,15},{8,0},{9,1},... | collective-permute-start | bytes 135176 | tf_op jit(solution)/shard_map/ppermute | solution.py:43
  113.7 2.4 %collective-permute-done.39.side_other = bf16[3,64,128]{2,1,0:T(8,128)(2,1)S(1)} collective-permute-done((bf16[3,64,128]{2,1,0:T(8,128)(2,1)S(1)}, bf16[3,64,128]{2,1,0:T(8,128)(2,1)S(1)}, u32[]{:S(2)}, u32[]{:S(2)}) %collective-permute-start.39) | collective-permute-done | bytes 49184 | tf_op jit(solution)/shard_map/ppermute | solution.py:50
  116.1 2.4 %shard_map.107 = bf16[32,64,128]{2,1,0:T(8,128)(2,1)} custom-call(s32[1]{0:T(128)} %bitcast.place, f32[8,128]{1,0:T(8,128)S(1)} %add_add_fusion.4.count, bf16[32,64,128]{2,1,0:T(8,128)(2,1)S(1)} %get-tuple-element.54.own.low, bf16[8,64,128]{2,1,0:T(8,128)(2,1)S(1)} %collective-permute-done.36.mate, bf16[8,64,128]{2,1,0:T(8,128)(2,1)S(1)} %collective-permute-done.37.other, ...), custom_call_target="tpu_custom_call" | custom-call | bytes 14400000 | tf_op jit(solution)/shard_map/pallas_call | solution.py:19
  118.5 0.8 shard_map.105
  (61 shorter events, 1.6 us)
Async XLA Ops:
  0.6 60.1 %copy-start.5 = (f32[37]{0:T(128)S(1)}, f32[37]{0:T(128)}, u32[]{:S(2)}) copy-start(f32[37]{0:T(128)} %param.9) | copy-start | bytes 448
  0.6 60.1 %copy-start.4 = (bf16[64,37]{0,1:T(8,128)(2,1)S(1)}, bf16[64,37]{0,1:T(8,128)(2,1)}, u32[]{:S(2)}) copy-start(bf16[64,37]{0,1:T(8,128)(2,1)} %param.8) | copy-start | bytes 14212
  0.7 1.0 copy-start.1
  1.7 0.7 copy-start.3
  3.1 14.6 %collective-permute-start.2 = (f32[8,128]{1,0:T(8,128)S(1)}, f32[8,128]{1,0:T(8,128)S(1)}, u32[]{:S(2)}, u32[]{:S(2)}) collective-permute-start(f32[8,128]{1,0:T(8,128)S(1)} %get-tuple-element.34), channel_id=1, source_target_pairs={{0,96},{1,97},{2,98},{3,99},{4,100},{5,101},{6,102},{7,103},{8,104... | collective-permute-start | bytes 12296 | tf_op jit(solution)/shard_map/ppermute | solution.py:43
  9.5 8.3 %collective-permute-start.1 = (f32[8,128]{1,0:T(8,128)S(1)}, f32[8,128]{1,0:T(8,128)S(1)}, u32[]{:S(2)}, u32[]{:S(2)}) collective-permute-start(f32[8,128]{1,0:T(8,128)S(1)} %get-tuple-element.34), channel_id=1, source_target_pairs={{0,64},{1,65},{2,66},{3,67},{4,68},{5,69},{6,70},{7,71},{8,72},{9,... | collective-permute-start | bytes 12296 | tf_op jit(solution)/shard_map/ppermute | solution.py:43
  10.5 7.3 %collective-permute-start = (f32[8,128]{1,0:T(8,128)S(1)}, f32[8,128]{1,0:T(8,128)S(1)}, u32[]{:S(2)}, u32[]{:S(2)}) collective-permute-start(f32[8,128]{1,0:T(8,128)S(1)} %get-tuple-element.34), channel_id=1, source_target_pairs={{0,32},{1,33},{2,34},{3,35},{4,36},{5,37},{6,38},{7,39},{8,40},{9,... | collective-permute-start | bytes 12296 | tf_op jit(solution)/shard_map/ppermute | solution.py:43
  11.9 10.0 %collective-permute-start.6 = (bf16[8,64,128]{2,1,0:T(8,128)(2,1)S(1)}, bf16[8,64,128]{2,1,0:T(8,128)(2,1)S(1)}, u32[]{:S(2)}, u32[]{:S(2)}) collective-permute-start(bf16[8,64,128]{2,1,0:T(8,128)(2,1)S(1)} %get-tuple-element.37), channel_id=1, source_target_pairs={{0,8},{8,0},{16,24},{24,16},{32,40},{40,32},{48,56},{56,48},{64,72... | collective-permute-start | bytes 393224 | tf_op jit(solution)/shard_map/ppermute | solution.py:50
  11.9 10.0 %collective-permute-start.7 = (bf16[8,64,128]{2,1,0:T(8,128)(2,1)S(1)}, bf16[8,64,128]{2,1,0:T(8,128)(2,1)S(1)}, u32[]{:S(2)}, u32[]{:S(2)}) collective-permute-start(bf16[8,64,128]{2,1,0:T(8,128)(2,1)S(1)} %get-tuple-element.38), channel_id=1, source_target_pairs={{8,16},{16,8},{24,32},{32,24},{40,48},{48,40},{56,64},{64,56},{72,... | collective-permute-start | bytes 393224 | tf_op jit(solution)/shard_map/ppermute | solution.py:50
  17.8 11.1 %collective-permute-start.5 = (f32[8,128]{1,0:T(8,128)S(1)}, f32[8,128]{1,0:T(8,128)S(1)}, u32[]{:S(2)}, u32[]{:S(2)}) collective-permute-start(f32[8,128]{1,0:T(8,128)S(1)} %add_add_fusion.7), channel_id=1, source_target_pairs={{0,129},{1,128},{2,131},{3,130},{4,133},{5,132},{6,135},{7,134},{8... | collective-permute-start | bytes 12296 | tf_op jit(solution)/shard_map/ppermute | solution.py:43
  17.9 11.0 %collective-permute-start.4 = (f32[8,128]{1,0:T(8,128)S(1)}, f32[8,128]{1,0:T(8,128)S(1)}, u32[]{:S(2)}, u32[]{:S(2)}) collective-permute-start(f32[8,128]{1,0:T(8,128)S(1)} %add_add_fusion.7), channel_id=1, source_target_pairs={{0,1},{1,0},{2,3},{3,2},{4,5},{5,4},{6,7},{7,6},{8,9},{9,8},{10,11... | collective-permute-start | bytes 12296 | tf_op jit(solution)/shard_map/ppermute | solution.py:43
  19.9 9.0 %collective-permute-start.3 = (f32[8,128]{1,0:T(8,128)S(1)}, f32[8,128]{1,0:T(8,128)S(1)}, u32[]{:S(2)}, u32[]{:S(2)}) collective-permute-start(f32[8,128]{1,0:T(8,128)S(1)} %add_add_fusion.7), channel_id=1, source_target_pairs={{0,128},{1,129},{2,130},{3,131},{4,132},{5,133},{6,134},{7,135},{8... | collective-permute-start | bytes 12296 | tf_op jit(solution)/shard_map/ppermute | solution.py:43
  22.5 6.5 %collective-permute-start.8 = (bf16[3,64,128]{2,1,0:T(8,128)(2,1)S(1)}, bf16[3,64,128]{2,1,0:T(8,128)(2,1)S(1)}, u32[]{:S(2)}, u32[]{:S(2)}) collective-permute-start(bf16[3,64,128]{2,1,0:T(8,128)(2,1)S(1)} %get-tuple-element.39), channel_id=1, source_target_pairs={{0,1},{1,0},{2,3},{3,2},{4,5},{5,4},{6,7},{7,6},{8,9},{9,8},{10,11... | collective-permute-start | bytes 147464 | tf_op jit(solution)/shard_map/ppermute | solution.py:50
  23.5 8.4 %collective-permute-start.9 = (bf16[3,64,128]{2,1,0:T(8,128)(2,1)S(1)}, bf16[3,64,128]{2,1,0:T(8,128)(2,1)S(1)}, u32[]{:S(2)}, u32[]{:S(2)}) collective-permute-start(bf16[3,64,128]{2,1,0:T(8,128)(2,1)S(1)} %get-tuple-element.40), channel_id=1, source_target_pairs={{1,2},{2,1},{3,4},{4,3},{5,6},{6,5},{9,10},{10,9},{11,12},{12,11},... | collective-permute-start | bytes 147464 | tf_op jit(solution)/shard_map/ppermute | solution.py:50
  31.9 0.9 copy-start
  32.8 0.7 copy-start.2
  36.0 6.8 %collective-permute-start.10 = (bf16[1056,128]{1,0:T(8,128)(2,1)S(1)}, bf16[1056,128]{1,0:T(8,128)(2,1)S(1)}, u32[]{:S(2)}, u32[]{:S(2)}) collective-permute-start(bf16[1056,128]{1,0:T(8,128)(2,1)S(1)} %get-tuple-element.43), channel_id=1, source_target_pairs={{0,2},{1,3},{2,0},{3,1},{4,6},{5,7},{6,4},{7,5},{8,10},{9,11},{10,... | collective-permute-start | bytes 811016 | tf_op jit(solution)/shard_map/ppermute | solution.py:43
  37.6 19.7 %collective-permute-start.18 = (bf16[1056,128]{1,0:T(8,128)(2,1)S(1)}, bf16[1056,128]{1,0:T(8,128)(2,1)S(1)}, u32[]{:S(2)}, u32[]{:S(2)}) collective-permute-start(bf16[1056,128]{1,0:T(8,128)(2,1)S(1)} %get-tuple-element.46), channel_id=1, source_target_pairs={{0,16},{1,48},{2,80},{3,112},{4,144},{5,176},{6,208},{7,240},{8,24... | collective-permute-start | bytes 811016 | tf_op jit(solution)/shard_map/ppermute | solution.py:43
  42.9 16.4 %collective-permute-start.17 = (bf16[1056,128]{1,0:T(8,128)(2,1)S(1)}, bf16[1056,128]{1,0:T(8,128)(2,1)S(1)}, u32[]{:S(2)}, u32[]{:S(2)}) collective-permute-start(bf16[1056,128]{1,0:T(8,128)(2,1)S(1)} %collective-permute-done.10), channel_id=1, source_target_pairs={{0,64},{1,96},{2,0},{3,32},{4,192},{5,224},{6,128},{7,160},{8,72},... | collective-permute-start | bytes 811016 | tf_op jit(solution)/shard_map/ppermute | solution.py:43
  48.3 4.8 %collective-permute-start.13 = (f32[8,128]{1,0:T(8,128)S(1)}, f32[8,128]{1,0:T(8,128)S(1)}, u32[]{:S(2)}, u32[]{:S(2)}) collective-permute-start(f32[8,128]{1,0:T(8,128)S(1)} %add_add_fusion.6), channel_id=1, source_target_pairs={{0,6},{1,7},{2,4},{3,5},{4,2},{5,3},{6,0},{7,1},{8,14},{9,15},{10,... | collective-permute-start | bytes 12296 | tf_op jit(solution)/shard_map/ppermute | solution.py:43
  48.4 5.1 %collective-permute-start.12 = (f32[8,128]{1,0:T(8,128)S(1)}, f32[8,128]{1,0:T(8,128)S(1)}, u32[]{:S(2)}, u32[]{:S(2)}) collective-permute-start(f32[8,128]{1,0:T(8,128)S(1)} %add_add_fusion.6), channel_id=1, source_target_pairs={{0,4},{1,5},{2,6},{3,7},{4,0},{5,1},{6,2},{7,3},{8,12},{9,13},{10,... | collective-permute-start | bytes 12296 | tf_op jit(solution)/shard_map/ppermute | solution.py:43
  49.8 4.3 %collective-permute-start.11 = (f32[8,128]{1,0:T(8,128)S(1)}, f32[8,128]{1,0:T(8,128)S(1)}, u32[]{:S(2)}, u32[]{:S(2)}) collective-permute-start(f32[8,128]{1,0:T(8,128)S(1)} %add_add_fusion.6), channel_id=1, source_target_pairs={{0,2},{1,3},{2,0},{3,1},{4,6},{5,7},{6,4},{7,5},{8,10},{9,11},{10,... | collective-permute-start | bytes 12296 | tf_op jit(solution)/shard_map/ppermute | solution.py:43
  54.1 5.4 %collective-permute-start.16 = (f32[8,128]{1,0:T(8,128)S(1)}, f32[8,128]{1,0:T(8,128)S(1)}, u32[]{:S(2)}, u32[]{:S(2)}) collective-permute-start(f32[8,128]{1,0:T(8,128)S(1)} %add_add_fusion.5), channel_id=1, source_target_pairs={{0,24},{1,25},{2,26},{3,27},{4,28},{5,29},{6,30},{7,31},{8,16},{9,... | collective-permute-start | bytes 12296 | tf_op jit(solution)/shard_map/ppermute | solution.py:43
  54.7 4.7 %collective-permute-start.15 = (f32[8,128]{1,0:T(8,128)S(1)}, f32[8,128]{1,0:T(8,128)S(1)}, u32[]{:S(2)}, u32[]{:S(2)}) collective-permute-start(f32[8,128]{1,0:T(8,128)S(1)} %add_add_fusion.5), channel_id=1, source_target_pairs={{0,16},{1,17},{2,18},{3,19},{4,20},{5,21},{6,22},{7,23},{8,24},{9,... | collective-permute-start | bytes 12296 | tf_op jit(solution)/shard_map/ppermute | solution.py:43
  57.3 2.1 %collective-permute-start.14 = (f32[8,128]{1,0:T(8,128)S(1)}, f32[8,128]{1,0:T(8,128)S(1)}, u32[]{:S(2)}, u32[]{:S(2)}) collective-permute-start(f32[8,128]{1,0:T(8,128)S(1)} %add_add_fusion.5), channel_id=1, source_target_pairs={{0,8},{1,9},{2,10},{3,11},{4,12},{5,13},{6,14},{7,15},{8,0},{9,1},... | collective-permute-start | bytes 12296 | tf_op jit(solution)/shard_map/ppermute | solution.py:43
  57.4 2.1 %collective-permute-start.20 = (bf16[528,128]{1,0:T(8,128)(2,1)S(1)}, bf16[528,128]{1,0:T(8,128)(2,1)S(1)}, u32[]{:S(2)}, u32[]{:S(2)}) collective-permute-start(bf16[528,128]{1,0:T(8,128)(2,1)S(1)} %slice.9), channel_id=1, source_target_pairs={{0,8},{1,9},{2,10},{3,11},{4,12},{5,13},{6,14},{7,15},{8,0},{9,1},... | collective-permute-start | bytes 405512 | tf_op jit(solution)/shard_map/ppermute | solution.py:43
  59.3 1.4 %collective-permute-start.19 = (bf16[528,128]{1,0:T(8,128)(2,1)S(1)}, bf16[528,128]{1,0:T(8,128)(2,1)S(1)}, u32[]{:S(2)}, u32[]{:S(2)}) collective-permute-start(bf16[528,128]{1,0:T(8,128)(2,1)S(1)} %slice.8), channel_id=1, source_target_pairs={{0,8},{1,9},{2,10},{3,11},{4,12},{5,13},{6,14},{7,15},{8,0},{9,1},... | collective-permute-start | bytes 405512 | tf_op jit(solution)/shard_map/ppermute | solution.py:43
  65.8 2.0 %collective-permute-start.21 = (f32[88,128]{1,0:T(8,128)S(1)}, f32[88,128]{1,0:T(8,128)S(1)}, u32[]{:S(2)}, u32[]{:S(2)}) collective-permute-start(f32[88,128]{1,0:T(8,128)S(1)} %get-tuple-element.50), channel_id=1, source_target_pairs={{0,8},{1,9},{2,10},{3,11},{4,12},{5,13},{6,14},{7,15},{8,0},{9,1},... | collective-permute-start | bytes 135176 | tf_op jit(solution)/shard_map/ppermute | solution.py:43
  66.1 4.5 %collective-permute-start.22 = (f32[88,128]{1,0:T(8,128)S(1)}, f32[88,128]{1,0:T(8,128)S(1)}, u32[]{:S(2)}, u32[]{:S(2)}) collective-permute-start(f32[88,128]{1,0:T(8,128)S(1)} %get-tuple-element.51), channel_id=1, source_target_pairs={{0,16},{1,17},{2,18},{3,19},{4,20},{5,21},{6,22},{7,23},{8,24},{9,... | collective-permute-start | bytes 135176 | tf_op jit(solution)/shard_map/ppermute | solution.py:43
  66.6 4.0 %collective-permute-start.23 = (f32[88,128]{1,0:T(8,128)S(1)}, f32[88,128]{1,0:T(8,128)S(1)}, u32[]{:S(2)}, u32[]{:S(2)}) collective-permute-start(f32[88,128]{1,0:T(8,128)S(1)} %get-tuple-element.52), channel_id=1, source_target_pairs={{0,24},{1,25},{2,26},{3,27},{4,28},{5,29},{6,30},{7,31},{8,16},{9,... | collective-permute-start | bytes 135176 | tf_op jit(solution)/shard_map/ppermute | solution.py:43
  70.6 15.3 %collective-permute-start.26 = (f32[88,128]{1,0:T(8,128)S(1)}, f32[88,128]{1,0:T(8,128)S(1)}, u32[]{:S(2)}, u32[]{:S(2)}) collective-permute-start(f32[88,128]{1,0:T(8,128)S(1)} %add_add_fusion.3), channel_id=1, source_target_pairs={{0,96},{1,97},{2,98},{3,99},{4,100},{5,101},{6,102},{7,103},{8,104... | collective-permute-start | bytes 135176 | tf_op jit(solution)/shard_map/ppermute | solution.py:43
  83.4 8.6 %collective-permute-start.25 = (f32[88,128]{1,0:T(8,128)S(1)}, f32[88,128]{1,0:T(8,128)S(1)}, u32[]{:S(2)}, u32[]{:S(2)}) collective-permute-start(f32[88,128]{1,0:T(8,128)S(1)} %add_add_fusion.3), channel_id=1, source_target_pairs={{0,64},{1,65},{2,66},{3,67},{4,68},{5,69},{6,70},{7,71},{8,72},{9,... | collective-permute-start | bytes 135176 | tf_op jit(solution)/shard_map/ppermute | solution.py:43
  85.7 6.4 %collective-permute-start.24 = (f32[88,128]{1,0:T(8,128)S(1)}, f32[88,128]{1,0:T(8,128)S(1)}, u32[]{:S(2)}, u32[]{:S(2)}) collective-permute-start(f32[88,128]{1,0:T(8,128)S(1)} %add_add_fusion.3), channel_id=1, source_target_pairs={{0,32},{1,33},{2,34},{3,35},{4,36},{5,37},{6,38},{7,39},{8,40},{9,... | collective-permute-start | bytes 135176 | tf_op jit(solution)/shard_map/ppermute | solution.py:43
  92.1 9.5 %collective-permute-start.29 = (f32[88,128]{1,0:T(8,128)S(1)}, f32[88,128]{1,0:T(8,128)S(1)}, u32[]{:S(2)}, u32[]{:S(2)}) collective-permute-start(f32[88,128]{1,0:T(8,128)S(1)} %add_add_fusion.2), channel_id=1, source_target_pairs={{0,129},{1,128},{2,131},{3,130},{4,133},{5,132},{6,135},{7,134},{8... | collective-permute-start | bytes 135176 | tf_op jit(solution)/shard_map/ppermute | solution.py:43
  92.5 9.1 %collective-permute-start.28 = (f32[88,128]{1,0:T(8,128)S(1)}, f32[88,128]{1,0:T(8,128)S(1)}, u32[]{:S(2)}, u32[]{:S(2)}) collective-permute-start(f32[88,128]{1,0:T(8,128)S(1)} %add_add_fusion.2), channel_id=1, source_target_pairs={{0,1},{1,0},{2,3},{3,2},{4,5},{5,4},{6,7},{7,6},{8,9},{9,8},{10,11... | collective-permute-start | bytes 135176 | tf_op jit(solution)/shard_map/ppermute | solution.py:43
  96.6 5.0 %collective-permute-start.27 = (f32[88,128]{1,0:T(8,128)S(1)}, f32[88,128]{1,0:T(8,128)S(1)}, u32[]{:S(2)}, u32[]{:S(2)}) collective-permute-start(f32[88,128]{1,0:T(8,128)S(1)} %add_add_fusion.2), channel_id=1, source_target_pairs={{0,128},{1,129},{2,130},{3,131},{4,132},{5,133},{6,134},{7,135},{8... | collective-permute-start | bytes 135176 | tf_op jit(solution)/shard_map/ppermute | solution.py:43
  96.6 9.2 %collective-permute-start.36 = (bf16[8,64,128]{2,1,0:T(8,128)(2,1)S(1)}, bf16[8,64,128]{2,1,0:T(8,128)(2,1)S(1)}, u32[]{:S(2)}, u32[]{:S(2)}) collective-permute-start(bf16[8,64,128]{2,1,0:T(8,128)(2,1)S(1)} %get-tuple-element.55), channel_id=1, source_target_pairs={{0,8},{8,0},{16,24},{24,16},{32,40},{40,32},{48,56},{56,48},{64,72... | collective-permute-start | bytes 393224 | tf_op jit(solution)/shard_map/ppermute | solution.py:50
  96.6 9.2 %collective-permute-start.37 = (bf16[8,64,128]{2,1,0:T(8,128)(2,1)S(1)}, bf16[8,64,128]{2,1,0:T(8,128)(2,1)S(1)}, u32[]{:S(2)}, u32[]{:S(2)}) collective-permute-start(bf16[8,64,128]{2,1,0:T(8,128)(2,1)S(1)} %get-tuple-element.56), channel_id=1, source_target_pairs={{8,16},{16,8},{24,32},{32,24},{40,48},{48,40},{56,64},{64,56},{72,... | collective-permute-start | bytes 393224 | tf_op jit(solution)/shard_map/ppermute | solution.py:50
  101.6 10.1 %collective-permute-start.32 = (f32[88,128]{1,0:T(8,128)S(1)}, f32[88,128]{1,0:T(8,128)S(1)}, u32[]{:S(2)}, u32[]{:S(2)}) collective-permute-start(f32[88,128]{1,0:T(8,128)S(1)} %add_add_fusion.1), channel_id=1, source_target_pairs={{0,6},{1,7},{2,4},{3,5},{4,2},{5,3},{6,0},{7,1},{8,14},{9,15},{10,... | collective-permute-start | bytes 135176 | tf_op jit(solution)/shard_map/ppermute | solution.py:43
  103.1 8.7 %collective-permute-start.31 = (f32[88,128]{1,0:T(8,128)S(1)}, f32[88,128]{1,0:T(8,128)S(1)}, u32[]{:S(2)}, u32[]{:S(2)}) collective-permute-start(f32[88,128]{1,0:T(8,128)S(1)} %add_add_fusion.1), channel_id=1, source_target_pairs={{0,4},{1,5},{2,6},{3,7},{4,0},{5,1},{6,2},{7,3},{8,12},{9,13},{10,... | collective-permute-start | bytes 135176 | tf_op jit(solution)/shard_map/ppermute | solution.py:43
  104.2 7.5 %collective-permute-start.30 = (f32[88,128]{1,0:T(8,128)S(1)}, f32[88,128]{1,0:T(8,128)S(1)}, u32[]{:S(2)}, u32[]{:S(2)}) collective-permute-start(f32[88,128]{1,0:T(8,128)S(1)} %add_add_fusion.1), channel_id=1, source_target_pairs={{0,2},{1,3},{2,0},{3,1},{4,6},{5,7},{6,4},{7,5},{8,10},{9,11},{10,... | collective-permute-start | bytes 135176 | tf_op jit(solution)/shard_map/ppermute | solution.py:43
  106.3 7.4 %collective-permute-start.38 = (bf16[3,64,128]{2,1,0:T(8,128)(2,1)S(1)}, bf16[3,64,128]{2,1,0:T(8,128)(2,1)S(1)}, u32[]{:S(2)}, u32[]{:S(2)}) collective-permute-start(bf16[3,64,128]{2,1,0:T(8,128)(2,1)S(1)} %get-tuple-element.57), channel_id=1, source_target_pairs={{0,1},{1,0},{2,3},{3,2},{4,5},{5,4},{6,7},{7,6},{8,9},{9,8},{10,11... | collective-permute-start | bytes 147464 | tf_op jit(solution)/shard_map/ppermute | solution.py:50
  107.8 8.4 %collective-permute-start.39 = (bf16[3,64,128]{2,1,0:T(8,128)(2,1)S(1)}, bf16[3,64,128]{2,1,0:T(8,128)(2,1)S(1)}, u32[]{:S(2)}, u32[]{:S(2)}) collective-permute-start(bf16[3,64,128]{2,1,0:T(8,128)(2,1)S(1)} %get-tuple-element.58), channel_id=1, source_target_pairs={{1,2},{2,1},{3,4},{4,3},{5,6},{6,5},{9,10},{10,9},{11,12},{12,11},... | collective-permute-start | bytes 147464 | tf_op jit(solution)/shard_map/ppermute | solution.py:50
  111.8 6.8 %collective-permute-start.35 = (f32[88,128]{1,0:T(8,128)S(1)}, f32[88,128]{1,0:T(8,128)S(1)}, u32[]{:S(2)}, u32[]{:S(2)}) collective-permute-start(f32[88,128]{1,0:T(8,128)S(1)} %add_add_fusion.got0), channel_id=1, source_target_pairs={{0,24},{1,25},{2,26},{3,27},{4,28},{5,29},{6,30},{7,31},{8,16},{9,... | collective-permute-start | bytes 135176 | tf_op jit(solution)/shard_map/ppermute | solution.py:43
  111.9 6.7 %collective-permute-start.34 = (f32[88,128]{1,0:T(8,128)S(1)}, f32[88,128]{1,0:T(8,128)S(1)}, u32[]{:S(2)}, u32[]{:S(2)}) collective-permute-start(f32[88,128]{1,0:T(8,128)S(1)} %add_add_fusion.got0), channel_id=1, source_target_pairs={{0,16},{1,17},{2,18},{3,19},{4,20},{5,21},{6,22},{7,23},{8,24},{9,... | collective-permute-start | bytes 135176 | tf_op jit(solution)/shard_map/ppermute | solution.py:43
  112.0 6.6 %collective-permute-start.33 = (f32[88,128]{1,0:T(8,128)S(1)}, f32[88,128]{1,0:T(8,128)S(1)}, u32[]{:S(2)}, u32[]{:S(2)}) collective-permute-start(f32[88,128]{1,0:T(8,128)S(1)} %add_add_fusion.got0), channel_id=1, source_target_pairs={{0,8},{1,9},{2,10},{3,11},{4,12},{5,13},{6,14},{7,15},{8,0},{9,1},... | collective-permute-start | bytes 135176 | tf_op jit(solution)/shard_map/ppermute | solution.py:43

commit v12 on v11

--- a/solution.py
+++ b/solution.py
@@ -412,7 +412,7 @@
         micros=1,
     )
     around = borders(place, act, mate, other)
-    counted = total_small(counted, (1, 2))
+    counted = total_small(counted, (0, 1, 2))
     counted, act = lax.optimization_barrier((counted, act))
     length = (rows + 1) * rows // 2
     wide, mixed, pay_near, pay_far = run(
@@ -426,7 +426,7 @@
     )
     passed, got = mirrored(pay_near, pay_far, parts)
     _, counted = lax.optimization_barrier((passed, counted))
-    count = total_small(counted, (3, 0))
+    count = total_small(counted, (3,))
     half = 9 * chans // 2
     lines = -(-(half + tall + 8) // 32) * 32
     grad, low, mate, other, *quarters = run(

time: 120 us -> 124 us (1.033)
  the two profiles are of different devices: /device:TPU:24 before, /device:TPU:12 now
where the time goes in v12:
time: 124 us
  starting transfers between devices  75.4 us (61%)
  waiting for transfers between devices  31.4 us (25%)
  Pallas kernels  12.5 us (10%)
  local copies, waits for them, and re-layouts  3.41 us (3%)
    ppermute x32, starting transfers between devices, send(): return lax.ppermute(block, GRID, pairs)  57.3 us
    ppermute x32, waiting for transfers between devices, send(): return lax.ppermute(block, GRID, pairs)  20.7 us
    ppermute x4, starting transfers between devices, swapped(): lax.ppermute(to_other, axis, others)  13.2 us
    pallas_call x7, Pallas kernels, run(): pl.pallas_call(body, out_shape=outs, in_specs=[SMEM] * scalars + [VMEM] *...  12.5 us
    ppermute x4, waiting for transfers between devices, swapped(): lax.ppermute(to_other, axis, others)  10.5 us
    ppermute x4, starting transfers between devices, swapped(): lax.ppermute(to_mate, axis, mates)  4.93 us
    unnamed x12, local copies, waits for them, and re-layouts  3.39 us
  transfers between devices with their start and end apart: 40, of which 12 were waited for; matrix products, arithmetic and copies ran while one was open for 0% of the time, Pallas kernels for 3%

profile of v12, /device:TPU:12, one launch (start us, length us, event | category | flops | bytes accessed | tf_op | source)
XLA Modules:
  0.0 123.8 jit_solution(5076604791075911487)
XLA Ops:
  0.7 1.0 copy-done.1
  1.7 0.7 copy-done.3
  2.4 0.7 shard_map.101
  3.1 1.4 %collective-permute-start.2 = (f32[8,128]{1,0:T(8,128)S(1)}, f32[8,128]{1,0:T(8,128)S(1)}, u32[]{:S(2)}, u32[]{:S(2)}) collective-permute-start(f32[8,128]{1,0:T(8,128)S(1)} %get-tuple-element.34), channel_id=1, source_target_pairs={{0,24},{1,25},{2,26},{3,27},{4,28},{5,29},{6,30},{7,31},{8,16},{9,... | collective-permute-start | bytes 12296 | tf_op jit(solution)/shard_map/ppermute | solution.py:43
  4.5 0.7 collective-permute-start.1
  5.2 1.0 collective-permute-done.2
  6.2 1.9 %collective-permute-done.1 = f32[8,128]{1,0:T(8,128)S(1)} collective-permute-done((f32[8,128]{1,0:T(8,128)S(1)}, f32[8,128]{1,0:T(8,128)S(1)}, u32[]{:S(2)}, u32[]{:S(2)}) %collective-permute-start.1) | collective-permute-done | bytes 4128 | tf_op jit(solution)/shard_map/ppermute | solution.py:43
  8.1 5.5 %collective-permute-start.5 = (f32[8,128]{1,0:T(8,128)S(1)}, f32[8,128]{1,0:T(8,128)S(1)}, u32[]{:S(2)}, u32[]{:S(2)}) collective-permute-start(f32[8,128]{1,0:T(8,128)S(1)} %add_add_fusion.7), channel_id=1, source_target_pairs={{0,96},{1,97},{2,98},{3,99},{4,100},{5,101},{6,102},{7,103},{8,104... | collective-permute-start | bytes 12296 | tf_op jit(solution)/shard_map/ppermute | solution.py:43
  13.6 1.4 %collective-permute-start.4 = (f32[8,128]{1,0:T(8,128)S(1)}, f32[8,128]{1,0:T(8,128)S(1)}, u32[]{:S(2)}, u32[]{:S(2)}) collective-permute-start(f32[8,128]{1,0:T(8,128)S(1)} %add_add_fusion.7), channel_id=1, source_target_pairs={{0,64},{1,65},{2,66},{3,67},{4,68},{5,69},{6,70},{7,71},{8,72},{9,... | collective-permute-start | bytes 12296 | tf_op jit(solution)/shard_map/ppermute | solution.py:43
  15.1 1.0 collective-permute-start.3
  16.1 5.5 %collective-permute-start.10 = (bf16[8,64,128]{2,1,0:T(8,128)(2,1)S(1)}, bf16[8,64,128]{2,1,0:T(8,128)(2,1)S(1)}, u32[]{:S(2)}, u32[]{:S(2)}) collective-permute-start(bf16[8,64,128]{2,1,0:T(8,128)(2,1)S(1)} %get-tuple-element.38), channel_id=1, source_target_pairs={{8,16},{16,8},{24,32},{32,24},{40,48},{48,40},{56,64},{64,56},{72,... | collective-permute-start | bytes 393224 | tf_op jit(solution)/shard_map/ppermute | solution.py:50
  21.6 1.2 collective-permute-start.8
  22.8 1.6 %collective-permute-start.7 = (f32[8,128]{1,0:T(8,128)S(1)}, f32[8,128]{1,0:T(8,128)S(1)}, u32[]{:S(2)}, u32[]{:S(2)}) collective-permute-start(f32[8,128]{1,0:T(8,128)S(1)} %add_add_fusion.6), channel_id=1, source_target_pairs={{0,1},{1,0},{2,3},{3,2},{4,5},{5,4},{6,7},{7,6},{8,9},{9,8},{10,11... | collective-permute-start | bytes 12296 | tf_op jit(solution)/shard_map/ppermute | solution.py:43
  24.4 1.4 %collective-permute-start.6 = (f32[8,128]{1,0:T(8,128)S(1)}, f32[8,128]{1,0:T(8,128)S(1)}, u32[]{:S(2)}, u32[]{:S(2)}) collective-permute-start(f32[8,128]{1,0:T(8,128)S(1)} %add_add_fusion.6), channel_id=1, source_target_pairs={{0,128},{1,129},{2,130},{3,131},{4,132},{5,133},{6,134},{7,135},{8... | collective-permute-start | bytes 12296 | tf_op jit(solution)/shard_map/ppermute | solution.py:43
  26.3 2.7 %collective-permute-start.11 = (bf16[3,64,128]{2,1,0:T(8,128)(2,1)S(1)}, bf16[3,64,128]{2,1,0:T(8,128)(2,1)S(1)}, u32[]{:S(2)}, u32[]{:S(2)}) collective-permute-start(bf16[3,64,128]{2,1,0:T(8,128)(2,1)S(1)} %get-tuple-element.39), channel_id=1, source_target_pairs={{0,1},{1,0},{2,3},{3,2},{4,5},{5,4},{6,7},{7,6},{8,9},{9,8},{10,11... | collective-permute-start | bytes 147464 | tf_op jit(solution)/shard_map/ppermute | solution.py:50
  29.0 2.8 %collective-permute-start.12 = (bf16[3,64,128]{2,1,0:T(8,128)(2,1)S(1)}, bf16[3,64,128]{2,1,0:T(8,128)(2,1)S(1)}, u32[]{:S(2)}, u32[]{:S(2)}) collective-permute-start(bf16[3,64,128]{2,1,0:T(8,128)(2,1)S(1)} %get-tuple-element.40), channel_id=1, source_target_pairs={{1,2},{2,1},{3,4},{4,3},{5,6},{6,5},{9,10},{10,9},{11,12},{12,11},... | collective-permute-start | bytes 147464 | tf_op jit(solution)/shard_map/ppermute | solution.py:50
  32.0 5.4 %collective-permute-done.12.side_other = bf16[3,64,128]{2,1,0:T(8,128)(2,1)S(1)} collective-permute-done((bf16[3,64,128]{2,1,0:T(8,128)(2,1)S(1)}, bf16[3,64,128]{2,1,0:T(8,128)(2,1)S(1)}, u32[]{:S(2)}, u32[]{:S(2)}) %collective-permute-start.12) | collective-permute-done | bytes 49184 | tf_op jit(solution)/shard_map/ppermute | solution.py:50
  37.4 0.9 copy-done
  38.3 0.7 copy-done.2
  39.0 2.5 %shard_map.103 = (bf16[48,192,128]{2,1,0:T(8,128)(2,1)S(1)}, bf16[32,64,128]{2,1,0:T(8,128)(2,1)S(1)}, bf16[1056,128]{1,0:T(8,128)(2,1)S(1)}, bf16[1056,128]{1,0:T(8,128)(2,1)S(1)}) custom-call(s32[1]{0:T(128)} %bitcast.place, bf16[32,64,128]{2,1,0:T(8,128)(2,1)S(1)} %get-tuple-element.36.own.act, bf16[8,64,128]{2,1,0:T(8,128)(2,1)S(1)} %collective-permute-done.9.mate, ...), custom_call_target="tpu_custom_call" | custom-call | bytes 18000000 | tf_op jit(solution)/shard_map/pallas_call | solution.py:19
  41.5 1.3 %collective-permute-start.13 = (bf16[1056,128]{1,0:T(8,128)(2,1)S(1)}, bf16[1056,128]{1,0:T(8,128)(2,1)S(1)}, u32[]{:S(2)}, u32[]{:S(2)}) collective-permute-start(bf16[1056,128]{1,0:T(8,128)(2,1)S(1)} %get-tuple-element.43), channel_id=1, source_target_pairs={{0,2},{1,3},{2,0},{3,1},{4,6},{5,7},{6,4},{7,5},{8,10},{9,11},{10,... | collective-permute-start | bytes 811016 | tf_op jit(solution)/shard_map/ppermute | solution.py:43
  43.1 7.7 %collective-permute-done.13 = bf16[1056,128]{1,0:T(8,128)(2,1)S(1)} collective-permute-done((bf16[1056,128]{1,0:T(8,128)(2,1)S(1)}, bf16[1056,128]{1,0:T(8,128)(2,1)S(1)}, u32[]{:S(2)}, u32[]{:S(2)}) %collective-permute-start.13) | collective-permute-done | bytes 270368 | tf_op jit(solution)/shard_map/ppermute | solution.py:43
  50.8 6.9 %collective-permute-start.17 = (bf16[1056,128]{1,0:T(8,128)(2,1)S(1)}, bf16[1056,128]{1,0:T(8,128)(2,1)S(1)}, u32[]{:S(2)}, u32[]{:S(2)}) collective-permute-start(bf16[1056,128]{1,0:T(8,128)(2,1)S(1)} %collective-permute-done.13), channel_id=1, source_target_pairs={{0,64},{1,96},{2,0},{3,32},{4,192},{5,224},{6,128},{7,160},{8,72},... | collective-permute-start | bytes 811016 | tf_op jit(solution)/shard_map/ppermute | solution.py:43
  57.6 8.4 %collective-permute-start.15 = (f32[8,128]{1,0:T(8,128)S(1)}, f32[8,128]{1,0:T(8,128)S(1)}, u32[]{:S(2)}, u32[]{:S(2)}) collective-permute-start(f32[8,128]{1,0:T(8,128)S(1)} %add_add_fusion.5), channel_id=1, source_target_pairs={{0,4},{1,5},{2,6},{3,7},{4,0},{5,1},{6,2},{7,3},{8,12},{9,13},{10,... | collective-permute-start | bytes 12296 | tf_op jit(solution)/shard_map/ppermute | solution.py:43
  66.0 1.2 collective-permute-start.14
  67.5 0.6 collective-permute-start.19
  68.0 1.6 %collective-permute-done.16 = f32[8,128]{1,0:T(8,128)S(1)} collective-permute-done((f32[8,128]{1,0:T(8,128)S(1)}, f32[8,128]{1,0:T(8,128)S(1)}, u32[]{:S(2)}, u32[]{:S(2)}) %collective-permute-start.16) | collective-permute-done | bytes 4128 | tf_op jit(solution)/shard_map/ppermute | solution.py:43
  69.7 5.1 %shard_map.104 = (f32[32,64,128]{2,1,0:T(8,128)S(1)}, bf16[32,64,128]{2,1,0:T(8,128)(2,1)S(1)}, bf16[8,64,128]{2,1,0:T(8,128)(2,1)S(1)}, bf16[8,64,128]{2,1,0:T(...) custom-call(s32[1]{0:T(128)} %bitcast.place, ...), custom_call_target="tpu_custom_call" | custom-call | bytes 21600000 | tf_op jit(solution)/shard_map/pallas_call | solution.py:19
  75.0 1.8 %collective-permute-start.23 = (f32[88,128]{1,0:T(8,128)S(1)}, f32[88,128]{1,0:T(8,128)S(1)}, u32[]{:S(2)}, u32[]{:S(2)}) collective-permute-start(f32[88,128]{1,0:T(8,128)S(1)} %get-tuple-element.52), channel_id=1, source_target_pairs={{0,24},{1,25},{2,26},{3,27},{4,28},{5,29},{6,30},{7,31},{8,16},{9,... | collective-permute-start | bytes 135176 | tf_op jit(solution)/shard_map/ppermute | solution.py:43
  76.7 2.7 %collective-permute-done.22 = f32[88,128]{1,0:T(8,128)S(1)} collective-permute-done((f32[88,128]{1,0:T(8,128)S(1)}, f32[88,128]{1,0:T(8,128)S(1)}, u32[]{:S(2)}, u32[]{:S(2)}) %collective-permute-start.22) | collective-permute-done | bytes 45088 | tf_op jit(solution)/shard_map/ppermute | solution.py:43
  79.4 1.4 %collective-permute-start.26 = (f32[88,128]{1,0:T(8,128)S(1)}, f32[88,128]{1,0:T(8,128)S(1)}, u32[]{:S(2)}, u32[]{:S(2)}) collective-permute-start(f32[88,128]{1,0:T(8,128)S(1)} %add_add_fusion.3), channel_id=1, source_target_pairs={{0,96},{1,97},{2,98},{3,99},{4,100},{5,101},{6,102},{7,103},{8,104... | collective-permute-start | bytes 135176 | tf_op jit(solution)/shard_map/ppermute | solution.py:43
  80.9 4.5 %collective-permute-start.25 = (f32[88,128]{1,0:T(8,128)S(1)}, f32[88,128]{1,0:T(8,128)S(1)}, u32[]{:S(2)}, u32[]{:S(2)}) collective-permute-start(f32[88,128]{1,0:T(8,128)S(1)} %add_add_fusion.3), channel_id=1, source_target_pairs={{0,64},{1,65},{2,66},{3,67},{4,68},{5,69},{6,70},{7,71},{8,72},{9,... | collective-permute-start | bytes 135176 | tf_op jit(solution)/shard_map/ppermute | solution.py:43
  85.4 0.6 collective-permute-start.24
  86.0 3.2 %collective-permute-done.25 = f32[88,128]{1,0:T(8,128)S(1)} collective-permute-done((f32[88,128]{1,0:T(8,128)S(1)}, f32[88,128]{1,0:T(8,128)S(1)}, u32[]{:S(2)}, u32[]{:S(2)}) %collective-permute-start.25) | collective-permute-done | bytes 45088 | tf_op jit(solution)/shard_map/ppermute | solution.py:43
  89.2 2.1 %collective-permute-done.24 = f32[88,128]{1,0:T(8,128)S(1)} collective-permute-done((f32[88,128]{1,0:T(8,128)S(1)}, f32[88,128]{1,0:T(8,128)S(1)}, u32[]{:S(2)}, u32[]{:S(2)}) %collective-permute-start.24) | collective-permute-done | bytes 45088 | tf_op jit(solution)/shard_map/ppermute | solution.py:43
  91.4 7.5 %collective-permute-start.29 = (f32[88,128]{1,0:T(8,128)S(1)}, f32[88,128]{1,0:T(8,128)S(1)}, u32[]{:S(2)}, u32[]{:S(2)}) collective-permute-start(f32[88,128]{1,0:T(8,128)S(1)} %add_add_fusion.2), channel_id=1, source_target_pairs={{0,129},{1,128},{2,131},{3,130},{4,133},{5,132},{6,135},{7,134},{8... | collective-permute-start | bytes 135176 | tf_op jit(solution)/shard_map/ppermute | solution.py:43
  98.9 2.2 %collective-permute-start.27 = (f32[88,128]{1,0:T(8,128)S(1)}, f32[88,128]{1,0:T(8,128)S(1)}, u32[]{:S(2)}, u32[]{:S(2)}) collective-permute-start(f32[88,128]{1,0:T(8,128)S(1)} %add_add_fusion.2), channel_id=1, source_target_pairs={{0,128},{1,129},{2,130},{3,131},{4,132},{5,133},{6,134},{7,135},{8... | collective-permute-start | bytes 135176 | tf_op jit(solution)/shard_map/ppermute | solution.py:43
  101.1 2.9 %collective-permute-start.37 = (bf16[8,64,128]{2,1,0:T(8,128)(2,1)S(1)}, bf16[8,64,128]{2,1,0:T(8,128)(2,1)S(1)}, u32[]{:S(2)}, u32[]{:S(2)}) collective-permute-start(bf16[8,64,128]{2,1,0:T(8,128)(2,1)S(1)} %get-tuple-element.56), channel_id=1, source_target_pairs={{8,16},{16,8},{24,32},{32,24},{40,48},{48,40},{56,64},{64,56},{72,... | collective-permute-start | bytes 393224 | tf_op jit(solution)/shard_map/ppermute | solution.py:50
  104.6 1.1 collective-permute-start.31
  105.6 3.0 %collective-permute-start.30 = (f32[88,128]{1,0:T(8,128)S(1)}, f32[88,128]{1,0:T(8,128)S(1)}, u32[]{:S(2)}, u32[]{:S(2)}) collective-permute-start(f32[88,128]{1,0:T(8,128)S(1)} %add_add_fusion.1), channel_id=1, source_target_pairs={{0,2},{1,3},{2,0},{3,1},{4,6},{5,7},{6,4},{7,5},{8,10},{9,11},{10,... | collective-permute-start | bytes 135176 | tf_op jit(solution)/shard_map/ppermute | solution.py:43
  108.7 0.8 collective-permute-done.37.other
  110.0 2.2 %collective-permute-start.38 = (bf16[3,64,128]{2,1,0:T(8,128)(2,1)S(1)}, bf16[3,64,128]{2,1,0:T(8,128)(2,1)S(1)}, u32[]{:S(2)}, u32[]{:S(2)}) collective-permute-start(bf16[3,64,128]{2,1,0:T(8,128)(2,1)S(1)} %get-tuple-element.57), channel_id=1, source_target_pairs={{0,1},{1,0},{2,3},{3,2},{4,5},{5,4},{6,7},{7,6},{8,9},{9,8},{10,11... | collective-permute-start | bytes 147464 | tf_op jit(solution)/shard_map/ppermute | solution.py:50
  112.2 2.0 %collective-permute-start.39 = (bf16[3,64,128]{2,1,0:T(8,128)(2,1)S(1)}, bf16[3,64,128]{2,1,0:T(8,128)(2,1)S(1)}, u32[]{:S(2)}, u32[]{:S(2)}) collective-permute-start(bf16[3,64,128]{2,1,0:T(8,128)(2,1)S(1)} %get-tuple-element.58), channel_id=1, source_target_pairs={{1,2},{2,1},{3,4},{4,3},{5,6},{6,5},{9,10},{10,9},{11,12},{12,11},... | collective-permute-start | bytes 147464 | tf_op jit(solution)/shard_map/ppermute | solution.py:50
  114.4 0.8 collective-permute-start.34
  115.2 1.1 collective-permute-start.33
  116.2 4.4 %collective-permute-done.39.side_other = bf16[3,64,128]{2,1,0:T(8,128)(2,1)S(1)} collective-permute-done((bf16[3,64,128]{2,1,0:T(8,128)(2,1)S(1)}, bf16[3,64,128]{2,1,0:T(8,128)(2,1)S(1)}, u32[]{:S(2)}, u32[]{:S(2)}) %collective-permute-start.39) | collective-permute-done | bytes 49184 | tf_op jit(solution)/shard_map/ppermute | solution.py:50
  120.6 2.4 %shard_map.107 = bf16[32,64,128]{2,1,0:T(8,128)(2,1)} custom-call(s32[1]{0:T(128)} %bitcast.place, f32[8,128]{1,0:T(8,128)S(1)} %add_add_fusion.4.count, bf16[32,64,128]{2,1,0:T(8,128)(2,1)S(1)} %get-tuple-element.54.own.low, bf16[8,64,128]{2,1,0:T(8,128)(2,1)S(1)} %collective-permute-done.36.mate, bf16[8,64,128]{2,1,0:T(8,128)(2,1)S(1)} %collective-permute-done.37.other, ...), custom_call_target="tpu_custom_call" | custom-call | bytes 14400000 | tf_op jit(solution)/shard_map/pallas_call | solution.py:19
  123.0 0.8 shard_map.105
  (61 shorter events, 2.7 us)
Async XLA Ops:
  0.6 69.0 %copy-start.5 = (f32[37]{0:T(128)S(1)}, f32[37]{0:T(128)}, u32[]{:S(2)}) copy-start(f32[37]{0:T(128)} %param.9) | copy-start | bytes 448
  0.6 69.0 %copy-start.4 = (bf16[64,37]{0,1:T(8,128)(2,1)S(1)}, bf16[64,37]{0,1:T(8,128)(2,1)}, u32[]{:S(2)}) copy-start(bf16[64,37]{0,1:T(8,128)(2,1)} %param.8) | copy-start | bytes 14212
  0.7 1.0 copy-start.1
  1.7 0.7 copy-start.3
  3.1 3.1 %collective-permute-start.2 = (f32[8,128]{1,0:T(8,128)S(1)}, f32[8,128]{1,0:T(8,128)S(1)}, u32[]{:S(2)}, u32[]{:S(2)}) collective-permute-start(f32[8,128]{1,0:T(8,128)S(1)} %get-tuple-element.34), channel_id=1, source_target_pairs={{0,24},{1,25},{2,26},{3,27},{4,28},{5,29},{6,30},{7,31},{8,16},{9,... | collective-permute-start | bytes 12296 | tf_op jit(solution)/shard_map/ppermute | solution.py:43
  4.5 3.6 %collective-permute-start.1 = (f32[8,128]{1,0:T(8,128)S(1)}, f32[8,128]{1,0:T(8,128)S(1)}, u32[]{:S(2)}, u32[]{:S(2)}) collective-permute-start(f32[8,128]{1,0:T(8,128)S(1)} %get-tuple-element.34), channel_id=1, source_target_pairs={{0,16},{1,17},{2,18},{3,19},{4,20},{5,21},{6,22},{7,23},{8,24},{9,... | collective-permute-start | bytes 12296 | tf_op jit(solution)/shard_map/ppermute | solution.py:43
  5.2 2.9 %collective-permute-start = (f32[8,128]{1,0:T(8,128)S(1)}, f32[8,128]{1,0:T(8,128)S(1)}, u32[]{:S(2)}, u32[]{:S(2)}) collective-permute-start(f32[8,128]{1,0:T(8,128)S(1)} %get-tuple-element.34), channel_id=1, source_target_pairs={{0,8},{1,9},{2,10},{3,11},{4,12},{5,13},{6,14},{7,15},{8,0},{9,1},... | collective-permute-start | bytes 12296 | tf_op jit(solution)/shard_map/ppermute | solution.py:43
  8.1 13.4 %collective-permute-start.5 = (f32[8,128]{1,0:T(8,128)S(1)}, f32[8,128]{1,0:T(8,128)S(1)}, u32[]{:S(2)}, u32[]{:S(2)}) collective-permute-start(f32[8,128]{1,0:T(8,128)S(1)} %add_add_fusion.7), channel_id=1, source_target_pairs={{0,96},{1,97},{2,98},{3,99},{4,100},{5,101},{6,102},{7,103},{8,104... | collective-permute-start | bytes 12296 | tf_op jit(solution)/shard_map/ppermute | solution.py:43
  13.6 8.0 %collective-permute-start.4 = (f32[8,128]{1,0:T(8,128)S(1)}, f32[8,128]{1,0:T(8,128)S(1)}, u32[]{:S(2)}, u32[]{:S(2)}) collective-permute-start(f32[8,128]{1,0:T(8,128)S(1)} %add_add_fusion.7), channel_id=1, source_target_pairs={{0,64},{1,65},{2,66},{3,67},{4,68},{5,69},{6,70},{7,71},{8,72},{9,... | collective-permute-start | bytes 12296 | tf_op jit(solution)/shard_map/ppermute | solution.py:43
  15.1 6.5 %collective-permute-start.3 = (f32[8,128]{1,0:T(8,128)S(1)}, f32[8,128]{1,0:T(8,128)S(1)}, u32[]{:S(2)}, u32[]{:S(2)}) collective-permute-start(f32[8,128]{1,0:T(8,128)S(1)} %add_add_fusion.7), channel_id=1, source_target_pairs={{0,32},{1,33},{2,34},{3,35},{4,36},{5,37},{6,38},{7,39},{8,40},{9,... | collective-permute-start | bytes 12296 | tf_op jit(solution)/shard_map/ppermute | solution.py:43
  16.1 9.7 %collective-permute-start.9 = (bf16[8,64,128]{2,1,0:T(8,128)(2,1)S(1)}, bf16[8,64,128]{2,1,0:T(8,128)(2,1)S(1)}, u32[]{:S(2)}, u32[]{:S(2)}) collective-permute-start(bf16[8,64,128]{2,1,0:T(8,128)(2,1)S(1)} %get-tuple-element.37), channel_id=1, source_target_pairs={{0,8},{8,0},{16,24},{24,16},{32,40},{40,32},{48,56},{56,48},{64,72... | collective-permute-start | bytes 393224 | tf_op jit(solution)/shard_map/ppermute | solution.py:50
  16.1 9.7 %collective-permute-start.10 = (bf16[8,64,128]{2,1,0:T(8,128)(2,1)S(1)}, bf16[8,64,128]{2,1,0:T(8,128)(2,1)S(1)}, u32[]{:S(2)}, u32[]{:S(2)}) collective-permute-start(bf16[8,64,128]{2,1,0:T(8,128)(2,1)S(1)} %get-tuple-element.38), channel_id=1, source_target_pairs={{8,16},{16,8},{24,32},{32,24},{40,48},{48,40},{56,64},{64,56},{72,... | collective-permute-start | bytes 393224 | tf_op jit(solution)/shard_map/ppermute | solution.py:50
  21.6 10.2 %collective-permute-start.8 = (f32[8,128]{1,0:T(8,128)S(1)}, f32[8,128]{1,0:T(8,128)S(1)}, u32[]{:S(2)}, u32[]{:S(2)}) collective-permute-start(f32[8,128]{1,0:T(8,128)S(1)} %add_add_fusion.6), channel_id=1, source_target_pairs={{0,129},{1,128},{2,131},{3,130},{4,133},{5,132},{6,135},{7,134},{8... | collective-permute-start | bytes 12296 | tf_op jit(solution)/shard_map/ppermute | solution.py:43
  22.8 9.0 %collective-permute-start.7 = (f32[8,128]{1,0:T(8,128)S(1)}, f32[8,128]{1,0:T(8,128)S(1)}, u32[]{:S(2)}, u32[]{:S(2)}) collective-permute-start(f32[8,128]{1,0:T(8,128)S(1)} %add_add_fusion.6), channel_id=1, source_target_pairs={{0,1},{1,0},{2,3},{3,2},{4,5},{5,4},{6,7},{7,6},{8,9},{9,8},{10,11... | collective-permute-start | bytes 12296 | tf_op jit(solution)/shard_map/ppermute | solution.py:43
  24.4 7.4 %collective-permute-start.6 = (f32[8,128]{1,0:T(8,128)S(1)}, f32[8,128]{1,0:T(8,128)S(1)}, u32[]{:S(2)}, u32[]{:S(2)}) collective-permute-start(f32[8,128]{1,0:T(8,128)S(1)} %add_add_fusion.6), channel_id=1, source_target_pairs={{0,128},{1,129},{2,130},{3,131},{4,132},{5,133},{6,134},{7,135},{8... | collective-permute-start | bytes 12296 | tf_op jit(solution)/shard_map/ppermute | solution.py:43
  26.3 5.7 %collective-permute-start.11 = (bf16[3,64,128]{2,1,0:T(8,128)(2,1)S(1)}, bf16[3,64,128]{2,1,0:T(8,128)(2,1)S(1)}, u32[]{:S(2)}, u32[]{:S(2)}) collective-permute-start(bf16[3,64,128]{2,1,0:T(8,128)(2,1)S(1)} %get-tuple-element.39), channel_id=1, source_target_pairs={{0,1},{1,0},{2,3},{3,2},{4,5},{5,4},{6,7},{7,6},{8,9},{9,8},{10,11... | collective-permute-start | bytes 147464 | tf_op jit(solution)/shard_map/ppermute | solution.py:50
  29.0 8.4 %collective-permute-start.12 = (bf16[3,64,128]{2,1,0:T(8,128)(2,1)S(1)}, bf16[3,64,128]{2,1,0:T(8,128)(2,1)S(1)}, u32[]{:S(2)}, u32[]{:S(2)}) collective-permute-start(bf16[3,64,128]{2,1,0:T(8,128)(2,1)S(1)} %get-tuple-element.40), channel_id=1, source_target_pairs={{1,2},{2,1},{3,4},{4,3},{5,6},{6,5},{9,10},{10,9},{11,12},{12,11},... | collective-permute-start | bytes 147464 | tf_op jit(solution)/shard_map/ppermute | solution.py:50
  37.4 0.9 copy-start
  38.3 0.7 copy-start.2
  41.5 9.2 %collective-permute-start.13 = (bf16[1056,128]{1,0:T(8,128)(2,1)S(1)}, bf16[1056,128]{1,0:T(8,128)(2,1)S(1)}, u32[]{:S(2)}, u32[]{:S(2)}) collective-permute-start(bf16[1056,128]{1,0:T(8,128)(2,1)S(1)} %get-tuple-element.43), channel_id=1, source_target_pairs={{0,2},{1,3},{2,0},{3,1},{4,6},{5,7},{6,4},{7,5},{8,10},{9,11},{10,... | collective-permute-start | bytes 811016 | tf_op jit(solution)/shard_map/ppermute | solution.py:43
  42.8 24.3 %collective-permute-start.18 = (bf16[1056,128]{1,0:T(8,128)(2,1)S(1)}, bf16[1056,128]{1,0:T(8,128)(2,1)S(1)}, u32[]{:S(2)}, u32[]{:S(2)}) collective-permute-start(bf16[1056,128]{1,0:T(8,128)(2,1)S(1)} %get-tuple-element.46), channel_id=1, source_target_pairs={{0,16},{1,48},{2,80},{3,112},{4,144},{5,176},{6,208},{7,240},{8,24... | collective-permute-start | bytes 811016 | tf_op jit(solution)/shard_map/ppermute | solution.py:43
  50.8 16.7 %collective-permute-start.17 = (bf16[1056,128]{1,0:T(8,128)(2,1)S(1)}, bf16[1056,128]{1,0:T(8,128)(2,1)S(1)}, u32[]{:S(2)}, u32[]{:S(2)}) collective-permute-start(bf16[1056,128]{1,0:T(8,128)(2,1)S(1)} %collective-permute-done.13), channel_id=1, source_target_pairs={{0,64},{1,96},{2,0},{3,32},{4,192},{5,224},{6,128},{7,160},{8,72},... | collective-permute-start | bytes 811016 | tf_op jit(solution)/shard_map/ppermute | solution.py:43
  57.6 12.0 %collective-permute-start.16 = (f32[8,128]{1,0:T(8,128)S(1)}, f32[8,128]{1,0:T(8,128)S(1)}, u32[]{:S(2)}, u32[]{:S(2)}) collective-permute-start(f32[8,128]{1,0:T(8,128)S(1)} %add_add_fusion.5), channel_id=1, source_target_pairs={{0,6},{1,7},{2,4},{3,5},{4,2},{5,3},{6,0},{7,1},{8,14},{9,15},{10,... | collective-permute-start | bytes 12296 | tf_op jit(solution)/shard_map/ppermute | solution.py:43
  57.6 12.0 %collective-permute-start.15 = (f32[8,128]{1,0:T(8,128)S(1)}, f32[8,128]{1,0:T(8,128)S(1)}, u32[]{:S(2)}, u32[]{:S(2)}) collective-permute-start(f32[8,128]{1,0:T(8,128)S(1)} %add_add_fusion.5), channel_id=1, source_target_pairs={{0,4},{1,5},{2,6},{3,7},{4,0},{5,1},{6,2},{7,3},{8,12},{9,13},{10,... | collective-permute-start | bytes 12296 | tf_op jit(solution)/shard_map/ppermute | solution.py:43
  66.0 3.7 %collective-permute-start.14 = (f32[8,128]{1,0:T(8,128)S(1)}, f32[8,128]{1,0:T(8,128)S(1)}, u32[]{:S(2)}, u32[]{:S(2)}) collective-permute-start(f32[8,128]{1,0:T(8,128)S(1)} %add_add_fusion.5), channel_id=1, source_target_pairs={{0,2},{1,3},{2,0},{3,1},{4,6},{5,7},{6,4},{7,5},{8,10},{9,11},{10,... | collective-permute-start | bytes 12296 | tf_op jit(solution)/shard_map/ppermute | solution.py:43
  67.2 2.5 %collective-permute-start.20 = (bf16[528,128]{1,0:T(8,128)(2,1)S(1)}, bf16[528,128]{1,0:T(8,128)(2,1)S(1)}, u32[]{:S(2)}, u32[]{:S(2)}) collective-permute-start(bf16[528,128]{1,0:T(8,128)(2,1)S(1)} %slice.9), channel_id=1, source_target_pairs={{0,8},{1,9},{2,10},{3,11},{4,12},{5,13},{6,14},{7,15},{8,0},{9,1},... | collective-permute-start | bytes 405512 | tf_op jit(solution)/shard_map/ppermute | solution.py:43
  67.5 2.2 %collective-permute-start.19 = (bf16[528,128]{1,0:T(8,128)(2,1)S(1)}, bf16[528,128]{1,0:T(8,128)(2,1)S(1)}, u32[]{:S(2)}, u32[]{:S(2)}) collective-permute-start(bf16[528,128]{1,0:T(8,128)(2,1)S(1)} %slice.8), channel_id=1, source_target_pairs={{0,8},{1,9},{2,10},{3,11},{4,12},{5,13},{6,14},{7,15},{8,0},{9,1},... | collective-permute-start | bytes 405512 | tf_op jit(solution)/shard_map/ppermute | solution.py:43
  74.8 2.0 %collective-permute-start.21 = (f32[88,128]{1,0:T(8,128)S(1)}, f32[88,128]{1,0:T(8,128)S(1)}, u32[]{:S(2)}, u32[]{:S(2)}) collective-permute-start(f32[88,128]{1,0:T(8,128)S(1)} %get-tuple-element.50), channel_id=1, source_target_pairs={{0,8},{1,9},{2,10},{3,11},{4,12},{5,13},{6,14},{7,15},{8,0},{9,1},... | collective-permute-start | bytes 135176 | tf_op jit(solution)/shard_map/ppermute | solution.py:43
  74.9 4.5 %collective-permute-start.22 = (f32[88,128]{1,0:T(8,128)S(1)}, f32[88,128]{1,0:T(8,128)S(1)}, u32[]{:S(2)}, u32[]{:S(2)}) collective-permute-start(f32[88,128]{1,0:T(8,128)S(1)} %get-tuple-element.51), channel_id=1, source_target_pairs={{0,16},{1,17},{2,18},{3,19},{4,20},{5,21},{6,22},{7,23},{8,24},{9,... | collective-permute-start | bytes 135176 | tf_op jit(solution)/shard_map/ppermute | solution.py:43
  75.0 4.5 %collective-permute-start.23 = (f32[88,128]{1,0:T(8,128)S(1)}, f32[88,128]{1,0:T(8,128)S(1)}, u32[]{:S(2)}, u32[]{:S(2)}) collective-permute-start(f32[88,128]{1,0:T(8,128)S(1)} %get-tuple-element.52), channel_id=1, source_target_pairs={{0,24},{1,25},{2,26},{3,27},{4,28},{5,29},{6,30},{7,31},{8,16},{9,... | collective-permute-start | bytes 135176 | tf_op jit(solution)/shard_map/ppermute | solution.py:43
  79.4 6.6 %collective-permute-start.26 = (f32[88,128]{1,0:T(8,128)S(1)}, f32[88,128]{1,0:T(8,128)S(1)}, u32[]{:S(2)}, u32[]{:S(2)}) collective-permute-start(f32[88,128]{1,0:T(8,128)S(1)} %add_add_fusion.3), channel_id=1, source_target_pairs={{0,96},{1,97},{2,98},{3,99},{4,100},{5,101},{6,102},{7,103},{8,104... | collective-permute-start | bytes 135176 | tf_op jit(solution)/shard_map/ppermute | solution.py:43
  80.9 8.4 %collective-permute-start.25 = (f32[88,128]{1,0:T(8,128)S(1)}, f32[88,128]{1,0:T(8,128)S(1)}, u32[]{:S(2)}, u32[]{:S(2)}) collective-permute-start(f32[88,128]{1,0:T(8,128)S(1)} %add_add_fusion.3), channel_id=1, source_target_pairs={{0,64},{1,65},{2,66},{3,67},{4,68},{5,69},{6,70},{7,71},{8,72},{9,... | collective-permute-start | bytes 135176 | tf_op jit(solution)/shard_map/ppermute | solution.py:43
  85.4 6.0 %collective-permute-start.24 = (f32[88,128]{1,0:T(8,128)S(1)}, f32[88,128]{1,0:T(8,128)S(1)}, u32[]{:S(2)}, u32[]{:S(2)}) collective-permute-start(f32[88,128]{1,0:T(8,128)S(1)} %add_add_fusion.3), channel_id=1, source_target_pairs={{0,32},{1,33},{2,34},{3,35},{4,36},{5,37},{6,38},{7,39},{8,40},{9,... | collective-permute-start | bytes 135176 | tf_op jit(solution)/shard_map/ppermute | solution.py:43
  91.4 12.6 %collective-permute-start.29 = (f32[88,128]{1,0:T(8,128)S(1)}, f32[88,128]{1,0:T(8,128)S(1)}, u32[]{:S(2)}, u32[]{:S(2)}) collective-permute-start(f32[88,128]{1,0:T(8,128)S(1)} %add_add_fusion.2), channel_id=1, source_target_pairs={{0,129},{1,128},{2,131},{3,130},{4,133},{5,132},{6,135},{7,134},{8... | collective-permute-start | bytes 135176 | tf_op jit(solution)/shard_map/ppermute | solution.py:43
  98.9 5.6 %collective-permute-start.28 = (f32[88,128]{1,0:T(8,128)S(1)}, f32[88,128]{1,0:T(8,128)S(1)}, u32[]{:S(2)}, u32[]{:S(2)}) collective-permute-start(f32[88,128]{1,0:T(8,128)S(1)} %add_add_fusion.2), channel_id=1, source_target_pairs={{0,1},{1,0},{2,3},{3,2},{4,5},{5,4},{6,7},{7,6},{8,9},{9,8},{10,11... | collective-permute-start | bytes 135176 | tf_op jit(solution)/shard_map/ppermute | solution.py:43
  98.9 5.6 %collective-permute-start.27 = (f32[88,128]{1,0:T(8,128)S(1)}, f32[88,128]{1,0:T(8,128)S(1)}, u32[]{:S(2)}, u32[]{:S(2)}) collective-permute-start(f32[88,128]{1,0:T(8,128)S(1)} %add_add_fusion.2), channel_id=1, source_target_pairs={{0,128},{1,129},{2,130},{3,131},{4,132},{5,133},{6,134},{7,135},{8... | collective-permute-start | bytes 135176 | tf_op jit(solution)/shard_map/ppermute | solution.py:43
  101.1 7.6 %collective-permute-start.36 = (bf16[8,64,128]{2,1,0:T(8,128)(2,1)S(1)}, bf16[8,64,128]{2,1,0:T(8,128)(2,1)S(1)}, u32[]{:S(2)}, u32[]{:S(2)}) collective-permute-start(bf16[8,64,128]{2,1,0:T(8,128)(2,1)S(1)} %get-tuple-element.55), channel_id=1, source_target_pairs={{0,8},{8,0},{16,24},{24,16},{32,40},{40,32},{48,56},{56,48},{64,72... | collective-permute-start | bytes 393224 | tf_op jit(solution)/shard_map/ppermute | solution.py:50
  101.1 8.4 %collective-permute-start.37 = (bf16[8,64,128]{2,1,0:T(8,128)(2,1)S(1)}, bf16[8,64,128]{2,1,0:T(8,128)(2,1)S(1)}, u32[]{:S(2)}, u32[]{:S(2)}) collective-permute-start(bf16[8,64,128]{2,1,0:T(8,128)(2,1)S(1)} %get-tuple-element.56), channel_id=1, source_target_pairs={{8,16},{16,8},{24,32},{32,24},{40,48},{48,40},{56,64},{64,56},{72,... | collective-permute-start | bytes 393224 | tf_op jit(solution)/shard_map/ppermute | solution.py:50
  104.5 9.7 %collective-permute-start.32 = (f32[88,128]{1,0:T(8,128)S(1)}, f32[88,128]{1,0:T(8,128)S(1)}, u32[]{:S(2)}, u32[]{:S(2)}) collective-permute-start(f32[88,128]{1,0:T(8,128)S(1)} %add_add_fusion.1), channel_id=1, source_target_pairs={{0,6},{1,7},{2,4},{3,5},{4,2},{5,3},{6,0},{7,1},{8,14},{9,15},{10,... | collective-permute-start | bytes 135176 | tf_op jit(solution)/shard_map/ppermute | solution.py:43
  104.6 9.7 %collective-permute-start.31 = (f32[88,128]{1,0:T(8,128)S(1)}, f32[88,128]{1,0:T(8,128)S(1)}, u32[]{:S(2)}, u32[]{:S(2)}) collective-permute-start(f32[88,128]{1,0:T(8,128)S(1)} %add_add_fusion.1), channel_id=1, source_target_pairs={{0,4},{1,5},{2,6},{3,7},{4,0},{5,1},{6,2},{7,3},{8,12},{9,13},{10,... | collective-permute-start | bytes 135176 | tf_op jit(solution)/shard_map/ppermute | solution.py:43
  105.6 8.6 %collective-permute-start.30 = (f32[88,128]{1,0:T(8,128)S(1)}, f32[88,128]{1,0:T(8,128)S(1)}, u32[]{:S(2)}, u32[]{:S(2)}) collective-permute-start(f32[88,128]{1,0:T(8,128)S(1)} %add_add_fusion.1), channel_id=1, source_target_pairs={{0,2},{1,3},{2,0},{3,1},{4,6},{5,7},{6,4},{7,5},{8,10},{9,11},{10,... | collective-permute-start | bytes 135176 | tf_op jit(solution)/shard_map/ppermute | solution.py:43
  110.0 6.3 %collective-permute-start.38 = (bf16[3,64,128]{2,1,0:T(8,128)(2,1)S(1)}, bf16[3,64,128]{2,1,0:T(8,128)(2,1)S(1)}, u32[]{:S(2)}, u32[]{:S(2)}) collective-permute-start(bf16[3,64,128]{2,1,0:T(8,128)(2,1)S(1)} %get-tuple-element.57), channel_id=1, source_target_pairs={{0,1},{1,0},{2,3},{3,2},{4,5},{5,4},{6,7},{7,6},{8,9},{9,8},{10,11... | collective-permute-start | bytes 147464 | tf_op jit(solution)/shard_map/ppermute | solution.py:50
  112.2 8.4 %collective-permute-start.39 = (bf16[3,64,128]{2,1,0:T(8,128)(2,1)S(1)}, bf16[3,64,128]{2,1,0:T(8,128)(2,1)S(1)}, u32[]{:S(2)}, u32[]{:S(2)}) collective-permute-start(bf16[3,64,128]{2,1,0:T(8,128)(2,1)S(1)} %get-tuple-element.58), channel_id=1, source_target_pairs={{1,2},{2,1},{3,4},{4,3},{5,6},{6,5},{9,10},{10,9},{11,12},{12,11},... | collective-permute-start | bytes 147464 | tf_op jit(solution)/shard_map/ppermute | solution.py:50
  114.3 8.7 %collective-permute-start.35 = (f32[88,128]{1,0:T(8,128)S(1)}, f32[88,128]{1,0:T(8,128)S(1)}, u32[]{:S(2)}, u32[]{:S(2)}) collective-permute-start(f32[88,128]{1,0:T(8,128)S(1)} %add_add_fusion.got0), channel_id=1, source_target_pairs={{0,24},{1,25},{2,26},{3,27},{4,28},{5,29},{6,30},{7,31},{8,16},{9,... | collective-permute-start | bytes 135176 | tf_op jit(solution)/shard_map/ppermute | solution.py:43
  114.4 8.6 %collective-permute-start.34 = (f32[88,128]{1,0:T(8,128)S(1)}, f32[88,128]{1,0:T(8,128)S(1)}, u32[]{:S(2)}, u32[]{:S(2)}) collective-permute-start(f32[88,128]{1,0:T(8,128)S(1)} %add_add_fusion.got0), channel_id=1, source_target_pairs={{0,16},{1,17},{2,18},{3,19},{4,20},{5,21},{6,22},{7,23},{8,24},{9,... | collective-permute-start | bytes 135176 | tf_op jit(solution)/shard_map/ppermute | solution.py:43
  115.2 7.8 %collective-permute-start.33 = (f32[88,128]{1,0:T(8,128)S(1)}, f32[88,128]{1,0:T(8,128)S(1)}, u32[]{:S(2)}, u32[]{:S(2)}) collective-permute-start(f32[88,128]{1,0:T(8,128)S(1)} %add_add_fusion.got0), channel_id=1, source_target_pairs={{0,8},{1,9},{2,10},{3,11},{4,12},{5,13},{6,14},{7,15},{8,0},{9,1},... | collective-permute-start | bytes 135176 | tf_op jit(solution)/shard_map/ppermute | solution.py:43

commit v13 on v11

--- a/solution.py
+++ b/solution.py
@@ -426,7 +426,7 @@
     )
     passed, got = mirrored(pay_near, pay_far, parts)
     _, counted = lax.optimization_barrier((passed, counted))
-    count = total_small(counted, (3, 0))
+    count = total_small(counted, (0, 3))
     half = 9 * chans // 2
     lines = -(-(half + tall + 8) // 32) * 32
     grad, low, mate, other, *quarters = run(

time: 120 us -> 122 us (1.017)
  waiting for transfers between devices: 18.5 us -> 23.2 us
  starting transfers between devices: 83.9 us -> 80.5 us
    ppermute x32, waiting for transfers between devices: 13.2 us -> 17.1 us  [send(): return lax.ppermute(block, GRID, pairs)]
    ppermute x4, starting transfers between devices: 20.1 us -> 18 us  [swapped(): lax.ppermute(to_other, axis, others)]
  transfers between devices with their start and end apart: 40 -> 40, of which waited for: 10 -> 12; matrix products, arithmetic and copies ran while one was open for 0% -> 0% of each run, Pallas kernels for 3% -> 3%
where the time goes in v13:
time: 122 us; the launch traced here: 121 us
  starting transfers between devices  80.5 us (66%)
  waiting for transfers between devices  23.2 us (19%)
  Pallas kernels  12.5 us (10%)
  local copies, waits for them, and re-layouts  3.41 us (3%)
    ppermute x32, starting transfers between devices, send(): return lax.ppermute(block, GRID, pairs)  60.8 us
    ppermute x4, starting transfers between devices, swapped(): lax.ppermute(to_other, axis, others)  18 us
    ppermute x32, waiting for transfers between devices, send(): return lax.ppermute(block, GRID, pairs)  17.1 us
    pallas_call x7, Pallas kernels, run(): pl.pallas_call(body, out_shape=outs, in_specs=[SMEM] * scalars + [VMEM] *...  12.5 us
    ppermute x4, waiting for transfers between devices, swapped(): lax.ppermute(to_other, axis, others)  6.07 us
    unnamed x12, local copies, waits for them, and re-layouts  3.39 us
  transfers between devices with their start and end apart: 40, of which 12 were waited for; matrix products, arithmetic and copies ran while one was open for 0% of the time, Pallas kernels for 3%

profile of v13, /device:TPU:24, one launch (start us, length us, event | category | flops | bytes accessed | tf_op | source)
XLA Modules:
  0.0 120.6 jit_solution(11228210683659713322)
XLA Ops:
  0.7 1.0 copy-done.1
  1.7 0.7 copy-done.3
  2.4 0.7 shard_map.101
  3.1 6.3 %collective-permute-start.2 = (f32[8,128]{1,0:T(8,128)S(1)}, f32[8,128]{1,0:T(8,128)S(1)}, u32[]{:S(2)}, u32[]{:S(2)}) collective-permute-start(f32[8,128]{1,0:T(8,128)S(1)} %get-tuple-element.34), channel_id=1, source_target_pairs={{0,96},{1,97},{2,98},{3,99},{4,100},{5,101},{6,102},{7,103},{8,104... | collective-permute-start | bytes 12296 | tf_op jit(solution)/shard_map/ppermute | solution.py:43
  9.5 1.0 collective-permute-start.1
  10.5 1.5 %collective-permute-start = (f32[8,128]{1,0:T(8,128)S(1)}, f32[8,128]{1,0:T(8,128)S(1)}, u32[]{:S(2)}, u32[]{:S(2)}) collective-permute-start(f32[8,128]{1,0:T(8,128)S(1)} %get-tuple-element.34), channel_id=1, source_target_pairs={{0,32},{1,33},{2,34},{3,35},{4,36},{5,37},{6,38},{7,39},{8,40},{9,... | collective-permute-start | bytes 12296 | tf_op jit(solution)/shard_map/ppermute | solution.py:43
  11.9 5.8 %collective-permute-start.7 = (bf16[8,64,128]{2,1,0:T(8,128)(2,1)S(1)}, bf16[8,64,128]{2,1,0:T(8,128)(2,1)S(1)}, u32[]{:S(2)}, u32[]{:S(2)}) collective-permute-start(bf16[8,64,128]{2,1,0:T(8,128)(2,1)S(1)} %get-tuple-element.38), channel_id=1, source_target_pairs={{8,16},{16,8},{24,32},{32,24},{40,48},{48,40},{56,64},{64,56},{72,... | collective-permute-start | bytes 393224 | tf_op jit(solution)/shard_map/ppermute | solution.py:50
  17.9 2.0 %collective-permute-start.4 = (f32[8,128]{1,0:T(8,128)S(1)}, f32[8,128]{1,0:T(8,128)S(1)}, u32[]{:S(2)}, u32[]{:S(2)}) collective-permute-start(f32[8,128]{1,0:T(8,128)S(1)} %add_add_fusion.7), channel_id=1, source_target_pairs={{0,1},{1,0},{2,3},{3,2},{4,5},{5,4},{6,7},{7,6},{8,9},{9,8},{10,11... | collective-permute-start | bytes 12296 | tf_op jit(solution)/shard_map/ppermute | solution.py:43
  19.9 2.1 %collective-permute-start.3 = (f32[8,128]{1,0:T(8,128)S(1)}, f32[8,128]{1,0:T(8,128)S(1)}, u32[]{:S(2)}, u32[]{:S(2)}) collective-permute-start(f32[8,128]{1,0:T(8,128)S(1)} %add_add_fusion.7), channel_id=1, source_target_pairs={{0,128},{1,129},{2,130},{3,131},{4,132},{5,133},{6,134},{7,135},{8... | collective-permute-start | bytes 12296 | tf_op jit(solution)/shard_map/ppermute | solution.py:43
  22.0 0.5 shard_map.102
  22.5 1.0 collective-permute-start.8
  23.5 5.4 %collective-permute-start.9 = (bf16[3,64,128]{2,1,0:T(8,128)(2,1)S(1)}, bf16[3,64,128]{2,1,0:T(8,128)(2,1)S(1)}, u32[]{:S(2)}, u32[]{:S(2)}) collective-permute-start(bf16[3,64,128]{2,1,0:T(8,128)(2,1)S(1)} %get-tuple-element.40), channel_id=1, source_target_pairs={{1,2},{2,1},{3,4},{4,3},{5,6},{6,5},{9,10},{10,9},{11,12},{12,11},... | collective-permute-start | bytes 147464 | tf_op jit(solution)/shard_map/ppermute | solution.py:50
  29.0 2.9 %collective-permute-done.9.side_other = bf16[3,64,128]{2,1,0:T(8,128)(2,1)S(1)} collective-permute-done((bf16[3,64,128]{2,1,0:T(8,128)(2,1)S(1)}, bf16[3,64,128]{2,1,0:T(8,128)(2,1)S(1)}, u32[]{:S(2)}, u32[]{:S(2)}) %collective-permute-start.9) | collective-permute-done | bytes 49184 | tf_op jit(solution)/shard_map/ppermute | solution.py:50
  31.9 0.9 copy-done
  32.8 0.7 copy-done.2
  33.5 2.5 %shard_map.103 = (bf16[48,192,128]{2,1,0:T(8,128)(2,1)S(1)}, bf16[32,64,128]{2,1,0:T(8,128)(2,1)S(1)}, bf16[1056,128]{1,0:T(8,128)(2,1)S(1)}, bf16[1056,128]{1,0:T(8,128)(2,1)S(1)}) custom-call(s32[1]{0:T(128)} %bitcast.place, bf16[32,64,128]{2,1,0:T(8,128)(2,1)S(1)} %get-tuple-element.36.own.act, bf16[8,64,128]{2,1,0:T(8,128)(2,1)S(1)} %collective-permute-done.6.mate, ...), custom_call_target="tpu_custom_call" | custom-call | bytes 18000000 | tf_op jit(solution)/shard_map/pallas_call | solution.py:19
  36.0 1.6 %collective-permute-start.10 = (bf16[1056,128]{1,0:T(8,128)(2,1)S(1)}, bf16[1056,128]{1,0:T(8,128)(2,1)S(1)}, u32[]{:S(2)}, u32[]{:S(2)}) collective-permute-start(bf16[1056,128]{1,0:T(8,128)(2,1)S(1)} %get-tuple-element.43), channel_id=1, source_target_pairs={{0,2},{1,3},{2,0},{3,1},{4,6},{5,7},{6,4},{7,5},{8,10},{9,11},{10,... | collective-permute-start | bytes 811016 | tf_op jit(solution)/shard_map/ppermute | solution.py:43
  37.6 5.2 %collective-permute-start.18 = (bf16[1056,128]{1,0:T(8,128)(2,1)S(1)}, bf16[1056,128]{1,0:T(8,128)(2,1)S(1)}, u32[]{:S(2)}, u32[]{:S(2)}) collective-permute-start(bf16[1056,128]{1,0:T(8,128)(2,1)S(1)} %get-tuple-element.46), channel_id=1, source_target_pairs={{0,16},{1,48},{2,80},{3,112},{4,144},{5,176},{6,208},{7,240},{8,24... | collective-permute-start | bytes 811016 | tf_op jit(solution)/shard_map/ppermute | solution.py:43
  42.9 5.5 %collective-permute-start.17 = (bf16[1056,128]{1,0:T(8,128)(2,1)S(1)}, bf16[1056,128]{1,0:T(8,128)(2,1)S(1)}, u32[]{:S(2)}, u32[]{:S(2)}) collective-permute-start(bf16[1056,128]{1,0:T(8,128)(2,1)S(1)} %collective-permute-done.10), channel_id=1, source_target_pairs={{0,64},{1,96},{2,0},{3,32},{4,192},{5,224},{6,128},{7,160},{8,72},... | collective-permute-start | bytes 811016 | tf_op jit(solution)/shard_map/ppermute | solution.py:43
  48.3 1.8 %collective-permute-start.13 = (f32[8,128]{1,0:T(8,128)S(1)}, f32[8,128]{1,0:T(8,128)S(1)}, u32[]{:S(2)}, u32[]{:S(2)}) collective-permute-start(f32[8,128]{1,0:T(8,128)S(1)} %add_add_fusion.6), channel_id=1, source_target_pairs={{0,24},{1,25},{2,26},{3,27},{4,28},{5,29},{6,30},{7,31},{8,16},{9,... | collective-permute-start | bytes 12296 | tf_op jit(solution)/shard_map/ppermute | solution.py:43
  50.1 1.4 %collective-permute-start.12 = (f32[8,128]{1,0:T(8,128)S(1)}, f32[8,128]{1,0:T(8,128)S(1)}, u32[]{:S(2)}, u32[]{:S(2)}) collective-permute-start(f32[8,128]{1,0:T(8,128)S(1)} %add_add_fusion.6), channel_id=1, source_target_pairs={{0,16},{1,17},{2,18},{3,19},{4,20},{5,21},{6,22},{7,23},{8,24},{9,... | collective-permute-start | bytes 12296 | tf_op jit(solution)/shard_map/ppermute | solution.py:43
  51.6 4.0 %collective-permute-done.13 = f32[8,128]{1,0:T(8,128)S(1)} collective-permute-done((f32[8,128]{1,0:T(8,128)S(1)}, f32[8,128]{1,0:T(8,128)S(1)}, u32[]{:S(2)}, u32[]{:S(2)}) %collective-permute-start.13) | collective-permute-done | bytes 4128 | tf_op jit(solution)/shard_map/ppermute | solution.py:43
  55.6 2.7 %collective-permute-done.12 = f32[8,128]{1,0:T(8,128)S(1)} collective-permute-done((f32[8,128]{1,0:T(8,128)S(1)}, f32[8,128]{1,0:T(8,128)S(1)}, u32[]{:S(2)}, u32[]{:S(2)}) %collective-permute-start.12) | collective-permute-done | bytes 4128 | tf_op jit(solution)/shard_map/ppermute | solution.py:43
  58.4 0.9 collective-permute-start.15
  59.3 3.2 %collective-permute-start.14 = (f32[8,128]{1,0:T(8,128)S(1)}, f32[8,128]{1,0:T(8,128)S(1)}, u32[]{:S(2)}, u32[]{:S(2)}) collective-permute-start(f32[8,128]{1,0:T(8,128)S(1)} %add_add_fusion.5), channel_id=1, source_target_pairs={{0,2},{1,3},{2,0},{3,1},{4,6},{5,7},{6,4},{7,5},{8,10},{9,11},{10,... | collective-permute-start | bytes 12296 | tf_op jit(solution)/shard_map/ppermute | solution.py:43
  62.8 0.6 collective-permute-start.19
  63.6 0.5 collective-permute-done.14
  64.4 5.1 %shard_map.104 = (f32[32,64,128]{2,1,0:T(8,128)S(1)}, bf16[32,64,128]{2,1,0:T(8,128)(2,1)S(1)}, bf16[8,64,128]{2,1,0:T(8,128)(2,1)S(1)}, bf16[8,64,128]{2,1,0:T(...) custom-call(s32[1]{0:T(128)} %bitcast.place, ...), custom_call_target="tpu_custom_call" | custom-call | bytes 21600000 | tf_op jit(solution)/shard_map/pallas_call | solution.py:19
  69.9 1.5 %collective-permute-start.23 = (f32[88,128]{1,0:T(8,128)S(1)}, f32[88,128]{1,0:T(8,128)S(1)}, u32[]{:S(2)}, u32[]{:S(2)}) collective-permute-start(f32[88,128]{1,0:T(8,128)S(1)} %get-tuple-element.52), channel_id=1, source_target_pairs={{0,24},{1,25},{2,26},{3,27},{4,28},{5,29},{6,30},{7,31},{8,16},{9,... | collective-permute-start | bytes 135176 | tf_op jit(solution)/shard_map/ppermute | solution.py:43
  71.4 2.7 %collective-permute-done.22 = f32[88,128]{1,0:T(8,128)S(1)} collective-permute-done((f32[88,128]{1,0:T(8,128)S(1)}, f32[88,128]{1,0:T(8,128)S(1)}, u32[]{:S(2)}, u32[]{:S(2)}) %collective-permute-start.22) | collective-permute-done | bytes 45088 | tf_op jit(solution)/shard_map/ppermute | solution.py:43
  74.1 8.2 %collective-permute-start.26 = (f32[88,128]{1,0:T(8,128)S(1)}, f32[88,128]{1,0:T(8,128)S(1)}, u32[]{:S(2)}, u32[]{:S(2)}) collective-permute-start(f32[88,128]{1,0:T(8,128)S(1)} %add_add_fusion.3), channel_id=1, source_target_pairs={{0,96},{1,97},{2,98},{3,99},{4,100},{5,101},{6,102},{7,103},{8,104... | collective-permute-start | bytes 135176 | tf_op jit(solution)/shard_map/ppermute | solution.py:43
  82.3 6.8 %collective-permute-start.25 = (f32[88,128]{1,0:T(8,128)S(1)}, f32[88,128]{1,0:T(8,128)S(1)}, u32[]{:S(2)}, u32[]{:S(2)}) collective-permute-start(f32[88,128]{1,0:T(8,128)S(1)} %add_add_fusion.3), channel_id=1, source_target_pairs={{0,64},{1,65},{2,66},{3,67},{4,68},{5,69},{6,70},{7,71},{8,72},{9,... | collective-permute-start | bytes 135176 | tf_op jit(solution)/shard_map/ppermute | solution.py:43
  89.1 4.1 %collective-permute-done.25 = f32[88,128]{1,0:T(8,128)S(1)} collective-permute-done((f32[88,128]{1,0:T(8,128)S(1)}, f32[88,128]{1,0:T(8,128)S(1)}, u32[]{:S(2)}, u32[]{:S(2)}) %collective-permute-start.25) | collective-permute-done | bytes 45088 | tf_op jit(solution)/shard_map/ppermute | solution.py:43
  93.2 2.0 %collective-permute-done.24 = f32[88,128]{1,0:T(8,128)S(1)} collective-permute-done((f32[88,128]{1,0:T(8,128)S(1)}, f32[88,128]{1,0:T(8,128)S(1)}, u32[]{:S(2)}, u32[]{:S(2)}) %collective-permute-start.24) | collective-permute-done | bytes 45088 | tf_op jit(solution)/shard_map/ppermute | solution.py:43
  95.7 3.7 %collective-permute-start.27 = (f32[88,128]{1,0:T(8,128)S(1)}, f32[88,128]{1,0:T(8,128)S(1)}, u32[]{:S(2)}, u32[]{:S(2)}) collective-permute-start(f32[88,128]{1,0:T(8,128)S(1)} %add_add_fusion.2), channel_id=1, source_target_pairs={{0,128},{1,129},{2,130},{3,131},{4,132},{5,133},{6,134},{7,135},{8... | collective-permute-start | bytes 135176 | tf_op jit(solution)/shard_map/ppermute | solution.py:43
  99.4 1.9 %collective-permute-start.37 = (bf16[8,64,128]{2,1,0:T(8,128)(2,1)S(1)}, bf16[8,64,128]{2,1,0:T(8,128)(2,1)S(1)}, u32[]{:S(2)}, u32[]{:S(2)}) collective-permute-start(bf16[8,64,128]{2,1,0:T(8,128)(2,1)S(1)} %get-tuple-element.56), channel_id=1, source_target_pairs={{8,16},{16,8},{24,32},{32,24},{40,48},{48,40},{56,64},{64,56},{72,... | collective-permute-start | bytes 393224 | tf_op jit(solution)/shard_map/ppermute | solution.py:50
  101.4 0.6 collective-permute-done.27
  102.0 1.4 %collective-permute-start.32 = (f32[88,128]{1,0:T(8,128)S(1)}, f32[88,128]{1,0:T(8,128)S(1)}, u32[]{:S(2)}, u32[]{:S(2)}) collective-permute-start(f32[88,128]{1,0:T(8,128)S(1)} %add_add_fusion.1), channel_id=1, source_target_pairs={{0,6},{1,7},{2,4},{3,5},{4,2},{5,3},{6,0},{7,1},{8,14},{9,15},{10,... | collective-permute-start | bytes 135176 | tf_op jit(solution)/shard_map/ppermute | solution.py:43
  103.3 1.4 %collective-permute-start.31 = (f32[88,128]{1,0:T(8,128)S(1)}, f32[88,128]{1,0:T(8,128)S(1)}, u32[]{:S(2)}, u32[]{:S(2)}) collective-permute-start(f32[88,128]{1,0:T(8,128)S(1)} %add_add_fusion.1), channel_id=1, source_target_pairs={{0,4},{1,5},{2,6},{3,7},{4,0},{5,1},{6,2},{7,3},{8,12},{9,13},{10,... | collective-permute-start | bytes 135176 | tf_op jit(solution)/shard_map/ppermute | solution.py:43
  104.7 1.4 %collective-permute-start.30 = (f32[88,128]{1,0:T(8,128)S(1)}, f32[88,128]{1,0:T(8,128)S(1)}, u32[]{:S(2)}, u32[]{:S(2)}) collective-permute-start(f32[88,128]{1,0:T(8,128)S(1)} %add_add_fusion.1), channel_id=1, source_target_pairs={{0,2},{1,3},{2,0},{3,1},{4,6},{5,7},{6,4},{7,5},{8,10},{9,11},{10,... | collective-permute-start | bytes 135176 | tf_op jit(solution)/shard_map/ppermute | solution.py:43
  106.1 1.7 %collective-permute-done.37.other = bf16[8,64,128]{2,1,0:T(8,128)(2,1)S(1)} collective-permute-done((bf16[8,64,128]{2,1,0:T(8,128)(2,1)S(1)}, bf16[8,64,128]{2,1,0:T(8,128)(2,1)S(1)}, u32[]{:S(2)}, u32[]{:S(2)}) %collective-permute-start.37) | collective-permute-done | bytes 131104 | tf_op jit(solution)/shard_map/ppermute | solution.py:50
  107.8 0.5 shard_map.106
  108.3 0.7 collective-permute-start.38
  109.0 4.9 %collective-permute-start.39 = (bf16[3,64,128]{2,1,0:T(8,128)(2,1)S(1)}, bf16[3,64,128]{2,1,0:T(8,128)(2,1)S(1)}, u32[]{:S(2)}, u32[]{:S(2)}) collective-permute-start(bf16[3,64,128]{2,1,0:T(8,128)(2,1)S(1)} %get-tuple-element.58), channel_id=1, source_target_pairs={{1,2},{2,1},{3,4},{4,3},{5,6},{6,5},{9,10},{10,9},{11,12},{12,11},... | collective-permute-start | bytes 147464 | tf_op jit(solution)/shard_map/ppermute | solution.py:50
  114.1 1.7 %collective-permute-start.33 = (f32[88,128]{1,0:T(8,128)S(1)}, f32[88,128]{1,0:T(8,128)S(1)}, u32[]{:S(2)}, u32[]{:S(2)}) collective-permute-start(f32[88,128]{1,0:T(8,128)S(1)} %add_add_fusion.got0), channel_id=1, source_target_pairs={{0,8},{1,9},{2,10},{3,11},{4,12},{5,13},{6,14},{7,15},{8,0},{9,1},... | collective-permute-start | bytes 135176 | tf_op jit(solution)/shard_map/ppermute | solution.py:43
  115.9 1.5 %collective-permute-done.39.side_other = bf16[3,64,128]{2,1,0:T(8,128)(2,1)S(1)} collective-permute-done((bf16[3,64,128]{2,1,0:T(8,128)(2,1)S(1)}, bf16[3,64,128]{2,1,0:T(8,128)(2,1)S(1)}, u32[]{:S(2)}, u32[]{:S(2)}) %collective-permute-start.39) | collective-permute-done | bytes 49184 | tf_op jit(solution)/shard_map/ppermute | solution.py:50
  117.4 2.4 %shard_map.107 = bf16[32,64,128]{2,1,0:T(8,128)(2,1)} custom-call(s32[1]{0:T(128)} %bitcast.place, f32[8,128]{1,0:T(8,128)S(1)} %add_add_fusion.4.count, bf16[32,64,128]{2,1,0:T(8,128)(2,1)S(1)} %get-tuple-element.54.own.low, bf16[8,64,128]{2,1,0:T(8,128)(2,1)S(1)} %collective-permute-done.36.mate, bf16[8,64,128]{2,1,0:T(8,128)(2,1)S(1)} %collective-permute-done.37.other, ...), custom_call_target="tpu_custom_call" | custom-call | bytes 14400000 | tf_op jit(solution)/shard_map/pallas_call | solution.py:19
  119.8 0.8 shard_map.105
  (61 shorter events, 2.3 us)
Async XLA Ops:
  0.6 63.8 %copy-start.5 = (f32[37]{0:T(128)S(1)}, f32[37]{0:T(128)}, u32[]{:S(2)}) copy-start(f32[37]{0:T(128)} %param.9) | copy-start | bytes 448
  0.6 63.8 %copy-start.4 = (bf16[64,37]{0,1:T(8,128)(2,1)S(1)}, bf16[64,37]{0,1:T(8,128)(2,1)}, u32[]{:S(2)}) copy-start(bf16[64,37]{0,1:T(8,128)(2,1)} %param.8) | copy-start | bytes 14212
  0.7 1.0 copy-start.1
  1.7 0.7 copy-start.3
  3.1 14.6 %collective-permute-start.2 = (f32[8,128]{1,0:T(8,128)S(1)}, f32[8,128]{1,0:T(8,128)S(1)}, u32[]{:S(2)}, u32[]{:S(2)}) collective-permute-start(f32[8,128]{1,0:T(8,128)S(1)} %get-tuple-element.34), channel_id=1, source_target_pairs={{0,96},{1,97},{2,98},{3,99},{4,100},{5,101},{6,102},{7,103},{8,104... | collective-permute-start | bytes 12296 | tf_op jit(solution)/shard_map/ppermute | solution.py:43
  9.5 8.3 %collective-permute-start.1 = (f32[8,128]{1,0:T(8,128)S(1)}, f32[8,128]{1,0:T(8,128)S(1)}, u32[]{:S(2)}, u32[]{:S(2)}) collective-permute-start(f32[8,128]{1,0:T(8,128)S(1)} %get-tuple-element.34), channel_id=1, source_target_pairs={{0,64},{1,65},{2,66},{3,67},{4,68},{5,69},{6,70},{7,71},{8,72},{9,... | collective-permute-start | bytes 12296 | tf_op jit(solution)/shard_map/ppermute | solution.py:43
  10.5 7.3 %collective-permute-start = (f32[8,128]{1,0:T(8,128)S(1)}, f32[8,128]{1,0:T(8,128)S(1)}, u32[]{:S(2)}, u32[]{:S(2)}) collective-permute-start(f32[8,128]{1,0:T(8,128)S(1)} %get-tuple-element.34), channel_id=1, source_target_pairs={{0,32},{1,33},{2,34},{3,35},{4,36},{5,37},{6,38},{7,39},{8,40},{9,... | collective-permute-start | bytes 12296 | tf_op jit(solution)/shard_map/ppermute | solution.py:43
  11.9 10.0 %collective-permute-start.6 = (bf16[8,64,128]{2,1,0:T(8,128)(2,1)S(1)}, bf16[8,64,128]{2,1,0:T(8,128)(2,1)S(1)}, u32[]{:S(2)}, u32[]{:S(2)}) collective-permute-start(bf16[8,64,128]{2,1,0:T(8,128)(2,1)S(1)} %get-tuple-element.37), channel_id=1, source_target_pairs={{0,8},{8,0},{16,24},{24,16},{32,40},{40,32},{48,56},{56,48},{64,72... | collective-permute-start | bytes 393224 | tf_op jit(solution)/shard_map/ppermute | solution.py:50
  11.9 10.0 %collective-permute-start.7 = (bf16[8,64,128]{2,1,0:T(8,128)(2,1)S(1)}, bf16[8,64,128]{2,1,0:T(8,128)(2,1)S(1)}, u32[]{:S(2)}, u32[]{:S(2)}) collective-permute-start(bf16[8,64,128]{2,1,0:T(8,128)(2,1)S(1)} %get-tuple-element.38), channel_id=1, source_target_pairs={{8,16},{16,8},{24,32},{32,24},{40,48},{48,40},{56,64},{64,56},{72,... | collective-permute-start | bytes 393224 | tf_op jit(solution)/shard_map/ppermute | solution.py:50
  17.8 11.1 %collective-permute-start.5 = (f32[8,128]{1,0:T(8,128)S(1)}, f32[8,128]{1,0:T(8,128)S(1)}, u32[]{:S(2)}, u32[]{:S(2)}) collective-permute-start(f32[8,128]{1,0:T(8,128)S(1)} %add_add_fusion.7), channel_id=1, source_target_pairs={{0,129},{1,128},{2,131},{3,130},{4,133},{5,132},{6,135},{7,134},{8... | collective-permute-start | bytes 12296 | tf_op jit(solution)/shard_map/ppermute | solution.py:43
  17.9 11.0 %collective-permute-start.4 = (f32[8,128]{1,0:T(8,128)S(1)}, f32[8,128]{1,0:T(8,128)S(1)}, u32[]{:S(2)}, u32[]{:S(2)}) collective-permute-start(f32[8,128]{1,0:T(8,128)S(1)} %add_add_fusion.7), channel_id=1, source_target_pairs={{0,1},{1,0},{2,3},{3,2},{4,5},{5,4},{6,7},{7,6},{8,9},{9,8},{10,11... | collective-permute-start | bytes 12296 | tf_op jit(solution)/shard_map/ppermute | solution.py:43
  19.9 9.0 %collective-permute-start.3 = (f32[8,128]{1,0:T(8,128)S(1)}, f32[8,128]{1,0:T(8,128)S(1)}, u32[]{:S(2)}, u32[]{:S(2)}) collective-permute-start(f32[8,128]{1,0:T(8,128)S(1)} %add_add_fusion.7), channel_id=1, source_target_pairs={{0,128},{1,129},{2,130},{3,131},{4,132},{5,133},{6,134},{7,135},{8... | collective-permute-start | bytes 12296 | tf_op jit(solution)/shard_map/ppermute | solution.py:43
  22.5 6.5 %collective-permute-start.8 = (bf16[3,64,128]{2,1,0:T(8,128)(2,1)S(1)}, bf16[3,64,128]{2,1,0:T(8,128)(2,1)S(1)}, u32[]{:S(2)}, u32[]{:S(2)}) collective-permute-start(bf16[3,64,128]{2,1,0:T(8,128)(2,1)S(1)} %get-tuple-element.39), channel_id=1, source_target_pairs={{0,1},{1,0},{2,3},{3,2},{4,5},{5,4},{6,7},{7,6},{8,9},{9,8},{10,11... | collective-permute-start | bytes 147464 | tf_op jit(solution)/shard_map/ppermute | solution.py:50
  23.5 8.4 %collective-permute-start.9 = (bf16[3,64,128]{2,1,0:T(8,128)(2,1)S(1)}, bf16[3,64,128]{2,1,0:T(8,128)(2,1)S(1)}, u32[]{:S(2)}, u32[]{:S(2)}) collective-permute-start(bf16[3,64,128]{2,1,0:T(8,128)(2,1)S(1)} %get-tuple-element.40), channel_id=1, source_target_pairs={{1,2},{2,1},{3,4},{4,3},{5,6},{6,5},{9,10},{10,9},{11,12},{12,11},... | collective-permute-start | bytes 147464 | tf_op jit(solution)/shard_map/ppermute | solution.py:50
  31.9 0.9 copy-start
  32.8 0.7 copy-start.2
  36.0 6.8 %collective-permute-start.10 = (bf16[1056,128]{1,0:T(8,128)(2,1)S(1)}, bf16[1056,128]{1,0:T(8,128)(2,1)S(1)}, u32[]{:S(2)}, u32[]{:S(2)}) collective-permute-start(bf16[1056,128]{1,0:T(8,128)(2,1)S(1)} %get-tuple-element.43), channel_id=1, source_target_pairs={{0,2},{1,3},{2,0},{3,1},{4,6},{5,7},{6,4},{7,5},{8,10},{9,11},{10,... | collective-permute-start | bytes 811016 | tf_op jit(solution)/shard_map/ppermute | solution.py:43
  37.6 24.9 %collective-permute-start.18 = (bf16[1056,128]{1,0:T(8,128)(2,1)S(1)}, bf16[1056,128]{1,0:T(8,128)(2,1)S(1)}, u32[]{:S(2)}, u32[]{:S(2)}) collective-permute-start(bf16[1056,128]{1,0:T(8,128)(2,1)S(1)} %get-tuple-element.46), channel_id=1, source_target_pairs={{0,16},{1,48},{2,80},{3,112},{4,144},{5,176},{6,208},{7,240},{8,24... | collective-permute-start | bytes 811016 | tf_op jit(solution)/shard_map/ppermute | solution.py:43
  42.9 19.9 %collective-permute-start.17 = (bf16[1056,128]{1,0:T(8,128)(2,1)S(1)}, bf16[1056,128]{1,0:T(8,128)(2,1)S(1)}, u32[]{:S(2)}, u32[]{:S(2)}) collective-permute-start(bf16[1056,128]{1,0:T(8,128)(2,1)S(1)} %collective-permute-done.10), channel_id=1, source_target_pairs={{0,64},{1,96},{2,0},{3,32},{4,192},{5,224},{6,128},{7,160},{8,72},... | collective-permute-start | bytes 811016 | tf_op jit(solution)/shard_map/ppermute | solution.py:43
  48.3 7.3 %collective-permute-start.13 = (f32[8,128]{1,0:T(8,128)S(1)}, f32[8,128]{1,0:T(8,128)S(1)}, u32[]{:S(2)}, u32[]{:S(2)}) collective-permute-start(f32[8,128]{1,0:T(8,128)S(1)} %add_add_fusion.6), channel_id=1, source_target_pairs={{0,24},{1,25},{2,26},{3,27},{4,28},{5,29},{6,30},{7,31},{8,16},{9,... | collective-permute-start | bytes 12296 | tf_op jit(solution)/shard_map/ppermute | solution.py:43
  50.1 8.2 %collective-permute-start.12 = (f32[8,128]{1,0:T(8,128)S(1)}, f32[8,128]{1,0:T(8,128)S(1)}, u32[]{:S(2)}, u32[]{:S(2)}) collective-permute-start(f32[8,128]{1,0:T(8,128)S(1)} %add_add_fusion.6), channel_id=1, source_target_pairs={{0,16},{1,17},{2,18},{3,19},{4,20},{5,21},{6,22},{7,23},{8,24},{9,... | collective-permute-start | bytes 12296 | tf_op jit(solution)/shard_map/ppermute | solution.py:43
  51.5 6.8 %collective-permute-start.11 = (f32[8,128]{1,0:T(8,128)S(1)}, f32[8,128]{1,0:T(8,128)S(1)}, u32[]{:S(2)}, u32[]{:S(2)}) collective-permute-start(f32[8,128]{1,0:T(8,128)S(1)} %add_add_fusion.6), channel_id=1, source_target_pairs={{0,8},{1,9},{2,10},{3,11},{4,12},{5,13},{6,14},{7,15},{8,0},{9,1},... | collective-permute-start | bytes 12296 | tf_op jit(solution)/shard_map/ppermute | solution.py:43
  58.3 5.1 %collective-permute-start.16 = (f32[8,128]{1,0:T(8,128)S(1)}, f32[8,128]{1,0:T(8,128)S(1)}, u32[]{:S(2)}, u32[]{:S(2)}) collective-permute-start(f32[8,128]{1,0:T(8,128)S(1)} %add_add_fusion.5), channel_id=1, source_target_pairs={{0,6},{1,7},{2,4},{3,5},{4,2},{5,3},{6,0},{7,1},{8,14},{9,15},{10,... | collective-permute-start | bytes 12296 | tf_op jit(solution)/shard_map/ppermute | solution.py:43
  58.4 5.2 %collective-permute-start.15 = (f32[8,128]{1,0:T(8,128)S(1)}, f32[8,128]{1,0:T(8,128)S(1)}, u32[]{:S(2)}, u32[]{:S(2)}) collective-permute-start(f32[8,128]{1,0:T(8,128)S(1)} %add_add_fusion.5), channel_id=1, source_target_pairs={{0,4},{1,5},{2,6},{3,7},{4,0},{5,1},{6,2},{7,3},{8,12},{9,13},{10,... | collective-permute-start | bytes 12296 | tf_op jit(solution)/shard_map/ppermute | solution.py:43
  59.3 4.8 %collective-permute-start.14 = (f32[8,128]{1,0:T(8,128)S(1)}, f32[8,128]{1,0:T(8,128)S(1)}, u32[]{:S(2)}, u32[]{:S(2)}) collective-permute-start(f32[8,128]{1,0:T(8,128)S(1)} %add_add_fusion.5), channel_id=1, source_target_pairs={{0,2},{1,3},{2,0},{3,1},{4,6},{5,7},{6,4},{7,5},{8,10},{9,11},{10,... | collective-permute-start | bytes 12296 | tf_op jit(solution)/shard_map/ppermute | solution.py:43
  62.5 1.6 %collective-permute-start.20 = (bf16[528,128]{1,0:T(8,128)(2,1)S(1)}, bf16[528,128]{1,0:T(8,128)(2,1)S(1)}, u32[]{:S(2)}, u32[]{:S(2)}) collective-permute-start(bf16[528,128]{1,0:T(8,128)(2,1)S(1)} %slice.9), channel_id=1, source_target_pairs={{0,8},{1,9},{2,10},{3,11},{4,12},{5,13},{6,14},{7,15},{8,0},{9,1},... | collective-permute-start | bytes 405512 | tf_op jit(solution)/shard_map/ppermute | solution.py:43
  62.8 1.6 %collective-permute-start.19 = (bf16[528,128]{1,0:T(8,128)(2,1)S(1)}, bf16[528,128]{1,0:T(8,128)(2,1)S(1)}, u32[]{:S(2)}, u32[]{:S(2)}) collective-permute-start(bf16[528,128]{1,0:T(8,128)(2,1)S(1)} %slice.8), channel_id=1, source_target_pairs={{0,8},{1,9},{2,10},{3,11},{4,12},{5,13},{6,14},{7,15},{8,0},{9,1},... | collective-permute-start | bytes 405512 | tf_op jit(solution)/shard_map/ppermute | solution.py:43
  69.5 2.0 %collective-permute-start.21 = (f32[88,128]{1,0:T(8,128)S(1)}, f32[88,128]{1,0:T(8,128)S(1)}, u32[]{:S(2)}, u32[]{:S(2)}) collective-permute-start(f32[88,128]{1,0:T(8,128)S(1)} %get-tuple-element.50), channel_id=1, source_target_pairs={{0,8},{1,9},{2,10},{3,11},{4,12},{5,13},{6,14},{7,15},{8,0},{9,1},... | collective-permute-start | bytes 135176 | tf_op jit(solution)/shard_map/ppermute | solution.py:43
  69.9 4.2 %collective-permute-start.22 = (f32[88,128]{1,0:T(8,128)S(1)}, f32[88,128]{1,0:T(8,128)S(1)}, u32[]{:S(2)}, u32[]{:S(2)}) collective-permute-start(f32[88,128]{1,0:T(8,128)S(1)} %get-tuple-element.51), channel_id=1, source_target_pairs={{0,16},{1,17},{2,18},{3,19},{4,20},{5,21},{6,22},{7,23},{8,24},{9,... | collective-permute-start | bytes 135176 | tf_op jit(solution)/shard_map/ppermute | solution.py:43
  69.9 4.2 %collective-permute-start.23 = (f32[88,128]{1,0:T(8,128)S(1)}, f32[88,128]{1,0:T(8,128)S(1)}, u32[]{:S(2)}, u32[]{:S(2)}) collective-permute-start(f32[88,128]{1,0:T(8,128)S(1)} %get-tuple-element.52), channel_id=1, source_target_pairs={{0,24},{1,25},{2,26},{3,27},{4,28},{5,29},{6,30},{7,31},{8,16},{9,... | collective-permute-start | bytes 135176 | tf_op jit(solution)/shard_map/ppermute | solution.py:43
  74.1 15.0 %collective-permute-start.26 = (f32[88,128]{1,0:T(8,128)S(1)}, f32[88,128]{1,0:T(8,128)S(1)}, u32[]{:S(2)}, u32[]{:S(2)}) collective-permute-start(f32[88,128]{1,0:T(8,128)S(1)} %add_add_fusion.3), channel_id=1, source_target_pairs={{0,96},{1,97},{2,98},{3,99},{4,100},{5,101},{6,102},{7,103},{8,104... | collective-permute-start | bytes 135176 | tf_op jit(solution)/shard_map/ppermute | solution.py:43
  82.3 10.9 %collective-permute-start.25 = (f32[88,128]{1,0:T(8,128)S(1)}, f32[88,128]{1,0:T(8,128)S(1)}, u32[]{:S(2)}, u32[]{:S(2)}) collective-permute-start(f32[88,128]{1,0:T(8,128)S(1)} %add_add_fusion.3), channel_id=1, source_target_pairs={{0,64},{1,65},{2,66},{3,67},{4,68},{5,69},{6,70},{7,71},{8,72},{9,... | collective-permute-start | bytes 135176 | tf_op jit(solution)/shard_map/ppermute | solution.py:43
  89.1 6.1 %collective-permute-start.24 = (f32[88,128]{1,0:T(8,128)S(1)}, f32[88,128]{1,0:T(8,128)S(1)}, u32[]{:S(2)}, u32[]{:S(2)}) collective-permute-start(f32[88,128]{1,0:T(8,128)S(1)} %add_add_fusion.3), channel_id=1, source_target_pairs={{0,32},{1,33},{2,34},{3,35},{4,36},{5,37},{6,38},{7,39},{8,40},{9,... | collective-permute-start | bytes 135176 | tf_op jit(solution)/shard_map/ppermute | solution.py:43
  95.3 6.1 %collective-permute-start.29 = (f32[88,128]{1,0:T(8,128)S(1)}, f32[88,128]{1,0:T(8,128)S(1)}, u32[]{:S(2)}, u32[]{:S(2)}) collective-permute-start(f32[88,128]{1,0:T(8,128)S(1)} %add_add_fusion.2), channel_id=1, source_target_pairs={{0,129},{1,128},{2,131},{3,130},{4,133},{5,132},{6,135},{7,134},{8... | collective-permute-start | bytes 135176 | tf_op jit(solution)/shard_map/ppermute | solution.py:43
  95.4 6.0 %collective-permute-start.28 = (f32[88,128]{1,0:T(8,128)S(1)}, f32[88,128]{1,0:T(8,128)S(1)}, u32[]{:S(2)}, u32[]{:S(2)}) collective-permute-start(f32[88,128]{1,0:T(8,128)S(1)} %add_add_fusion.2), channel_id=1, source_target_pairs={{0,1},{1,0},{2,3},{3,2},{4,5},{5,4},{6,7},{7,6},{8,9},{9,8},{10,11... | collective-permute-start | bytes 135176 | tf_op jit(solution)/shard_map/ppermute | solution.py:43
  95.7 6.2 %collective-permute-start.27 = (f32[88,128]{1,0:T(8,128)S(1)}, f32[88,128]{1,0:T(8,128)S(1)}, u32[]{:S(2)}, u32[]{:S(2)}) collective-permute-start(f32[88,128]{1,0:T(8,128)S(1)} %add_add_fusion.2), channel_id=1, source_target_pairs={{0,128},{1,129},{2,130},{3,131},{4,132},{5,133},{6,134},{7,135},{8... | collective-permute-start | bytes 135176 | tf_op jit(solution)/shard_map/ppermute | solution.py:43
  99.4 6.7 %collective-permute-start.36 = (bf16[8,64,128]{2,1,0:T(8,128)(2,1)S(1)}, bf16[8,64,128]{2,1,0:T(8,128)(2,1)S(1)}, u32[]{:S(2)}, u32[]{:S(2)}) collective-permute-start(bf16[8,64,128]{2,1,0:T(8,128)(2,1)S(1)} %get-tuple-element.55), channel_id=1, source_target_pairs={{0,8},{8,0},{16,24},{24,16},{32,40},{40,32},{48,56},{56,48},{64,72... | collective-permute-start | bytes 393224 | tf_op jit(solution)/shard_map/ppermute | solution.py:50
  99.4 8.4 %collective-permute-start.37 = (bf16[8,64,128]{2,1,0:T(8,128)(2,1)S(1)}, bf16[8,64,128]{2,1,0:T(8,128)(2,1)S(1)}, u32[]{:S(2)}, u32[]{:S(2)}) collective-permute-start(bf16[8,64,128]{2,1,0:T(8,128)(2,1)S(1)} %get-tuple-element.56), channel_id=1, source_target_pairs={{8,16},{16,8},{24,32},{32,24},{40,48},{48,40},{56,64},{64,56},{72,... | collective-permute-start | bytes 393224 | tf_op jit(solution)/shard_map/ppermute | solution.py:50
  102.0 11.9 %collective-permute-start.32 = (f32[88,128]{1,0:T(8,128)S(1)}, f32[88,128]{1,0:T(8,128)S(1)}, u32[]{:S(2)}, u32[]{:S(2)}) collective-permute-start(f32[88,128]{1,0:T(8,128)S(1)} %add_add_fusion.1), channel_id=1, source_target_pairs={{0,6},{1,7},{2,4},{3,5},{4,2},{5,3},{6,0},{7,1},{8,14},{9,15},{10,... | collective-permute-start | bytes 135176 | tf_op jit(solution)/shard_map/ppermute | solution.py:43
  103.3 10.6 %collective-permute-start.31 = (f32[88,128]{1,0:T(8,128)S(1)}, f32[88,128]{1,0:T(8,128)S(1)}, u32[]{:S(2)}, u32[]{:S(2)}) collective-permute-start(f32[88,128]{1,0:T(8,128)S(1)} %add_add_fusion.1), channel_id=1, source_target_pairs={{0,4},{1,5},{2,6},{3,7},{4,0},{5,1},{6,2},{7,3},{8,12},{9,13},{10,... | collective-permute-start | bytes 135176 | tf_op jit(solution)/shard_map/ppermute | solution.py:43
  104.7 9.2 %collective-permute-start.30 = (f32[88,128]{1,0:T(8,128)S(1)}, f32[88,128]{1,0:T(8,128)S(1)}, u32[]{:S(2)}, u32[]{:S(2)}) collective-permute-start(f32[88,128]{1,0:T(8,128)S(1)} %add_add_fusion.1), channel_id=1, source_target_pairs={{0,2},{1,3},{2,0},{3,1},{4,6},{5,7},{6,4},{7,5},{8,10},{9,11},{10,... | collective-permute-start | bytes 135176 | tf_op jit(solution)/shard_map/ppermute | solution.py:43
  108.3 7.6 %collective-permute-start.38 = (bf16[3,64,128]{2,1,0:T(8,128)(2,1)S(1)}, bf16[3,64,128]{2,1,0:T(8,128)(2,1)S(1)}, u32[]{:S(2)}, u32[]{:S(2)}) collective-permute-start(bf16[3,64,128]{2,1,0:T(8,128)(2,1)S(1)} %get-tuple-element.57), channel_id=1, source_target_pairs={{0,1},{1,0},{2,3},{3,2},{4,5},{5,4},{6,7},{7,6},{8,9},{9,8},{10,11... | collective-permute-start | bytes 147464 | tf_op jit(solution)/shard_map/ppermute | solution.py:50
  109.0 8.4 %collective-permute-start.39 = (bf16[3,64,128]{2,1,0:T(8,128)(2,1)S(1)}, bf16[3,64,128]{2,1,0:T(8,128)(2,1)S(1)}, u32[]{:S(2)}, u32[]{:S(2)}) collective-permute-start(bf16[3,64,128]{2,1,0:T(8,128)(2,1)S(1)} %get-tuple-element.58), channel_id=1, source_target_pairs={{1,2},{2,1},{3,4},{4,3},{5,6},{6,5},{9,10},{10,9},{11,12},{12,11},... | collective-permute-start | bytes 147464 | tf_op jit(solution)/shard_map/ppermute | solution.py:50
  113.9 5.8 %collective-permute-start.35 = (f32[88,128]{1,0:T(8,128)S(1)}, f32[88,128]{1,0:T(8,128)S(1)}, u32[]{:S(2)}, u32[]{:S(2)}) collective-permute-start(f32[88,128]{1,0:T(8,128)S(1)} %add_add_fusion.got0), channel_id=1, source_target_pairs={{0,24},{1,25},{2,26},{3,27},{4,28},{5,29},{6,30},{7,31},{8,16},{9,... | collective-permute-start | bytes 135176 | tf_op jit(solution)/shard_map/ppermute | solution.py:43
  114.0 5.7 %collective-permute-start.34 = (f32[88,128]{1,0:T(8,128)S(1)}, f32[88,128]{1,0:T(8,128)S(1)}, u32[]{:S(2)}, u32[]{:S(2)}) collective-permute-start(f32[88,128]{1,0:T(8,128)S(1)} %add_add_fusion.got0), channel_id=1, source_target_pairs={{0,16},{1,17},{2,18},{3,19},{4,20},{5,21},{6,22},{7,23},{8,24},{9,... | collective-permute-start | bytes 135176 | tf_op jit(solution)/shard_map/ppermute | solution.py:43
  114.1 5.6 %collective-permute-start.33 = (f32[88,128]{1,0:T(8,128)S(1)}, f32[88,128]{1,0:T(8,128)S(1)}, u32[]{:S(2)}, u32[]{:S(2)}) collective-permute-start(f32[88,128]{1,0:T(8,128)S(1)} %add_add_fusion.got0), channel_id=1, source_target_pairs={{0,8},{1,9},{2,10},{3,11},{4,12},{5,13},{6,14},{7,15},{8,0},{9,1},... | collective-permute-start | bytes 135176 | tf_op jit(solution)/shard_map/ppermute | solution.py:43
